TPU v7x, 32 devices: a whole 2x2x4 slice. The times are simulated.
32 devices in a mesh: frame: 4 (over y, x), space: 8 (over z, core).
Axes of the slice: x: 2, y: 2, z: 4, core: 2. Of those that a mesh axis runs over, the one named last changes fastest.
Arguments:
- queries: bfloat16 [4096, 3072], P(('frame', 'space')), as said below
- keys: bfloat16 [4096, 3072], P(('frame', 'space')), as said below
- values: bfloat16 [4096, 3072], P(('frame', 'space')), may hold values from -5 to 5
- level_weight: float32 [3, 24, 4096], P(None, None, ('frame', 'space')), may hold values from 0.2 to 2
- frame_len: int32 [32, 4], P(('frame', 'space')), may hold values from 1 to 53, 128 in all within a row
- window_back: int32 [32, 4], P(('frame', 'space')), may hold values from 2 to 63
Outputs:
- mixed: bfloat16 [4096, 3072], P(('frame', 'space'))
Inputs may be any that keep to these rules, and one draw needn't show every extreme that they name: `queries`: entries up to 60 in magnitude. `keys`: entries up to 4 in magnitude. `frame_len`: each row is the frame lengths of one device's 128 tokens, summing to 128; the longest frame of each row has exactly 53 tokens.
All inputs are finite; a program needn't handle non-finite values.
Results may differ from a plain program's by a relative error of at most 0.0085.
Values may be sent and summed in bfloat16 or wider, within the bound.
No kernel may reach another device: no remote copies, remote signals or barrier semaphores. Data moves between devices by JAX's collectives and lax.ppermute only.
A program may use at most 64 MiB of HBM per device.

v0:
```python
import math

import jax
import jax.numpy as jnp
from jax import lax
from jax.sharding import PartitionSpec as P

HEADS = 24
HEAD_DIM = 128


EPSILON = 1e-06


def unit_rows(matrix):
    return (matrix * lax.rsqrt(jnp.mean(matrix * matrix, -1, keepdims=True) + EPSILON)).astype(
        jnp.bfloat16
    )


def visible_mask(lengths, backward, count):
    starts = jnp.cumsum(lengths) - lengths
    lowest = jnp.maximum(starts - backward, 0)
    position = jnp.arange(count, dtype=jnp.int32)
    inside = (position[:, None] >= starts[None, :]).astype(jnp.int32)
    frame_of = jnp.sum(inside, 1) - 1
    onehot = frame_of[:, None] == jnp.arange(lengths.shape[0], dtype=jnp.int32)[None, :]
    floor_row = jnp.sum(jnp.where(onehot, lowest[None, :], 0), 1)
    return (position[None, :] <= position[:, None]) & (position[None, :] >= floor_row[:, None])


def causal_mix(query_heads, key_heads, value_heads, visible, heads, head_dim):
    pieces = []
    for first_head in range(0, heads, 4):
        query_part = query_heads[:, first_head : first_head + 4]
        key_part = key_heads[:, first_head : first_head + 4]
        value_part = value_heads[:, first_head : first_head + 4]
        scores = jnp.einsum(
            "thd,shd->hts", query_part, key_part, preferred_element_type=jnp.float32
        ) / math.sqrt(head_dim)
        scores = jnp.where(visible[None], scores, -jnp.inf)
        row_max = jnp.max(scores, -1, keepdims=True)
        weights = jnp.exp(scores - row_max)
        totals = jnp.sum(weights, -1)
        mixed_part = jnp.einsum(
            "hts,shd->thd",
            weights.astype(jnp.bfloat16),
            value_part,
            preferred_element_type=jnp.float32,
        )
        pieces.append(mixed_part / jnp.transpose(totals)[:, :, None])
    return jnp.concatenate(pieces, 1)


def body(queries, keys, values, level_weight, frame_len, window_back):
    tok_rows = queries.shape[0]
    frames_total = lax.axis_size("frame")
    frame_pos = lax.axis_index("frame")
    space_count = lax.axis_size("space")
    query_heads = queries.reshape(tok_rows, HEADS, HEAD_DIM)
    key_heads = keys.reshape(tok_rows, HEADS, HEAD_DIM)
    value_heads = values.reshape(tok_rows, HEADS, HEAD_DIM)
    normal_k = unit_rows(key_heads.astype(jnp.float32))
    local_state = jnp.einsum(
        "thd,the->hde", normal_k, value_heads, preferred_element_type=jnp.float32
    )
    state_rows = local_state.reshape(HEADS * HEAD_DIM, HEAD_DIM)
    block_part = lax.psum_scatter(state_rows, "space", scatter_dimension=0, tiled=True)
    tree_depth = frames_total.bit_length() - 1
    levels = []
    all_blocks = lax.all_gather(
        block_part[None].astype(jnp.bfloat16), "frame", axis=0, tiled=True
    ).astype(jnp.float32)
    block_ids = jnp.arange(frames_total, dtype=jnp.int32)
    for bit_index in range(tree_depth):
        start_block = frame_pos // 2 ** (bit_index + 1) * 2 ** (bit_index + 1)
        bit_set = frame_pos // 2**bit_index % 2
        inside = (
            (block_ids >= start_block) & (block_ids < start_block + 2**bit_index) & (bit_set == 1)
        )
        levels.append(jnp.sum(jnp.where(inside[:, None, None], all_blocks, 0.0), 0))
    level_rows = jnp.stack(levels).astype(jnp.bfloat16)
    level_rows = lax.all_gather(level_rows, "space", axis=1, tiled=True)
    level_heads = level_rows.reshape(tree_depth, HEADS, HEAD_DIM, HEAD_DIM)
    visible = visible_mask(frame_len[0], window_back[0], tok_rows)
    local_mix = causal_mix(query_heads, key_heads, value_heads, visible, HEADS, HEAD_DIM)
    result = local_mix * jnp.transpose(level_weight[0])[:, :, None]
    normal_q = unit_rows(query_heads.astype(jnp.float32))
    level_reads = jnp.einsum(
        "thd,lhde->lthe", normal_q, level_heads, preferred_element_type=jnp.float32
    )
    block_tokens = tok_rows * space_count
    for level_index in range(tree_depth):
        level_scale = 1.0 / math.sqrt(HEAD_DIM * 2**level_index * block_tokens)
        result = result + jnp.transpose(level_weight[1 + level_index])[:, :, None] * (
            level_scale * level_reads[level_index]
        )
    return result.reshape(tok_rows, HEADS * HEAD_DIM).astype(jnp.bfloat16)


def solution(mesh):
    return jax.shard_map(
        body,
        mesh=mesh,
        in_specs=(
            P(("frame", "space"), None),
            P(("frame", "space"), None),
            P(("frame", "space"), None),
            P(None, None, ("frame", "space")),
            P(("frame", "space"), None),
            P(("frame", "space"), None),
        ),
        out_specs=P(("frame", "space"), None),
        check_vma=False,
    )
```

profile of v0, /device:TPU:0, one launch (start us, length us, event | category | flops | bytes accessed | tf_op | source)
XLA Modules:
  0.0 96.1 jit_solution(5063917029954363267)
XLA Ops:
  6.5 1.6 %copy.52 = bf16[128,3072]{0,1:T(8,128)(2,1)S(1)} copy(bf16[128,3072]{1,0:T(8,128)(2,1)} %param.7) | data formatting | bytes 1572864 | tf_op args[1]
  8.1 0.4 copy.54
  8.7 1.8 %fusion.30 = f32[24,128,128]{2,1,0:T(8,128)} fusion(bf16[128,24,128]{0,2,1:T(8,128)(2,1)S(1)} %bitcast.124, bf16[128,24,128]{0,2,1:T(8,128)(2,1)S(1)} %bitcast.111, f32[128,24]{0,1:T(8,128)S(1)} %add_rsqrt_fusion.1), kind=kOutput, calls=%fused_computation.50 | convolution fusion | flops 101842944 | bytes 3158016 | tf_op jit(solution)/shard_map/thd,the->hde/dot_general | solution.py:64
  10.6 1.0 %copy-done.3 = bf16[128,3072]{1,0:T(8,128)(2,1)S(1)} copy-done((bf16[128,3072]{1,0:T(8,128)(2,1)S(1)}, bf16[128,3072]{1,0:T(8,128)(2,1)}, u32[]{:S(2)}) %copy-start.3) | copy-done | bytes 786456
  11.7 0.4 copy.50
  12.5 0.3 fusion.72
  12.8 0.3 fusion.73
  13.1 0.3 fusion.74
  13.4 0.3 fusion.75
  13.7 0.9 fusion.76
  14.7 32.9 %reduce-scatter.2.cloned.1.call-done = f32[384,128]{1,0:T(8,128)} async-done(((f32[3072,128]{1,0:T(8,128)}), f32[384,128]{1,0:T(8,128)}) %reduce-scatter.2.cloned.1.call-update) | async-done | bytes 196624 | tf_op jit(solution)/shard_map/reduce_scatter | solution.py:68
  47.6 0.9 convert_element_type.55
  48.6 9.4 %all-gather = bf16[1536,128]{1,0:T(8,128)(2,1)S(1)} all-gather(bf16[384,128]{1,0:T(8,128)(2,1)S(1)} %convert_element_type.55), channel_id=2, replica_groups=mesh['frame'=4,'space'=8] {'frame'}, dimensions={0}, use_global_device_ids=true | all-gather | bytes 491520 | tf_op jit(solution)/shard_map/all_gather | solution.py:71
  57.9 0.3 fusion.26
  58.2 0.7 pad_maximum_fusion
  58.9 1.0 %fusion.42 = f32[4,128]{1,0:T(4,128)S(1)} fusion(f32[4,128,128]{1,2,0:T(8,128)} %get-tuple-element.23, f32[4,128]{1,0:T(4,128)S(1)} %get-tuple-element.22), kind=kLoop, calls=%fused_computation.68 | loop fusion | flops 130560 | bytes 266240 | tf_op jit(solution)/shard_map/reduce_sum | solution.py:44
  59.9 0.3 fusion.77
  60.5 0.2 fusion.23
  60.7 0.2 fusion.21
  61.1 0.6 copy-done.4
  61.8 0.2 fusion.15
  62.1 1.6 %copy.76 = f32[128,3072]{1,0:T(8,128)} copy(f32[128,3072]{0,1:T(8,128)S(1)} %bitcast.119) | data formatting | bytes 3145728 | tf_op jit(solution)/shard_map/mul | solution.py:87
  64.2 17.2 %all-gather.3.cloned.1.call-done = bf16[2,3072,128]{2,1,0:T(8,128)(2,1)} async-done(((bf16[2,384,128]{2,1,0:T(8,128)(2,1)}), bf16[2,3072,128]{2,1,0:T(8,128)(2,1)}) %all-gather.3.cloned.1.call-update) | async-done | bytes 1572880 | tf_op jit(solution)/shard_map/all_gather | solution.py:83
  81.4 2.0 %convolution_bitcast_fusion = f32[2,128,24,128]{1,3,0,2:T(8,128)S(1)} fusion(bf16[2,24,128,128]{3,2,1,0:T(8,128)(2,1)} %bitcast.132, bf16[128,24,128]{0,2,1:T(8,128)(2,1)S(1)} %bitcast.109, f32[128,24]{0,1:T(8,128)S(1)} %add_rsqrt_fusion), kind=kOutput, calls=%fused_computation.4 | convolution fusion | flops 202506240 | bytes 5517312 | tf_op jit(solution)/shard_map/thd,lhde->lthe/dot_general | solution.py:89
  83.4 0.2 fusion.71
  83.6 1.6 %copy.75 = f32[128,3072]{1,0:T(8,128)} copy(f32[128,3072]{0,1:T(8,128)S(1)} %bitcast.121) | data formatting | bytes 3145728 | tf_op jit(solution)/shard_map/squeeze | solution.py:96
  85.3 0.5 copy.78
  85.7 0.5 mul.97
  86.2 0.5 mul.104
  86.7 0.4 copy-done
  87.1 0.5 copy-done.1
  87.6 1.6 %fusion.5 = bf16[128,3072]{1,0:T(8,128)(2,1)} fusion(f32[128,3072]{1,0:T(8,128)S(1)} %copy.78, f32[16,8,24,128]{3,2,1,0:T(8,128)S(1)} %bitcast.123, f32[128,3072]{1,0:T(8,128)S(1)} %copy-done, f32[128,3072]{1,0:T(8,128)S(1)} %copy-done.1, f32[16,8,24,128]{3,2,1,0:T(8,128)S(1)} %bitcast.122), kind=kLoop, calls=%fused_computation.11 | loop fusion | flops 1966080 | bytes 8650752 | tf_op jit(solution)/shard_map/convert_element_type | solution.py:98
  (39 shorter events, 2.0 us)
Async XLA Ops:
  6.5 1.6 %copy-start.2 = (bf16[128,3072]{1,0:T(8,128)(2,1)S(1)}, bf16[128,3072]{1,0:T(8,128)(2,1)}, u32[]{:S(2)}) copy-start(bf16[128,3072]{1,0:T(8,128)(2,1)} %param.8) | copy-start | bytes 2359300
  6.5 41.1 %reduce-scatter.2.cloned.1.call-start = ((), (), s32[]{:S(2)}) async-start(), calls=%async_computation.1 | async-start | bytes 1769472 | tf_op jit(solution)/shard_map/reduce_scatter | solution.py:68
  10.5 1.1 %copy-start.3 = (bf16[128,3072]{1,0:T(8,128)(2,1)S(1)}, bf16[128,3072]{1,0:T(8,128)(2,1)}, u32[]{:S(2)}) copy-start(bf16[128,3072]{1,0:T(8,128)(2,1)} %param.6) | copy-start | bytes 2359300
  10.5 1.5 %copy-start.6 = (s32[1,4]{1,0:T(1,128)S(1)}, s32[1,4]{1,0:T(1,128)}, u32[]{:S(2)}) copy-start(s32[1,4]{1,0:T(1,128)} %param.10) | copy-start | bytes 52
  10.5 1.7 %copy-start.7 = (s32[1,4]{1,0:T(1,128)S(1)}, s32[1,4]{1,0:T(1,128)}, u32[]{:S(2)}) copy-start(s32[1,4]{1,0:T(1,128)} %param.11) | copy-start | bytes 52
  10.6 70.8 %all-gather.3.cloned.1.call-start = ((), (), s32[]{:S(2)}) async-start(), calls=%async_computation.2 | async-start | bytes 1769472 | tf_op jit(solution)/shard_map/all_gather | solution.py:83
  48.6 11.7 %copy-start.5 = (f32[3,24,128]{2,1,0:T(8,128)S(1)}, f32[3,24,128]{2,1,0:T(8,128)}, u32[]{:S(2)}) copy-start(f32[3,24,128]{2,1,0:T(8,128)} %param.9) | copy-start | bytes 110596
  60.7 1.0 copy-start.4
  85.7 1.4 %copy-start = (f32[128,3072]{1,0:T(8,128)S(1)}, f32[128,3072]{1,0:T(8,128)}, u32[]{:S(2)}) copy-start(f32[128,3072]{1,0:T(8,128)} %copy.76) | copy-start | bytes 4718596
  85.7 1.9 %copy-start.1 = (f32[128,3072]{1,0:T(8,128)S(1)}, f32[128,3072]{1,0:T(8,128)}, u32[]{:S(2)}) copy-start(f32[128,3072]{1,0:T(8,128)} %copy.75) | copy-start | bytes 4718596
Sparse Core Ops, SparseCore 0:
  10.7 36.8 reduce-scatter.1
  59.1 22.2 all-gather.2
where the time goes:
time: 96.4 us; the launch traced here: 96.1 us
  waiting for transfers between devices  50.2 us (52%)
  between operations  13.7 us (14%)
  local copies, waits for them, and re-layouts  9.88 us (10%)
  blocking collectives  9.38 us (10%)
  matrix products  7.17 us (7%)
  other arithmetic  5.73 us (6%)
    reduce_scatter x1, waiting for transfers between devices, body(): lax.psum_scatter(state_rows, 'space', scatter_dimension=0, tiled=True)  32.9 us
    all_gather x1, waiting for transfers between devices, body(): level_rows = lax.all_gather(level_rows, 'space', axis=1, tiled=True)  17.2 us
    all_gather x1, blocking collectives, body(): lax.all_gather(block_part[None].astype(jnp.bfloat16), 'frame', axis=0, ti...  9.38 us
    unnamed x19, local copies, waits for them, and re-layouts  4.84 us
    dot_general x6, matrix products, causal_mix(): jnp.einsum('thd,shd->hts', query_part, key_part, preferred_element_type=j...  2.21 us
    squeeze x2, local copies, waits for them, and re-layouts, body(): level_reads[level_index]  2.08 us
    dot_general x1, matrix products, body(): jnp.einsum('thd,lhde->lthe', normal_q, level_heads, preferred_element_typ...  2.03 us
  transfers between devices with their start and end apart: 2, of which 2 were waited for; matrix products, arithmetic and copies ran while one was open for 8% of the time, Pallas kernels for 0%

commit v1 on v0

v1 whole, which is shorter than its diff:
```python
import functools
import math

import jax
import jax.numpy as jnp
from jax import lax
from jax.experimental import pallas as pl
from jax.experimental.pallas import tpu as pltpu
from jax.sharding import PartitionSpec as P

HEADS = 24
HEAD_DIM = 128
EPSILON = 1e-06
VMEM_LIMIT = 40 * 1024 * 1024

F32, BF16 = jnp.float32, jnp.bfloat16
WHOLE = pl.BlockSpec(memory_space=pltpu.VMEM)
SCALARS = pl.BlockSpec(memory_space=pltpu.SMEM)
PARAMS = pltpu.CompilerParams(vmem_limit_bytes=VMEM_LIMIT)


def inverse_rms(rows):
    return lax.rsqrt(jnp.mean(rows * rows, -1, keepdims=True) + EPSILON)


def columns(head):
    return pl.ds(pl.multiple_of(head * HEAD_DIM, HEAD_DIM), HEAD_DIM)


def state_kernel(first_ref, key_ref, value_ref, out_ref):
    for h in range(out_ref.shape[0] // HEAD_DIM):
        at = columns(first_ref[0] + h)
        key_rows = key_ref[:, at].astype(F32)
        normal = (key_rows * inverse_rms(key_rows)).astype(BF16)
        state = lax.dot_general(
            normal, value_ref[:, at], (((0,), (0,)), ((), ())), preferred_element_type=F32
        )
        out_ref[h * HEAD_DIM : (h + 1) * HEAD_DIM, :] = state.astype(out_ref.dtype)


def local_state(first_head, keys, values, heads, dtype):
    dim = HEAD_DIM
    rows = keys.shape[0]
    return pl.pallas_call(
        state_kernel,
        out_shape=jax.ShapeDtypeStruct((heads * dim, dim), dtype),
        in_specs=[SCALARS, WHOLE, WHOLE],
        out_specs=WHOLE,
        compiler_params=PARAMS,
        cost_estimate=pl.CostEstimate(
            flops=2 * heads * rows * dim * dim,
            bytes_accessed=6 * heads * rows * dim,
            transcendentals=heads * rows,
        ),
    )(first_head, keys, values)


def split_kernel(order_ref, mine_ref, other_ref, own_ref, *piece_refs):
    rows = own_ref.shape[0]
    for d, ref in enumerate((own_ref,) + piece_refs):
        at = pl.ds(pl.multiple_of(order_ref[d] * rows, rows), rows)
        ref[...] = (mine_ref[at, :] + other_ref[at, :].astype(F32)).astype(ref.dtype)


def split_pieces(order, mine, other, chips):
    rows = mine.shape[0] // chips
    shape = (rows, HEAD_DIM)
    return pl.pallas_call(
        split_kernel,
        out_shape=[jax.ShapeDtypeStruct(shape, F32)]
        + [jax.ShapeDtypeStruct(shape, BF16)] * (chips - 1),
        in_specs=[SCALARS, WHOLE, WHOLE],
        out_specs=[WHOLE] * chips,
        compiler_params=PARAMS,
    )(order, mine, other)


def local_kernel(
    length_ref, back_ref, scale_ref, query_ref, key_ref, value_ref, weight_ref, local_ref, read_ref
):
    tokens = query_ref.shape[0]
    levels = read_ref.shape[0]
    row = lax.broadcasted_iota(jnp.int32, (tokens, tokens), 0)
    col = lax.broadcasted_iota(jnp.int32, (tokens, tokens), 1)
    start = jnp.int32(0)
    floor = jnp.zeros((tokens, tokens), jnp.int32)
    for k in range(length_ref.shape[1]):
        lowest = jnp.maximum(start - back_ref[0, k], 0)
        floor = jnp.where(row >= start, lowest, floor)
        start = start + length_ref[0, k]
    visible = (col <= row) & (col >= floor)
    for h in range(HEADS):
        at = slice(h * HEAD_DIM, (h + 1) * HEAD_DIM)
        query = query_ref[:, at]
        scores = lax.dot_general(
            query, key_ref[:, at], (((1,), (1,)), ((), ())), preferred_element_type=F32
        ) * (1.0 / math.sqrt(HEAD_DIM))
        scores = jnp.where(visible, scores, -jnp.inf)
        weights = jnp.exp(scores - jnp.max(scores, -1, keepdims=True))
        total = jnp.sum(weights, -1, keepdims=True)
        mixed = jnp.dot(weights.astype(BF16), value_ref[:, at], preferred_element_type=F32)
        local_ref[:, at] = mixed * (weight_ref[:, h : h + 1] / total)
        query = query.astype(F32)
        inverse = inverse_rms(query)
        for level in range(levels):
            which = (1 + level) * HEADS + h
            gain = inverse * (weight_ref[:, which : which + 1] * scale_ref[level])
            read_ref[level, :, at] = (query * gain).astype(BF16)


def local_part(frame_len, window_back, scales, queries, keys, values, weights):
    tokens, width = queries.shape
    levels = scales.shape[0]
    return pl.pallas_call(
        local_kernel,
        out_shape=[
            jax.ShapeDtypeStruct((tokens, width), F32),
            jax.ShapeDtypeStruct((levels, tokens, width), BF16),
        ],
        in_specs=[SCALARS] * 3 + [WHOLE] * 4,
        out_specs=[WHOLE] * 2,
        compiler_params=PARAMS,
        cost_estimate=pl.CostEstimate(
            flops=4 * tokens * tokens * width,
            bytes_accessed=14 * tokens * width,
            transcendentals=tokens * tokens * HEADS,
        ),
    )(frame_len, window_back, scales, queries, keys, values, weights)


def read_kernel(levels, first_ref, local_ref, read_ref, *refs):
    out_ref, piece_refs = refs[-1], refs[:-1]
    count = len(piece_refs) // levels
    for piece in range(count):
        heads = piece_refs[piece * levels].shape[0] // HEAD_DIM
        for h in range(heads):
            at = columns(first_ref[piece] + h)
            rows = slice(h * HEAD_DIM, (h + 1) * HEAD_DIM)
            result = local_ref[:, at]
            for level in range(levels):
                result = result + jnp.dot(
                    read_ref[level, :, at],
                    piece_refs[piece * levels + level][rows, :],
                    preferred_element_type=F32,
                )
            out_ref[:, at] = result.astype(BF16)


def read_levels(first, local, reads, pieces, levels):
    tokens, width = local.shape
    return pl.pallas_call(
        functools.partial(read_kernel, levels),
        out_shape=jax.ShapeDtypeStruct((tokens, width), BF16),
        in_specs=[SCALARS] + [WHOLE] * (2 + len(pieces)),
        out_specs=WHOLE,
        compiler_params=PARAMS,
    )(first, local, reads, *pieces)


def body(frames, space, queries, keys, values, level_weight, frame_len, window_back):
    tokens = queries.shape[0]
    frame_pos = lax.axis_index("frame")
    space_pos = lax.axis_index("space")
    depth = frames.bit_length() - 1
    group = math.gcd(space, HEADS)
    group = group & -group
    chips = group // 2
    core = space_pos % 2
    chip = space_pos // 2 % chips
    half_heads = HEADS // 2
    piece_heads = half_heads // chips

    def across_space(array, mask):
        return lax.ppermute(array, "space", [(s, s ^ mask) for s in range(space)])

    def across(array, mask, keep):
        pairs = [
            (f * space + s, f * space + (s ^ mask))
            for f in range(frames)
            if keep(f)
            for s in range(space)
        ]
        return lax.ppermute(array, ("frame", "space"), pairs)

    mine_at = (core * half_heads).astype(jnp.int32).reshape(1)
    other_at = ((1 - core) * half_heads).astype(jnp.int32).reshape(1)
    useful = lambda f: f < frames - 1
    outgoing = local_state(other_at, keys, values, half_heads, BF16)
    incoming = across(outgoing, 1, useful)
    mine = local_state(mine_at, keys, values, half_heads, F32)
    order = jnp.stack([chip ^ d for d in range(chips)]).astype(jnp.int32)
    own, *sends = split_pieces(order, mine, incoming, chips)
    got = [across(sends[d - 1], 2 * d, useful) for d in range(1, chips)]
    total = own
    for piece in got:
        total = total + piece.astype(F32)
    mask = group
    while mask < space:
        total = total + across_space(total.astype(BF16), mask).astype(F32)
        mask *= 2

    pieces = []
    for level in range(depth):
        last = level == depth - 1
        step = 1 << level
        wanted = lambda f: f & step or (not last and f >> level + 1 != frames - 1 >> level + 1)
        pairs = [(f ^ step, f) for f in range(frames) if wanted(f)]
        received = lax.ppermute(total.astype(BF16), "frame", pairs)
        if not last:
            total = total + received.astype(F32)
        has = lambda f, step=step: bool(f & step)
        by_chip = [received] + [across(received, 2 * d, has) for d in range(1, chips)]
        pieces.append([(piece, across(piece, 1, has)) for piece in by_chip])

    scales = jnp.stack(
        [
            ((frame_pos >> level) & 1).astype(F32)
            / math.sqrt(HEAD_DIM * 2**level * tokens * space)
            for level in range(depth)
        ]
    )
    weights = level_weight.reshape(-1, tokens).T
    local, reads = local_part(frame_len, window_back, scales, queries, keys, values, weights)

    flat, first = [], []
    for d in range(chips):
        for c in range(2):
            first.append((core ^ c) * half_heads + (chip ^ d) * piece_heads)
            flat.extend(pieces[level][d][c] for level in range(depth))
    return read_levels(jnp.stack(first).astype(jnp.int32), local, reads, flat, depth)


def solution(mesh):
    rows = P(("frame", "space"), None)
    return jax.shard_map(
        functools.partial(body, mesh.shape["frame"], mesh.shape["space"]),
        mesh=mesh,
        in_specs=(rows, rows, rows, P(None, None, ("frame", "space")), rows, rows),
        out_specs=rows,
        check_vma=False,
    )
```

time: 96.4 us -> 79.8 us (0.83)
  the two profiles are of different devices: /device:TPU:0 before, /device:TPU:7 now
where the time goes in v1:
time: 79.8 us; the launch traced here: 79.2 us
  starting transfers between devices  45.2 us (57%)
  waiting for transfers between devices  17.4 us (22%)
  Pallas kernels  13.3 us (17%)
  local copies, waits for them, and re-layouts  2.56 us (3%)
    ppermute x18, starting transfers between devices, across(): return lax.ppermute(array, ('frame', 'space'), pairs)  42.6 us
    ppermute x2, waiting for transfers between devices, body(): received = lax.ppermute(total.astype(BF16), 'frame', pairs)  17.3 us
    pallas_call x1, Pallas kernels, local_part(): pl.pallas_call(local_kernel, out_shape=[jax.ShapeDtypeStruct((tokens, wid...  9.35 us
    ppermute x2, starting transfers between devices, body(): received = lax.ppermute(total.astype(BF16), 'frame', pairs)  2.58 us
    unnamed x16, local copies, waits for them, and re-layouts  2.38 us
    pallas_call x1, Pallas kernels, read_levels(): pl.pallas_call(functools.partial(read_kernel, levels), out_shape=jax.Shap...  2.32 us
  transfers between devices with their start and end apart: 20, of which 1 were waited for; matrix products, arithmetic and copies ran while one was open for 0% of the time, Pallas kernels for 12%

profile of v1, /device:TPU:7, one launch (start us, length us, event | category | flops | bytes accessed | tf_op | source)
XLA Modules:
  0.0 79.2 jit_solution(12391931452677247591)
XLA Ops:
  0.0 1.1 %copy-done = bf16[128,3072]{1,0:T(8,128)(2,1)S(1)} copy-done((bf16[128,3072]{1,0:T(8,128)(2,1)S(1)}, bf16[128,3072]{1,0:T(8,128)(2,1)}, u32[]{:S(2)}) %copy-start) | copy-done | bytes 786456
  1.1 1.1 %copy-done.2 = bf16[128,3072]{1,0:T(8,128)(2,1)S(1)} copy-done((bf16[128,3072]{1,0:T(8,128)(2,1)S(1)}, bf16[128,3072]{1,0:T(8,128)(2,1)}, u32[]{:S(2)}) %copy-start.2) | copy-done | bytes 786456
  2.3 0.5 shard_map.66
  2.8 0.7 collective-permute-start
  3.5 0.1 copy-done.3
  3.6 0.5 shard_map.65.mine_ref
  4.2 0.1 pad_add_fusion.order_ref
  4.3 0.6 shard_map.67
  4.9 0.7 collective-permute-start.1
  5.6 0.7 collective-permute-start.2
  6.3 0.7 collective-permute-start.3
  7.0 1.3 %collective-permute-start.4 = (bf16[384,128]{1,0:T(8,128)(2,1)S(1)}, bf16[384,128]{1,0:T(8,128)(2,1)S(1)}, u32[]{:S(2)}, u32[]{:S(2)}) collective-permute-start(bf16[384,128]{1,0:T(8,128)(2,1)S(1)} %fusion), channel_id=1, source_target_pairs={{8,0},{0,8},{16,24},{9,1},{1,9},{17,25},{10,2},{2,10},{18,26},{11,... | collective-permute-start | bytes 294920 | tf_op jit(solution)/shard_map/ppermute | solution.py:208
  8.3 17.3 %collective-permute-done.4.refs_0_ = bf16[384,128]{1,0:T(8,128)(2,1)S(1)} collective-permute-done((bf16[384,128]{1,0:T(8,128)(2,1)S(1)}, bf16[384,128]{1,0:T(8,128)(2,1)S(1)}, u32[]{:S(2)}, u32[]{:S(2)}) %collective-permute-start.4) | collective-permute-done | bytes 98336 | tf_op jit(solution)/shard_map/ppermute | solution.py:208
  25.7 1.3 %collective-permute-start.5 = (bf16[384,128]{1,0:T(8,128)(2,1)S(1)}, bf16[384,128]{1,0:T(8,128)(2,1)S(1)}, u32[]{:S(2)}, u32[]{:S(2)}) collective-permute-start(bf16[384,128]{1,0:T(8,128)(2,1)S(1)} %add_convert_fusion), channel_id=1, source_target_pairs={{0,16},{8,24},{1,17},{9,25},{2,18},{10,26},{3,19},{11,27},{4,20},{... | collective-permute-start | bytes 294920 | tf_op jit(solution)/shard_map/ppermute | solution.py:208
  27.0 2.1 %collective-permute-start.16 = (bf16[384,128]{1,0:T(8,128)(2,1)S(1)}, bf16[384,128]{1,0:T(8,128)(2,1)S(1)}, u32[]{:S(2)}, u32[]{:S(2)}) collective-permute-start(bf16[384,128]{1,0:T(8,128)(2,1)S(1)} %collective-permute-done.4.refs_0_), channel_id=1, source_target_pairs={{8,14},{9,15},{10,12},{11,13},{12,10},{13,11},{14,8},{15,9},{24,30... | collective-permute-start | bytes 294920 | tf_op jit(solution)/shard_map/ppermute | solution.py:183
  29.1 5.1 %collective-permute-start.12 = (bf16[384,128]{1,0:T(8,128)(2,1)S(1)}, bf16[384,128]{1,0:T(8,128)(2,1)S(1)}, u32[]{:S(2)}, u32[]{:S(2)}) collective-permute-start(bf16[384,128]{1,0:T(8,128)(2,1)S(1)} %collective-permute-done.4.refs_0_), channel_id=1, source_target_pairs={{8,12},{9,13},{10,14},{11,15},{12,8},{13,9},{14,10},{15,11},{24,28... | collective-permute-start | bytes 294920 | tf_op jit(solution)/shard_map/ppermute | solution.py:183
  34.2 2.1 %collective-permute-start.8 = (bf16[384,128]{1,0:T(8,128)(2,1)S(1)}, bf16[384,128]{1,0:T(8,128)(2,1)S(1)}, u32[]{:S(2)}, u32[]{:S(2)}) collective-permute-start(bf16[384,128]{1,0:T(8,128)(2,1)S(1)} %collective-permute-done.4.refs_0_), channel_id=1, source_target_pairs={{8,10},{9,11},{10,8},{11,9},{12,14},{13,15},{14,12},{15,13},{24,26... | collective-permute-start | bytes 294920 | tf_op jit(solution)/shard_map/ppermute | solution.py:183
  36.3 5.7 %collective-permute-start.6 = (bf16[384,128]{1,0:T(8,128)(2,1)S(1)}, bf16[384,128]{1,0:T(8,128)(2,1)S(1)}, u32[]{:S(2)}, u32[]{:S(2)}) collective-permute-start(bf16[384,128]{1,0:T(8,128)(2,1)S(1)} %collective-permute-done.4.refs_0_), channel_id=1, source_target_pairs={{8,9},{9,8},{10,11},{11,10},{12,13},{13,12},{14,15},{15,14},{24,25... | collective-permute-start | bytes 294920 | tf_op jit(solution)/shard_map/ppermute | solution.py:183
  42.0 3.8 %collective-permute-start.17 = (bf16[384,128]{1,0:T(8,128)(2,1)S(1)}, bf16[384,128]{1,0:T(8,128)(2,1)S(1)}, u32[]{:S(2)}, u32[]{:S(2)}) collective-permute-start(bf16[384,128]{1,0:T(8,128)(2,1)S(1)} %collective-permute-done.5.refs_1_), channel_id=1, source_target_pairs={{16,22},{17,23},{18,20},{19,21},{20,18},{21,19},{22,16},{23,17},{2... | collective-permute-start | bytes 294920 | tf_op jit(solution)/shard_map/ppermute | solution.py:183
  45.8 1.9 %collective-permute-start.13 = (bf16[384,128]{1,0:T(8,128)(2,1)S(1)}, bf16[384,128]{1,0:T(8,128)(2,1)S(1)}, u32[]{:S(2)}, u32[]{:S(2)}) collective-permute-start(bf16[384,128]{1,0:T(8,128)(2,1)S(1)} %collective-permute-done.5.refs_1_), channel_id=1, source_target_pairs={{16,20},{17,21},{18,22},{19,23},{20,16},{21,17},{22,18},{23,19},{2... | collective-permute-start | bytes 294920 | tf_op jit(solution)/shard_map/ppermute | solution.py:183
  47.7 3.6 %collective-permute-start.9 = (bf16[384,128]{1,0:T(8,128)(2,1)S(1)}, bf16[384,128]{1,0:T(8,128)(2,1)S(1)}, u32[]{:S(2)}, u32[]{:S(2)}) collective-permute-start(bf16[384,128]{1,0:T(8,128)(2,1)S(1)} %collective-permute-done.5.refs_1_), channel_id=1, source_target_pairs={{16,18},{17,19},{18,16},{19,17},{20,22},{21,23},{22,20},{23,21},{2... | collective-permute-start | bytes 294920 | tf_op jit(solution)/shard_map/ppermute | solution.py:183
  51.3 2.8 %collective-permute-start.7 = (bf16[384,128]{1,0:T(8,128)(2,1)S(1)}, bf16[384,128]{1,0:T(8,128)(2,1)S(1)}, u32[]{:S(2)}, u32[]{:S(2)}) collective-permute-start(bf16[384,128]{1,0:T(8,128)(2,1)S(1)} %collective-permute-done.5.refs_1_), channel_id=1, source_target_pairs={{16,17},{17,16},{18,19},{19,18},{20,21},{21,20},{22,23},{23,22},{2... | collective-permute-start | bytes 294920 | tf_op jit(solution)/shard_map/ppermute | solution.py:183
  54.1 1.9 %collective-permute-start.18 = (bf16[384,128]{1,0:T(8,128)(2,1)S(1)}, bf16[384,128]{1,0:T(8,128)(2,1)S(1)}, u32[]{:S(2)}, u32[]{:S(2)}) collective-permute-start(bf16[384,128]{1,0:T(8,128)(2,1)S(1)} %collective-permute-done.16.refs_12_), channel_id=1, source_target_pairs={{8,9},{9,8},{10,11},{11,10},{12,13},{13,12},{14,15},{15,14},{24,25... | collective-permute-start | bytes 294920 | tf_op jit(solution)/shard_map/ppermute | solution.py:183
  56.1 0.1 copy.8
  56.2 0.1 stack.59.first_ref
  56.2 2.4 %collective-permute-start.14 = (bf16[384,128]{1,0:T(8,128)(2,1)S(1)}, bf16[384,128]{1,0:T(8,128)(2,1)S(1)}, u32[]{:S(2)}, u32[]{:S(2)}) collective-permute-start(bf16[384,128]{1,0:T(8,128)(2,1)S(1)} %collective-permute-done.12.refs_8_), channel_id=1, source_target_pairs={{8,9},{9,8},{10,11},{11,10},{12,13},{13,12},{14,15},{15,14},{24,25... | collective-permute-start | bytes 294920 | tf_op jit(solution)/shard_map/ppermute | solution.py:183
  58.7 1.9 %collective-permute-start.10 = (bf16[384,128]{1,0:T(8,128)(2,1)S(1)}, bf16[384,128]{1,0:T(8,128)(2,1)S(1)}, u32[]{:S(2)}, u32[]{:S(2)}) collective-permute-start(bf16[384,128]{1,0:T(8,128)(2,1)S(1)} %collective-permute-done.8.refs_4_), channel_id=1, source_target_pairs={{8,9},{9,8},{10,11},{11,10},{12,13},{13,12},{14,15},{15,14},{24,25... | collective-permute-start | bytes 294920 | tf_op jit(solution)/shard_map/ppermute | solution.py:183
  60.6 2.4 %collective-permute-start.19 = (bf16[384,128]{1,0:T(8,128)(2,1)S(1)}, bf16[384,128]{1,0:T(8,128)(2,1)S(1)}, u32[]{:S(2)}, u32[]{:S(2)}) collective-permute-start(bf16[384,128]{1,0:T(8,128)(2,1)S(1)} %collective-permute-done.17.refs_13_), channel_id=1, source_target_pairs={{16,17},{17,16},{18,19},{19,18},{20,21},{21,20},{22,23},{23,22},{2... | collective-permute-start | bytes 294920 | tf_op jit(solution)/shard_map/ppermute | solution.py:183
  63.0 1.9 %collective-permute-start.15 = (bf16[384,128]{1,0:T(8,128)(2,1)S(1)}, bf16[384,128]{1,0:T(8,128)(2,1)S(1)}, u32[]{:S(2)}, u32[]{:S(2)}) collective-permute-start(bf16[384,128]{1,0:T(8,128)(2,1)S(1)} %collective-permute-done.13.refs_9_), channel_id=1, source_target_pairs={{16,17},{17,16},{18,19},{19,18},{20,21},{21,20},{22,23},{23,22},{2... | collective-permute-start | bytes 294920 | tf_op jit(solution)/shard_map/ppermute | solution.py:183
  65.0 2.4 %collective-permute-start.11 = (bf16[384,128]{1,0:T(8,128)(2,1)S(1)}, bf16[384,128]{1,0:T(8,128)(2,1)S(1)}, u32[]{:S(2)}, u32[]{:S(2)}) collective-permute-start(bf16[384,128]{1,0:T(8,128)(2,1)S(1)} %collective-permute-done.9.refs_5_), channel_id=1, source_target_pairs={{16,17},{17,16},{18,19},{19,18},{20,21},{21,20},{22,23},{23,22},{2... | collective-permute-start | bytes 294920 | tf_op jit(solution)/shard_map/ppermute | solution.py:183
  67.5 9.3 %shard_map.64 = (f32[128,3072]{1,0:T(8,128)S(1)}, bf16[2,128,3072]{2,1,0:T(8,128)(2,1)S(1)}) custom-call(s32[1,4]{1,0:T(1,128)S(1)} %copy-done.5, s32[1,4]{1,0:T(1,128)S(1)} %copy-done.6, f32[2]{0:T(128)S(1)} %pad_maximum_fusion.scale_ref, bf16[128,3072]{1,0:T(8,128)(2,1)S(1)} %copy-done.4, bf16[128,3072]{1,0:T(8,128)(2,1)S(1)} %copy-done.1, ...), custom_call_target="tpu_custom_call" | custom-call | flops 201326592 | bytes 5505024 | tf_op jit(solution)/shard_map/pallas_call | solution.py:114
  76.9 2.3 %shard_map.68 = bf16[128,3072]{1,0:T(8,128)(2,1)} custom-call(s32[8]{0:T(128)S(1)} %stack.59.first_ref, f32[128,3072]{1,0:T(8,128)S(1)} %get-tuple-element.11.local_ref, bf16[2,128,3072]{2,1,0:T(8,128)(2,1)S(1)} %get-tuple-element.12.read_ref, bf16[384,128]{1,0:T(8,128)(2,1)S(1)} %collective-permute-done.4.refs_0_, ...), custom_call_target="tpu_custom_call" | custom-call | tf_op jit(solution)/shard_map/pallas_call | solution.py:151
  (35 shorter events, 0.3 us)
Async XLA Ops:
  0.0 1.1 %copy-start = (bf16[128,3072]{1,0:T(8,128)(2,1)S(1)}, bf16[128,3072]{1,0:T(8,128)(2,1)}, u32[]{:S(2)}) copy-start(bf16[128,3072]{1,0:T(8,128)(2,1)} %key_ref.5) | copy-start | bytes 2359300
  1.1 1.1 %copy-start.2 = (bf16[128,3072]{1,0:T(8,128)(2,1)S(1)}, bf16[128,3072]{1,0:T(8,128)(2,1)}, u32[]{:S(2)}) copy-start(bf16[128,3072]{1,0:T(8,128)(2,1)} %value_ref.5) | copy-start | bytes 2359300
  2.3 1.3 %copy-start.1 = (bf16[128,3072]{1,0:T(8,128)(2,1)S(1)}, bf16[128,3072]{1,0:T(8,128)(2,1)}, u32[]{:S(2)}) copy-start(bf16[128,3072]{1,0:T(8,128)(2,1)} %key_ref.5) | copy-start | bytes 2359300
  2.3 1.4 %copy-start.3 = (bf16[128,3072]{1,0:T(8,128)(2,1)S(1)}, bf16[128,3072]{1,0:T(8,128)(2,1)}, u32[]{:S(2)}) copy-start(bf16[128,3072]{1,0:T(8,128)(2,1)} %value_ref.5) | copy-start | bytes 2359300
  2.8 1.5 %collective-permute-start = (bf16[1536,128]{1,0:T(8,128)(2,1)S(1)}, bf16[1536,128]{1,0:T(8,128)(2,1)S(1)}, u32[]{:S(2)}, u32[]{:S(2)}) collective-permute-start(bf16[1536,128]{1,0:T(8,128)(2,1)S(1)} %shard_map.66), channel_id=1, source_target_pairs={{0,1},{1,0},{2,3},{3,2},{4,5},{5,4},{6,7},{7,6},{8,9},{9,8},{10,11... | collective-permute-start | bytes 1179656 | tf_op jit(solution)/shard_map/ppermute | solution.py:183
  4.2 51.9 %copy-start.7 = (f32[3,24,128]{2,1,0:T(8,128)S(1)}, f32[3,24,128]{2,1,0:T(8,128)}, u32[]{:S(2)}) copy-start(f32[3,24,128]{2,1,0:T(8,128)} %param.9) | copy-start | bytes 110596
  4.2 63.3 %copy-start.4 = (bf16[128,3072]{1,0:T(8,128)(2,1)S(1)}, bf16[128,3072]{1,0:T(8,128)(2,1)}, u32[]{:S(2)}) copy-start(bf16[128,3072]{1,0:T(8,128)(2,1)} %query_ref.1) | copy-start | bytes 2359300
  4.2 63.3 %copy-start.5 = (s32[1,4]{1,0:T(1,128)S(1)}, s32[1,4]{1,0:T(1,128)}, u32[]{:S(2)}) copy-start(s32[1,4]{1,0:T(1,128)} %length_ref.1) | copy-start | bytes 52
  4.2 63.3 %copy-start.6 = (s32[1,4]{1,0:T(1,128)S(1)}, s32[1,4]{1,0:T(1,128)}, u32[]{:S(2)}) copy-start(s32[1,4]{1,0:T(1,128)} %back_ref.1) | copy-start | bytes 52
  4.9 2.0 %collective-permute-start.1 = (bf16[384,128]{1,0:T(8,128)(2,1)S(1)}, bf16[384,128]{1,0:T(8,128)(2,1)S(1)}, u32[]{:S(2)}, u32[]{:S(2)}) collective-permute-start(bf16[384,128]{1,0:T(8,128)(2,1)S(1)} %get-tuple-element.14), channel_id=1, source_target_pairs={{0,2},{1,3},{2,0},{3,1},{4,6},{5,7},{6,4},{7,5},{8,10},{9,11},{10,... | collective-permute-start | bytes 294920 | tf_op jit(solution)/shard_map/ppermute | solution.py:183
  5.6 1.4 %collective-permute-start.2 = (bf16[384,128]{1,0:T(8,128)(2,1)S(1)}, bf16[384,128]{1,0:T(8,128)(2,1)S(1)}, u32[]{:S(2)}, u32[]{:S(2)}) collective-permute-start(bf16[384,128]{1,0:T(8,128)(2,1)S(1)} %get-tuple-element.15), channel_id=1, source_target_pairs={{0,4},{1,5},{2,6},{3,7},{4,0},{5,1},{6,2},{7,3},{8,12},{9,13},{10,... | collective-permute-start | bytes 294920 | tf_op jit(solution)/shard_map/ppermute | solution.py:183
  6.3 0.7 collective-permute-start.3
  7.0 18.6 %collective-permute-start.4 = (bf16[384,128]{1,0:T(8,128)(2,1)S(1)}, bf16[384,128]{1,0:T(8,128)(2,1)S(1)}, u32[]{:S(2)}, u32[]{:S(2)}) collective-permute-start(bf16[384,128]{1,0:T(8,128)(2,1)S(1)} %fusion), channel_id=1, source_target_pairs={{8,0},{0,8},{16,24},{9,1},{1,9},{17,25},{10,2},{2,10},{18,26},{11,... | collective-permute-start | bytes 294920 | tf_op jit(solution)/shard_map/ppermute | solution.py:208
  25.7 16.3 %collective-permute-start.5 = (bf16[384,128]{1,0:T(8,128)(2,1)S(1)}, bf16[384,128]{1,0:T(8,128)(2,1)S(1)}, u32[]{:S(2)}, u32[]{:S(2)}) collective-permute-start(bf16[384,128]{1,0:T(8,128)(2,1)S(1)} %add_convert_fusion), channel_id=1, source_target_pairs={{0,16},{8,24},{1,17},{9,25},{2,18},{10,26},{3,19},{11,27},{4,20},{... | collective-permute-start | bytes 294920 | tf_op jit(solution)/shard_map/ppermute | solution.py:208
  27.0 18.8 %collective-permute-start.16 = (bf16[384,128]{1,0:T(8,128)(2,1)S(1)}, bf16[384,128]{1,0:T(8,128)(2,1)S(1)}, u32[]{:S(2)}, u32[]{:S(2)}) collective-permute-start(bf16[384,128]{1,0:T(8,128)(2,1)S(1)} %collective-permute-done.4.refs_0_), channel_id=1, source_target_pairs={{8,14},{9,15},{10,12},{11,13},{12,10},{13,11},{14,8},{15,9},{24,30... | collective-permute-start | bytes 294920 | tf_op jit(solution)/shard_map/ppermute | solution.py:183
  29.1 18.6 %collective-permute-start.12 = (bf16[384,128]{1,0:T(8,128)(2,1)S(1)}, bf16[384,128]{1,0:T(8,128)(2,1)S(1)}, u32[]{:S(2)}, u32[]{:S(2)}) collective-permute-start(bf16[384,128]{1,0:T(8,128)(2,1)S(1)} %collective-permute-done.4.refs_0_), channel_id=1, source_target_pairs={{8,12},{9,13},{10,14},{11,15},{12,8},{13,9},{14,10},{15,11},{24,28... | collective-permute-start | bytes 294920 | tf_op jit(solution)/shard_map/ppermute | solution.py:183
  34.2 17.1 %collective-permute-start.8 = (bf16[384,128]{1,0:T(8,128)(2,1)S(1)}, bf16[384,128]{1,0:T(8,128)(2,1)S(1)}, u32[]{:S(2)}, u32[]{:S(2)}) collective-permute-start(bf16[384,128]{1,0:T(8,128)(2,1)S(1)} %collective-permute-done.4.refs_0_), channel_id=1, source_target_pairs={{8,10},{9,11},{10,8},{11,9},{12,14},{13,15},{14,12},{15,13},{24,26... | collective-permute-start | bytes 294920 | tf_op jit(solution)/shard_map/ppermute | solution.py:183
  36.3 17.8 %collective-permute-start.6 = (bf16[384,128]{1,0:T(8,128)(2,1)S(1)}, bf16[384,128]{1,0:T(8,128)(2,1)S(1)}, u32[]{:S(2)}, u32[]{:S(2)}) collective-permute-start(bf16[384,128]{1,0:T(8,128)(2,1)S(1)} %collective-permute-done.4.refs_0_), channel_id=1, source_target_pairs={{8,9},{9,8},{10,11},{11,10},{12,13},{13,12},{14,15},{15,14},{24,25... | collective-permute-start | bytes 294920 | tf_op jit(solution)/shard_map/ppermute | solution.py:183
  42.0 14.3 %collective-permute-start.17 = (bf16[384,128]{1,0:T(8,128)(2,1)S(1)}, bf16[384,128]{1,0:T(8,128)(2,1)S(1)}, u32[]{:S(2)}, u32[]{:S(2)}) collective-permute-start(bf16[384,128]{1,0:T(8,128)(2,1)S(1)} %collective-permute-done.5.refs_1_), channel_id=1, source_target_pairs={{16,22},{17,23},{18,20},{19,21},{20,18},{21,19},{22,16},{23,17},{2... | collective-permute-start | bytes 294920 | tf_op jit(solution)/shard_map/ppermute | solution.py:183
  45.8 12.9 %collective-permute-start.13 = (bf16[384,128]{1,0:T(8,128)(2,1)S(1)}, bf16[384,128]{1,0:T(8,128)(2,1)S(1)}, u32[]{:S(2)}, u32[]{:S(2)}) collective-permute-start(bf16[384,128]{1,0:T(8,128)(2,1)S(1)} %collective-permute-done.5.refs_1_), channel_id=1, source_target_pairs={{16,20},{17,21},{18,22},{19,23},{20,16},{21,17},{22,18},{23,19},{2... | collective-permute-start | bytes 294920 | tf_op jit(solution)/shard_map/ppermute | solution.py:183
  47.7 12.9 %collective-permute-start.9 = (bf16[384,128]{1,0:T(8,128)(2,1)S(1)}, bf16[384,128]{1,0:T(8,128)(2,1)S(1)}, u32[]{:S(2)}, u32[]{:S(2)}) collective-permute-start(bf16[384,128]{1,0:T(8,128)(2,1)S(1)} %collective-permute-done.5.refs_1_), channel_id=1, source_target_pairs={{16,18},{17,19},{18,16},{19,17},{20,22},{21,23},{22,20},{23,21},{2... | collective-permute-start | bytes 294920 | tf_op jit(solution)/shard_map/ppermute | solution.py:183
  51.3 11.7 %collective-permute-start.7 = (bf16[384,128]{1,0:T(8,128)(2,1)S(1)}, bf16[384,128]{1,0:T(8,128)(2,1)S(1)}, u32[]{:S(2)}, u32[]{:S(2)}) collective-permute-start(bf16[384,128]{1,0:T(8,128)(2,1)S(1)} %collective-permute-done.5.refs_1_), channel_id=1, source_target_pairs={{16,17},{17,16},{18,19},{19,18},{20,21},{21,20},{22,23},{23,22},{2... | collective-permute-start | bytes 294920 | tf_op jit(solution)/shard_map/ppermute | solution.py:183
  54.1 10.9 %collective-permute-start.18 = (bf16[384,128]{1,0:T(8,128)(2,1)S(1)}, bf16[384,128]{1,0:T(8,128)(2,1)S(1)}, u32[]{:S(2)}, u32[]{:S(2)}) collective-permute-start(bf16[384,128]{1,0:T(8,128)(2,1)S(1)} %collective-permute-done.16.refs_12_), channel_id=1, source_target_pairs={{8,9},{9,8},{10,11},{11,10},{12,13},{13,12},{14,15},{15,14},{24,25... | collective-permute-start | bytes 294920 | tf_op jit(solution)/shard_map/ppermute | solution.py:183
  56.2 20.6 %collective-permute-start.14 = (bf16[384,128]{1,0:T(8,128)(2,1)S(1)}, bf16[384,128]{1,0:T(8,128)(2,1)S(1)}, u32[]{:S(2)}, u32[]{:S(2)}) collective-permute-start(bf16[384,128]{1,0:T(8,128)(2,1)S(1)} %collective-permute-done.12.refs_8_), channel_id=1, source_target_pairs={{8,9},{9,8},{10,11},{11,10},{12,13},{13,12},{14,15},{15,14},{24,25... | collective-permute-start | bytes 294920 | tf_op jit(solution)/shard_map/ppermute | solution.py:183
  58.7 18.2 %collective-permute-start.10 = (bf16[384,128]{1,0:T(8,128)(2,1)S(1)}, bf16[384,128]{1,0:T(8,128)(2,1)S(1)}, u32[]{:S(2)}, u32[]{:S(2)}) collective-permute-start(bf16[384,128]{1,0:T(8,128)(2,1)S(1)} %collective-permute-done.8.refs_4_), channel_id=1, source_target_pairs={{8,9},{9,8},{10,11},{11,10},{12,13},{13,12},{14,15},{15,14},{24,25... | collective-permute-start | bytes 294920 | tf_op jit(solution)/shard_map/ppermute | solution.py:183
  60.6 16.2 %collective-permute-start.19 = (bf16[384,128]{1,0:T(8,128)(2,1)S(1)}, bf16[384,128]{1,0:T(8,128)(2,1)S(1)}, u32[]{:S(2)}, u32[]{:S(2)}) collective-permute-start(bf16[384,128]{1,0:T(8,128)(2,1)S(1)} %collective-permute-done.17.refs_13_), channel_id=1, source_target_pairs={{16,17},{17,16},{18,19},{19,18},{20,21},{21,20},{22,23},{23,22},{2... | collective-permute-start | bytes 294920 | tf_op jit(solution)/shard_map/ppermute | solution.py:183
  63.0 13.8 %collective-permute-start.15 = (bf16[384,128]{1,0:T(8,128)(2,1)S(1)}, bf16[384,128]{1,0:T(8,128)(2,1)S(1)}, u32[]{:S(2)}, u32[]{:S(2)}) collective-permute-start(bf16[384,128]{1,0:T(8,128)(2,1)S(1)} %collective-permute-done.13.refs_9_), channel_id=1, source_target_pairs={{16,17},{17,16},{18,19},{19,18},{20,21},{21,20},{22,23},{23,22},{2... | collective-permute-start | bytes 294920 | tf_op jit(solution)/shard_map/ppermute | solution.py:183
  65.0 11.9 %collective-permute-start.11 = (bf16[384,128]{1,0:T(8,128)(2,1)S(1)}, bf16[384,128]{1,0:T(8,128)(2,1)S(1)}, u32[]{:S(2)}, u32[]{:S(2)}) collective-permute-start(bf16[384,128]{1,0:T(8,128)(2,1)S(1)} %collective-permute-done.9.refs_5_), channel_id=1, source_target_pairs={{16,17},{17,16},{18,19},{19,18},{20,21},{21,20},{22,23},{23,22},{2... | collective-permute-start | bytes 294920 | tf_op jit(solution)/shard_map/ppermute | solution.py:183

commit v2 on v1

v2 whole, which is shorter than its diff:
```python
import functools
import math

import jax
import jax.numpy as jnp
from jax import lax
from jax.experimental import pallas as pl
from jax.experimental.pallas import tpu as pltpu
from jax.sharding import Mesh, PartitionSpec as P

HEADS = 24
HEAD_DIM = 128
EPSILON = 1e-06
VMEM_LIMIT = 40 * 1024 * 1024

F32, BF16 = jnp.float32, jnp.bfloat16
WHOLE = pl.BlockSpec(memory_space=pltpu.VMEM)
SCALARS = pl.BlockSpec(memory_space=pltpu.SMEM)
IN_HBM = pl.BlockSpec(memory_space=pltpu.HBM)
PARAMS = pltpu.CompilerParams(vmem_limit_bytes=VMEM_LIMIT)


def inverse_rms(rows):
    return lax.rsqrt(jnp.mean(rows * rows, -1, keepdims=True) + EPSILON)


def columns(head, width=HEAD_DIM):
    return pl.ds(pl.multiple_of(head * width, width), width)


def state_kernel(chunk, first_ref, key_ref, value_ref, out_ref, keys, values, sems):
    heads = out_ref.shape[0] // HEAD_DIM
    copies = []
    for n, h in enumerate(range(0, heads, chunk)):
        width = chunk * HEAD_DIM
        source = pl.ds(pl.multiple_of((first_ref[0] + h) * HEAD_DIM, HEAD_DIM), width)
        target = pl.ds(h * HEAD_DIM, width)
        for s, (ref, held) in enumerate(((key_ref, keys), (value_ref, values))):
            copy = pltpu.make_async_copy(ref.at[:, source], held.at[:, target], sems.at[n, s])
            copy.start()
            copies.append(copy)
    for h in range(heads):
        if h % chunk == 0:
            copies[h // chunk * 2].wait()
            copies[h // chunk * 2 + 1].wait()
        at = slice(h * HEAD_DIM, (h + 1) * HEAD_DIM)
        key_rows = keys[:, at].astype(F32)
        normal = (key_rows * inverse_rms(key_rows)).astype(BF16)
        state = lax.dot_general(
            normal, values[:, at], (((0,), (0,)), ((), ())), preferred_element_type=F32
        )
        out_ref[at, :] = state.astype(out_ref.dtype)


def local_state(first_head, keys, values, heads, dtype):
    dim, rows = HEAD_DIM, keys.shape[0]
    chunk = math.gcd(heads, 3)
    held = pltpu.VMEM((rows, heads * dim), BF16)
    return pl.pallas_call(
        functools.partial(state_kernel, chunk),
        out_shape=jax.ShapeDtypeStruct((heads * dim, dim), dtype),
        in_specs=[SCALARS, IN_HBM, IN_HBM],
        out_specs=WHOLE,
        scratch_shapes=[held, held, pltpu.SemaphoreType.DMA((heads // chunk, 2))],
        compiler_params=pltpu.CompilerParams(vmem_limit_bytes=56 * 1024 * 1024),
        cost_estimate=pl.CostEstimate(
            flops=2 * heads * rows * dim * dim,
            bytes_accessed=6 * heads * rows * dim,
            transcendentals=heads * rows,
        ),
    )(first_head, keys, values)


def level_kernel(frames, sources, targets, part_ref, out_ref):
    depth = frames.bit_length() - 1
    rows = part_ref.shape[0] // (frames * sources)
    states = []
    for f in range(frames - 1):
        total = None
        for s in range(sources):
            start = (f * sources + s) * rows
            part = part_ref[start : start + rows, :].astype(F32)
            total = part if total is None else total + part
        states.append(total)
    zero = jnp.zeros((rows, HEAD_DIM), BF16)
    for f in range(frames):
        for level in range(depth):
            value = zero
            if f >> level & 1:
                first = f >> level + 1 << level + 1
                value = sum(states[first + 1 : first + 2**level], states[first]).astype(BF16)
            for t in range(targets):
                start = ((f * targets + t) * depth + level) * rows
                out_ref[start : start + rows, :] = value


def level_blocks(parts, frames, sources, targets):
    depth = frames.bit_length() - 1
    rows = parts.shape[0] // (frames * sources)
    return pl.pallas_call(
        functools.partial(level_kernel, frames, sources, targets),
        out_shape=jax.ShapeDtypeStruct((frames * targets * depth * rows, HEAD_DIM), BF16),
        in_specs=[WHOLE],
        out_specs=WHOLE,
        compiler_params=PARAMS,
    )(parts)


def local_kernel(
    length_ref, back_ref, scale_ref, query_ref, key_ref, value_ref, weight_ref, local_ref, read_ref
):
    tokens = query_ref.shape[0]
    levels = weight_ref.shape[0] - 1
    key_at = lax.broadcasted_iota(jnp.int32, (tokens, tokens), 0)
    query_at = lax.broadcasted_iota(jnp.int32, (tokens, tokens), 1)
    start = jnp.int32(0)
    floor = jnp.zeros((tokens, tokens), jnp.int32)
    for k in range(length_ref.shape[1]):
        lowest = jnp.maximum(start - back_ref[0, k], 0)
        floor = jnp.where(query_at >= start, lowest, floor)
        start = start + length_ref[0, k]
    hidden = jnp.where((key_at <= query_at) & (key_at >= floor), 0.0, -jnp.inf).astype(F32)
    scale = math.log2(math.e) / math.sqrt(HEAD_DIM)
    for h in range(HEADS):
        at = slice(h * HEAD_DIM, (h + 1) * HEAD_DIM)
        query = query_ref[:, at]
        scores = lax.dot_general(
            key_ref[:, at], query, (((1,), (1,)), ((), ())), preferred_element_type=F32
        )
        scores = scores * scale + hidden
        weights = jnp.exp2(scores - jnp.max(scores, 0, keepdims=True))
        total = jnp.sum(weights, 0, keepdims=True)
        weights = weights * (weight_ref[0, h : h + 1, :] / total)
        local_ref[:, at] = lax.dot_general(
            weights.astype(BF16), value_ref[:, at], (((0,), (0,)), ((), ())), preferred_element_type=F32
        )
        query = query.astype(F32).T
        inverse = lax.rsqrt(jnp.mean(query * query, 0, keepdims=True) + EPSILON)
        for level in range(levels):
            gain = inverse * (weight_ref[1 + level, h : h + 1, :] * scale_ref[level])
            first = (h * levels + level) * HEAD_DIM
            read_ref[:, first : first + HEAD_DIM] = (query * gain).T.astype(BF16)


def local_part(frame_len, window_back, scales, queries, keys, values, weights):
    tokens, width = queries.shape
    levels = scales.shape[0]
    return pl.pallas_call(
        local_kernel,
        out_shape=[
            jax.ShapeDtypeStruct((tokens, width), F32),
            jax.ShapeDtypeStruct((tokens, levels * width), BF16),
        ],
        in_specs=[SCALARS] * 3 + [WHOLE] * 4,
        out_specs=[WHOLE] * 2,
        compiler_params=PARAMS,
        cost_estimate=pl.CostEstimate(
            flops=4 * tokens * tokens * width,
            bytes_accessed=14 * tokens * width,
            transcendentals=tokens * tokens * HEADS,
        ),
    )(frame_len, window_back, scales, queries, keys, values, weights)


def read_kernel(levels, block, first_ref, local_ref, read_ref, *refs):
    out_ref, state_refs = refs[-1], refs[:-1]
    heads = HEADS // len(state_refs)
    for n, state_ref in enumerate(state_refs):
        for h in range(heads):
            rows = []
            for level in range(levels):
                row, end = h * HEAD_DIM, (h + 1) * HEAD_DIM
                while row < end:
                    stop = min(end, (row // block + 1) * block)
                    start = (row // block * levels + level) * block + row % block
                    rows.append(state_ref[start : start + stop - row, :])
                    row = stop
            head = first_ref[n] + h
            result = local_ref[:, columns(head)] + jnp.dot(
                read_ref[:, columns(head, levels * HEAD_DIM)],
                jnp.concatenate(rows, 0),
                preferred_element_type=F32,
            )
            out_ref[:, columns(head)] = result.astype(BF16)


def read_levels(first, local, reads, states, levels, block):
    tokens, width = local.shape
    return pl.pallas_call(
        functools.partial(read_kernel, levels, block),
        out_shape=jax.ShapeDtypeStruct((tokens, width), BF16),
        in_specs=[SCALARS] + [WHOLE] * (2 + len(states)),
        out_specs=WHOLE,
        compiler_params=PARAMS,
    )(first, local, reads, *states)


def body(sizes, queries, keys, values, level_weight, frame_len, window_back):
    frames, outer, chips = sizes
    tokens = queries.shape[0]
    frame_pos = lax.axis_index("frame")
    core = lax.axis_index("core").astype(jnp.int32)
    depth = frames.bit_length() - 1
    half = HEADS // 2
    first = jnp.stack([core * half, (1 - core) * half])

    outgoing = local_state(first[1:], keys, values, half, BF16)
    incoming = lax.ppermute(outgoing, "core", [(0, 1), (1, 0)])
    mine = local_state(first[:1], keys, values, half, F32)
    chip_sum = (mine + incoming.astype(F32)).astype(BF16)
    parts = lax.all_to_all(chip_sum, ("frame", "chip"), 0, 0, tiled=True)
    block = parts.shape[0] // (frames * chips)
    sources = chips
    if outer > 1:
        parts = parts.astype(F32).reshape(frames, chips, block, HEAD_DIM).sum(1)
        parts = lax.psum(parts, "outer").reshape(frames * block, HEAD_DIM)
        sources = 1
    blocks = level_blocks(parts, frames, sources, chips)
    own = lax.all_to_all(blocks, ("frame", "chip"), 0, 0, tiled=True)
    other = lax.ppermute(own, "core", [(0, 1), (1, 0)])

    scales = jnp.stack(
        [
            (frame_pos >> level & 1).astype(F32)
            / math.sqrt(HEAD_DIM * 2**level * tokens * outer * chips * 2)
            for level in range(depth)
        ]
    )
    local, reads = local_part(frame_len, window_back, scales, queries, keys, values, level_weight)
    return read_levels(first, local, reads, (own, other), depth, block)


def solution(mesh):
    frames, space = mesh.shape["frame"], mesh.shape["space"]
    chips = 1
    while HEADS * HEAD_DIM // 2 % (frames * chips * 2 * 32) == 0 and space % (chips * 4) == 0 and chips < 4:
        chips *= 2
    sizes = (frames, space // (2 * chips), chips)
    names = ("frame", "outer", "chip", "core")
    fine = Mesh(mesh.devices.reshape(sizes + (2,)), names)
    rows = P(names, None)
    return jax.shard_map(
        functools.partial(body, sizes),
        mesh=fine,
        in_specs=(rows, rows, rows, P(None, None, names), rows, rows),
        out_specs=rows,
        check_vma=False,
    )
```

time: 79.8 us -> 65 us (0.81)
  the two profiles are of different devices: /device:TPU:7 before, /device:TPU:0 now
where the time goes in v2:
time: 65 us; the launch traced here: 64.6 us
  blocking collectives  46.6 us (72%)
  Pallas kernels  16 us (25%)
  other arithmetic  1.37 us (2%)
    all_to_all x1, blocking collectives, body(): own = lax.all_to_all(blocks, ('frame', 'chip'), 0, 0, tiled=True)  24.8 us
    all_to_all x1, blocking collectives, body(): parts = lax.all_to_all(chip_sum, ('frame', 'chip'), 0, 0, tiled=True)  21.7 us
    pallas_call x1, Pallas kernels, local_part(): pl.pallas_call(local_kernel, out_shape=[jax.ShapeDtypeStruct((tokens, wid...  7.18 us
    pallas_call x2, Pallas kernels, local_state(): pl.pallas_call(functools.partial(state_kernel, chunk), out_shape=jax.Shap...  6.1 us
    pallas_call x1, Pallas kernels, read_levels(): pl.pallas_call(functools.partial(read_kernel, levels, block), out_shape=j...  2.66 us
  transfers between devices with their start and end apart: 2, of which 0 were waited for; matrix products, arithmetic and copies ran while one was open for 0% of the time, Pallas kernels for 16%

profile of v2, /device:TPU:0, one launch (start us, length us, event | category | flops | bytes accessed | tf_op | source)
XLA Modules:
  0.0 64.6 jit_solution(14553397679611315015)
XLA Ops:
  0.0 3.0 %shard_map.66 = bf16[1536,128]{1,0:T(8,128)(2,1)} custom-call(s32[1]{0:T(128)} %bitcast.1.first_ref, bf16[128,3072]{1,0:T(8,128)(2,1)} %key_ref.5, bf16[128,3072]{1,0:T(8,128)(2,1)} %value_ref.5), custom_call_target="tpu_custom_call" | custom-call | flops 50331648 | bytes 1179648 | tf_op jit(solution)/shard_map/pallas_call | solution.py:59
  3.0 0.5 collective-permute-start
  3.5 3.1 %shard_map.65 = f32[1536,128]{1,0:T(8,128)} custom-call(s32[1]{0:T(128)} %bitcast.first_ref, bf16[128,3072]{1,0:T(8,128)(2,1)} %key_ref.5, bf16[128,3072]{1,0:T(8,128)(2,1)} %value_ref.5), custom_call_target="tpu_custom_call" | custom-call | flops 50331648 | bytes 1179648 | tf_op jit(solution)/shard_map/pallas_call | solution.py:59
  6.6 0.0 collective-permute-done
  6.6 1.2 %add_convert_fusion = bf16[1536,128]{1,0:T(8,128)(2,1)S(1)} fusion(f32[1536,128]{1,0:T(8,128)} %shard_map.65, bf16[1536,128]{1,0:T(8,128)(2,1)S(1)} %collective-permute-done), kind=kLoop, calls=%fused_computation | loop fusion | flops 589824 | bytes 1572864 | tf_op jit(solution)/shard_map/convert_element_type | solution.py:210
  7.9 21.7 %all_to_all.22 = bf16[16,96,128]{2,1,0:T(8,128)(2,1)S(1)} all-to-all(bf16[16,96,128]{2,1,0:T(8,128)(2,1)S(1)} %bitcast.12), channel_id=1, replica_groups=mesh['frame'=4,'outer'=1,'chip'=4,'core'=2] {'frame','chip'}, dimensions={0} | all-to-all | bytes 786432 | tf_op jit(solution)/shard_map/all_to_all | solution.py:211
  29.6 0.0 copy-start
  29.6 0.0 copy-start.1
  29.6 0.0 copy-start.2
  29.6 0.0 copy-start.3
  29.6 0.0 copy-start.4
  29.6 0.0 copy-start.5
  29.6 0.1 shard_map.67
  29.7 24.8 %all_to_all.23 = bf16[16,192,128]{2,1,0:T(8,128)(2,1)S(1)} all-to-all(bf16[16,192,128]{2,1,0:T(8,128)(2,1)S(1)} %bitcast.8), channel_id=1, replica_groups=mesh['frame'=4,'outer'=1,'chip'=4,'core'=2] {'frame','chip'}, dimensions={0} | all-to-all | bytes 1572864 | tf_op jit(solution)/shard_map/all_to_all | solution.py:219
  54.5 0.0 collective-permute-start.1
  54.5 0.1 pad_maximum_fusion.scale_ref
  54.6 0.0 copy-done
  54.6 0.0 copy-done.1
  54.6 0.0 copy-done.2
  54.6 0.0 copy-done.3
  54.6 0.0 copy-done.4
  54.6 0.0 copy-done.5
  54.7 7.2 %shard_map.64 = (f32[128,3072]{1,0:T(8,128)S(1)}, bf16[128,6144]{1,0:T(8,128)(2,1)S(1)}) custom-call(s32[1,4]{1,0:T(1,128)S(1)} %copy-done.4, s32[1,4]{1,0:T(1,128)S(1)} %copy-done.5, f32[2]{0:T(128)S(1)} %pad_maximum_fusion.scale_ref, bf16[128,3072]{1,0:T(8,128)(2,1)S(1)} %copy-done.2, bf16[128,3072]{1,0:T(8,128)(2,1)S(1)} %copy-done, ...), custom_call_target="tpu_custom_call" | custom-call | flops 201326592 | bytes 5505024 | tf_op jit(solution)/shard_map/pallas_call | solution.py:148
  61.8 0.1 pad_add_fusion.first_ref
  61.9 0.0 collective-permute-done.1.refs_1_
  61.9 2.7 %shard_map.68 = bf16[128,3072]{1,0:T(8,128)(2,1)} custom-call(s32[2]{0:T(128)S(1)} %pad_add_fusion.first_ref, f32[128,3072]{1,0:T(8,128)S(1)} %get-tuple-element.7.local_ref, bf16[128,6144]{1,0:T(8,128)(2,1)S(1)} %get-tuple-element.8.read_ref, bf16[3072,128]{1,0:T(8,128)(2,1)S(1)} %bitcast.10, bf16[3072,128]{1,0:T(8,128)(2,1)} %collective-permute-done.1.refs_1_), custom_call_target="tpu_custom_call" | custom-call | tf_op jit(solution)/shard_map/pallas_call | solution.py:189
Async XLA Ops:
  3.0 3.6 %collective-permute-start = (bf16[1536,128]{1,0:T(8,128)(2,1)}, bf16[1536,128]{1,0:T(8,128)(2,1)S(1)}, u32[]{:S(2)}, u32[]{:S(2)}) collective-permute-start(bf16[1536,128]{1,0:T(8,128)(2,1)} %shard_map.66), channel_id=1, source_target_pairs={{0,1},{1,0},{2,3},{3,2},{4,5},{5,4},{6,7},{7,6},{8,9},{9,8},{10,11... | collective-permute-start | bytes 1179656 | tf_op jit(solution)/shard_map/ppermute | solution.py:208
  29.6 25.0 %copy-start = (bf16[128,3072]{1,0:T(8,128)(2,1)S(1)}, bf16[128,3072]{1,0:T(8,128)(2,1)}, u32[]{:S(2)}) copy-start(bf16[128,3072]{1,0:T(8,128)(2,1)} %key_ref.5) | copy-start | bytes 2359300
  29.6 25.0 %copy-start.1 = (bf16[128,3072]{1,0:T(8,128)(2,1)S(1)}, bf16[128,3072]{1,0:T(8,128)(2,1)}, u32[]{:S(2)}) copy-start(bf16[128,3072]{1,0:T(8,128)(2,1)} %value_ref.5) | copy-start | bytes 2359300
  29.6 25.0 %copy-start.2 = (bf16[128,3072]{1,0:T(8,128)(2,1)S(1)}, bf16[128,3072]{1,0:T(8,128)(2,1)}, u32[]{:S(2)}) copy-start(bf16[128,3072]{1,0:T(8,128)(2,1)} %query_ref.1) | copy-start | bytes 2359300
  29.6 25.0 %copy-start.3 = (f32[3,24,128]{2,1,0:T(8,128)S(1)}, f32[3,24,128]{2,1,0:T(8,128)}, u32[]{:S(2)}) copy-start(f32[3,24,128]{2,1,0:T(8,128)} %weight_ref.1) | copy-start | bytes 110596
  29.6 25.0 %copy-start.4 = (s32[1,4]{1,0:T(1,128)S(1)}, s32[1,4]{1,0:T(1,128)}, u32[]{:S(2)}) copy-start(s32[1,4]{1,0:T(1,128)} %length_ref.1) | copy-start | bytes 52
  29.6 25.0 %copy-start.5 = (s32[1,4]{1,0:T(1,128)S(1)}, s32[1,4]{1,0:T(1,128)}, u32[]{:S(2)}) copy-start(s32[1,4]{1,0:T(1,128)} %back_ref.1) | copy-start | bytes 52
  54.5 7.4 %collective-permute-start.1 = (bf16[3072,128]{1,0:T(8,128)(2,1)S(1)}, bf16[3072,128]{1,0:T(8,128)(2,1)}, u32[]{:S(2)}, u32[]{:S(2)}) collective-permute-start(bf16[3072,128]{1,0:T(8,128)(2,1)S(1)} %bitcast.9), channel_id=1, source_target_pairs={{0,1},{1,0},{2,3},{3,2},{4,5},{5,4},{6,7},{7,6},{8,9},{9,8},{10,11... | collective-permute-start | bytes 2359304 | tf_op jit(solution)/shard_map/ppermute | solution.py:220

commit v3 on v2

v3 whole, which is shorter than its diff:
```python
import functools
import math

import jax
import jax.numpy as jnp
from jax import lax
from jax.experimental import pallas as pl
from jax.experimental.pallas import tpu as pltpu
from jax.sharding import Mesh, PartitionSpec as P

HEADS = 24
HEAD_DIM = 128
EPSILON = 1e-06
VMEM_LIMIT = 40 * 1024 * 1024

F32, BF16 = jnp.float32, jnp.bfloat16
WHOLE = pl.BlockSpec(memory_space=pltpu.VMEM)
SCALARS = pl.BlockSpec(memory_space=pltpu.SMEM)
IN_HBM = pl.BlockSpec(memory_space=pltpu.HBM)
PARAMS = pltpu.CompilerParams(vmem_limit_bytes=VMEM_LIMIT)


def inverse_rms(rows):
    return lax.rsqrt(jnp.mean(rows * rows, -1, keepdims=True) + EPSILON)


def columns(head, width=HEAD_DIM):
    return pl.ds(pl.multiple_of(head * width, width), width)


def state_kernel(chunk, first_ref, key_ref, value_ref, out_ref, keys, values, sems):
    heads = out_ref.shape[0] // HEAD_DIM
    copies = []
    for n, h in enumerate(range(0, heads, chunk)):
        width = chunk * HEAD_DIM
        source = pl.ds(pl.multiple_of((first_ref[0] + h) * HEAD_DIM, HEAD_DIM), width)
        target = pl.ds(h * HEAD_DIM, width)
        for s, (ref, held) in enumerate(((key_ref, keys), (value_ref, values))):
            copy = pltpu.make_async_copy(ref.at[:, source], held.at[:, target], sems.at[n, s])
            copy.start()
            copies.append(copy)
    for h in range(heads):
        if h % chunk == 0:
            copies[h // chunk * 2].wait()
            copies[h // chunk * 2 + 1].wait()
        at = slice(h * HEAD_DIM, (h + 1) * HEAD_DIM)
        key_rows = keys[:, at].astype(F32)
        normal = (key_rows * inverse_rms(key_rows)).astype(BF16)
        state = lax.dot_general(
            normal, values[:, at], (((0,), (0,)), ((), ())), preferred_element_type=F32
        )
        out_ref[at, :] = state.astype(out_ref.dtype)


def local_state(first_head, keys, values, heads, dtype):
    dim, rows = HEAD_DIM, keys.shape[0]
    chunk = math.gcd(heads, 3)
    held = pltpu.VMEM((rows, heads * dim), BF16)
    keys, values = (pltpu.with_memory_space_constraint(x, pltpu.HBM) for x in (keys, values))
    return pl.pallas_call(
        functools.partial(state_kernel, chunk),
        out_shape=pltpu.VMEM((heads * dim, dim), dtype),
        in_specs=[SCALARS, IN_HBM, IN_HBM],
        out_specs=WHOLE,
        scratch_shapes=[held, held, pltpu.SemaphoreType.DMA((heads // chunk, 2))],
        compiler_params=PARAMS,
        cost_estimate=pl.CostEstimate(
            flops=2 * heads * rows * dim * dim,
            bytes_accessed=6 * heads * rows * dim,
            transcendentals=heads * rows,
        ),
    )(first_head, keys, values)


def piece_kernel(order_ref, mine_ref, other_ref, own_ref, *piece_refs):
    rows = own_ref.shape[0]
    for d, ref in enumerate((own_ref,) + piece_refs):
        at = pl.ds(pl.multiple_of(order_ref[d] * rows, rows), rows)
        ref[...] = (mine_ref[at, :] + other_ref[at, :].astype(F32)).astype(ref.dtype)


def chip_pieces(order, mine, other, chips):
    shape = (mine.shape[0] // chips, HEAD_DIM)
    return pl.pallas_call(
        piece_kernel,
        out_shape=[jax.ShapeDtypeStruct(shape, F32)]
        + [jax.ShapeDtypeStruct(shape, BF16)] * (chips - 1),
        in_specs=[SCALARS, WHOLE, WHOLE],
        out_specs=[WHOLE] * chips,
        compiler_params=PARAMS,
    )(order, mine, other)


def sum_kernel(after_ref, own_ref, *refs):
    total = own_ref[...]
    for ref in refs[:-1]:
        total = total + ref[...].astype(F32)
    refs[-1][...] = total.astype(refs[-1].dtype)


def sum_pieces(after, own, parts, dtype):
    return pl.pallas_call(
        sum_kernel,
        out_shape=jax.ShapeDtypeStruct(own.shape, dtype),
        in_specs=[pl.BlockSpec(memory_space=pl.ANY)] + [WHOLE] * (1 + len(parts)),
        out_specs=WHOLE,
        compiler_params=PARAMS,
    )(after, own, *parts)


def local_kernel(
    length_ref, back_ref, coef_ref, query_ref, key_ref, value_ref, weight_ref, after_ref, local_ref, *read_refs
):
    tokens = query_ref.shape[0]
    levels = weight_ref.shape[0] - 1
    key_at = lax.broadcasted_iota(jnp.int32, (tokens, tokens), 0)
    query_at = lax.broadcasted_iota(jnp.int32, (tokens, tokens), 1)
    start = jnp.int32(0)
    floor = jnp.zeros((tokens, tokens), jnp.int32)
    for k in range(length_ref.shape[1]):
        lowest = jnp.maximum(start - back_ref[0, k], 0)
        floor = jnp.where(query_at >= start, lowest, floor)
        start = start + length_ref[0, k]
    hidden = jnp.where((key_at <= query_at) & (key_at >= floor), 0.0, -jnp.inf).astype(F32)
    scale = math.log2(math.e) / math.sqrt(HEAD_DIM)
    for h in range(HEADS):
        at = slice(h * HEAD_DIM, (h + 1) * HEAD_DIM)
        query = query_ref[:, at]
        scores = lax.dot_general(
            key_ref[:, at], query, (((1,), (1,)), ((), ())), preferred_element_type=F32
        )
        scores = scores * scale + hidden
        weights = jnp.exp2(scores - jnp.max(scores, 0, keepdims=True))
        total = jnp.sum(weights, 0, keepdims=True)
        weights = weights * (weight_ref[0, h : h + 1, :] / total)
        local_ref[:, at] = lax.dot_general(
            weights.astype(BF16), value_ref[:, at], (((0,), (0,)), ((), ())), preferred_element_type=F32
        )
        query = query.astype(F32).T
        inverse = lax.rsqrt(jnp.mean(query * query, 0, keepdims=True) + EPSILON)
        for slot, read_ref in enumerate(read_refs):
            gain = sum(
                weight_ref[1 + level, h : h + 1, :] * coef_ref[slot, level] for level in range(levels)
            )
            read_ref[:, at] = (query * (inverse * gain)).T.astype(BF16)


def local_part(frame_len, window_back, coefs, queries, keys, values, weights, after):
    tokens, width = queries.shape
    slots = coefs.shape[0]
    return pl.pallas_call(
        local_kernel,
        out_shape=[jax.ShapeDtypeStruct((tokens, width), F32)]
        + [jax.ShapeDtypeStruct((tokens, width), BF16)] * slots,
        in_specs=[SCALARS] * 3 + [WHOLE] * 4 + [pl.BlockSpec(memory_space=pl.ANY)],
        out_specs=[WHOLE] * (1 + slots),
        compiler_params=PARAMS,
        cost_estimate=pl.CostEstimate(
            flops=4 * tokens * tokens * width,
            bytes_accessed=14 * tokens * width,
            transcendentals=tokens * tokens * HEADS,
        ),
    )(frame_len, window_back, coefs, queries, keys, values, weights, after)


def read_kernel(first_ref, base_ref, read_ref, *refs):
    out_ref, state_refs = refs[-1], refs[:-1]
    for n, state_ref in enumerate(state_refs):
        for h in range(state_ref.shape[0] // HEAD_DIM):
            at = columns(first_ref[n] + h)
            result = base_ref[:, at] + jnp.dot(
                read_ref[:, at],
                state_ref[h * HEAD_DIM : (h + 1) * HEAD_DIM, :],
                preferred_element_type=F32,
            )
            out_ref[:, at] = result.astype(out_ref.dtype)


def read_states(first, base, reads, states, dtype):
    return pl.pallas_call(
        read_kernel,
        out_shape=jax.ShapeDtypeStruct(base.shape, dtype),
        in_specs=[SCALARS] + [WHOLE] * (2 + len(states)),
        out_specs=WHOLE,
        compiler_params=PARAMS,
        cost_estimate=pl.CostEstimate(
            flops=2 * base.shape[0] * base.shape[1] * HEAD_DIM,
            bytes_accessed=8 * base.shape[0] * base.shape[1],
            transcendentals=0,
        ),
    )(first, base, reads, *states)


def swap(array, axis, mask, size):
    return lax.ppermute(array, axis, [(n, n ^ mask) for n in range(size)])


def level_scale(level, tokens):
    return 1.0 / math.sqrt(HEAD_DIM * 2**level * tokens)


def plain_body(sizes, queries, keys, values, level_weight, frame_len, window_back):
    frames, outer, chips = sizes
    frame = lax.axis_index("frame")
    space = ("outer", "chip", "core")
    zero = jnp.zeros((1,), jnp.int32)
    state = lax.psum(local_state(zero, keys, values, HEADS, F32), space)
    states = lax.all_gather(state.astype(BF16), "frame").astype(F32)
    ids = jnp.arange(frames)[:, None, None]
    depth = frames.bit_length() - 1
    tokens = queries.shape[0] * outer * chips * 2
    coefs = jnp.diag(jnp.array([level_scale(level, tokens) for level in range(depth)], F32))
    result, *reads = local_part(
        frame_len, window_back, coefs, queries, keys, values, level_weight, states
    )
    for level in range(depth):
        first = (frame >> level + 1) << level + 1
        inside = (ids >= first) & (ids < first + 2**level) & ((frame >> level) % 2 == 1)
        total = jnp.sum(jnp.where(inside, states, 0.0), 0).astype(BF16)
        result = read_states(zero, result, reads[level], [total], F32)
    return result.astype(BF16)


def body(sizes, queries, keys, values, level_weight, frame_len, window_back):
    frames, outer, chips = sizes
    tokens = queries.shape[0]
    frame = lax.axis_index("frame")
    chip = lax.axis_index("chip").astype(jnp.int32)
    core = lax.axis_index("core").astype(jnp.int32)
    half = HEADS // 2
    mine_at, other_at = (core * half).reshape(1), ((1 - core) * half).reshape(1)

    outgoing = local_state(other_at, keys, values, half, BF16)
    incoming = swap(outgoing, "core", 1, 2)
    mine = local_state(mine_at, keys, values, half, F32)
    order = jnp.stack([chip ^ d for d in range(chips)])
    own, *sends = chip_pieces(order, mine, incoming, chips)
    got = [swap(sends[d - 1], "chip", d, chips) for d in range(1, chips)]

    all_tokens = tokens * outer * chips * 2
    low, high = level_scale(0, all_tokens), level_scale(1, all_tokens)
    coefs = jnp.stack(
        [
            jnp.stack([jnp.where(frame % 2 == 1, low, 0.0), jnp.where(frame == 2, high, 0.0)]),
            jnp.stack([jnp.float32(0.0), jnp.where(frame == 3, high, 0.0)]),
        ]
    ).astype(F32)
    local, read_x, read_y = local_part(
        frame_len, window_back, coefs, queries, keys, values, level_weight, own
    )

    state = sum_pieces(local, own, got, F32 if outer > 1 else BF16)
    if outer > 1:
        state = lax.psum(state, "outer").astype(BF16)
    near, across, diagonal = (swap(state, "frame", mask, frames) for mask in (1, 2, 3))
    both = (across.astype(F32) + diagonal.astype(F32)).astype(BF16)
    slot = jnp.where(frame == 2, both, near)

    x_own = [slot] + [swap(slot, "chip", d, chips) for d in range(1, chips)]
    y_own = [swap(piece, "frame", 1, frames) for piece in x_own]
    x_all = [(piece, swap(piece, "core", 1, 2)) for piece in x_own]
    y_all = [(piece, swap(piece, "core", 1, 2)) for piece in y_own]
    first = jnp.stack(
        [(core ^ c) * half + (chip ^ d) * (half // chips) for d in range(chips) for c in range(2)]
    )
    result = read_states(first, local, read_x, [x for pair in x_all for x in pair], F32)
    return read_states(first, result, read_y, [y for pair in y_all for y in pair], BF16)


def solution(mesh):
    frames, space = mesh.shape["frame"], mesh.shape["space"]
    chips = 1
    while HEADS % (chips * 4) == 0 and space % (chips * 4) == 0 and chips < 4:
        chips *= 2
    sizes = (frames, space // (2 * chips), chips)
    names = ("frame", "outer", "chip", "core")
    fine = Mesh(mesh.devices.reshape(sizes + (2,)), names)
    rows = P(names, None)
    return jax.shard_map(
        functools.partial(body if frames == 4 else plain_body, sizes),
        mesh=fine,
        in_specs=(rows, rows, rows, P(None, None, names), rows, rows),
        out_specs=rows,
        check_vma=False,
    )
```

time: 65 us -> 54.1 us (0.83)
  blocking collectives: 46.6 us -> 0 us
  starting transfers between devices: 0.52 us -> 18.7 us
  waiting for transfers between devices: 0.01 us -> 13.4 us
  local copies, waits for them, and re-layouts: 0.03 us -> 4.7 us
  other arithmetic: 1.37 us -> 0.21 us
    all_to_all x2 -> x0, blocking collectives: 46.6 us -> none  [the longest x1 24.8 us: body(): own = lax.all_to_all(blocks, ('frame', 'chip'), 0, 0, tiled=True)]
    ppermute x2 -> x22, starting transfers between devices: 0.52 us -> 18.7 us  [swap(): return lax.ppermute(array, axis, [(n, n ^ mask) for n in range(size)])]
    ppermute x2 -> x22, waiting for transfers between devices: 0.01 us -> 13.4 us  [swap(): return lax.ppermute(array, axis, [(n, n ^ mask) for n in range(size)])]
    unnamed x12 -> x24, local copies, waits for them, and re-layouts: 0.03 us -> 4.62 us
    convert_element_type x1 -> x0, other arithmetic: 1.21 us -> none  [body(): chip_sum = (mine + incoming.astype(F32)).astype(BF16)]
    pallas_call x4 -> x6, Pallas kernels: 8.84 us -> 9.39 us  [the longest x2 4.64 us: local_state(): pl.pallas_call(functools.partial(state_kernel, chunk), out_shape=pltpu.VM...]
  transfers between devices with their start and end apart: 2 -> 22, of which waited for: 0 -> 10; matrix products, arithmetic and copies ran while one was open for 0% -> 0% of each run, Pallas kernels for 16% -> 21%
where the time goes in v3:
time: 54.1 us; the launch traced here: 53.8 us
  starting transfers between devices  18.7 us (35%)
  Pallas kernels  16.6 us (31%)
  waiting for transfers between devices  13.4 us (25%)
  local copies, waits for them, and re-layouts  4.7 us (9%)
    ppermute x22, starting transfers between devices, swap(): return lax.ppermute(array, axis, [(n, n ^ mask) for n in range(size)])  18.7 us
    ppermute x22, waiting for transfers between devices, swap(): return lax.ppermute(array, axis, [(n, n ^ mask) for n in range(size)])  13.4 us
    pallas_call x1, Pallas kernels, local_part(): pl.pallas_call(local_kernel, out_shape=[jax.ShapeDtypeStruct((tokens, wid...  7.2 us
    pallas_call x2, Pallas kernels, local_state(): pl.pallas_call(functools.partial(state_kernel, chunk), out_shape=pltpu.VM...  4.64 us
    unnamed x24, local copies, waits for them, and re-layouts  4.62 us
    pallas_call x2, Pallas kernels, read_states(): pl.pallas_call(read_kernel, out_shape=jax.ShapeDtypeStruct(base.shape, dt...  4.06 us
  transfers between devices with their start and end apart: 22, of which 10 were waited for; matrix products, arithmetic and copies ran while one was open for 0% of the time, Pallas kernels for 21%

profile of v3, /device:TPU:0, one launch (start us, length us, event | category | flops | bytes accessed | tf_op | source)
XLA Modules:
  0.0 53.8 jit_solution(7448633889411992935)
XLA Ops:
  0.0 2.2 %shard_map.65 = bf16[1536,128]{1,0:T(8,128)(2,1)S(1)} custom-call(s32[1]{0:T(128)} %bitcast.18.first_ref, bf16[128,3072]{1,0:T(8,128)(2,1)} %key_ref.5, bf16[128,3072]{1,0:T(8,128)(2,1)} %value_ref.5), custom_call_target="tpu_custom_call" | custom-call | flops 50331648 | bytes 1179648 | tf_op jit(solution)/shard_map/pallas_call | solution.py:60
  2.3 0.5 collective-permute-start
  2.8 2.4 %shard_map.64.mine_ref = f32[1536,128]{1,0:T(8,128)S(1)} custom-call(s32[1]{0:T(128)} %bitcast.17.first_ref, bf16[128,3072]{1,0:T(8,128)(2,1)} %key_ref.5, bf16[128,3072]{1,0:T(8,128)(2,1)} %value_ref.5), custom_call_target="tpu_custom_call" | custom-call | flops 50331648 | bytes 1179648 | tf_op jit(solution)/shard_map/pallas_call | solution.py:60
  5.4 0.6 %shard_map.66 = (f32[384,128]{1,0:T(8,128)S(1)}, bf16[384,128]{1,0:T(8,128)(2,1)S(1)}, bf16[384,128]{1,0:T(8,128)(2,1)S(1)}, bf16[384,128]{1,0:T(8,128)(2,1)S(1)}) custom-call(s32[4]{0:T(128)S(1)} %pad_add_fusion.order_ref, f32[1536,128]{1,0:T(8,128)S(1)} %shard_map.64.mine_ref, bf16[1536,128]{1,0:T(8,128)(2,1)S(1)} %collective-permute-done.other_ref), custom_call_target="tpu_custom_call" | custom-call | tf_op jit(solution)/shard_map/pallas_call | solution.py:84
  6.0 2.7 %collective-permute-start.1 = (bf16[384,128]{1,0:T(8,128)(2,1)S(1)}, bf16[384,128]{1,0:T(8,128)(2,1)S(1)}, u32[]{:S(2)}, u32[]{:S(2)}) collective-permute-start(bf16[384,128]{1,0:T(8,128)(2,1)S(1)} %get-tuple-element.15), channel_id=1, source_target_pairs={{0,2},{2,0},{4,6},{6,4},{1,3},{3,1},{5,7},{7,5},{8,10},{10,8},{12,... | collective-permute-start | bytes 294920 | tf_op jit(solution)/shard_map/ppermute | solution.py:195
  8.7 2.6 %collective-permute-start.2 = (bf16[384,128]{1,0:T(8,128)(2,1)S(1)}, bf16[384,128]{1,0:T(8,128)(2,1)S(1)}, u32[]{:S(2)}, u32[]{:S(2)}) collective-permute-start(bf16[384,128]{1,0:T(8,128)(2,1)S(1)} %get-tuple-element.16), channel_id=1, source_target_pairs={{0,4},{2,6},{4,0},{6,2},{1,5},{3,7},{5,1},{7,3},{8,12},{10,14},{12... | collective-permute-start | bytes 294920 | tf_op jit(solution)/shard_map/ppermute | solution.py:195
  11.4 7.2 %shard_map.67 = (f32[128,3072]{1,0:T(8,128)S(1)}, bf16[128,3072]{1,0:T(8,128)(2,1)S(1)}, bf16[128,3072]{1,0:T(8,128)(2,1)S(1)}) custom-call(s32[1,4]{1,0:T(1,128)S(1)} %copy-done.10, s32[1,4]{1,0:T(1,128)S(1)} %copy-done.11, f32[2,2]{1,0:T(2,128)S(1)} %pad_maximum_fusion.coef_ref, bf16[128,3072]{1,0:T(8,128)(2,1)S(1)} %copy-done.2, ...), custom_call_target="tpu_custom_call" | custom-call | flops 201326592 | bytes 5505024 | tf_op jit(solution)/shard_map/pallas_call | solution.py:151
  18.6 0.9 %collective-permute-done.2.refs_1_ = bf16[384,128]{1,0:T(8,128)(2,1)S(1)} collective-permute-done((bf16[384,128]{1,0:T(8,128)(2,1)S(1)}, bf16[384,128]{1,0:T(8,128)(2,1)S(1)}, u32[]{:S(2)}, u32[]{:S(2)}) %collective-permute-start.2) | collective-permute-done | bytes 98336 | tf_op jit(solution)/shard_map/ppermute | solution.py:195
  19.5 1.6 %collective-permute-start.4 = (bf16[384,128]{1,0:T(8,128)(2,1)S(1)}, bf16[384,128]{1,0:T(8,128)(2,1)S(1)}, u32[]{:S(2)}, u32[]{:S(2)}) collective-permute-start(bf16[384,128]{1,0:T(8,128)(2,1)S(1)} %shard_map.68), channel_id=1, source_target_pairs={{0,16},{8,24},{16,0},{24,8},{1,17},{9,25},{17,1},{25,9},{2,18},{10... | collective-permute-start | bytes 294920 | tf_op jit(solution)/shard_map/ppermute | solution.py:195
  21.1 1.4 %collective-permute-start.5 = (bf16[384,128]{1,0:T(8,128)(2,1)S(1)}, bf16[384,128]{1,0:T(8,128)(2,1)S(1)}, u32[]{:S(2)}, u32[]{:S(2)}) collective-permute-start(bf16[384,128]{1,0:T(8,128)(2,1)S(1)} %shard_map.68), channel_id=1, source_target_pairs={{0,24},{8,16},{16,8},{24,0},{1,25},{9,17},{17,9},{25,1},{2,26},{10... | collective-permute-start | bytes 294920 | tf_op jit(solution)/shard_map/ppermute | solution.py:195
  22.6 0.5 collective-permute-start.6
  23.1 2.2 %collective-permute-done.4 = bf16[384,128]{1,0:T(8,128)(2,1)S(1)} collective-permute-done((bf16[384,128]{1,0:T(8,128)(2,1)S(1)}, bf16[384,128]{1,0:T(8,128)(2,1)S(1)}, u32[]{:S(2)}, u32[]{:S(2)}) %collective-permute-start.4) | collective-permute-done | bytes 98336 | tf_op jit(solution)/shard_map/ppermute | solution.py:195
  25.3 1.4 %collective-permute-done.5 = bf16[384,128]{1,0:T(8,128)(2,1)S(1)} collective-permute-done((bf16[384,128]{1,0:T(8,128)(2,1)S(1)}, bf16[384,128]{1,0:T(8,128)(2,1)S(1)}, u32[]{:S(2)}, u32[]{:S(2)}) %collective-permute-start.5) | collective-permute-done | bytes 98336 | tf_op jit(solution)/shard_map/ppermute | solution.py:195
  27.2 3.0 %collective-permute-start.10 = (bf16[384,128]{1,0:T(8,128)(2,1)S(1)}, bf16[384,128]{1,0:T(8,128)(2,1)S(1)}, u32[]{:S(2)}, u32[]{:S(2)}) collective-permute-start(bf16[384,128]{1,0:T(8,128)(2,1)S(1)} %fusion.refs_0_), channel_id=1, source_target_pairs={{0,4},{2,6},{4,0},{6,2},{1,5},{3,7},{5,1},{7,3},{8,12},{10,14},{12... | collective-permute-start | bytes 294920 | tf_op jit(solution)/shard_map/ppermute | solution.py:195
  30.2 1.3 %collective-permute-start.12 = (bf16[384,128]{1,0:T(8,128)(2,1)S(1)}, bf16[384,128]{1,0:T(8,128)(2,1)S(1)}, u32[]{:S(2)}, u32[]{:S(2)}) collective-permute-start(bf16[384,128]{1,0:T(8,128)(2,1)S(1)} %fusion.refs_0_), channel_id=1, source_target_pairs={{0,6},{2,4},{4,2},{6,0},{1,7},{3,5},{5,3},{7,1},{8,14},{10,12},{12... | collective-permute-start | bytes 294920 | tf_op jit(solution)/shard_map/ppermute | solution.py:195
  31.5 1.2 %collective-permute-start.14 = (bf16[384,128]{1,0:T(8,128)(2,1)S(1)}, bf16[384,128]{1,0:T(8,128)(2,1)S(1)}, u32[]{:S(2)}, u32[]{:S(2)}) collective-permute-start(bf16[384,128]{1,0:T(8,128)(2,1)S(1)} %fusion.refs_0_), channel_id=1, source_target_pairs={{0,8},{8,0},{16,24},{24,16},{1,9},{9,1},{17,25},{25,17},{2,10},{10... | collective-permute-start | bytes 294920 | tf_op jit(solution)/shard_map/ppermute | solution.py:195
  32.8 2.9 %collective-permute-done.10.refs_4_ = bf16[384,128]{1,0:T(8,128)(2,1)S(1)} collective-permute-done((bf16[384,128]{1,0:T(8,128)(2,1)S(1)}, bf16[384,128]{1,0:T(8,128)(2,1)S(1)}, u32[]{:S(2)}, u32[]{:S(2)}) %collective-permute-start.10) | collective-permute-done | bytes 98336 | tf_op jit(solution)/shard_map/ppermute | solution.py:195
  35.7 1.3 %collective-permute-done.12.refs_6_ = bf16[384,128]{1,0:T(8,128)(2,1)S(1)} collective-permute-done((bf16[384,128]{1,0:T(8,128)(2,1)S(1)}, bf16[384,128]{1,0:T(8,128)(2,1)S(1)}, u32[]{:S(2)}, u32[]{:S(2)}) %collective-permute-start.12) | collective-permute-done | bytes 98336 | tf_op jit(solution)/shard_map/ppermute | solution.py:195
  37.0 0.8 %collective-permute-done.8.refs_2_ = bf16[384,128]{1,0:T(8,128)(2,1)} collective-permute-done((bf16[384,128]{1,0:T(8,128)(2,1)S(1)}, bf16[384,128]{1,0:T(8,128)(2,1)}, u32[]{:S(2)}, u32[]{:S(2)}) %collective-permute-start.8) | collective-permute-done | bytes 98336 | tf_op jit(solution)/shard_map/ppermute | solution.py:195
  37.7 1.2 %collective-permute-start.16 = (bf16[384,128]{1,0:T(8,128)(2,1)}, bf16[384,128]{1,0:T(8,128)(2,1)}, u32[]{:S(2)}, u32[]{:S(2)}) collective-permute-start(bf16[384,128]{1,0:T(8,128)(2,1)} %collective-permute-done.8.refs_2_), channel_id=1, source_target_pairs={{0,8},{8,0},{16,24},{24,16},{1,9},{9,1},{17,25},{25,17},{2,10},{10... | collective-permute-start | bytes 294920 | tf_op jit(solution)/shard_map/ppermute | solution.py:195
  39.0 0.6 %copy-done.3 = bf16[384,128]{1,0:T(8,128)(2,1)} copy-done((bf16[384,128]{1,0:T(8,128)(2,1)}, bf16[384,128]{1,0:T(8,128)(2,1)S(1)}, u32[]{:S(2)}) %copy-start.3) | copy-done | bytes 98328
  39.6 0.8 %collective-permute-start.18 = (bf16[384,128]{1,0:T(8,128)(2,1)S(1)}, bf16[384,128]{1,0:T(8,128)(2,1)}, u32[]{:S(2)}, u32[]{:S(2)}) collective-permute-start(bf16[384,128]{1,0:T(8,128)(2,1)S(1)} %collective-permute-done.10.refs_4_), channel_id=1, source_target_pairs={{0,8},{8,0},{16,24},{24,16},{1,9},{9,1},{17,25},{25,17},{2,10},{10... | collective-permute-start | bytes 294920 | tf_op jit(solution)/shard_map/ppermute | solution.py:195
  40.4 1.2 %collective-permute-start.20 = (bf16[384,128]{1,0:T(8,128)(2,1)S(1)}, bf16[384,128]{1,0:T(8,128)(2,1)}, u32[]{:S(2)}, u32[]{:S(2)}) collective-permute-start(bf16[384,128]{1,0:T(8,128)(2,1)S(1)} %collective-permute-done.12.refs_6_), channel_id=1, source_target_pairs={{0,8},{8,0},{16,24},{24,16},{1,9},{9,1},{17,25},{25,17},{2,10},{10... | collective-permute-start | bytes 294920 | tf_op jit(solution)/shard_map/ppermute | solution.py:195
  41.6 0.6 %copy-done.5 = bf16[384,128]{1,0:T(8,128)(2,1)} copy-done((bf16[384,128]{1,0:T(8,128)(2,1)}, bf16[384,128]{1,0:T(8,128)(2,1)S(1)}, u32[]{:S(2)}) %copy-start.5) | copy-done | bytes 98328
  42.3 0.6 %copy-done.7 = bf16[384,128]{1,0:T(8,128)(2,1)} copy-done((bf16[384,128]{1,0:T(8,128)(2,1)}, bf16[384,128]{1,0:T(8,128)(2,1)S(1)}, u32[]{:S(2)}) %copy-start.7) | copy-done | bytes 98328
  43.7 2.1 %collective-permute-done.18.refs_4_ = bf16[384,128]{1,0:T(8,128)(2,1)} collective-permute-done((bf16[384,128]{1,0:T(8,128)(2,1)S(1)}, bf16[384,128]{1,0:T(8,128)(2,1)}, u32[]{:S(2)}, u32[]{:S(2)}) %collective-permute-start.18) | collective-permute-done | bytes 98336 | tf_op jit(solution)/shard_map/ppermute | solution.py:195
  45.8 1.1 %collective-permute-done.20.refs_6_ = bf16[384,128]{1,0:T(8,128)(2,1)} collective-permute-done((bf16[384,128]{1,0:T(8,128)(2,1)S(1)}, bf16[384,128]{1,0:T(8,128)(2,1)}, u32[]{:S(2)}, u32[]{:S(2)}) %collective-permute-start.20) | collective-permute-done | bytes 98336 | tf_op jit(solution)/shard_map/ppermute | solution.py:195
  47.0 0.9 %copy-done.4 = bf16[384,128]{1,0:T(8,128)(2,1)S(1)} copy-done((bf16[384,128]{1,0:T(8,128)(2,1)S(1)}, bf16[384,128]{1,0:T(8,128)(2,1)}, u32[]{:S(2)}) %copy-start.4) | copy-done | bytes 98328
  47.9 0.9 %copy-done.6 = bf16[384,128]{1,0:T(8,128)(2,1)S(1)} copy-done((bf16[384,128]{1,0:T(8,128)(2,1)S(1)}, bf16[384,128]{1,0:T(8,128)(2,1)}, u32[]{:S(2)}) %copy-start.6) | copy-done | bytes 98328
  48.8 0.9 %copy-done.8 = bf16[384,128]{1,0:T(8,128)(2,1)S(1)} copy-done((bf16[384,128]{1,0:T(8,128)(2,1)S(1)}, bf16[384,128]{1,0:T(8,128)(2,1)}, u32[]{:S(2)}) %copy-start.8) | copy-done | bytes 98328
  49.7 1.5 %shard_map.69.base_ref = f32[128,3072]{1,0:T(8,128)S(1)} custom-call(s32[8]{0:T(128)S(1)} %stack.74.first_ref, f32[128,3072]{1,0:T(8,128)S(1)} %get-tuple-element.13.after_ref.base_ref, bf16[128,3072]{1,0:T(8,128)(2,1)S(1)} %get-tuple-element.14.read_ref, bf16[384,128]{1,0:T(8,128)(2,1)S(1)} %fusion.refs_0_, bf16[384,128]{1,0:T(8,128)(2,1)S(1)} %copy-done.4, ...), custom_call_target="tpu_custom_call" | custom-call | flops 100663296 | bytes 3145728 | tf_op jit(solution)/shard_map/pallas_call | solution.py:180
  51.2 2.6 %shard_map.70 = bf16[128,3072]{1,0:T(8,128)(2,1)} custom-call(s32[8]{0:T(128)S(1)} %stack.74.first_ref, f32[128,3072]{1,0:T(8,128)S(1)} %shard_map.69.base_ref, bf16[128,3072]{1,0:T(8,128)(2,1)S(1)} %get-tuple-element.18.read_ref, bf16[384,128]{1,0:T(8,128)(2,1)S(1)} %collective-permute-done.14.refs_0_, bf16[384,128]{1,0:T(8,128)(2,1)} %collective-permute-done.15.refs_1_, ...), custom_call_target="tpu_custom_call" | custom-call | flops 100663296 | bytes 3145728 | tf_op jit(solution)/shard_map/pallas_call | solution.py:180
  (48 shorter events, 1.7 us)
Async XLA Ops:
  2.3 3.1 %collective-permute-start = (bf16[1536,128]{1,0:T(8,128)(2,1)S(1)}, bf16[1536,128]{1,0:T(8,128)(2,1)S(1)}, u32[]{:S(2)}, u32[]{:S(2)}) collective-permute-start(bf16[1536,128]{1,0:T(8,128)(2,1)S(1)} %shard_map.65), channel_id=1, source_target_pairs={{0,1},{1,0},{2,3},{3,2},{4,5},{5,4},{6,7},{7,6},{8,9},{9,8},{10,11... | collective-permute-start | bytes 1179656 | tf_op jit(solution)/shard_map/ppermute | solution.py:195
  2.8 8.6 %copy-start = (bf16[128,3072]{1,0:T(8,128)(2,1)S(1)}, bf16[128,3072]{1,0:T(8,128)(2,1)}, u32[]{:S(2)}) copy-start(bf16[128,3072]{1,0:T(8,128)(2,1)} %key_ref.5) | copy-start | bytes 2359300
  2.8 8.6 %copy-start.1 = (bf16[128,3072]{1,0:T(8,128)(2,1)S(1)}, bf16[128,3072]{1,0:T(8,128)(2,1)}, u32[]{:S(2)}) copy-start(bf16[128,3072]{1,0:T(8,128)(2,1)} %value_ref.5) | copy-start | bytes 2359300
  2.8 8.6 %copy-start.2 = (bf16[128,3072]{1,0:T(8,128)(2,1)S(1)}, bf16[128,3072]{1,0:T(8,128)(2,1)}, u32[]{:S(2)}) copy-start(bf16[128,3072]{1,0:T(8,128)(2,1)} %query_ref.1) | copy-start | bytes 2359300
  2.8 8.6 %copy-start.9 = (f32[3,24,128]{2,1,0:T(8,128)S(1)}, f32[3,24,128]{2,1,0:T(8,128)}, u32[]{:S(2)}) copy-start(f32[3,24,128]{2,1,0:T(8,128)} %weight_ref.1) | copy-start | bytes 110596
  2.8 8.6 %copy-start.10 = (s32[1,4]{1,0:T(1,128)S(1)}, s32[1,4]{1,0:T(1,128)}, u32[]{:S(2)}) copy-start(s32[1,4]{1,0:T(1,128)} %length_ref.1) | copy-start | bytes 52
  2.8 8.6 %copy-start.11 = (s32[1,4]{1,0:T(1,128)S(1)}, s32[1,4]{1,0:T(1,128)}, u32[]{:S(2)}) copy-start(s32[1,4]{1,0:T(1,128)} %back_ref.1) | copy-start | bytes 52
  6.0 12.6 %collective-permute-start.1 = (bf16[384,128]{1,0:T(8,128)(2,1)S(1)}, bf16[384,128]{1,0:T(8,128)(2,1)S(1)}, u32[]{:S(2)}, u32[]{:S(2)}) collective-permute-start(bf16[384,128]{1,0:T(8,128)(2,1)S(1)} %get-tuple-element.15), channel_id=1, source_target_pairs={{0,2},{2,0},{4,6},{6,4},{1,3},{3,1},{5,7},{7,5},{8,10},{10,8},{12,... | collective-permute-start | bytes 294920 | tf_op jit(solution)/shard_map/ppermute | solution.py:195
  8.7 10.8 %collective-permute-start.2 = (bf16[384,128]{1,0:T(8,128)(2,1)S(1)}, bf16[384,128]{1,0:T(8,128)(2,1)S(1)}, u32[]{:S(2)}, u32[]{:S(2)}) collective-permute-start(bf16[384,128]{1,0:T(8,128)(2,1)S(1)} %get-tuple-element.16), channel_id=1, source_target_pairs={{0,4},{2,6},{4,0},{6,2},{1,5},{3,7},{5,1},{7,3},{8,12},{10,14},{12... | collective-permute-start | bytes 294920 | tf_op jit(solution)/shard_map/ppermute | solution.py:195
  11.3 8.2 %collective-permute-start.3 = (bf16[384,128]{1,0:T(8,128)(2,1)S(1)}, bf16[384,128]{1,0:T(8,128)(2,1)S(1)}, u32[]{:S(2)}, u32[]{:S(2)}) collective-permute-start(bf16[384,128]{1,0:T(8,128)(2,1)S(1)} %get-tuple-element.17), channel_id=1, source_target_pairs={{0,6},{2,4},{4,2},{6,0},{1,7},{3,5},{5,3},{7,1},{8,14},{10,12},{12... | collective-permute-start | bytes 294920 | tf_op jit(solution)/shard_map/ppermute | solution.py:195
  19.5 5.7 %collective-permute-start.4 = (bf16[384,128]{1,0:T(8,128)(2,1)S(1)}, bf16[384,128]{1,0:T(8,128)(2,1)S(1)}, u32[]{:S(2)}, u32[]{:S(2)}) collective-permute-start(bf16[384,128]{1,0:T(8,128)(2,1)S(1)} %shard_map.68), channel_id=1, source_target_pairs={{0,16},{8,24},{16,0},{24,8},{1,17},{9,25},{17,1},{25,9},{2,18},{10... | collective-permute-start | bytes 294920 | tf_op jit(solution)/shard_map/ppermute | solution.py:195
  21.1 5.6 %collective-permute-start.5 = (bf16[384,128]{1,0:T(8,128)(2,1)S(1)}, bf16[384,128]{1,0:T(8,128)(2,1)S(1)}, u32[]{:S(2)}, u32[]{:S(2)}) collective-permute-start(bf16[384,128]{1,0:T(8,128)(2,1)S(1)} %shard_map.68), channel_id=1, source_target_pairs={{0,24},{8,16},{16,8},{24,0},{1,25},{9,17},{17,9},{25,1},{2,26},{10... | collective-permute-start | bytes 294920 | tf_op jit(solution)/shard_map/ppermute | solution.py:195
  22.6 4.6 %collective-permute-start.6 = (bf16[384,128]{1,0:T(8,128)(2,1)S(1)}, bf16[384,128]{1,0:T(8,128)(2,1)S(1)}, u32[]{:S(2)}, u32[]{:S(2)}) collective-permute-start(bf16[384,128]{1,0:T(8,128)(2,1)S(1)} %shard_map.68), channel_id=1, source_target_pairs={{0,8},{8,0},{16,24},{24,16},{1,9},{9,1},{17,25},{25,17},{2,10},{10... | collective-permute-start | bytes 294920 | tf_op jit(solution)/shard_map/ppermute | solution.py:195
  27.2 8.5 %collective-permute-start.10 = (bf16[384,128]{1,0:T(8,128)(2,1)S(1)}, bf16[384,128]{1,0:T(8,128)(2,1)S(1)}, u32[]{:S(2)}, u32[]{:S(2)}) collective-permute-start(bf16[384,128]{1,0:T(8,128)(2,1)S(1)} %fusion.refs_0_), channel_id=1, source_target_pairs={{0,4},{2,6},{4,0},{6,2},{1,5},{3,7},{5,1},{7,3},{8,12},{10,14},{12... | collective-permute-start | bytes 294920 | tf_op jit(solution)/shard_map/ppermute | solution.py:195
  30.2 6.7 %collective-permute-start.12 = (bf16[384,128]{1,0:T(8,128)(2,1)S(1)}, bf16[384,128]{1,0:T(8,128)(2,1)S(1)}, u32[]{:S(2)}, u32[]{:S(2)}) collective-permute-start(bf16[384,128]{1,0:T(8,128)(2,1)S(1)} %fusion.refs_0_), channel_id=1, source_target_pairs={{0,6},{2,4},{4,2},{6,0},{1,7},{3,5},{5,3},{7,1},{8,14},{10,12},{12... | collective-permute-start | bytes 294920 | tf_op jit(solution)/shard_map/ppermute | solution.py:195
  31.5 6.2 %collective-permute-start.8 = (bf16[384,128]{1,0:T(8,128)(2,1)S(1)}, bf16[384,128]{1,0:T(8,128)(2,1)}, u32[]{:S(2)}, u32[]{:S(2)}) collective-permute-start(bf16[384,128]{1,0:T(8,128)(2,1)S(1)} %fusion.refs_0_), channel_id=1, source_target_pairs={{0,2},{2,0},{4,6},{6,4},{1,3},{3,1},{5,7},{7,5},{8,10},{10,8},{12,... | collective-permute-start | bytes 294920 | tf_op jit(solution)/shard_map/ppermute | solution.py:195
  31.5 7.4 %collective-permute-start.7 = (bf16[384,128]{1,0:T(8,128)(2,1)S(1)}, bf16[384,128]{1,0:T(8,128)(2,1)S(1)}, u32[]{:S(2)}, u32[]{:S(2)}) collective-permute-start(bf16[384,128]{1,0:T(8,128)(2,1)S(1)} %fusion.refs_0_), channel_id=1, source_target_pairs={{0,1},{1,0},{2,3},{3,2},{4,5},{5,4},{6,7},{7,6},{8,9},{9,8},{10,11... | collective-permute-start | bytes 294920 | tf_op jit(solution)/shard_map/ppermute | solution.py:195
  31.5 8.9 %collective-permute-start.14 = (bf16[384,128]{1,0:T(8,128)(2,1)S(1)}, bf16[384,128]{1,0:T(8,128)(2,1)S(1)}, u32[]{:S(2)}, u32[]{:S(2)}) collective-permute-start(bf16[384,128]{1,0:T(8,128)(2,1)S(1)} %fusion.refs_0_), channel_id=1, source_target_pairs={{0,8},{8,0},{16,24},{24,16},{1,9},{9,1},{17,25},{25,17},{2,10},{10... | collective-permute-start | bytes 294920 | tf_op jit(solution)/shard_map/ppermute | solution.py:195
  35.7 5.9 %collective-permute-start.11 = (bf16[384,128]{1,0:T(8,128)(2,1)S(1)}, bf16[384,128]{1,0:T(8,128)(2,1)S(1)}, u32[]{:S(2)}, u32[]{:S(2)}) collective-permute-start(bf16[384,128]{1,0:T(8,128)(2,1)S(1)} %collective-permute-done.10.refs_4_), channel_id=1, source_target_pairs={{0,1},{1,0},{2,3},{3,2},{4,5},{5,4},{6,7},{7,6},{8,9},{9,8},{10,11... | collective-permute-start | bytes 294920 | tf_op jit(solution)/shard_map/ppermute | solution.py:195
  37.0 5.3 %collective-permute-start.13 = (bf16[384,128]{1,0:T(8,128)(2,1)S(1)}, bf16[384,128]{1,0:T(8,128)(2,1)S(1)}, u32[]{:S(2)}, u32[]{:S(2)}) collective-permute-start(bf16[384,128]{1,0:T(8,128)(2,1)S(1)} %collective-permute-done.12.refs_6_), channel_id=1, source_target_pairs={{0,1},{1,0},{2,3},{3,2},{4,5},{5,4},{6,7},{7,6},{8,9},{9,8},{10,11... | collective-permute-start | bytes 294920 | tf_op jit(solution)/shard_map/ppermute | solution.py:195
  37.7 5.9 %collective-permute-start.16 = (bf16[384,128]{1,0:T(8,128)(2,1)}, bf16[384,128]{1,0:T(8,128)(2,1)}, u32[]{:S(2)}, u32[]{:S(2)}) collective-permute-start(bf16[384,128]{1,0:T(8,128)(2,1)} %collective-permute-done.8.refs_2_), channel_id=1, source_target_pairs={{0,8},{8,0},{16,24},{24,16},{1,9},{9,1},{17,25},{25,17},{2,10},{10... | collective-permute-start | bytes 294920 | tf_op jit(solution)/shard_map/ppermute | solution.py:195
  39.6 6.2 %collective-permute-start.18 = (bf16[384,128]{1,0:T(8,128)(2,1)S(1)}, bf16[384,128]{1,0:T(8,128)(2,1)}, u32[]{:S(2)}, u32[]{:S(2)}) collective-permute-start(bf16[384,128]{1,0:T(8,128)(2,1)S(1)} %collective-permute-done.10.refs_4_), channel_id=1, source_target_pairs={{0,8},{8,0},{16,24},{24,16},{1,9},{9,1},{17,25},{25,17},{2,10},{10... | collective-permute-start | bytes 294920 | tf_op jit(solution)/shard_map/ppermute | solution.py:195
  40.4 6.5 %collective-permute-start.20 = (bf16[384,128]{1,0:T(8,128)(2,1)S(1)}, bf16[384,128]{1,0:T(8,128)(2,1)}, u32[]{:S(2)}, u32[]{:S(2)}) collective-permute-start(bf16[384,128]{1,0:T(8,128)(2,1)S(1)} %collective-permute-done.12.refs_6_), channel_id=1, source_target_pairs={{0,8},{8,0},{16,24},{24,16},{1,9},{9,1},{17,25},{25,17},{2,10},{10... | collective-permute-start | bytes 294920 | tf_op jit(solution)/shard_map/ppermute | solution.py:195
  42.3 4.7 %collective-permute-start.9 = (bf16[384,128]{1,0:T(8,128)(2,1)}, bf16[384,128]{1,0:T(8,128)(2,1)}, u32[]{:S(2)}, u32[]{:S(2)}) collective-permute-start(bf16[384,128]{1,0:T(8,128)(2,1)} %collective-permute-done.8.refs_2_), channel_id=1, source_target_pairs={{0,1},{1,0},{2,3},{3,2},{4,5},{5,4},{6,7},{7,6},{8,9},{9,8},{10,11... | collective-permute-start | bytes 294920 | tf_op jit(solution)/shard_map/ppermute | solution.py:195
  42.3 0.6 %copy-start.7 = (bf16[384,128]{1,0:T(8,128)(2,1)}, bf16[384,128]{1,0:T(8,128)(2,1)S(1)}, u32[]{:S(2)}) copy-start(bf16[384,128]{1,0:T(8,128)(2,1)S(1)} %collective-permute-done.13.refs_7_) | copy-start | bytes 294916
  42.9 8.2 %collective-permute-start.15 = (bf16[384,128]{1,0:T(8,128)(2,1)S(1)}, bf16[384,128]{1,0:T(8,128)(2,1)}, u32[]{:S(2)}, u32[]{:S(2)}) collective-permute-start(bf16[384,128]{1,0:T(8,128)(2,1)S(1)} %collective-permute-done.14.refs_0_), channel_id=1, source_target_pairs={{0,1},{1,0},{2,3},{3,2},{4,5},{5,4},{6,7},{7,6},{8,9},{9,8},{10,11... | collective-permute-start | bytes 294920 | tf_op jit(solution)/shard_map/ppermute | solution.py:195
  43.7 7.5 %collective-permute-start.17 = (bf16[384,128]{1,0:T(8,128)(2,1)}, bf16[384,128]{1,0:T(8,128)(2,1)}, u32[]{:S(2)}, u32[]{:S(2)}) collective-permute-start(bf16[384,128]{1,0:T(8,128)(2,1)} %collective-permute-done.16.refs_2_), channel_id=1, source_target_pairs={{0,1},{1,0},{2,3},{3,2},{4,5},{5,4},{6,7},{7,6},{8,9},{9,8},{10,11... | collective-permute-start | bytes 294920 | tf_op jit(solution)/shard_map/ppermute | solution.py:195
  45.8 5.4 %collective-permute-start.19 = (bf16[384,128]{1,0:T(8,128)(2,1)}, bf16[384,128]{1,0:T(8,128)(2,1)}, u32[]{:S(2)}, u32[]{:S(2)}) collective-permute-start(bf16[384,128]{1,0:T(8,128)(2,1)} %collective-permute-done.18.refs_4_), channel_id=1, source_target_pairs={{0,1},{1,0},{2,3},{3,2},{4,5},{5,4},{6,7},{7,6},{8,9},{9,8},{10,11... | collective-permute-start | bytes 294920 | tf_op jit(solution)/shard_map/ppermute | solution.py:195
  46.9 4.3 %collective-permute-start.21 = (bf16[384,128]{1,0:T(8,128)(2,1)}, bf16[384,128]{1,0:T(8,128)(2,1)}, u32[]{:S(2)}, u32[]{:S(2)}) collective-permute-start(bf16[384,128]{1,0:T(8,128)(2,1)} %collective-permute-done.20.refs_6_), channel_id=1, source_target_pairs={{0,1},{1,0},{2,3},{3,2},{4,5},{5,4},{6,7},{7,6},{8,9},{9,8},{10,11... | collective-permute-start | bytes 294920 | tf_op jit(solution)/shard_map/ppermute | solution.py:195
  47.0 0.9 %copy-start.4 = (bf16[384,128]{1,0:T(8,128)(2,1)S(1)}, bf16[384,128]{1,0:T(8,128)(2,1)}, u32[]{:S(2)}) copy-start(bf16[384,128]{1,0:T(8,128)(2,1)} %copy-done.3) | copy-start | bytes 294916
  47.9 0.9 %copy-start.6 = (bf16[384,128]{1,0:T(8,128)(2,1)S(1)}, bf16[384,128]{1,0:T(8,128)(2,1)}, u32[]{:S(2)}) copy-start(bf16[384,128]{1,0:T(8,128)(2,1)} %copy-done.5) | copy-start | bytes 294916
  48.8 0.9 %copy-start.8 = (bf16[384,128]{1,0:T(8,128)(2,1)S(1)}, bf16[384,128]{1,0:T(8,128)(2,1)}, u32[]{:S(2)}) copy-start(bf16[384,128]{1,0:T(8,128)(2,1)} %copy-done.7) | copy-start | bytes 294916
  (2 other events, 1.3 us)

commit v4 on v3

v4 whole, which is shorter than its diff:
```python
import functools
import math

import jax
import jax.numpy as jnp
from jax import lax
from jax.experimental import pallas as pl
from jax.experimental.pallas import tpu as pltpu
from jax.sharding import Mesh, PartitionSpec as P

HEADS = 24
HEAD_DIM = 128
EPSILON = 1e-06
VMEM_LIMIT = 40 * 1024 * 1024

F32, BF16 = jnp.float32, jnp.bfloat16
WHOLE = pl.BlockSpec(memory_space=pltpu.VMEM)
SCALARS = pl.BlockSpec(memory_space=pltpu.SMEM)
IN_HBM = pl.BlockSpec(memory_space=pltpu.HBM)
PARAMS = pltpu.CompilerParams(vmem_limit_bytes=VMEM_LIMIT)


def inverse_rms(rows):
    return lax.rsqrt(jnp.mean(rows * rows, -1, keepdims=True) + EPSILON)


def columns(head, count=1):
    return pl.ds(pl.multiple_of(head * HEAD_DIM, HEAD_DIM), count * HEAD_DIM)


def core_heads():
    core = lax.axis_index("core")
    return core * (HEADS // 2), (1 - core) * (HEADS // 2)


def in_vmem(*arrays):
    return [pltpu.with_memory_space_constraint(array, pltpu.VMEM) for array in arrays]


def states_of(first, keys, values, out_ref):
    for h in range(out_ref.shape[0] // HEAD_DIM):
        at = columns(first + h)
        key_rows = keys[:, at].astype(F32)
        normal = (key_rows * inverse_rms(key_rows)).astype(BF16)
        state = lax.dot_general(
            normal, values[:, at], (((0,), (0,)), ((), ())), preferred_element_type=F32
        )
        out_ref[h * HEAD_DIM : (h + 1) * HEAD_DIM, :] = state.astype(out_ref.dtype)


def first_kernel(key_ref, value_ref, out_ref, keys, values, sems):
    mine, other = core_heads()
    copies = []
    for n, first in enumerate((other, mine)):
        at = columns(first, HEADS // 2)
        for s, (ref, held) in enumerate(((key_ref, keys), (value_ref, values))):
            copies.append(pltpu.make_async_copy(ref.at[:, at], held.at[:, at], sems.at[n, s]))
            copies[-1].start()
    copies[0].wait()
    copies[1].wait()
    states_of(other, keys, values, out_ref)
    copies[2].wait()
    copies[3].wait()


def outgoing_state(keys, values):
    dim, half = HEAD_DIM, HEADS // 2
    rows = keys.shape[0]
    keys, values = (pltpu.with_memory_space_constraint(x, pltpu.HBM) for x in (keys, values))
    return pl.pallas_call(
        first_kernel,
        out_shape=[pltpu.VMEM((half * dim, dim), BF16)] + [pltpu.VMEM(keys.shape, BF16)] * 2,
        in_specs=[IN_HBM, IN_HBM],
        out_specs=[WHOLE] * 3,
        scratch_shapes=[pltpu.SemaphoreType.DMA((2, 2))],
        compiler_params=PARAMS,
        cost_estimate=pl.CostEstimate(
            flops=2 * half * rows * dim * dim, bytes_accessed=8 * half * rows * dim, transcendentals=0
        ),
    )(keys, values)


def own_kernel(key_ref, value_ref, out_ref):
    states_of(core_heads()[0], key_ref, value_ref, out_ref)


def own_state(keys, values):
    dim, half = HEAD_DIM, HEADS // 2
    rows = keys.shape[0]
    return pl.pallas_call(
        own_kernel,
        out_shape=pltpu.VMEM((half * dim, dim), F32),
        in_specs=[WHOLE, WHOLE],
        out_specs=WHOLE,
        compiler_params=PARAMS,
        cost_estimate=pl.CostEstimate(
            flops=2 * half * rows * dim * dim, bytes_accessed=8 * half * rows * dim, transcendentals=0
        ),
    )(*in_vmem(keys, values))


def piece_kernel(mine_ref, other_ref, own_ref, *piece_refs):
    chip = lax.axis_index("chip")
    rows = own_ref.shape[0]
    for d, ref in enumerate((own_ref,) + piece_refs):
        at = pl.ds(pl.multiple_of((chip ^ d) * rows, rows), rows)
        ref[...] = (mine_ref[at, :] + other_ref[at, :].astype(F32)).astype(ref.dtype)


def chip_pieces(mine, other, chips):
    shape = (mine.shape[0] // chips, HEAD_DIM)
    return pl.pallas_call(
        piece_kernel,
        out_shape=[pltpu.VMEM(shape, F32)] + [pltpu.VMEM(shape, BF16)] * (chips - 1),
        in_specs=[WHOLE, WHOLE],
        out_specs=[WHOLE] * chips,
        compiler_params=PARAMS,
    )(mine, other)


def sum_kernel(after_ref, own_ref, *refs):
    total = own_ref[...]
    for ref in refs[:-1]:
        total = total + ref[...].astype(F32)
    refs[-1][...] = total.astype(refs[-1].dtype)


def sum_pieces(after, own, parts, dtype):
    return pl.pallas_call(
        sum_kernel,
        out_shape=pltpu.VMEM(own.shape, dtype),
        in_specs=[pl.BlockSpec(memory_space=pl.ANY)] + [WHOLE] * (1 + len(parts)),
        out_specs=WHOLE,
        compiler_params=PARAMS,
    )(after, own, *parts)


def pack_kernel(groups, after, *refs):
    inputs, outputs = refs[after : len(refs) - len(groups)], refs[len(refs) - len(groups) :]
    for group, out_ref in zip(groups, outputs):
        rows = out_ref.shape[0] // len(group)
        for n, which in enumerate(group):
            out_ref[n * rows : (n + 1) * rows, :] = inputs[which][...]


def pack(groups, pieces, after):
    rows = pieces[0].shape[0]
    return pl.pallas_call(
        functools.partial(pack_kernel, groups, len(after)),
        out_shape=[pltpu.VMEM((rows * len(group), HEAD_DIM), BF16) for group in groups],
        in_specs=[pl.BlockSpec(memory_space=pl.ANY)] * len(after) + [WHOLE] * len(pieces),
        out_specs=[WHOLE] * len(groups),
        compiler_params=PARAMS,
    )(*after, *in_vmem(*pieces))


def local_kernel(
    coefs, turn, length_ref, back_ref, query_ref, key_ref, value_ref, weight_ref, after_ref, local_ref, *read_refs
):
    tokens = query_ref.shape[0]
    first = core_heads()[turn]
    heads = local_ref.shape[1] // HEAD_DIM
    key_at = lax.broadcasted_iota(jnp.int32, (tokens, tokens), 0)
    query_at = lax.broadcasted_iota(jnp.int32, (tokens, tokens), 1)
    start = jnp.int32(0)
    floor = jnp.zeros((tokens, tokens), jnp.int32)
    for k in range(length_ref.shape[1]):
        lowest = jnp.maximum(start - back_ref[0, k], 0)
        floor = jnp.where(query_at >= start, lowest, floor)
        start = start + length_ref[0, k]
    hidden = jnp.where((key_at <= query_at) & (key_at >= floor), 0.0, -jnp.inf).astype(F32)
    scale = math.log2(math.e) / math.sqrt(HEAD_DIM)
    ones = jnp.full((HEAD_DIM, HEAD_DIM), 1.0 / HEAD_DIM, BF16)
    half = HEADS // 2
    by_slot = []
    for slot_coefs in coefs(lax.axis_index("frame")):
        total = None
        for level, coef in slot_coefs:
            term = weight_ref[1 + level, pl.ds(first, heads), :] * coef
            total = term if total is None else total + term
        by_slot.append(total)
    pad = -len(by_slot) * heads % HEAD_DIM
    gains = jnp.concatenate(by_slot + [jnp.zeros((pad, tokens), F32)], 0).T

    def scores_of(h):
        at = columns(first + h)
        return lax.dot_general(
            key_ref[:, at], query_ref[:, at], (((1,), (1,)), ((), ())), preferred_element_type=F32
        )

    upcoming = scores_of(0)
    for h in range(heads):
        scores = upcoming * scale + hidden
        if h + 1 < heads:
            upcoming = scores_of(h + 1)
        weights = jnp.exp2(scores - jnp.max(scores, 0, keepdims=True))
        total = jnp.sum(weights, 0, keepdims=True)
        weights = weights * (weight_ref[0, pl.ds(first + h, 1), :] / total)
        at = slice(h * HEAD_DIM, (h + 1) * HEAD_DIM)
        local_ref[:, at] = lax.dot_general(
            weights.astype(BF16),
            value_ref[:, columns(first + h)],
            (((0,), (0,)), ((), ())),
            preferred_element_type=F32,
        )
        query = query_ref[:, columns(first + h)].astype(F32)
        mean = jnp.dot((query * query).astype(BF16), ones, preferred_element_type=F32)
        query = query * lax.rsqrt(mean + EPSILON)
        for slot, read_ref in enumerate(read_refs):
            which = slot * heads + h
            read_ref[:, at] = (query * gains[:, which : which + 1]).astype(BF16)


def local_part(coefs, slots, turn, frame_len, window_back, queries, keys, values, weights, after):
    tokens, width = queries.shape
    width //= 2
    return pl.pallas_call(
        functools.partial(local_kernel, coefs, turn),
        out_shape=[pltpu.VMEM((tokens, width), F32)] + [pltpu.VMEM((tokens, width), BF16)] * slots,
        in_specs=[SCALARS] * 2 + [WHOLE] * 4 + [pl.BlockSpec(memory_space=pl.ANY)],
        out_specs=[WHOLE] * (1 + slots),
        compiler_params=PARAMS,
        cost_estimate=pl.CostEstimate(
            flops=4 * tokens * tokens * width,
            bytes_accessed=14 * tokens * width,
            transcendentals=tokens * width,
        ),
    )(frame_len, window_back, queries, *in_vmem(keys, values), weights, after)


def read_heads(d, chips, base_ref, states):
    count = HEADS // 2 // chips
    first = (lax.axis_index("chip") ^ d) * count
    for h in range(count):
        at = columns(first + h)
        result = base_ref[:, at]
        for read_ref, state_ref, row in states:
            result = result + jnp.dot(
                read_ref[:, at],
                state_ref[row + h * HEAD_DIM : row + (h + 1) * HEAD_DIM, :],
                preferred_element_type=F32,
            )
        yield at, result


def middle_kernel(chips, early, local_ref, x_ref, y_ref, state_ref, out_ref):
    rows = state_ref.shape[0] // (chips + early)
    for d in range(chips):
        states = [(x_ref, state_ref, d * rows)]
        if d < early:
            states.append((y_ref, state_ref, (chips + d) * rows))
        for at, result in read_heads(d, chips, local_ref, states):
            out_ref[:, at] = result


def read_middle(chips, early, local, x, y, states):
    return pl.pallas_call(
        functools.partial(middle_kernel, chips, early),
        out_shape=pltpu.VMEM(local.shape, F32),
        in_specs=[WHOLE] * 4,
        out_specs=WHOLE,
        compiler_params=PARAMS,
        cost_estimate=pl.CostEstimate(
            flops=2 * local.size * HEAD_DIM, bytes_accessed=8 * local.size, transcendentals=0
        ),
    )(*in_vmem(local, x, y, states))


def late_half(chips, early, base_ref, y_ref, state_ref, out_ref):
    rows = state_ref.shape[0] // max(chips - early, 1)
    for d in range(chips):
        states = [(y_ref, state_ref, (d - early) * rows)] if d >= early else []
        for at, result in read_heads(d, chips, base_ref, states):
            out_ref[:, at] = result.astype(BF16)


def read_late(chips, early, base, y, states):
    return pl.pallas_call(
        functools.partial(late_half, chips, early),
        out_shape=pltpu.VMEM(base.shape, BF16),
        in_specs=[WHOLE] * 3,
        out_specs=WHOLE,
        compiler_params=PARAMS,
        cost_estimate=pl.CostEstimate(
            flops=base.size * HEAD_DIM, bytes_accessed=6 * base.size, transcendentals=0
        ),
    )(*in_vmem(base, y, states))


def last_kernel(chips, early, done_ref, base_ref, y_ref, state_ref, out_ref, held, sems):
    mine, other = core_heads()
    first = pltpu.make_async_copy(done_ref, out_ref.at[:, columns(mine, HEADS // 2)], sems.at[0])
    first.start()
    late_half(chips, early, base_ref, y_ref, state_ref, held)
    second = pltpu.make_async_copy(held, out_ref.at[:, columns(other, HEADS // 2)], sems.at[1])
    second.start()
    first.wait()
    second.wait()


def read_last(chips, early, done, base, y, states):
    tokens, width = base.shape
    return pl.pallas_call(
        functools.partial(last_kernel, chips, early),
        out_shape=jax.ShapeDtypeStruct((tokens, 2 * width), BF16),
        in_specs=[WHOLE] * 4,
        out_specs=pl.BlockSpec(memory_space=pl.ANY),
        scratch_shapes=[pltpu.VMEM((tokens, width), BF16), pltpu.SemaphoreType.DMA((2,))],
        compiler_params=PARAMS,
        cost_estimate=pl.CostEstimate(
            flops=base.size * HEAD_DIM, bytes_accessed=10 * base.size, transcendentals=0
        ),
    )(*in_vmem(done, base, y, states))


def swap(array, axis, mask, size):
    return lax.ppermute(array, axis, [(n, n ^ mask) for n in range(size)])


def body(sizes, queries, keys, values, level_weight, frame_len, window_back):
    frames, outer, chips = sizes
    frame = lax.axis_index("frame")
    low, high = (
        1.0 / math.sqrt(HEAD_DIM * 2**level * queries.shape[0] * outer * chips * 2) for level in (0, 1)
    )

    def coefs(f):
        x_low = jnp.where(f % 2 == 1, low, 0.0)
        x_high = jnp.where(f == 2, high, 0.0)
        return [[(0, x_low), (1, x_high)], [(1, jnp.where(f == 3, high, 0.0))]]

    local = functools.partial(local_part, coefs, 2)
    rest = (frame_len, window_back, queries)

    outgoing, keys, values = outgoing_state(keys, values)
    incoming = swap(outgoing, "core", 1, 2)
    mine = own_state(keys, values)
    own, *sends = chip_pieces(mine, incoming, chips)
    got = {d: swap(sends[d - 1], "chip", d, chips) for d in reversed(range(1, chips))}

    local_0, x_0, y_0 = local(0, *rest, keys, values, level_weight, own)
    state = sum_pieces(local_0, own, list(got.values()), F32 if outer > 1 else BF16)
    if outer > 1:
        state = lax.psum(state, "outer").astype(BF16)
    near, across, diagonal = (swap(state, "frame", mask, frames) for mask in (1, 2, 3))
    both = (across.astype(F32) + diagonal.astype(F32)).astype(BF16)
    slot = jnp.where(frame == 2, both, near)

    early = min(2, chips)
    x = [swap(slot, "chip", d, chips) for d in range(1, chips)]
    near_pairs = [
        (f * chips + c, (f ^ 1) * chips + (c ^ 1)) for f in range(frames) for c in range(chips)
    ]
    y = [swap(slot, "frame", 1, frames), lax.ppermute(slot, ("frame", "chip"), near_pairs)][:early]
    local_1, x_1, y_1 = local(1, *rest, keys, values, level_weight, slot)
    pieces = [slot] + x + y
    own_states, late = pack(
        [list(range(chips + early)), list(range(early, chips)) or [0]], pieces, [local_1]
    )
    late_own = swap(late, "frame", 1, frames)
    other_states = swap(own_states, "core", 1, 2)
    base_0 = read_middle(chips, early, local_0, x_0, y_0, own_states)
    base_1 = read_middle(chips, early, local_1, x_1, y_1, other_states)
    late_own, base_0, base_1 = lax.optimization_barrier((late_own, base_0, base_1))
    late_other = swap(late_own, "core", 1, 2)
    done = read_late(chips, early, base_0, y_0, late_own)
    return read_last(chips, early, done, base_1, y_1, late_other)


def solution(mesh):
    frames, space = mesh.shape["frame"], mesh.shape["space"]
    chips = 1
    while HEADS % (chips * 4) == 0 and space % (chips * 4) == 0 and chips < 4:
        chips *= 2
    sizes = (frames, space // (2 * chips), chips)
    names = ("frame", "outer", "chip", "core")
    fine = Mesh(mesh.devices.reshape(sizes + (2,)), names)
    rows = P(names, None)
    return jax.shard_map(
        functools.partial(body, sizes),
        mesh=fine,
        in_specs=(rows, rows, rows, P(None, None, names), rows, rows),
        out_specs=rows,
        check_vma=False,
    )
```

time: 54.1 us -> 48.9 us (0.904)
  waiting for transfers between devices: 13.4 us -> 21.6 us
  Pallas kernels: 16.6 us -> 8.41 us
  local copies, waits for them, and re-layouts: 4.7 us -> 0.05 us
  starting transfers between devices: 18.7 us -> 17.5 us
  other arithmetic: 0.21 us -> 1.03 us
    pallas_call x7 -> x11, Pallas kernels: 16.6 us -> 8.41 us  [the longest x2 3.43 us: local_part(): pl.pallas_call(functools.partial(local_kernel, coefs, turn), out_shape=[p...]
    ppermute x22 -> x14, waiting for transfers between devices: 13.4 us -> 20.9 us  [swap(): return lax.ppermute(array, axis, [(n, n ^ mask) for n in range(size)])]
    unnamed x24 -> x14, local copies, waits for them, and re-layouts: 4.62 us -> 0.05 us
    ppermute x22 -> x14, starting transfers between devices: 18.7 us -> 16.1 us  [swap(): return lax.ppermute(array, axis, [(n, n ^ mask) for n in range(size)])]
    ppermute x0 -> x1, starting transfers between devices: none -> 1.42 us  [body(): lax.ppermute(slot, ('frame', 'chip'), near_pairs)]
    select_n x1, other arithmetic: 0.04 us -> 1.03 us  [body(): slot = jnp.where(frame == 2, both, near)]
    ppermute x0 -> x1, waiting for transfers between devices: none -> 0.76 us  [body(): lax.ppermute(slot, ('frame', 'chip'), near_pairs)]
  transfers between devices with their start and end apart: 22 -> 15, of which waited for: 10 -> 11; matrix products, arithmetic and copies ran while one was open for 0% -> 0% of each run, Pallas kernels for 21% -> 10%
where the time goes in v4:
time: 48.9 us; the launch traced here: 48.8 us
  waiting for transfers between devices  21.6 us (44%)
  starting transfers between devices  17.5 us (36%)
  Pallas kernels  8.41 us (17%)
  other arithmetic  1.03 us (2%)
    ppermute x14, waiting for transfers between devices, swap(): return lax.ppermute(array, axis, [(n, n ^ mask) for n in range(size)])  20.9 us
    ppermute x14, starting transfers between devices, swap(): return lax.ppermute(array, axis, [(n, n ^ mask) for n in range(size)])  16.1 us
    pallas_call x2, Pallas kernels, local_part(): pl.pallas_call(functools.partial(local_kernel, coefs, turn), out_shape=[p...  3.43 us
    pallas_call x1, Pallas kernels, outgoing_state(): pl.pallas_call(first_kernel, out_shape=[pltpu.VMEM((half * dim, dim), BF1...  1.68 us
    ppermute x1, starting transfers between devices, body(): lax.ppermute(slot, ('frame', 'chip'), near_pairs)  1.42 us
    select_n x1, other arithmetic, body(): slot = jnp.where(frame == 2, both, near)  1.03 us
    pallas_call x1, Pallas kernels, read_last(): pl.pallas_call(functools.partial(last_kernel, chips, early), out_shape=ja...  1.02 us
  transfers between devices with their start and end apart: 15, of which 11 were waited for; matrix products, arithmetic and copies ran while one was open for 0% of the time, Pallas kernels for 10%

profile of v4, /device:TPU:0, one launch (start us, length us, event | category | flops | bytes accessed | tf_op | source)
XLA Modules:
  0.0 48.8 jit_solution(7352982460085201965)
XLA Ops:
  0.0 1.7 %shard_map.64 = (bf16[1536,128]{1,0:T(8,128)(2,1)S(1)}, bf16[128,3072]{1,0:T(8,128)(2,1)S(1)}, bf16[128,3072]{1,0:T(8,128)(2,1)S(1)}) custom-call(bf16[128,3072]{1,0:T(8,128)(2,1)} %key_ref.1, bf16[128,3072]{1,0:T(8,128)(2,1)} %value_ref.1), custom_call_target="tpu_custom_call" | custom-call | flops 50331648 | bytes 1572864 | tf_op jit(solution)/shard_map/pallas_call | solution.py:70
  1.7 0.5 %collective-permute-start = (bf16[1536,128]{1,0:T(8,128)(2,1)S(1)}, bf16[1536,128]{1,0:T(8,128)(2,1)S(1)}, u32[]{:S(2)}, u32[]{:S(2)}) collective-permute-start(bf16[1536,128]{1,0:T(8,128)(2,1)S(1)} %get-tuple-element.25), channel_id=1, source_target_pairs={{0,1},{1,0},{2,3},{3,2},{4,5},{5,4},{6,7},{7,6},{8,9},{9,8},{10,11... | collective-permute-start | bytes 1179656 | tf_op jit(solution)/shard_map/ppermute | solution.py:317
  2.2 0.5 %shard_map.65.mine_ref = f32[1536,128]{1,0:T(8,128)S(1)} custom-call(bf16[128,3072]{1,0:T(8,128)(2,1)S(1)} %get-tuple-element.23.key_ref, bf16[128,3072]{1,0:T(8,128)(2,1)S(1)} %get-tuple-element.24.value_ref), custom_call_target="tpu_custom_call" | custom-call | flops 50331648 | bytes 1572864 | tf_op jit(solution)/shard_map/pallas_call | solution.py:90
  2.8 0.8 %collective-permute-done.other_ref = bf16[1536,128]{1,0:T(8,128)(2,1)S(1)} collective-permute-done((bf16[1536,128]{1,0:T(8,128)(2,1)S(1)}, bf16[1536,128]{1,0:T(8,128)(2,1)S(1)}, u32[]{:S(2)}, u32[]{:S(2)}) %collective-permute-start) | collective-permute-done | bytes 393248 | tf_op jit(solution)/shard_map/ppermute | solution.py:317
  3.6 5.0 %collective-permute-start.1 = (bf16[384,128]{1,0:T(8,128)(2,1)S(1)}, bf16[384,128]{1,0:T(8,128)(2,1)S(1)}, u32[]{:S(2)}, u32[]{:S(2)}) collective-permute-start(bf16[384,128]{1,0:T(8,128)(2,1)S(1)} %get-tuple-element.28), channel_id=1, source_target_pairs={{0,6},{2,4},{4,2},{6,0},{1,7},{3,5},{5,3},{7,1},{8,14},{10,12},{12... | collective-permute-start | bytes 294920 | tf_op jit(solution)/shard_map/ppermute | solution.py:317
  8.7 0.6 %collective-permute-start.3 = (bf16[384,128]{1,0:T(8,128)(2,1)S(1)}, bf16[384,128]{1,0:T(8,128)(2,1)S(1)}, u32[]{:S(2)}, u32[]{:S(2)}) collective-permute-start(bf16[384,128]{1,0:T(8,128)(2,1)S(1)} %get-tuple-element.30), channel_id=1, source_target_pairs={{0,2},{2,0},{4,6},{6,4},{1,3},{3,1},{5,7},{7,5},{8,10},{10,8},{12,... | collective-permute-start | bytes 294920 | tf_op jit(solution)/shard_map/ppermute | solution.py:317
  9.4 1.7 %shard_map.67 = (f32[128,1536]{1,0:T(8,128)S(1)}, bf16[128,1536]{1,0:T(8,128)(2,1)S(1)}, bf16[128,1536]{1,0:T(8,128)(2,1)S(1)}) custom-call(s32[1,4]{1,0:T(1,128)S(1)} %copy-done.5, s32[1,4]{1,0:T(1,128)S(1)} %copy-done.6, bf16[128,3072]{1,0:T(8,128)(2,1)S(1)} %copy-done, bf16[128,3072]{1,0:T(8,128)(2,1)S(1)} %get-tuple-element.23.key_ref, ...), custom_call_target="tpu_custom_call" | custom-call | flops 100663296 | bytes 2752512 | tf_op jit(solution)/shard_map/pallas_call | solution.py:217
  11.1 1.3 %collective-permute-done.1.refs_0_ = bf16[384,128]{1,0:T(8,128)(2,1)S(1)} collective-permute-done((bf16[384,128]{1,0:T(8,128)(2,1)S(1)}, bf16[384,128]{1,0:T(8,128)(2,1)S(1)}, u32[]{:S(2)}, u32[]{:S(2)}) %collective-permute-start.1) | collective-permute-done | bytes 98336 | tf_op jit(solution)/shard_map/ppermute | solution.py:317
  12.4 4.9 %collective-permute-done.2.refs_1_ = bf16[384,128]{1,0:T(8,128)(2,1)S(1)} collective-permute-done((bf16[384,128]{1,0:T(8,128)(2,1)S(1)}, bf16[384,128]{1,0:T(8,128)(2,1)S(1)}, u32[]{:S(2)}, u32[]{:S(2)}) %collective-permute-start.2) | collective-permute-done | bytes 98336 | tf_op jit(solution)/shard_map/ppermute | solution.py:317
  17.3 0.7 %shard_map.68 = bf16[384,128]{1,0:T(8,128)(2,1)} custom-call(f32[128,1536]{1,0:T(8,128)S(1)} %get-tuple-element.27.after_ref.local_ref, f32[384,128]{1,0:T(8,128)S(1)} %get-tuple-element.26.after_ref.own_ref, bf16[384,128]{1,0:T(8,128)(2,1)S(1)} %collective-permute-done.1.refs_0_, bf16[384,128]{1,0:T(8,128)(2,1)S(1)} %collective-permute-done.2.refs_1_, ...), custom_call_target="tpu_custom_call" | custom-call | tf_op jit(solution)/shard_map/pallas_call | solution.py:129
  17.9 1.5 %collective-permute-start.6 = (bf16[384,128]{1,0:T(8,128)(2,1)}, bf16[384,128]{1,0:T(8,128)(2,1)}, u32[]{:S(2)}, u32[]{:S(2)}) collective-permute-start(bf16[384,128]{1,0:T(8,128)(2,1)} %shard_map.68), channel_id=1, source_target_pairs={{0,8},{8,0},{16,24},{24,16},{1,9},{9,1},{17,25},{25,17},{2,10},{10... | collective-permute-start | bytes 294920 | tf_op jit(solution)/shard_map/ppermute | solution.py:317
  19.4 1.5 %collective-permute-start.5 = (bf16[384,128]{1,0:T(8,128)(2,1)}, bf16[384,128]{1,0:T(8,128)(2,1)}, u32[]{:S(2)}, u32[]{:S(2)}) collective-permute-start(bf16[384,128]{1,0:T(8,128)(2,1)} %shard_map.68), channel_id=1, source_target_pairs={{0,24},{8,16},{16,8},{24,0},{1,25},{9,17},{17,9},{25,1},{2,26},{10... | collective-permute-start | bytes 294920 | tf_op jit(solution)/shard_map/ppermute | solution.py:317
  20.9 0.5 %collective-permute-start.4 = (bf16[384,128]{1,0:T(8,128)(2,1)}, bf16[384,128]{1,0:T(8,128)(2,1)}, u32[]{:S(2)}, u32[]{:S(2)}) collective-permute-start(bf16[384,128]{1,0:T(8,128)(2,1)} %shard_map.68), channel_id=1, source_target_pairs={{0,16},{8,24},{16,0},{24,8},{1,17},{9,25},{17,1},{25,9},{2,18},{10... | collective-permute-start | bytes 294920 | tf_op jit(solution)/shard_map/ppermute | solution.py:317
  21.4 2.1 %collective-permute-done.6 = bf16[384,128]{1,0:T(8,128)(2,1)} collective-permute-done((bf16[384,128]{1,0:T(8,128)(2,1)}, bf16[384,128]{1,0:T(8,128)(2,1)}, u32[]{:S(2)}, u32[]{:S(2)}) %collective-permute-start.6) | collective-permute-done | bytes 98336 | tf_op jit(solution)/shard_map/ppermute | solution.py:317
  23.5 2.0 %collective-permute-done.5 = bf16[384,128]{1,0:T(8,128)(2,1)} collective-permute-done((bf16[384,128]{1,0:T(8,128)(2,1)}, bf16[384,128]{1,0:T(8,128)(2,1)}, u32[]{:S(2)}, u32[]{:S(2)}) %collective-permute-start.5) | collective-permute-done | bytes 98336 | tf_op jit(solution)/shard_map/ppermute | solution.py:317
  25.5 1.0 %collective-permute-done.4 = bf16[384,128]{1,0:T(8,128)(2,1)} collective-permute-done((bf16[384,128]{1,0:T(8,128)(2,1)}, bf16[384,128]{1,0:T(8,128)(2,1)}, u32[]{:S(2)}, u32[]{:S(2)}) %collective-permute-start.4) | collective-permute-done | bytes 98336 | tf_op jit(solution)/shard_map/ppermute | solution.py:317
  26.5 1.0 %fusion.after_ref.refs_1_ = bf16[384,128]{1,0:T(8,128)(2,1)S(1)} fusion(bf16[384,128]{1,0:T(8,128)(2,1)} %collective-permute-done.6, bf16[384,128]{1,0:T(8,128)(2,1)} %collective-permute-done.5, bf16[384,128]{1,0:T(8,128)(2,1)} %collective-permute-done.4, pred[]{:T(512)S(6)} %eq.3), kind=kLoop, calls=%fused_computation.1 | loop fusion | flops 245760 | bytes 393217 | tf_op jit(solution)/shard_map/jit(_where)/select_n | solution.py:347
  27.5 1.4 %collective-permute-start.11 = (bf16[384,128]{1,0:T(8,128)(2,1)S(1)}, bf16[384,128]{1,0:T(8,128)(2,1)S(1)}, u32[]{:S(2)}, u32[]{:S(2)}) collective-permute-start(bf16[384,128]{1,0:T(8,128)(2,1)S(1)} %fusion.after_ref.refs_1_), channel_id=1, source_target_pairs={{0,10},{2,8},{4,14},{6,12},{8,2},{10,0},{12,6},{14,4},{16,26},{18,... | collective-permute-start | bytes 294920 | tf_op jit(solution)/shard_map/ppermute | solution.py:354
  28.9 0.6 %collective-permute-start.10 = (bf16[384,128]{1,0:T(8,128)(2,1)S(1)}, bf16[384,128]{1,0:T(8,128)(2,1)S(1)}, u32[]{:S(2)}, u32[]{:S(2)}) collective-permute-start(bf16[384,128]{1,0:T(8,128)(2,1)S(1)} %fusion.after_ref.refs_1_), channel_id=1, source_target_pairs={{0,8},{8,0},{16,24},{24,16},{1,9},{9,1},{17,25},{25,17},{2,10},{10... | collective-permute-start | bytes 294920 | tf_op jit(solution)/shard_map/ppermute | solution.py:317
  29.6 2.0 %collective-permute-start.9 = (bf16[384,128]{1,0:T(8,128)(2,1)S(1)}, bf16[384,128]{1,0:T(8,128)(2,1)S(1)}, u32[]{:S(2)}, u32[]{:S(2)}) collective-permute-start(bf16[384,128]{1,0:T(8,128)(2,1)S(1)} %fusion.after_ref.refs_1_), channel_id=1, source_target_pairs={{0,6},{2,4},{4,2},{6,0},{1,7},{3,5},{5,3},{7,1},{8,14},{10,12},{12... | collective-permute-start | bytes 294920 | tf_op jit(solution)/shard_map/ppermute | solution.py:317
  31.5 1.0 %collective-permute-start.8 = (bf16[384,128]{1,0:T(8,128)(2,1)S(1)}, bf16[384,128]{1,0:T(8,128)(2,1)S(1)}, u32[]{:S(2)}, u32[]{:S(2)}) collective-permute-start(bf16[384,128]{1,0:T(8,128)(2,1)S(1)} %fusion.after_ref.refs_1_), channel_id=1, source_target_pairs={{0,4},{2,6},{4,0},{6,2},{1,5},{3,7},{5,1},{7,3},{8,12},{10,14},{12... | collective-permute-start | bytes 294920 | tf_op jit(solution)/shard_map/ppermute | solution.py:317
  32.5 1.4 %collective-permute-start.7 = (bf16[384,128]{1,0:T(8,128)(2,1)S(1)}, bf16[384,128]{1,0:T(8,128)(2,1)S(1)}, u32[]{:S(2)}, u32[]{:S(2)}) collective-permute-start(bf16[384,128]{1,0:T(8,128)(2,1)S(1)} %fusion.after_ref.refs_1_), channel_id=1, source_target_pairs={{0,2},{2,0},{4,6},{6,4},{1,3},{3,1},{5,7},{7,5},{8,10},{10,8},{12,... | collective-permute-start | bytes 294920 | tf_op jit(solution)/shard_map/ppermute | solution.py:317
  34.0 1.7 %shard_map.69 = (f32[128,1536]{1,0:T(8,128)S(1)}, bf16[128,1536]{1,0:T(8,128)(2,1)S(1)}, bf16[128,1536]{1,0:T(8,128)(2,1)S(1)}) custom-call(s32[1,4]{1,0:T(1,128)S(1)} %copy-done.5, s32[1,4]{1,0:T(1,128)S(1)} %copy-done.6, bf16[128,3072]{1,0:T(8,128)(2,1)S(1)} %copy-done, bf16[128,3072]{1,0:T(8,128)(2,1)S(1)} %get-tuple-element.23.key_ref, ...), custom_call_target="tpu_custom_call" | custom-call | flops 100663296 | bytes 2752512 | tf_op jit(solution)/shard_map/pallas_call | solution.py:217
  35.7 0.8 %collective-permute-done.11.refs_6_ = bf16[384,128]{1,0:T(8,128)(2,1)S(1)} collective-permute-done((bf16[384,128]{1,0:T(8,128)(2,1)S(1)}, bf16[384,128]{1,0:T(8,128)(2,1)S(1)}, u32[]{:S(2)}, u32[]{:S(2)}) %collective-permute-start.11) | collective-permute-done | bytes 98336 | tf_op jit(solution)/shard_map/ppermute | solution.py:354
  36.5 2.3 %collective-permute-done.8.refs_3_ = bf16[384,128]{1,0:T(8,128)(2,1)S(1)} collective-permute-done((bf16[384,128]{1,0:T(8,128)(2,1)S(1)}, bf16[384,128]{1,0:T(8,128)(2,1)S(1)}, u32[]{:S(2)}, u32[]{:S(2)}) %collective-permute-start.8) | collective-permute-done | bytes 98336 | tf_op jit(solution)/shard_map/ppermute | solution.py:317
  39.0 1.3 %collective-permute-start.12 = (bf16[768,128]{1,0:T(8,128)(2,1)S(1)}, bf16[768,128]{1,0:T(8,128)(2,1)S(1)}, u32[]{:S(2)}, u32[]{:S(2)}) collective-permute-start(bf16[768,128]{1,0:T(8,128)(2,1)S(1)} %get-tuple-element.32), channel_id=1, source_target_pairs={{0,8},{8,0},{16,24},{24,16},{1,9},{9,1},{17,25},{25,17},{2,10},{10... | collective-permute-start | bytes 589832 | tf_op jit(solution)/shard_map/ppermute | solution.py:317
  40.3 0.3 shard_map.71.base_ref
  40.6 0.3 collective-permute-done.13.state_ref
  41.0 0.3 shard_map.72.base_ref
  41.3 5.0 %collective-permute-done.12.state_ref = bf16[768,128]{1,0:T(8,128)(2,1)S(1)} collective-permute-done((bf16[768,128]{1,0:T(8,128)(2,1)S(1)}, bf16[768,128]{1,0:T(8,128)(2,1)S(1)}, u32[]{:S(2)}, u32[]{:S(2)}) %collective-permute-start.12) | collective-permute-done | bytes 196640 | tf_op jit(solution)/shard_map/ppermute | solution.py:317
  46.6 1.2 %collective-permute-done.14.state_ref = bf16[768,128]{1,0:T(8,128)(2,1)S(1)} collective-permute-done((bf16[768,128]{1,0:T(8,128)(2,1)S(1)}, bf16[768,128]{1,0:T(8,128)(2,1)S(1)}, u32[]{:S(2)}, u32[]{:S(2)}) %collective-permute-start.14) | collective-permute-done | bytes 196640 | tf_op jit(solution)/shard_map/ppermute | solution.py:317
  47.7 1.0 %shard_map.74 = bf16[128,3072]{1,0:T(8,128)(2,1)} custom-call(bf16[128,1536]{1,0:T(8,128)(2,1)S(1)} %shard_map.73.done_ref, f32[128,1536]{1,0:T(8,128)S(1)} %shard_map.72.base_ref, bf16[128,1536]{1,0:T(8,128)(2,1)S(1)} %get-tuple-element.37.y_ref, bf16[768,128]{1,0:T(8,128)(2,1)S(1)} %collective-permute-done.14.state_ref), custom_call_target="tpu_custom_call" | custom-call | flops 25165824 | bytes 1966080 | tf_op jit(solution)/shard_map/pallas_call | solution.py:303
  (24 shorter events, 0.6 us)
Async XLA Ops:
  1.7 1.9 %collective-permute-start = (bf16[1536,128]{1,0:T(8,128)(2,1)S(1)}, bf16[1536,128]{1,0:T(8,128)(2,1)S(1)}, u32[]{:S(2)}, u32[]{:S(2)}) collective-permute-start(bf16[1536,128]{1,0:T(8,128)(2,1)S(1)} %get-tuple-element.25), channel_id=1, source_target_pairs={{0,1},{1,0},{2,3},{3,2},{4,5},{5,4},{6,7},{7,6},{8,9},{9,8},{10,11... | collective-permute-start | bytes 1179656 | tf_op jit(solution)/shard_map/ppermute | solution.py:317
  2.7 6.6 %copy-start = (bf16[128,3072]{1,0:T(8,128)(2,1)S(1)}, bf16[128,3072]{1,0:T(8,128)(2,1)}, u32[]{:S(2)}) copy-start(bf16[128,3072]{1,0:T(8,128)(2,1)} %query_ref.3) | copy-start | bytes 2359300
  2.8 6.6 %copy-start.3 = (f32[3,24,128]{2,1,0:T(8,128)S(1)}, f32[3,24,128]{2,1,0:T(8,128)}, u32[]{:S(2)}) copy-start(f32[3,24,128]{2,1,0:T(8,128)} %weight_ref.3) | copy-start | bytes 110596
  3.6 8.7 %collective-permute-start.1 = (bf16[384,128]{1,0:T(8,128)(2,1)S(1)}, bf16[384,128]{1,0:T(8,128)(2,1)S(1)}, u32[]{:S(2)}, u32[]{:S(2)}) collective-permute-start(bf16[384,128]{1,0:T(8,128)(2,1)S(1)} %get-tuple-element.28), channel_id=1, source_target_pairs={{0,6},{2,4},{4,2},{6,0},{1,7},{3,5},{5,3},{7,1},{8,14},{10,12},{12... | collective-permute-start | bytes 294920 | tf_op jit(solution)/shard_map/ppermute | solution.py:317
  8.7 8.6 %collective-permute-start.2 = (bf16[384,128]{1,0:T(8,128)(2,1)S(1)}, bf16[384,128]{1,0:T(8,128)(2,1)S(1)}, u32[]{:S(2)}, u32[]{:S(2)}) collective-permute-start(bf16[384,128]{1,0:T(8,128)(2,1)S(1)} %get-tuple-element.29), channel_id=1, source_target_pairs={{0,4},{2,6},{4,0},{6,2},{1,5},{3,7},{5,1},{7,3},{8,12},{10,14},{12... | collective-permute-start | bytes 294920 | tf_op jit(solution)/shard_map/ppermute | solution.py:317
  8.7 0.7 %copy-start.5 = (s32[1,4]{1,0:T(1,128)S(1)}, s32[1,4]{1,0:T(1,128)}, u32[]{:S(2)}) copy-start(s32[1,4]{1,0:T(1,128)} %length_ref.3) | copy-start | bytes 52
  8.7 0.7 %copy-start.6 = (s32[1,4]{1,0:T(1,128)S(1)}, s32[1,4]{1,0:T(1,128)}, u32[]{:S(2)}) copy-start(s32[1,4]{1,0:T(1,128)} %back_ref.3) | copy-start | bytes 52
  8.7 8.6 %collective-permute-start.3 = (bf16[384,128]{1,0:T(8,128)(2,1)S(1)}, bf16[384,128]{1,0:T(8,128)(2,1)S(1)}, u32[]{:S(2)}, u32[]{:S(2)}) collective-permute-start(bf16[384,128]{1,0:T(8,128)(2,1)S(1)} %get-tuple-element.30), channel_id=1, source_target_pairs={{0,2},{2,0},{4,6},{6,4},{1,3},{3,1},{5,7},{7,5},{8,10},{10,8},{12,... | collective-permute-start | bytes 294920 | tf_op jit(solution)/shard_map/ppermute | solution.py:317
  11.1 6.9 %copy-start.1 = (bf16[128,1536]{1,0:T(8,128)(2,1)}, bf16[128,1536]{1,0:T(8,128)(2,1)S(1)}, u32[]{:S(2)}) copy-start(bf16[128,1536]{1,0:T(8,128)(2,1)S(1)} %get-tuple-element.33.x_ref) | copy-start | bytes 1179652
  17.9 5.5 %collective-permute-start.6 = (bf16[384,128]{1,0:T(8,128)(2,1)}, bf16[384,128]{1,0:T(8,128)(2,1)}, u32[]{:S(2)}, u32[]{:S(2)}) collective-permute-start(bf16[384,128]{1,0:T(8,128)(2,1)} %shard_map.68), channel_id=1, source_target_pairs={{0,8},{8,0},{16,24},{24,16},{1,9},{9,1},{17,25},{25,17},{2,10},{10... | collective-permute-start | bytes 294920 | tf_op jit(solution)/shard_map/ppermute | solution.py:317
  19.4 6.1 %collective-permute-start.5 = (bf16[384,128]{1,0:T(8,128)(2,1)}, bf16[384,128]{1,0:T(8,128)(2,1)}, u32[]{:S(2)}, u32[]{:S(2)}) collective-permute-start(bf16[384,128]{1,0:T(8,128)(2,1)} %shard_map.68), channel_id=1, source_target_pairs={{0,24},{8,16},{16,8},{24,0},{1,25},{9,17},{17,9},{25,1},{2,26},{10... | collective-permute-start | bytes 294920 | tf_op jit(solution)/shard_map/ppermute | solution.py:317
  20.9 5.6 %collective-permute-start.4 = (bf16[384,128]{1,0:T(8,128)(2,1)}, bf16[384,128]{1,0:T(8,128)(2,1)}, u32[]{:S(2)}, u32[]{:S(2)}) collective-permute-start(bf16[384,128]{1,0:T(8,128)(2,1)} %shard_map.68), channel_id=1, source_target_pairs={{0,16},{8,24},{16,0},{24,8},{1,17},{9,25},{17,1},{25,9},{2,18},{10... | collective-permute-start | bytes 294920 | tf_op jit(solution)/shard_map/ppermute | solution.py:317
  21.4 12.5 %copy-start.4 = (f32[3,24,128]{2,1,0:T(8,128)S(1)}, f32[3,24,128]{2,1,0:T(8,128)}, u32[]{:S(2)}) copy-start(f32[3,24,128]{2,1,0:T(8,128)} %weight_ref.3) | copy-start | bytes 110596
  27.5 8.9 %collective-permute-start.11 = (bf16[384,128]{1,0:T(8,128)(2,1)S(1)}, bf16[384,128]{1,0:T(8,128)(2,1)S(1)}, u32[]{:S(2)}, u32[]{:S(2)}) collective-permute-start(bf16[384,128]{1,0:T(8,128)(2,1)S(1)} %fusion.after_ref.refs_1_), channel_id=1, source_target_pairs={{0,10},{2,8},{4,14},{6,12},{8,2},{10,0},{12,6},{14,4},{16,26},{18,... | collective-permute-start | bytes 294920 | tf_op jit(solution)/shard_map/ppermute | solution.py:354
  28.9 7.5 %collective-permute-start.10 = (bf16[384,128]{1,0:T(8,128)(2,1)S(1)}, bf16[384,128]{1,0:T(8,128)(2,1)S(1)}, u32[]{:S(2)}, u32[]{:S(2)}) collective-permute-start(bf16[384,128]{1,0:T(8,128)(2,1)S(1)} %fusion.after_ref.refs_1_), channel_id=1, source_target_pairs={{0,8},{8,0},{16,24},{24,16},{1,9},{9,1},{17,25},{25,17},{2,10},{10... | collective-permute-start | bytes 294920 | tf_op jit(solution)/shard_map/ppermute | solution.py:317
  29.6 6.9 %collective-permute-start.9 = (bf16[384,128]{1,0:T(8,128)(2,1)S(1)}, bf16[384,128]{1,0:T(8,128)(2,1)S(1)}, u32[]{:S(2)}, u32[]{:S(2)}) collective-permute-start(bf16[384,128]{1,0:T(8,128)(2,1)S(1)} %fusion.after_ref.refs_1_), channel_id=1, source_target_pairs={{0,6},{2,4},{4,2},{6,0},{1,7},{3,5},{5,3},{7,1},{8,14},{10,12},{12... | collective-permute-start | bytes 294920 | tf_op jit(solution)/shard_map/ppermute | solution.py:317
  31.5 7.3 %collective-permute-start.8 = (bf16[384,128]{1,0:T(8,128)(2,1)S(1)}, bf16[384,128]{1,0:T(8,128)(2,1)S(1)}, u32[]{:S(2)}, u32[]{:S(2)}) collective-permute-start(bf16[384,128]{1,0:T(8,128)(2,1)S(1)} %fusion.after_ref.refs_1_), channel_id=1, source_target_pairs={{0,4},{2,6},{4,0},{6,2},{1,5},{3,7},{5,1},{7,3},{8,12},{10,14},{12... | collective-permute-start | bytes 294920 | tf_op jit(solution)/shard_map/ppermute | solution.py:317
  32.5 6.3 %collective-permute-start.7 = (bf16[384,128]{1,0:T(8,128)(2,1)S(1)}, bf16[384,128]{1,0:T(8,128)(2,1)S(1)}, u32[]{:S(2)}, u32[]{:S(2)}) collective-permute-start(bf16[384,128]{1,0:T(8,128)(2,1)S(1)} %fusion.after_ref.refs_1_), channel_id=1, source_target_pairs={{0,2},{2,0},{4,6},{6,4},{1,3},{3,1},{5,7},{7,5},{8,10},{10,8},{12,... | collective-permute-start | bytes 294920 | tf_op jit(solution)/shard_map/ppermute | solution.py:317
  38.8 1.5 %copy-start.2 = (bf16[128,1536]{1,0:T(8,128)(2,1)S(1)}, bf16[128,1536]{1,0:T(8,128)(2,1)}, u32[]{:S(2)}) copy-start(bf16[128,1536]{1,0:T(8,128)(2,1)} %copy-done.1) | copy-start | bytes 1179652
  38.9 2.1 %collective-permute-start.13 = (bf16[2304,128]{1,0:T(8,128)(2,1)S(1)}, bf16[2304,128]{1,0:T(8,128)(2,1)S(1)}, u32[]{:S(2)}, u32[]{:S(2)}) collective-permute-start(bf16[2304,128]{1,0:T(8,128)(2,1)S(1)} %get-tuple-element.35.state_ref), channel_id=1, source_target_pairs={{0,1},{1,0},{2,3},{3,2},{4,5},{5,4},{6,7},{7,6},{8,9},{9,8},{10,11... | collective-permute-start | bytes 1769480 | tf_op jit(solution)/shard_map/ppermute | solution.py:317
  39.0 7.3 %collective-permute-start.12 = (bf16[768,128]{1,0:T(8,128)(2,1)S(1)}, bf16[768,128]{1,0:T(8,128)(2,1)S(1)}, u32[]{:S(2)}, u32[]{:S(2)}) collective-permute-start(bf16[768,128]{1,0:T(8,128)(2,1)S(1)} %get-tuple-element.32), channel_id=1, source_target_pairs={{0,8},{8,0},{16,24},{24,16},{1,9},{9,1},{17,25},{25,17},{2,10},{10... | collective-permute-start | bytes 589832 | tf_op jit(solution)/shard_map/ppermute | solution.py:317
  46.3 1.4 %collective-permute-start.14 = (bf16[768,128]{1,0:T(8,128)(2,1)S(1)}, bf16[768,128]{1,0:T(8,128)(2,1)S(1)}, u32[]{:S(2)}, u32[]{:S(2)}) collective-permute-start(bf16[768,128]{1,0:T(8,128)(2,1)S(1)} %collective-permute-done.12.state_ref), channel_id=1, source_target_pairs={{0,1},{1,0},{2,3},{3,2},{4,5},{5,4},{6,7},{7,6},{8,9},{9,8},{10,11... | collective-permute-start | bytes 589832 | tf_op jit(solution)/shard_map/ppermute | solution.py:317

commit v5 on v4

--- a/solution.py
+++ b/solution.py
@@ -16,6 +16,7 @@
 F32, BF16 = jnp.float32, jnp.bfloat16
 WHOLE = pl.BlockSpec(memory_space=pltpu.VMEM)
 SCALARS = pl.BlockSpec(memory_space=pltpu.SMEM)
+ANYWHERE = pl.BlockSpec(memory_space=pl.ANY)
 IN_HBM = pl.BlockSpec(memory_space=pltpu.HBM)
 PARAMS = pltpu.CompilerParams(vmem_limit_bytes=VMEM_LIMIT)
 
@@ -99,23 +100,32 @@
     )(*in_vmem(keys, values))
 
 
-def piece_kernel(mine_ref, other_ref, own_ref, *piece_refs):
+def piece_kernel(chunks, chips, mine_ref, other_ref, *refs):
     chip = lax.axis_index("chip")
-    rows = own_ref.shape[0]
-    for d, ref in enumerate((own_ref,) + piece_refs):
-        at = pl.ds(pl.multiple_of((chip ^ d) * rows, rows), rows)
-        ref[...] = (mine_ref[at, :] + other_ref[at, :].astype(F32)).astype(ref.dtype)
-
-
-def chip_pieces(mine, other, chips):
-    shape = (mine.shape[0] // chips, HEAD_DIM)
-    return pl.pallas_call(
-        piece_kernel,
-        out_shape=[pltpu.VMEM(shape, F32)] + [pltpu.VMEM(shape, BF16)] * (chips - 1),
+    shard = mine_ref.shape[0] // chips
+    refs = iter(refs)
+    for d in range(chips):
+        offset = 0
+        for chunk in chunks:
+            rows = chunk * HEAD_DIM
+            at = pl.ds(pl.multiple_of((chip ^ d) * shard + offset, HEAD_DIM), rows)
+            ref = next(refs)
+            ref[...] = (mine_ref[at, :] + other_ref[at, :].astype(F32)).astype(ref.dtype)
+            offset += rows
+
+
+def chip_pieces(chunks, chips, mine, other):
+    shapes = [
+        pltpu.VMEM((chunk * HEAD_DIM, HEAD_DIM), BF16 if d else F32) for d in range(chips) for chunk in chunks
+    ]
+    pieces = pl.pallas_call(
+        functools.partial(piece_kernel, chunks, chips),
+        out_shape=shapes,
         in_specs=[WHOLE, WHOLE],
-        out_specs=[WHOLE] * chips,
-        compiler_params=PARAMS,
-    )(mine, other)
+        out_specs=[WHOLE] * len(shapes),
+        compiler_params=PARAMS,
+    )(*in_vmem(mine, other))
+    return [pieces[n :: len(chunks)] for n in range(len(chunks))]
 
 
 def sum_kernel(after_ref, own_ref, *refs):
@@ -129,10 +139,26 @@
     return pl.pallas_call(
         sum_kernel,
         out_shape=pltpu.VMEM(own.shape, dtype),
-        in_specs=[pl.BlockSpec(memory_space=pl.ANY)] + [WHOLE] * (1 + len(parts)),
+        in_specs=[ANYWHERE] + [WHOLE] * (1 + len(parts)),
         out_specs=WHOLE,
         compiler_params=PARAMS,
-    )(after, own, *parts)
+    )(after, *in_vmem(own, *parts))
+
+
+def slot_kernel(after_ref, near_ref, across_ref, diagonal_ref, out_ref):
+    both = across_ref[...].astype(F32) + diagonal_ref[...].astype(F32)
+    near = near_ref[...].astype(F32)
+    out_ref[...] = jnp.where(lax.axis_index("frame") == 2, both, near).astype(BF16)
+
+
+def choose_slot(after, near, across, diagonal):
+    return pl.pallas_call(
+        slot_kernel,
+        out_shape=pltpu.VMEM(near.shape, BF16),
+        in_specs=[ANYWHERE] + [WHOLE] * 3,
+        out_specs=WHOLE,
+        compiler_params=PARAMS,
+    )(after, *in_vmem(near, across, diagonal))
 
 
 def pack_kernel(groups, after, *refs):
@@ -148,7 +174,7 @@
     return pl.pallas_call(
         functools.partial(pack_kernel, groups, len(after)),
         out_shape=[pltpu.VMEM((rows * len(group), HEAD_DIM), BF16) for group in groups],
-        in_specs=[pl.BlockSpec(memory_space=pl.ANY)] * len(after) + [WHOLE] * len(pieces),
+        in_specs=[ANYWHERE] * len(after) + [WHOLE] * len(pieces),
         out_specs=[WHOLE] * len(groups),
         compiler_params=PARAMS,
     )(*after, *in_vmem(*pieces))
@@ -217,7 +243,7 @@
     return pl.pallas_call(
         functools.partial(local_kernel, coefs, turn),
         out_shape=[pltpu.VMEM((tokens, width), F32)] + [pltpu.VMEM((tokens, width), BF16)] * slots,
-        in_specs=[SCALARS] * 2 + [WHOLE] * 4 + [pl.BlockSpec(memory_space=pl.ANY)],
+        in_specs=[SCALARS] * 2 + [WHOLE] * 4 + [ANYWHERE],
         out_specs=[WHOLE] * (1 + slots),
         compiler_params=PARAMS,
         cost_estimate=pl.CostEstimate(
@@ -228,89 +254,97 @@
     )(frame_len, window_back, queries, *in_vmem(keys, values), weights, after)
 
 
-def read_heads(d, chips, base_ref, states):
-    count = HEADS // 2 // chips
-    first = (lax.axis_index("chip") ^ d) * count
-    for h in range(count):
+def read_heads(d, chips, heads, base_ref, states):
+    first = (lax.axis_index("chip") ^ d) * (HEADS // 2 // chips)
+    for n, h in enumerate(heads):
         at = columns(first + h)
         result = base_ref[:, at]
         for read_ref, state_ref, row in states:
             result = result + jnp.dot(
                 read_ref[:, at],
-                state_ref[row + h * HEAD_DIM : row + (h + 1) * HEAD_DIM, :],
+                state_ref[row + n * HEAD_DIM : row + (n + 1) * HEAD_DIM, :],
                 preferred_element_type=F32,
             )
         yield at, result
 
 
-def middle_kernel(chips, early, local_ref, x_ref, y_ref, state_ref, out_ref):
-    rows = state_ref.shape[0] // (chips + early)
-    for d in range(chips):
-        states = [(x_ref, state_ref, d * rows)]
-        if d < early:
-            states.append((y_ref, state_ref, (chips + d) * rows))
-        for at, result in read_heads(d, chips, local_ref, states):
-            out_ref[:, at] = result
-
-
-def read_middle(chips, early, local, x, y, states):
-    return pl.pallas_call(
-        functools.partial(middle_kernel, chips, early),
+def heads_of(chunks):
+    return [range(sum(chunks[:n]), sum(chunks[: n + 1])) for n in range(len(chunks))]
+
+
+def middle_kernel(chunks, chips, early, local_ref, x_ref, y_ref, *refs):
+    out_ref = refs[-1]
+    for heads, state_ref in zip(heads_of(chunks), refs):
+        rows = len(heads) * HEAD_DIM
+        for d in range(chips):
+            states = [(x_ref, state_ref, d * rows)]
+            if d < early:
+                states.append((y_ref, state_ref, (chips + d) * rows))
+            for at, result in read_heads(d, chips, heads, local_ref, states):
+                out_ref[:, at] = result
+
+
+def read_middle(chunks, chips, early, local, x, y, states):
+    return pl.pallas_call(
+        functools.partial(middle_kernel, chunks, chips, early),
         out_shape=pltpu.VMEM(local.shape, F32),
-        in_specs=[WHOLE] * 4,
+        in_specs=[WHOLE] * (3 + len(states)),
         out_specs=WHOLE,
         compiler_params=PARAMS,
         cost_estimate=pl.CostEstimate(
             flops=2 * local.size * HEAD_DIM, bytes_accessed=8 * local.size, transcendentals=0
         ),
-    )(*in_vmem(local, x, y, states))
-
-
-def late_half(chips, early, base_ref, y_ref, state_ref, out_ref):
-    rows = state_ref.shape[0] // max(chips - early, 1)
-    for d in range(chips):
-        states = [(y_ref, state_ref, (d - early) * rows)] if d >= early else []
-        for at, result in read_heads(d, chips, base_ref, states):
-            out_ref[:, at] = result.astype(BF16)
-
-
-def read_late(chips, early, base, y, states):
-    return pl.pallas_call(
-        functools.partial(late_half, chips, early),
+    )(*in_vmem(local, x, y, *states))
+
+
+def late_half(chunks, chips, early, base_ref, y_ref, *refs):
+    out_ref = refs[-1]
+    for heads, state_ref in zip(heads_of(chunks), refs):
+        rows = len(heads) * HEAD_DIM
+        for d in range(chips):
+            states = [(y_ref, state_ref, (d - early) * rows)] if d >= early else []
+            for at, result in read_heads(d, chips, heads, base_ref, states):
+                out_ref[:, at] = result.astype(BF16)
+
+
+def read_late(chunks, chips, early, base, y, states):
+    return pl.pallas_call(
+        functools.partial(late_half, chunks, chips, early),
         out_shape=pltpu.VMEM(base.shape, BF16),
-        in_specs=[WHOLE] * 3,
+        in_specs=[WHOLE] * (2 + len(states)),
         out_specs=WHOLE,
         compiler_params=PARAMS,
         cost_estimate=pl.CostEstimate(
             flops=base.size * HEAD_DIM, bytes_accessed=6 * base.size, transcendentals=0
         ),
-    )(*in_vmem(base, y, states))
-
-
-def last_kernel(chips, early, done_ref, base_ref, y_ref, state_ref, out_ref, held, sems):
+    )(*in_vmem(base, y, *states))
+
+
+def last_kernel(chunks, chips, early, done_ref, base_ref, y_ref, *refs):
+    *state_refs, out_ref, held, sems = refs
     mine, other = core_heads()
     first = pltpu.make_async_copy(done_ref, out_ref.at[:, columns(mine, HEADS // 2)], sems.at[0])
     first.start()
-    late_half(chips, early, base_ref, y_ref, state_ref, held)
+    late_half(chunks, chips, early, base_ref, y_ref, *state_refs, held)
     second = pltpu.make_async_copy(held, out_ref.at[:, columns(other, HEADS // 2)], sems.at[1])
     second.start()
     first.wait()
     second.wait()
 
 
-def read_last(chips, early, done, base, y, states):
+def read_last(chunks, chips, early, done, base, y, states):
     tokens, width = base.shape
     return pl.pallas_call(
-        functools.partial(last_kernel, chips, early),
+        functools.partial(last_kernel, chunks, chips, early),
         out_shape=jax.ShapeDtypeStruct((tokens, 2 * width), BF16),
-        in_specs=[WHOLE] * 4,
-        out_specs=pl.BlockSpec(memory_space=pl.ANY),
+        in_specs=[WHOLE] * (3 + len(states)),
+        out_specs=ANYWHERE,
         scratch_shapes=[pltpu.VMEM((tokens, width), BF16), pltpu.SemaphoreType.DMA((2,))],
         compiler_params=PARAMS,
         cost_estimate=pl.CostEstimate(
             flops=base.size * HEAD_DIM, bytes_accessed=10 * base.size, transcendentals=0
         ),
-    )(*in_vmem(done, base, y, states))
+    )(*in_vmem(done, base, y, *states))
 
 
 def swap(array, axis, mask, size):
@@ -332,39 +366,51 @@
     local = functools.partial(local_part, coefs, 2)
     rest = (frame_len, window_back, queries)
 
+    count = HEADS // 2 // chips
+    chunks = tuple(n for n in (count - count // 3, count // 3) if n)
+    early = min(2, chips)
+    near_pairs = [
+        (f * chips + c, (f ^ 1) * chips + (c ^ 1)) for f in range(frames) for c in range(chips)
+    ]
+    shape = (chunks, chips, early)
+
     outgoing, keys, values = outgoing_state(keys, values)
     incoming = swap(outgoing, "core", 1, 2)
     mine = own_state(keys, values)
-    own, *sends = chip_pieces(mine, incoming, chips)
-    got = {d: swap(sends[d - 1], "chip", d, chips) for d in reversed(range(1, chips))}
-
-    local_0, x_0, y_0 = local(0, *rest, keys, values, level_weight, own)
-    state = sum_pieces(local_0, own, list(got.values()), F32 if outer > 1 else BF16)
-    if outer > 1:
-        state = lax.psum(state, "outer").astype(BF16)
-    near, across, diagonal = (swap(state, "frame", mask, frames) for mask in (1, 2, 3))
-    both = (across.astype(F32) + diagonal.astype(F32)).astype(BF16)
-    slot = jnp.where(frame == 2, both, near)
-
-    early = min(2, chips)
-    x = [swap(slot, "chip", d, chips) for d in range(1, chips)]
-    near_pairs = [
-        (f * chips + c, (f ^ 1) * chips + (c ^ 1)) for f in range(frames) for c in range(chips)
-    ]
-    y = [swap(slot, "frame", 1, frames), lax.ppermute(slot, ("frame", "chip"), near_pairs)][:early]
-    local_1, x_1, y_1 = local(1, *rest, keys, values, level_weight, slot)
-    pieces = [slot] + x + y
-    own_states, late = pack(
-        [list(range(chips + early)), list(range(early, chips)) or [0]], pieces, [local_1]
-    )
-    late_own = swap(late, "frame", 1, frames)
-    other_states = swap(own_states, "core", 1, 2)
-    base_0 = read_middle(chips, early, local_0, x_0, y_0, own_states)
-    base_1 = read_middle(chips, early, local_1, x_1, y_1, other_states)
+    cut = chip_pieces(chunks, chips, mine, incoming)
+    got = [[swap(pieces[d], "chip", d, chips) for d in reversed(range(1, chips))] for pieces in cut]
+
+    local_0, x_0, y_0 = local(0, *rest, keys, values, level_weight, cut[0][0])
+    after, parts = local_0, []
+    for pieces, arrived in zip(cut, got):
+        after = sum_pieces(after, pieces[0], arrived, F32 if outer > 1 else BF16)
+        state = lax.psum(after, "outer").astype(BF16) if outer > 1 else after
+        parts.append([swap(state, "frame", mask, frames) for mask in (3, 2, 1)])
+
+    gathered = []
+    for diagonal, across, near in parts:
+        slot = after = choose_slot(after, near, across, diagonal)
+        x = [swap(slot, "chip", d, chips) for d in reversed(range(1, chips))][::-1]
+        y = [swap(slot, "frame", 1, frames), lax.ppermute(slot, ("frame", "chip"), near_pairs)][:early]
+        gathered.append([slot] + x + y)
+    local_1, x_1, y_1 = local(1, *rest, keys, values, level_weight, after)
+
+    after = local_1
+    own, other, late_own = [], [], []
+    for pieces in gathered:
+        states, late = pack(
+            [list(range(chips + early)), list(range(early, chips)) or [0]], pieces, [after]
+        )
+        after = states
+        late_own.append(swap(late, "frame", 1, frames))
+        own.append(states)
+        other.append(swap(states, "core", 1, 2))
+    base_0 = read_middle(*shape, local_0, x_0, y_0, own)
+    base_1 = read_middle(*shape, local_1, x_1, y_1, other)
     late_own, base_0, base_1 = lax.optimization_barrier((late_own, base_0, base_1))
-    late_other = swap(late_own, "core", 1, 2)
-    done = read_late(chips, early, base_0, y_0, late_own)
-    return read_last(chips, early, done, base_1, y_1, late_other)
+    late_other = [swap(late, "core", 1, 2) for late in late_own]
+    done = read_late(*shape, base_0, y_0, late_own)
+    return read_last(*shape, done, base_1, y_1, late_other)
 
 
 def solution(mesh):

time: 48.9 us -> 57.9 us (1.18)
  starting transfers between devices: 17.5 us -> 37.9 us
  waiting for transfers between devices: 21.6 us -> 11.9 us
  other arithmetic: 1.03 us -> 0 us
  Pallas kernels: 8.41 us -> 7.82 us
    ppermute x14 -> x27, starting transfers between devices: 16.1 us -> 32.7 us  [swap(): return lax.ppermute(array, axis, [(n, n ^ mask) for n in range(size)])]
    ppermute x14 -> x27, waiting for transfers between devices: 20.9 us -> 11.9 us  [swap(): return lax.ppermute(array, axis, [(n, n ^ mask) for n in range(size)])]
    ppermute x1 -> x2, starting transfers between devices: 1.42 us -> 5.18 us  [body(): lax.ppermute(slot, ('frame', 'chip'), near_pairs)]
    select_n x1 -> x0, other arithmetic: 1.03 us -> none  [body(): slot = jnp.where(frame == 2, both, near)]
    ppermute x1 -> x2, waiting for transfers between devices: 0.76 us -> 0.01 us  [body(): lax.ppermute(slot, ('frame', 'chip'), near_pairs)]
    pallas_call x1 -> x2, Pallas kernels: 0.68 us -> 0.05 us  [sum_pieces(): pl.pallas_call(sum_kernel, out_shape=pltpu.VMEM(own.shape, dtype), in_spe...]
    pallas_call x5 -> x7, Pallas kernels: 2.01 us -> 2.03 us  [the longest x1 1.01 us: read_last(): pl.pallas_call(functools.partial(last_kernel, chunks, chips, early), out_...]
  transfers between devices with their start and end apart: 15 -> 29, of which waited for: 11 -> 10; matrix products, arithmetic and copies ran while one was open for 0% -> 0% of each run, Pallas kernels for 10% -> 9%
where the time goes in v5:
time: 57.9 us; the launch traced here: 57.8 us
  starting transfers between devices  37.9 us (65%)
  waiting for transfers between devices  11.9 us (21%)
  Pallas kernels  7.82 us (14%)
    ppermute x27, starting transfers between devices, swap(): return lax.ppermute(array, axis, [(n, n ^ mask) for n in range(size)])  32.7 us
    ppermute x27, waiting for transfers between devices, swap(): return lax.ppermute(array, axis, [(n, n ^ mask) for n in range(size)])  11.9 us
    ppermute x2, starting transfers between devices, body(): lax.ppermute(slot, ('frame', 'chip'), near_pairs)  5.18 us
    pallas_call x2, Pallas kernels, local_part(): pl.pallas_call(functools.partial(local_kernel, coefs, turn), out_shape=[p...  3.45 us
    pallas_call x1, Pallas kernels, outgoing_state(): pl.pallas_call(first_kernel, out_shape=[pltpu.VMEM((half * dim, dim), BF1...  1.69 us
  transfers between devices with their start and end apart: 29, of which 10 were waited for; matrix products, arithmetic and copies ran while one was open for 0% of the time, Pallas kernels for 9%

profile of v5, /device:TPU:0, one launch (start us, length us, event | category | flops | bytes accessed | tf_op | source)
XLA Modules:
  0.0 57.8 jit_solution(3277781119423543808)
XLA Ops:
  0.0 1.7 %shard_map.64 = (bf16[1536,128]{1,0:T(8,128)(2,1)S(1)}, bf16[128,3072]{1,0:T(8,128)(2,1)S(1)}, bf16[128,3072]{1,0:T(8,128)(2,1)S(1)}) custom-call(bf16[128,3072]{1,0:T(8,128)(2,1)} %key_ref.1, bf16[128,3072]{1,0:T(8,128)(2,1)} %value_ref.1), custom_call_target="tpu_custom_call" | custom-call | flops 50331648 | bytes 1572864 | tf_op jit(solution)/shard_map/pallas_call | solution.py:71
  2.7 0.8 %collective-permute-done.other_ref = bf16[1536,128]{1,0:T(8,128)(2,1)S(1)} collective-permute-done((bf16[1536,128]{1,0:T(8,128)(2,1)S(1)}, bf16[1536,128]{1,0:T(8,128)(2,1)S(1)}, u32[]{:S(2)}, u32[]{:S(2)}) %collective-permute-start) | collective-permute-done | bytes 393248 | tf_op jit(solution)/shard_map/ppermute | solution.py:351
  3.6 5.1 %collective-permute-start.1 = (bf16[256,128]{1,0:T(8,128)(2,1)S(1)}, bf16[256,128]{1,0:T(8,128)(2,1)S(1)}, u32[]{:S(2)}, u32[]{:S(2)}) collective-permute-start(bf16[256,128]{1,0:T(8,128)(2,1)S(1)} %get-tuple-element.35), channel_id=1, source_target_pairs={{0,6},{2,4},{4,2},{6,0},{1,7},{3,5},{5,3},{7,1},{8,14},{10,12},{12... | collective-permute-start | bytes 196616 | tf_op jit(solution)/shard_map/ppermute | solution.py:351
  8.7 0.6 %collective-permute-start.3 = (bf16[256,128]{1,0:T(8,128)(2,1)S(1)}, bf16[256,128]{1,0:T(8,128)(2,1)S(1)}, u32[]{:S(2)}, u32[]{:S(2)}) collective-permute-start(bf16[256,128]{1,0:T(8,128)(2,1)S(1)} %get-tuple-element.37), channel_id=1, source_target_pairs={{0,2},{2,0},{4,6},{6,4},{1,3},{3,1},{5,7},{7,5},{8,10},{10,8},{12,... | collective-permute-start | bytes 196616 | tf_op jit(solution)/shard_map/ppermute | solution.py:351
  9.4 3.7 %collective-permute-start.4 = (bf16[128,128]{1,0:T(8,128)(2,1)S(1)}, bf16[128,128]{1,0:T(8,128)(2,1)S(1)}, u32[]{:S(2)}, u32[]{:S(2)}) collective-permute-start(bf16[128,128]{1,0:T(8,128)(2,1)S(1)} %get-tuple-element.39), channel_id=1, source_target_pairs={{0,6},{2,4},{4,2},{6,0},{1,7},{3,5},{5,3},{7,1},{8,14},{10,12},{12... | collective-permute-start | bytes 98312 | tf_op jit(solution)/shard_map/ppermute | solution.py:351
  13.1 1.7 %shard_map.67 = (f32[128,1536]{1,0:T(8,128)S(1)}, bf16[128,1536]{1,0:T(8,128)(2,1)S(1)}, bf16[128,1536]{1,0:T(8,128)(2,1)S(1)}) custom-call(s32[1,4]{1,0:T(1,128)S(1)} %copy-done.2, s32[1,4]{1,0:T(1,128)S(1)} %copy-done.3, bf16[128,3072]{1,0:T(8,128)(2,1)S(1)} %copy-done, bf16[128,3072]{1,0:T(8,128)(2,1)S(1)} %get-tuple-element.30.key_ref, ...), custom_call_target="tpu_custom_call" | custom-call | flops 100663296 | bytes 2752512 | tf_op jit(solution)/shard_map/pallas_call | solution.py:243
  15.3 2.5 %collective-permute-start.9 = (bf16[256,128]{1,0:T(8,128)(2,1)S(1)}, bf16[256,128]{1,0:T(8,128)(2,1)S(1)}, u32[]{:S(2)}, u32[]{:S(2)}) collective-permute-start(bf16[256,128]{1,0:T(8,128)(2,1)S(1)} %shard_map.68.after_ref), channel_id=1, source_target_pairs={{0,24},{8,16},{16,8},{24,0},{1,25},{9,17},{17,9},{25,1},{2,26},{10... | collective-permute-start | bytes 196616 | tf_op jit(solution)/shard_map/ppermute | solution.py:351
  17.8 0.6 %collective-permute-start.5 = (bf16[128,128]{1,0:T(8,128)(2,1)S(1)}, bf16[128,128]{1,0:T(8,128)(2,1)S(1)}, u32[]{:S(2)}, u32[]{:S(2)}) collective-permute-start(bf16[128,128]{1,0:T(8,128)(2,1)S(1)} %get-tuple-element.40), channel_id=1, source_target_pairs={{0,4},{2,6},{4,0},{6,2},{1,5},{3,7},{5,1},{7,3},{8,12},{10,14},{12... | collective-permute-start | bytes 98312 | tf_op jit(solution)/shard_map/ppermute | solution.py:351
  19.0 0.5 collective-permute-start.7
  19.5 2.4 %collective-permute-start.6 = (bf16[128,128]{1,0:T(8,128)(2,1)S(1)}, bf16[128,128]{1,0:T(8,128)(2,1)S(1)}, u32[]{:S(2)}, u32[]{:S(2)}) collective-permute-start(bf16[128,128]{1,0:T(8,128)(2,1)S(1)} %get-tuple-element.41), channel_id=1, source_target_pairs={{0,2},{2,0},{4,6},{6,4},{1,3},{3,1},{5,7},{7,5},{8,10},{10,8},{12,... | collective-permute-start | bytes 98312 | tf_op jit(solution)/shard_map/ppermute | solution.py:351
  21.9 1.1 %collective-permute-done.5.refs_1_ = bf16[128,128]{1,0:T(8,128)(2,1)S(1)} collective-permute-done((bf16[128,128]{1,0:T(8,128)(2,1)S(1)}, bf16[128,128]{1,0:T(8,128)(2,1)S(1)}, u32[]{:S(2)}, u32[]{:S(2)}) %collective-permute-start.5) | collective-permute-done | bytes 32800 | tf_op jit(solution)/shard_map/ppermute | solution.py:351
  23.0 0.8 %collective-permute-done.6.refs_2_ = bf16[128,128]{1,0:T(8,128)(2,1)S(1)} collective-permute-done((bf16[128,128]{1,0:T(8,128)(2,1)S(1)}, bf16[128,128]{1,0:T(8,128)(2,1)S(1)}, u32[]{:S(2)}, u32[]{:S(2)}) %collective-permute-start.6) | collective-permute-done | bytes 32800 | tf_op jit(solution)/shard_map/ppermute | solution.py:351
  23.9 2.5 %collective-permute-start.12 = (bf16[128,128]{1,0:T(8,128)(2,1)S(1)}, bf16[128,128]{1,0:T(8,128)(2,1)S(1)}, u32[]{:S(2)}, u32[]{:S(2)}) collective-permute-start(bf16[128,128]{1,0:T(8,128)(2,1)S(1)} %shard_map.69.after_ref), channel_id=1, source_target_pairs={{0,24},{8,16},{16,8},{24,0},{1,25},{9,17},{17,9},{25,1},{2,26},{10... | collective-permute-start | bytes 98312 | tf_op jit(solution)/shard_map/ppermute | solution.py:351
  26.9 0.5 collective-permute-start.10
  27.4 3.0 %collective-permute-start.17 = (bf16[256,128]{1,0:T(8,128)(2,1)S(1)}, bf16[256,128]{1,0:T(8,128)(2,1)S(1)}, u32[]{:S(2)}, u32[]{:S(2)}) collective-permute-start(bf16[256,128]{1,0:T(8,128)(2,1)S(1)} %shard_map.70.after_ref.refs_1_), channel_id=1, source_target_pairs={{0,10},{2,8},{4,14},{6,12},{8,2},{10,0},{12,6},{14,4},{16,26},{18,... | collective-permute-start | bytes 196616 | tf_op jit(solution)/shard_map/ppermute | solution.py:394
  30.5 0.5 collective-permute-start.16
  31.0 1.3 %collective-permute-start.15 = (bf16[256,128]{1,0:T(8,128)(2,1)S(1)}, bf16[256,128]{1,0:T(8,128)(2,1)S(1)}, u32[]{:S(2)}, u32[]{:S(2)}) collective-permute-start(bf16[256,128]{1,0:T(8,128)(2,1)S(1)} %shard_map.70.after_ref.refs_1_), channel_id=1, source_target_pairs={{0,6},{2,4},{4,2},{6,0},{1,7},{3,5},{5,3},{7,1},{8,14},{10,12},{12... | collective-permute-start | bytes 196616 | tf_op jit(solution)/shard_map/ppermute | solution.py:351
  32.7 2.7 %collective-permute-start.13 = (bf16[256,128]{1,0:T(8,128)(2,1)S(1)}, bf16[256,128]{1,0:T(8,128)(2,1)S(1)}, u32[]{:S(2)}, u32[]{:S(2)}) collective-permute-start(bf16[256,128]{1,0:T(8,128)(2,1)S(1)} %shard_map.70.after_ref.refs_1_), channel_id=1, source_target_pairs={{0,2},{2,0},{4,6},{6,4},{1,3},{3,1},{5,7},{7,5},{8,10},{10,8},{12,... | collective-permute-start | bytes 196616 | tf_op jit(solution)/shard_map/ppermute | solution.py:351
  35.4 1.7 %shard_map.72 = (f32[128,1536]{1,0:T(8,128)S(1)}, bf16[128,1536]{1,0:T(8,128)(2,1)S(1)}, bf16[128,1536]{1,0:T(8,128)(2,1)S(1)}) custom-call(s32[1,4]{1,0:T(1,128)S(1)} %copy-done.2, s32[1,4]{1,0:T(1,128)S(1)} %copy-done.3, bf16[128,3072]{1,0:T(8,128)(2,1)S(1)} %copy-done, bf16[128,3072]{1,0:T(8,128)(2,1)S(1)} %get-tuple-element.30.key_ref, ...), custom_call_target="tpu_custom_call" | custom-call | flops 100663296 | bytes 2752512 | tf_op jit(solution)/shard_map/pallas_call | solution.py:243
  37.2 1.3 %collective-permute-done.14.refs_3_ = bf16[256,128]{1,0:T(8,128)(2,1)S(1)} collective-permute-done((bf16[256,128]{1,0:T(8,128)(2,1)S(1)}, bf16[256,128]{1,0:T(8,128)(2,1)S(1)}, u32[]{:S(2)}, u32[]{:S(2)}) %collective-permute-start.14) | collective-permute-done | bytes 65568 | tf_op jit(solution)/shard_map/ppermute | solution.py:351
  38.6 2.2 %collective-permute-start.23 = (bf16[128,128]{1,0:T(8,128)(2,1)S(1)}, bf16[128,128]{1,0:T(8,128)(2,1)S(1)}, u32[]{:S(2)}, u32[]{:S(2)}) collective-permute-start(bf16[128,128]{1,0:T(8,128)(2,1)S(1)} %shard_map.71.after_ref.refs_1_), channel_id=1, source_target_pairs={{0,10},{2,8},{4,14},{6,12},{8,2},{10,0},{12,6},{14,4},{16,26},{18,... | collective-permute-start | bytes 98312 | tf_op jit(solution)/shard_map/ppermute | solution.py:394
  40.8 0.5 collective-permute-start.22
  41.3 1.3 %collective-permute-start.21 = (bf16[128,128]{1,0:T(8,128)(2,1)S(1)}, bf16[128,128]{1,0:T(8,128)(2,1)S(1)}, u32[]{:S(2)}, u32[]{:S(2)}) collective-permute-start(bf16[128,128]{1,0:T(8,128)(2,1)S(1)} %shard_map.71.after_ref.refs_1_), channel_id=1, source_target_pairs={{0,6},{2,4},{4,2},{6,0},{1,7},{3,5},{5,3},{7,1},{8,14},{10,12},{12... | collective-permute-start | bytes 98312 | tf_op jit(solution)/shard_map/ppermute | solution.py:351
  42.7 1.0 %collective-permute-start.20 = (bf16[128,128]{1,0:T(8,128)(2,1)S(1)}, bf16[128,128]{1,0:T(8,128)(2,1)S(1)}, u32[]{:S(2)}, u32[]{:S(2)}) collective-permute-start(bf16[128,128]{1,0:T(8,128)(2,1)S(1)} %shard_map.71.after_ref.refs_1_), channel_id=1, source_target_pairs={{0,4},{2,6},{4,0},{6,2},{1,5},{3,7},{5,1},{7,3},{8,12},{10,14},{12... | collective-permute-start | bytes 98312 | tf_op jit(solution)/shard_map/ppermute | solution.py:351
  43.6 2.1 %collective-permute-start.19 = (bf16[128,128]{1,0:T(8,128)(2,1)S(1)}, bf16[128,128]{1,0:T(8,128)(2,1)S(1)}, u32[]{:S(2)}, u32[]{:S(2)}) collective-permute-start(bf16[128,128]{1,0:T(8,128)(2,1)S(1)} %shard_map.71.after_ref.refs_1_), channel_id=1, source_target_pairs={{0,2},{2,0},{4,6},{6,4},{1,3},{3,1},{5,7},{7,5},{8,10},{10,8},{12,... | collective-permute-start | bytes 98312 | tf_op jit(solution)/shard_map/ppermute | solution.py:351
  45.7 1.4 %collective-permute-done.21.refs_4_ = bf16[128,128]{1,0:T(8,128)(2,1)S(1)} collective-permute-done((bf16[128,128]{1,0:T(8,128)(2,1)S(1)}, bf16[128,128]{1,0:T(8,128)(2,1)S(1)}, u32[]{:S(2)}, u32[]{:S(2)}) %collective-permute-start.21) | collective-permute-done | bytes 32800 | tf_op jit(solution)/shard_map/ppermute | solution.py:351
  47.1 0.7 %collective-permute-done.20.refs_3_ = bf16[128,128]{1,0:T(8,128)(2,1)S(1)} collective-permute-done((bf16[128,128]{1,0:T(8,128)(2,1)S(1)}, bf16[128,128]{1,0:T(8,128)(2,1)S(1)}, u32[]{:S(2)}, u32[]{:S(2)}) %collective-permute-start.20) | collective-permute-done | bytes 32800 | tf_op jit(solution)/shard_map/ppermute | solution.py:351
  48.0 1.5 %collective-permute-start.18 = (bf16[512,128]{1,0:T(8,128)(2,1)S(1)}, bf16[512,128]{1,0:T(8,128)(2,1)S(1)}, u32[]{:S(2)}, u32[]{:S(2)}) collective-permute-start(bf16[512,128]{1,0:T(8,128)(2,1)S(1)} %get-tuple-element.43), channel_id=1, source_target_pairs={{0,8},{8,0},{16,24},{24,16},{1,9},{9,1},{17,25},{25,17},{2,10},{10... | collective-permute-start | bytes 393224 | tf_op jit(solution)/shard_map/ppermute | solution.py:351
  49.6 0.5 collective-permute-start.24
  50.8 4.5 %collective-permute-done.24.refs_1_ = bf16[256,128]{1,0:T(8,128)(2,1)S(1)} collective-permute-done((bf16[256,128]{1,0:T(8,128)(2,1)S(1)}, bf16[256,128]{1,0:T(8,128)(2,1)S(1)}, u32[]{:S(2)}, u32[]{:S(2)}) %collective-permute-start.24) | collective-permute-done | bytes 65568 | tf_op jit(solution)/shard_map/ppermute | solution.py:351
  56.1 0.7 %collective-permute-done.28.refs_1_ = bf16[256,128]{1,0:T(8,128)(2,1)S(1)} collective-permute-done((bf16[256,128]{1,0:T(8,128)(2,1)S(1)}, bf16[256,128]{1,0:T(8,128)(2,1)S(1)}, u32[]{:S(2)}, u32[]{:S(2)}) %collective-permute-start.28) | collective-permute-done | bytes 65568 | tf_op jit(solution)/shard_map/ppermute | solution.py:351
  56.8 1.0 %shard_map.78 = bf16[128,3072]{1,0:T(8,128)(2,1)} custom-call(bf16[128,1536]{1,0:T(8,128)(2,1)S(1)} %shard_map.77.done_ref, f32[128,1536]{1,0:T(8,128)S(1)} %shard_map.76.base_ref, bf16[128,1536]{1,0:T(8,128)(2,1)S(1)} %get-tuple-element.50.y_ref, bf16[512,128]{1,0:T(8,128)(2,1)S(1)} %collective-permute-done.27.refs_0_, ...), custom_call_target="tpu_custom_call" | custom-call | flops 25165824 | bytes 1966080 | tf_op jit(solution)/shard_map/pallas_call | solution.py:337
  (49 shorter events, 4.8 us)
Async XLA Ops:
  1.7 1.8 %collective-permute-start = (bf16[1536,128]{1,0:T(8,128)(2,1)S(1)}, bf16[1536,128]{1,0:T(8,128)(2,1)S(1)}, u32[]{:S(2)}, u32[]{:S(2)}) collective-permute-start(bf16[1536,128]{1,0:T(8,128)(2,1)S(1)} %get-tuple-element.32), channel_id=1, source_target_pairs={{0,1},{1,0},{2,3},{3,2},{4,5},{5,4},{6,7},{7,6},{8,9},{9,8},{10,11... | collective-permute-start | bytes 1179656 | tf_op jit(solution)/shard_map/ppermute | solution.py:351
  2.7 10.4 %copy-start = (bf16[128,3072]{1,0:T(8,128)(2,1)S(1)}, bf16[128,3072]{1,0:T(8,128)(2,1)}, u32[]{:S(2)}) copy-start(bf16[128,3072]{1,0:T(8,128)(2,1)} %query_ref.3) | copy-start | bytes 2359300
  2.7 10.4 %copy-start.1 = (f32[3,24,128]{2,1,0:T(8,128)S(1)}, f32[3,24,128]{2,1,0:T(8,128)}, u32[]{:S(2)}) copy-start(f32[3,24,128]{2,1,0:T(8,128)} %weight_ref.3) | copy-start | bytes 110596
  3.6 11.2 %collective-permute-start.1 = (bf16[256,128]{1,0:T(8,128)(2,1)S(1)}, bf16[256,128]{1,0:T(8,128)(2,1)S(1)}, u32[]{:S(2)}, u32[]{:S(2)}) collective-permute-start(bf16[256,128]{1,0:T(8,128)(2,1)S(1)} %get-tuple-element.35), channel_id=1, source_target_pairs={{0,6},{2,4},{4,2},{6,0},{1,7},{3,5},{5,3},{7,1},{8,14},{10,12},{12... | collective-permute-start | bytes 196616 | tf_op jit(solution)/shard_map/ppermute | solution.py:351
  8.7 6.6 %collective-permute-start.2 = (bf16[256,128]{1,0:T(8,128)(2,1)S(1)}, bf16[256,128]{1,0:T(8,128)(2,1)S(1)}, u32[]{:S(2)}, u32[]{:S(2)}) collective-permute-start(bf16[256,128]{1,0:T(8,128)(2,1)S(1)} %get-tuple-element.36), channel_id=1, source_target_pairs={{0,4},{2,6},{4,0},{6,2},{1,5},{3,7},{5,1},{7,3},{8,12},{10,14},{12... | collective-permute-start | bytes 196616 | tf_op jit(solution)/shard_map/ppermute | solution.py:351
  8.7 6.6 %collective-permute-start.3 = (bf16[256,128]{1,0:T(8,128)(2,1)S(1)}, bf16[256,128]{1,0:T(8,128)(2,1)S(1)}, u32[]{:S(2)}, u32[]{:S(2)}) collective-permute-start(bf16[256,128]{1,0:T(8,128)(2,1)S(1)} %get-tuple-element.37), channel_id=1, source_target_pairs={{0,2},{2,0},{4,6},{6,4},{1,3},{3,1},{5,7},{7,5},{8,10},{10,8},{12,... | collective-permute-start | bytes 196616 | tf_op jit(solution)/shard_map/ppermute | solution.py:351
  9.4 3.8 %copy-start.3 = (s32[1,4]{1,0:T(1,128)S(1)}, s32[1,4]{1,0:T(1,128)}, u32[]{:S(2)}) copy-start(s32[1,4]{1,0:T(1,128)} %back_ref.3) | copy-start | bytes 52
  9.4 10.1 %collective-permute-start.4 = (bf16[128,128]{1,0:T(8,128)(2,1)S(1)}, bf16[128,128]{1,0:T(8,128)(2,1)S(1)}, u32[]{:S(2)}, u32[]{:S(2)}) collective-permute-start(bf16[128,128]{1,0:T(8,128)(2,1)S(1)} %get-tuple-element.39), channel_id=1, source_target_pairs={{0,6},{2,4},{4,2},{6,0},{1,7},{3,5},{5,3},{7,1},{8,14},{10,12},{12... | collective-permute-start | bytes 98312 | tf_op jit(solution)/shard_map/ppermute | solution.py:351
  15.3 11.5 %collective-permute-start.9 = (bf16[256,128]{1,0:T(8,128)(2,1)S(1)}, bf16[256,128]{1,0:T(8,128)(2,1)S(1)}, u32[]{:S(2)}, u32[]{:S(2)}) collective-permute-start(bf16[256,128]{1,0:T(8,128)(2,1)S(1)} %shard_map.68.after_ref), channel_id=1, source_target_pairs={{0,24},{8,16},{16,8},{24,0},{1,25},{9,17},{17,9},{25,1},{2,26},{10... | collective-permute-start | bytes 196616 | tf_op jit(solution)/shard_map/ppermute | solution.py:351
  17.8 5.2 %collective-permute-start.5 = (bf16[128,128]{1,0:T(8,128)(2,1)S(1)}, bf16[128,128]{1,0:T(8,128)(2,1)S(1)}, u32[]{:S(2)}, u32[]{:S(2)}) collective-permute-start(bf16[128,128]{1,0:T(8,128)(2,1)S(1)} %get-tuple-element.40), channel_id=1, source_target_pairs={{0,4},{2,6},{4,0},{6,2},{1,5},{3,7},{5,1},{7,3},{8,12},{10,14},{12... | collective-permute-start | bytes 98312 | tf_op jit(solution)/shard_map/ppermute | solution.py:351
  18.4 9.0 %collective-permute-start.8 = (bf16[256,128]{1,0:T(8,128)(2,1)S(1)}, bf16[256,128]{1,0:T(8,128)(2,1)S(1)}, u32[]{:S(2)}, u32[]{:S(2)}) collective-permute-start(bf16[256,128]{1,0:T(8,128)(2,1)S(1)} %shard_map.68.after_ref), channel_id=1, source_target_pairs={{0,16},{8,24},{16,0},{24,8},{1,17},{9,25},{17,1},{25,9},{2,18},{10... | collective-permute-start | bytes 196616 | tf_op jit(solution)/shard_map/ppermute | solution.py:351
  19.0 8.5 %collective-permute-start.7 = (bf16[256,128]{1,0:T(8,128)(2,1)S(1)}, bf16[256,128]{1,0:T(8,128)(2,1)S(1)}, u32[]{:S(2)}, u32[]{:S(2)}) collective-permute-start(bf16[256,128]{1,0:T(8,128)(2,1)S(1)} %shard_map.68.after_ref), channel_id=1, source_target_pairs={{0,8},{8,0},{16,24},{24,16},{1,9},{9,1},{17,25},{25,17},{2,10},{10... | collective-permute-start | bytes 196616 | tf_op jit(solution)/shard_map/ppermute | solution.py:351
  19.5 4.3 %collective-permute-start.6 = (bf16[128,128]{1,0:T(8,128)(2,1)S(1)}, bf16[128,128]{1,0:T(8,128)(2,1)S(1)}, u32[]{:S(2)}, u32[]{:S(2)}) collective-permute-start(bf16[128,128]{1,0:T(8,128)(2,1)S(1)} %get-tuple-element.41), channel_id=1, source_target_pairs={{0,2},{2,0},{4,6},{6,4},{1,3},{3,1},{5,7},{7,5},{8,10},{10,8},{12,... | collective-permute-start | bytes 98312 | tf_op jit(solution)/shard_map/ppermute | solution.py:351
  23.9 7.2 %collective-permute-start.12 = (bf16[128,128]{1,0:T(8,128)(2,1)S(1)}, bf16[128,128]{1,0:T(8,128)(2,1)S(1)}, u32[]{:S(2)}, u32[]{:S(2)}) collective-permute-start(bf16[128,128]{1,0:T(8,128)(2,1)S(1)} %shard_map.69.after_ref), channel_id=1, source_target_pairs={{0,24},{8,16},{16,8},{24,0},{1,25},{9,17},{17,9},{25,1},{2,26},{10... | collective-permute-start | bytes 98312 | tf_op jit(solution)/shard_map/ppermute | solution.py:351
  26.4 6.0 %collective-permute-start.11 = (bf16[128,128]{1,0:T(8,128)(2,1)S(1)}, bf16[128,128]{1,0:T(8,128)(2,1)S(1)}, u32[]{:S(2)}, u32[]{:S(2)}) collective-permute-start(bf16[128,128]{1,0:T(8,128)(2,1)S(1)} %shard_map.69.after_ref), channel_id=1, source_target_pairs={{0,16},{8,24},{16,0},{24,8},{1,17},{9,25},{17,1},{25,9},{2,18},{10... | collective-permute-start | bytes 98312 | tf_op jit(solution)/shard_map/ppermute | solution.py:351
  26.9 5.8 %collective-permute-start.10 = (bf16[128,128]{1,0:T(8,128)(2,1)S(1)}, bf16[128,128]{1,0:T(8,128)(2,1)S(1)}, u32[]{:S(2)}, u32[]{:S(2)}) collective-permute-start(bf16[128,128]{1,0:T(8,128)(2,1)S(1)} %shard_map.69.after_ref), channel_id=1, source_target_pairs={{0,8},{8,0},{16,24},{24,16},{1,9},{9,1},{17,25},{25,17},{2,10},{10... | collective-permute-start | bytes 98312 | tf_op jit(solution)/shard_map/ppermute | solution.py:351
  27.4 9.7 %collective-permute-start.17 = (bf16[256,128]{1,0:T(8,128)(2,1)S(1)}, bf16[256,128]{1,0:T(8,128)(2,1)S(1)}, u32[]{:S(2)}, u32[]{:S(2)}) collective-permute-start(bf16[256,128]{1,0:T(8,128)(2,1)S(1)} %shard_map.70.after_ref.refs_1_), channel_id=1, source_target_pairs={{0,10},{2,8},{4,14},{6,12},{8,2},{10,0},{12,6},{14,4},{16,26},{18,... | collective-permute-start | bytes 196616 | tf_op jit(solution)/shard_map/ppermute | solution.py:394
  30.5 6.7 %collective-permute-start.16 = (bf16[256,128]{1,0:T(8,128)(2,1)S(1)}, bf16[256,128]{1,0:T(8,128)(2,1)S(1)}, u32[]{:S(2)}, u32[]{:S(2)}) collective-permute-start(bf16[256,128]{1,0:T(8,128)(2,1)S(1)} %shard_map.70.after_ref.refs_1_), channel_id=1, source_target_pairs={{0,8},{8,0},{16,24},{24,16},{1,9},{9,1},{17,25},{25,17},{2,10},{10... | collective-permute-start | bytes 196616 | tf_op jit(solution)/shard_map/ppermute | solution.py:351
  31.0 6.2 %collective-permute-start.15 = (bf16[256,128]{1,0:T(8,128)(2,1)S(1)}, bf16[256,128]{1,0:T(8,128)(2,1)S(1)}, u32[]{:S(2)}, u32[]{:S(2)}) collective-permute-start(bf16[256,128]{1,0:T(8,128)(2,1)S(1)} %shard_map.70.after_ref.refs_1_), channel_id=1, source_target_pairs={{0,6},{2,4},{4,2},{6,0},{1,7},{3,5},{5,3},{7,1},{8,14},{10,12},{12... | collective-permute-start | bytes 196616 | tf_op jit(solution)/shard_map/ppermute | solution.py:351
  32.4 6.1 %collective-permute-start.14 = (bf16[256,128]{1,0:T(8,128)(2,1)S(1)}, bf16[256,128]{1,0:T(8,128)(2,1)S(1)}, u32[]{:S(2)}, u32[]{:S(2)}) collective-permute-start(bf16[256,128]{1,0:T(8,128)(2,1)S(1)} %shard_map.70.after_ref.refs_1_), channel_id=1, source_target_pairs={{0,4},{2,6},{4,0},{6,2},{1,5},{3,7},{5,1},{7,3},{8,12},{10,14},{12... | collective-permute-start | bytes 196616 | tf_op jit(solution)/shard_map/ppermute | solution.py:351
  32.7 5.8 %collective-permute-start.13 = (bf16[256,128]{1,0:T(8,128)(2,1)S(1)}, bf16[256,128]{1,0:T(8,128)(2,1)S(1)}, u32[]{:S(2)}, u32[]{:S(2)}) collective-permute-start(bf16[256,128]{1,0:T(8,128)(2,1)S(1)} %shard_map.70.after_ref.refs_1_), channel_id=1, source_target_pairs={{0,2},{2,0},{4,6},{6,4},{1,3},{3,1},{5,7},{7,5},{8,10},{10,8},{12,... | collective-permute-start | bytes 196616 | tf_op jit(solution)/shard_map/ppermute | solution.py:351
  38.5 11.9 %collective-permute-start.25 = (bf16[1536,128]{1,0:T(8,128)(2,1)S(1)}, bf16[1536,128]{1,0:T(8,128)(2,1)S(1)}, u32[]{:S(2)}, u32[]{:S(2)}) collective-permute-start(bf16[1536,128]{1,0:T(8,128)(2,1)S(1)} %get-tuple-element.44.refs_0_), channel_id=1, source_target_pairs={{0,1},{1,0},{2,3},{3,2},{4,5},{5,4},{6,7},{7,6},{8,9},{9,8},{10,11... | collective-permute-start | bytes 1179656 | tf_op jit(solution)/shard_map/ppermute | solution.py:351
  38.6 5.0 %collective-permute-start.23 = (bf16[128,128]{1,0:T(8,128)(2,1)S(1)}, bf16[128,128]{1,0:T(8,128)(2,1)S(1)}, u32[]{:S(2)}, u32[]{:S(2)}) collective-permute-start(bf16[128,128]{1,0:T(8,128)(2,1)S(1)} %shard_map.71.after_ref.refs_1_), channel_id=1, source_target_pairs={{0,10},{2,8},{4,14},{6,12},{8,2},{10,0},{12,6},{14,4},{16,26},{18,... | collective-permute-start | bytes 98312 | tf_op jit(solution)/shard_map/ppermute | solution.py:394
  40.8 4.9 %collective-permute-start.22 = (bf16[128,128]{1,0:T(8,128)(2,1)S(1)}, bf16[128,128]{1,0:T(8,128)(2,1)S(1)}, u32[]{:S(2)}, u32[]{:S(2)}) collective-permute-start(bf16[128,128]{1,0:T(8,128)(2,1)S(1)} %shard_map.71.after_ref.refs_1_), channel_id=1, source_target_pairs={{0,8},{8,0},{16,24},{24,16},{1,9},{9,1},{17,25},{25,17},{2,10},{10... | collective-permute-start | bytes 98312 | tf_op jit(solution)/shard_map/ppermute | solution.py:351
  41.3 5.8 %collective-permute-start.21 = (bf16[128,128]{1,0:T(8,128)(2,1)S(1)}, bf16[128,128]{1,0:T(8,128)(2,1)S(1)}, u32[]{:S(2)}, u32[]{:S(2)}) collective-permute-start(bf16[128,128]{1,0:T(8,128)(2,1)S(1)} %shard_map.71.after_ref.refs_1_), channel_id=1, source_target_pairs={{0,6},{2,4},{4,2},{6,0},{1,7},{3,5},{5,3},{7,1},{8,14},{10,12},{12... | collective-permute-start | bytes 98312 | tf_op jit(solution)/shard_map/ppermute | solution.py:351
  42.7 5.2 %collective-permute-start.20 = (bf16[128,128]{1,0:T(8,128)(2,1)S(1)}, bf16[128,128]{1,0:T(8,128)(2,1)S(1)}, u32[]{:S(2)}, u32[]{:S(2)}) collective-permute-start(bf16[128,128]{1,0:T(8,128)(2,1)S(1)} %shard_map.71.after_ref.refs_1_), channel_id=1, source_target_pairs={{0,4},{2,6},{4,0},{6,2},{1,5},{3,7},{5,1},{7,3},{8,12},{10,14},{12... | collective-permute-start | bytes 98312 | tf_op jit(solution)/shard_map/ppermute | solution.py:351
  43.6 4.3 %collective-permute-start.19 = (bf16[128,128]{1,0:T(8,128)(2,1)S(1)}, bf16[128,128]{1,0:T(8,128)(2,1)S(1)}, u32[]{:S(2)}, u32[]{:S(2)}) collective-permute-start(bf16[128,128]{1,0:T(8,128)(2,1)S(1)} %shard_map.71.after_ref.refs_1_), channel_id=1, source_target_pairs={{0,2},{2,0},{4,6},{6,4},{1,3},{3,1},{5,7},{7,5},{8,10},{10,8},{12,... | collective-permute-start | bytes 98312 | tf_op jit(solution)/shard_map/ppermute | solution.py:351
  47.9 2.5 %collective-permute-start.26 = (bf16[768,128]{1,0:T(8,128)(2,1)S(1)}, bf16[768,128]{1,0:T(8,128)(2,1)S(1)}, u32[]{:S(2)}, u32[]{:S(2)}) collective-permute-start(bf16[768,128]{1,0:T(8,128)(2,1)S(1)} %get-tuple-element.48.refs_1_), channel_id=1, source_target_pairs={{0,1},{1,0},{2,3},{3,2},{4,5},{5,4},{6,7},{7,6},{8,9},{9,8},{10,11... | collective-permute-start | bytes 589832 | tf_op jit(solution)/shard_map/ppermute | solution.py:351
  48.0 7.3 %collective-permute-start.18 = (bf16[512,128]{1,0:T(8,128)(2,1)S(1)}, bf16[512,128]{1,0:T(8,128)(2,1)S(1)}, u32[]{:S(2)}, u32[]{:S(2)}) collective-permute-start(bf16[512,128]{1,0:T(8,128)(2,1)S(1)} %get-tuple-element.43), channel_id=1, source_target_pairs={{0,8},{8,0},{16,24},{24,16},{1,9},{9,1},{17,25},{25,17},{2,10},{10... | collective-permute-start | bytes 393224 | tf_op jit(solution)/shard_map/ppermute | solution.py:351
  49.6 5.8 %collective-permute-start.24 = (bf16[256,128]{1,0:T(8,128)(2,1)S(1)}, bf16[256,128]{1,0:T(8,128)(2,1)S(1)}, u32[]{:S(2)}, u32[]{:S(2)}) collective-permute-start(bf16[256,128]{1,0:T(8,128)(2,1)S(1)} %get-tuple-element.45), channel_id=1, source_target_pairs={{0,8},{8,0},{16,24},{24,16},{1,9},{9,1},{17,25},{25,17},{2,10},{10... | collective-permute-start | bytes 196616 | tf_op jit(solution)/shard_map/ppermute | solution.py:351
  55.3 1.4 %collective-permute-start.27 = (bf16[512,128]{1,0:T(8,128)(2,1)S(1)}, bf16[512,128]{1,0:T(8,128)(2,1)S(1)}, u32[]{:S(2)}, u32[]{:S(2)}) collective-permute-start(bf16[512,128]{1,0:T(8,128)(2,1)S(1)} %collective-permute-done.18.refs_0_), channel_id=1, source_target_pairs={{0,1},{1,0},{2,3},{3,2},{4,5},{5,4},{6,7},{7,6},{8,9},{9,8},{10,11... | collective-permute-start | bytes 393224 | tf_op jit(solution)/shard_map/ppermute | solution.py:351
  55.3 1.4 %collective-permute-start.28 = (bf16[256,128]{1,0:T(8,128)(2,1)S(1)}, bf16[256,128]{1,0:T(8,128)(2,1)S(1)}, u32[]{:S(2)}, u32[]{:S(2)}) collective-permute-start(bf16[256,128]{1,0:T(8,128)(2,1)S(1)} %collective-permute-done.24.refs_1_), channel_id=1, source_target_pairs={{0,1},{1,0},{2,3},{3,2},{4,5},{5,4},{6,7},{7,6},{8,9},{9,8},{10,11... | collective-permute-start | bytes 196616 | tf_op jit(solution)/shard_map/ppermute | solution.py:351
  (1 other events, 3.8 us)

commit v6 on v4

--- a/solution.py
+++ b/solution.py
@@ -16,7 +16,9 @@
 F32, BF16 = jnp.float32, jnp.bfloat16
 WHOLE = pl.BlockSpec(memory_space=pltpu.VMEM)
 SCALARS = pl.BlockSpec(memory_space=pltpu.SMEM)
+ANYWHERE = pl.BlockSpec(memory_space=pl.ANY)
 IN_HBM = pl.BlockSpec(memory_space=pltpu.HBM)
+SMALL = pl.CostEstimate(flops=1024, bytes_accessed=1024, transcendentals=0)
 PARAMS = pltpu.CompilerParams(vmem_limit_bytes=VMEM_LIMIT)
 
 
@@ -115,7 +117,8 @@
         in_specs=[WHOLE, WHOLE],
         out_specs=[WHOLE] * chips,
         compiler_params=PARAMS,
-    )(mine, other)
+        cost_estimate=SMALL,
+    )(*in_vmem(mine, other))
 
 
 def sum_kernel(after_ref, own_ref, *refs):
@@ -129,29 +132,56 @@
     return pl.pallas_call(
         sum_kernel,
         out_shape=pltpu.VMEM(own.shape, dtype),
-        in_specs=[pl.BlockSpec(memory_space=pl.ANY)] + [WHOLE] * (1 + len(parts)),
-        out_specs=WHOLE,
-        compiler_params=PARAMS,
-    )(after, own, *parts)
-
-
-def pack_kernel(groups, after, *refs):
-    inputs, outputs = refs[after : len(refs) - len(groups)], refs[len(refs) - len(groups) :]
-    for group, out_ref in zip(groups, outputs):
-        rows = out_ref.shape[0] // len(group)
-        for n, which in enumerate(group):
-            out_ref[n * rows : (n + 1) * rows, :] = inputs[which][...]
-
-
-def pack(groups, pieces, after):
-    rows = pieces[0].shape[0]
-    return pl.pallas_call(
-        functools.partial(pack_kernel, groups, len(after)),
-        out_shape=[pltpu.VMEM((rows * len(group), HEAD_DIM), BF16) for group in groups],
-        in_specs=[pl.BlockSpec(memory_space=pl.ANY)] * len(after) + [WHOLE] * len(pieces),
-        out_specs=[WHOLE] * len(groups),
-        compiler_params=PARAMS,
-    )(*after, *in_vmem(*pieces))
+        in_specs=[ANYWHERE] + [WHOLE] * (1 + len(parts)),
+        out_specs=WHOLE,
+        compiler_params=PARAMS,
+        cost_estimate=SMALL,
+    )(after, *in_vmem(own, *parts))
+
+
+def slot_kernel(own_ref, near_ref, out_ref):
+    near = near_ref[...].astype(F32)
+    both = own_ref[...].astype(F32) + near
+    out_ref[...] = jnp.where(lax.axis_index("frame") == 0, both, near).astype(BF16)
+
+
+def choose_slot(own, near):
+    return pl.pallas_call(
+        slot_kernel,
+        out_shape=pltpu.VMEM(near.shape, BF16),
+        in_specs=[WHOLE] * 2,
+        out_specs=WHOLE,
+        compiler_params=PARAMS,
+        cost_estimate=SMALL,
+    )(*in_vmem(own, near))
+
+
+def pack_kernel(after, plain, pairs, *refs):
+    out_ref, refs = refs[-1], refs[after:-1]
+    row = 0
+    for ref in refs[:plain]:
+        out_ref[row : row + ref.shape[0], :] = ref[...]
+        row += ref.shape[0]
+    for n in range(pairs):
+        first, second = refs[plain + n], refs[plain + pairs + n]
+        chosen = jnp.where(
+            lax.axis_index("frame") == 2, first[...].astype(F32), second[...].astype(F32)
+        )
+        out_ref[row : row + first.shape[0], :] = chosen.astype(BF16)
+        row += first.shape[0]
+
+
+def pack(plain, pairs, after):
+    firsts, seconds = [p[0] for p in pairs], [p[1] for p in pairs]
+    rows = sum(array.shape[0] for array in plain + firsts)
+    return pl.pallas_call(
+        functools.partial(pack_kernel, len(after), len(plain), len(pairs)),
+        out_shape=pltpu.VMEM((rows, HEAD_DIM), BF16),
+        in_specs=[ANYWHERE] * len(after) + [WHOLE] * (len(plain) + 2 * len(pairs)),
+        out_specs=WHOLE,
+        compiler_params=PARAMS,
+        cost_estimate=SMALL,
+    )(*after, *in_vmem(*plain, *firsts, *seconds))
 
 
 def local_kernel(
@@ -217,7 +247,7 @@
     return pl.pallas_call(
         functools.partial(local_kernel, coefs, turn),
         out_shape=[pltpu.VMEM((tokens, width), F32)] + [pltpu.VMEM((tokens, width), BF16)] * slots,
-        in_specs=[SCALARS] * 2 + [WHOLE] * 4 + [pl.BlockSpec(memory_space=pl.ANY)],
+        in_specs=[SCALARS] * 2 + [WHOLE] * 4 + [ANYWHERE],
         out_specs=[WHOLE] * (1 + slots),
         compiler_params=PARAMS,
         cost_estimate=pl.CostEstimate(
@@ -266,10 +296,10 @@
     )(*in_vmem(local, x, y, states))
 
 
-def late_half(chips, early, base_ref, y_ref, state_ref, out_ref):
-    rows = state_ref.shape[0] // max(chips - early, 1)
+def late_half(chips, early, base_ref, y_ref, *refs):
+    out_ref = refs[-1]
     for d in range(chips):
-        states = [(y_ref, state_ref, (d - early) * rows)] if d >= early else []
+        states = [(y_ref, refs[0], 0)] if d >= early else []
         for at, result in read_heads(d, chips, base_ref, states):
             out_ref[:, at] = result.astype(BF16)
 
@@ -278,20 +308,21 @@
     return pl.pallas_call(
         functools.partial(late_half, chips, early),
         out_shape=pltpu.VMEM(base.shape, BF16),
-        in_specs=[WHOLE] * 3,
+        in_specs=[WHOLE] * (2 + len(states)),
         out_specs=WHOLE,
         compiler_params=PARAMS,
         cost_estimate=pl.CostEstimate(
             flops=base.size * HEAD_DIM, bytes_accessed=6 * base.size, transcendentals=0
         ),
-    )(*in_vmem(base, y, states))
-
-
-def last_kernel(chips, early, done_ref, base_ref, y_ref, state_ref, out_ref, held, sems):
+    )(*in_vmem(base, y, *states))
+
+
+def last_kernel(chips, early, done_ref, base_ref, y_ref, *refs):
+    *state_refs, out_ref, held, sems = refs
     mine, other = core_heads()
     first = pltpu.make_async_copy(done_ref, out_ref.at[:, columns(mine, HEADS // 2)], sems.at[0])
     first.start()
-    late_half(chips, early, base_ref, y_ref, state_ref, held)
+    late_half(chips, early, base_ref, y_ref, *state_refs, held)
     second = pltpu.make_async_copy(held, out_ref.at[:, columns(other, HEADS // 2)], sems.at[1])
     second.start()
     first.wait()
@@ -303,66 +334,61 @@
     return pl.pallas_call(
         functools.partial(last_kernel, chips, early),
         out_shape=jax.ShapeDtypeStruct((tokens, 2 * width), BF16),
-        in_specs=[WHOLE] * 4,
-        out_specs=pl.BlockSpec(memory_space=pl.ANY),
+        in_specs=[WHOLE] * (3 + len(states)),
+        out_specs=ANYWHERE,
         scratch_shapes=[pltpu.VMEM((tokens, width), BF16), pltpu.SemaphoreType.DMA((2,))],
         compiler_params=PARAMS,
         cost_estimate=pl.CostEstimate(
             flops=base.size * HEAD_DIM, bytes_accessed=10 * base.size, transcendentals=0
         ),
-    )(*in_vmem(done, base, y, states))
+    )(*in_vmem(done, base, y, *states))
 
 
 def swap(array, axis, mask, size):
     return lax.ppermute(array, axis, [(n, n ^ mask) for n in range(size)])
 
 
+def from_first(array, target, frames):
+    places = {0: target, target: 0}
+    return lax.ppermute(array, "frame", [(f, places.get(f, f)) for f in range(frames)])
+
+
 def body(sizes, queries, keys, values, level_weight, frame_len, window_back):
     frames, outer, chips = sizes
-    frame = lax.axis_index("frame")
     low, high = (
         1.0 / math.sqrt(HEAD_DIM * 2**level * queries.shape[0] * outer * chips * 2) for level in (0, 1)
     )
 
     def coefs(f):
-        x_low = jnp.where(f % 2 == 1, low, 0.0)
-        x_high = jnp.where(f == 2, high, 0.0)
-        return [[(0, x_low), (1, x_high)], [(1, jnp.where(f == 3, high, 0.0))]]
+        return [[(0, jnp.where(f % 2 == 1, low, 0.0))], [(1, jnp.where(f >= 2, high, 0.0))]]
 
     local = functools.partial(local_part, coefs, 2)
     rest = (frame_len, window_back, queries)
+    early = chips - 1 if chips > 1 else 1
 
     outgoing, keys, values = outgoing_state(keys, values)
     incoming = swap(outgoing, "core", 1, 2)
     mine = own_state(keys, values)
     own, *sends = chip_pieces(mine, incoming, chips)
-    got = {d: swap(sends[d - 1], "chip", d, chips) for d in reversed(range(1, chips))}
-
+    got = [swap(sends[d - 1], "chip", d, chips) for d in reversed(range(1, chips))]
     local_0, x_0, y_0 = local(0, *rest, keys, values, level_weight, own)
-    state = sum_pieces(local_0, own, list(got.values()), F32 if outer > 1 else BF16)
+    state = sum_pieces(local_0, own, got, F32 if outer > 1 else BF16)
     if outer > 1:
         state = lax.psum(state, "outer").astype(BF16)
-    near, across, diagonal = (swap(state, "frame", mask, frames) for mask in (1, 2, 3))
-    both = (across.astype(F32) + diagonal.astype(F32)).astype(BF16)
-    slot = jnp.where(frame == 2, both, near)
-
-    early = min(2, chips)
-    x = [swap(slot, "chip", d, chips) for d in range(1, chips)]
-    near_pairs = [
-        (f * chips + c, (f ^ 1) * chips + (c ^ 1)) for f in range(frames) for c in range(chips)
-    ]
-    y = [swap(slot, "frame", 1, frames), lax.ppermute(slot, ("frame", "chip"), near_pairs)][:early]
+    slot = choose_slot(state, swap(state, "frame", 1, frames))
+
+    x = [slot] + [swap(slot, "chip", d, chips) for d in range(1, chips)]
     local_1, x_1, y_1 = local(1, *rest, keys, values, level_weight, slot)
-    pieces = [slot] + x + y
-    own_states, late = pack(
-        [list(range(chips + early)), list(range(early, chips)) or [0]], pieces, [local_1]
-    )
-    late_own = swap(late, "frame", 1, frames)
+    fan = [pack(x[:2], [], [local_1])] + x[2:]
+    pairs = [(from_first(piece, 2, frames), from_first(piece, 3, frames)) for piece in fan]
+    late = pairs[1:][-1:]
+    own_states = pack(x, pairs[: len(pairs) - len(late)], [])
     other_states = swap(own_states, "core", 1, 2)
     base_0 = read_middle(chips, early, local_0, x_0, y_0, own_states)
     base_1 = read_middle(chips, early, local_1, x_1, y_1, other_states)
-    late_own, base_0, base_1 = lax.optimization_barrier((late_own, base_0, base_1))
-    late_other = swap(late_own, "core", 1, 2)
+    late, base_0, base_1 = lax.optimization_barrier((late, base_0, base_1))
+    late_own = [pack([], late, [])] if late else []
+    late_other = [swap(piece, "core", 1, 2) for piece in late_own]
     done = read_late(chips, early, base_0, y_0, late_own)
     return read_last(chips, early, done, base_1, y_1, late_other)
 

time: 48.9 us -> 57 us (1.17)
  starting transfers between devices: 17.5 us -> 28.1 us
  waiting for transfers between devices: 21.6 us -> 20.5 us
  other arithmetic: 1.03 us -> 0 us
    ppermute x1 -> x6, starting transfers between devices: 1.42 us -> 14.7 us  [from_first(): lax.ppermute(array, 'frame', [(f, places.get(f, f)) for f in range(frames)])]
    ppermute x14 -> x10, waiting for transfers between devices: 20.9 us -> 11.1 us  [swap(): return lax.ppermute(array, axis, [(n, n ^ mask) for n in range(size)])]
    ppermute x1 -> x6, waiting for transfers between devices: 0.76 us -> 9.35 us  [from_first(): lax.ppermute(array, 'frame', [(f, places.get(f, f)) for f in range(frames)])]
    ppermute x14 -> x10, starting transfers between devices: 16.1 us -> 13.5 us  [swap(): return lax.ppermute(array, axis, [(n, n ^ mask) for n in range(size)])]
    select_n x1 -> x0, other arithmetic: 1.03 us -> none  [body(): slot = jnp.where(frame == 2, both, near)]
    pallas_call x1, Pallas kernels: 0.68 us -> 0.05 us  [sum_pieces(): pl.pallas_call(sum_kernel, out_shape=pltpu.VMEM(own.shape, dtype), in_spe...]
  transfers between devices with their start and end apart: 15 -> 16, of which waited for: 11 -> 9; matrix products, arithmetic and copies ran while one was open for 0% -> 0% of each run, Pallas kernels for 10% -> 9%
where the time goes in v6:
time: 57 us; the launch traced here: 56.7 us
  starting transfers between devices  28.1 us (49%)
  waiting for transfers between devices  20.5 us (36%)
  Pallas kernels  7.9 us (14%)
    ppermute x6, starting transfers between devices, from_first(): lax.ppermute(array, 'frame', [(f, places.get(f, f)) for f in range(frames)])  14.7 us
    ppermute x10, starting transfers between devices, swap(): return lax.ppermute(array, axis, [(n, n ^ mask) for n in range(size)])  13.5 us
    ppermute x10, waiting for transfers between devices, swap(): return lax.ppermute(array, axis, [(n, n ^ mask) for n in range(size)])  11.1 us
    ppermute x6, waiting for transfers between devices, from_first(): lax.ppermute(array, 'frame', [(f, places.get(f, f)) for f in range(frames)])  9.35 us
    pallas_call x2, Pallas kernels, local_part(): pl.pallas_call(functools.partial(local_kernel, coefs, turn), out_shape=[p...  3.43 us
    pallas_call x1, Pallas kernels, outgoing_state(): pl.pallas_call(first_kernel, out_shape=[pltpu.VMEM((half * dim, dim), BF1...  1.69 us
  transfers between devices with their start and end apart: 16, of which 9 were waited for; matrix products, arithmetic and copies ran while one was open for 0% of the time, Pallas kernels for 9%

profile of v6, /device:TPU:0, one launch (start us, length us, event | category | flops | bytes accessed | tf_op | source)
XLA Modules:
  0.0 56.7 jit_solution(7815328333128826354)
XLA Ops:
  0.0 1.7 %shard_map.64 = (bf16[1536,128]{1,0:T(8,128)(2,1)S(1)}, bf16[128,3072]{1,0:T(8,128)(2,1)S(1)}, bf16[128,3072]{1,0:T(8,128)(2,1)S(1)}) custom-call(bf16[128,3072]{1,0:T(8,128)(2,1)} %key_ref.1, bf16[128,3072]{1,0:T(8,128)(2,1)} %value_ref.1), custom_call_target="tpu_custom_call" | custom-call | flops 50331648 | bytes 1572864 | tf_op jit(solution)/shard_map/pallas_call | solution.py:72
  1.7 0.5 collective-permute-start
  2.2 0.5 shard_map.65.mine_ref
  2.7 0.8 %collective-permute-done.other_ref = bf16[1536,128]{1,0:T(8,128)(2,1)S(1)} collective-permute-done((bf16[1536,128]{1,0:T(8,128)(2,1)S(1)}, bf16[1536,128]{1,0:T(8,128)(2,1)S(1)}, u32[]{:S(2)}, u32[]{:S(2)}) %collective-permute-start) | collective-permute-done | bytes 393248 | tf_op jit(solution)/shard_map/ppermute | solution.py:348
  3.6 5.1 %collective-permute-start.1 = (bf16[384,128]{1,0:T(8,128)(2,1)S(1)}, bf16[384,128]{1,0:T(8,128)(2,1)S(1)}, u32[]{:S(2)}, u32[]{:S(2)}) collective-permute-start(bf16[384,128]{1,0:T(8,128)(2,1)S(1)} %get-tuple-element.27), channel_id=1, source_target_pairs={{0,6},{2,4},{4,2},{6,0},{1,7},{3,5},{5,3},{7,1},{8,14},{10,12},{12... | collective-permute-start | bytes 294920 | tf_op jit(solution)/shard_map/ppermute | solution.py:348
  8.7 0.6 %collective-permute-start.3 = (bf16[384,128]{1,0:T(8,128)(2,1)S(1)}, bf16[384,128]{1,0:T(8,128)(2,1)S(1)}, u32[]{:S(2)}, u32[]{:S(2)}) collective-permute-start(bf16[384,128]{1,0:T(8,128)(2,1)S(1)} %get-tuple-element.29), channel_id=1, source_target_pairs={{0,2},{2,0},{4,6},{6,4},{1,3},{3,1},{5,7},{7,5},{8,10},{10,8},{12,... | collective-permute-start | bytes 294920 | tf_op jit(solution)/shard_map/ppermute | solution.py:348
  9.4 1.7 %shard_map.67 = (f32[128,1536]{1,0:T(8,128)S(1)}, bf16[128,1536]{1,0:T(8,128)(2,1)S(1)}, bf16[128,1536]{1,0:T(8,128)(2,1)S(1)}) custom-call(s32[1,4]{1,0:T(1,128)S(1)} %copy-done.2, s32[1,4]{1,0:T(1,128)S(1)} %copy-done.3, bf16[128,3072]{1,0:T(8,128)(2,1)S(1)} %copy-done, bf16[128,3072]{1,0:T(8,128)(2,1)S(1)} %get-tuple-element.22.key_ref, ...), custom_call_target="tpu_custom_call" | custom-call | flops 100663296 | bytes 2752512 | tf_op jit(solution)/shard_map/pallas_call | solution.py:247
  11.1 1.3 %collective-permute-done.1.refs_0_ = bf16[384,128]{1,0:T(8,128)(2,1)S(1)} collective-permute-done((bf16[384,128]{1,0:T(8,128)(2,1)S(1)}, bf16[384,128]{1,0:T(8,128)(2,1)S(1)}, u32[]{:S(2)}, u32[]{:S(2)}) %collective-permute-start.1) | collective-permute-done | bytes 98336 | tf_op jit(solution)/shard_map/ppermute | solution.py:348
  12.4 4.9 %collective-permute-done.2.refs_1_ = bf16[384,128]{1,0:T(8,128)(2,1)S(1)} collective-permute-done((bf16[384,128]{1,0:T(8,128)(2,1)S(1)}, bf16[384,128]{1,0:T(8,128)(2,1)S(1)}, u32[]{:S(2)}, u32[]{:S(2)}) %collective-permute-start.2) | collective-permute-done | bytes 98336 | tf_op jit(solution)/shard_map/ppermute | solution.py:348
  17.3 1.6 %collective-permute-start.4 = (bf16[384,128]{1,0:T(8,128)(2,1)S(1)}, bf16[384,128]{1,0:T(8,128)(2,1)S(1)}, u32[]{:S(2)}, u32[]{:S(2)}) collective-permute-start(bf16[384,128]{1,0:T(8,128)(2,1)S(1)} %shard_map.68.own_ref), channel_id=1, source_target_pairs={{0,8},{8,0},{16,24},{24,16},{1,9},{9,1},{17,25},{25,17},{2,10},{10... | collective-permute-start | bytes 294920 | tf_op jit(solution)/shard_map/ppermute | solution.py:348
  18.9 3.1 %collective-permute-done.4.near_ref = bf16[384,128]{1,0:T(8,128)(2,1)S(1)} collective-permute-done((bf16[384,128]{1,0:T(8,128)(2,1)S(1)}, bf16[384,128]{1,0:T(8,128)(2,1)S(1)}, u32[]{:S(2)}, u32[]{:S(2)}) %collective-permute-start.4) | collective-permute-done | bytes 98336 | tf_op jit(solution)/shard_map/ppermute | solution.py:348
  22.1 0.6 %collective-permute-start.8 = (bf16[384,128]{1,0:T(8,128)(2,1)S(1)}, bf16[384,128]{1,0:T(8,128)(2,1)S(1)}, u32[]{:S(2)}, u32[]{:S(2)}) collective-permute-start(bf16[384,128]{1,0:T(8,128)(2,1)S(1)} %shard_map.69.after_ref.refs_1_.refs_0_), channel_id=1, source_target_pairs={{0,2},{2,0},{4,6},{6,4},{1,3},{3,1},{5,7},{7,5},{8,10},{10,8},{12,... | collective-permute-start | bytes 294920 | tf_op jit(solution)/shard_map/ppermute | solution.py:348
  22.7 2.5 %collective-permute-start.9 = (bf16[384,128]{1,0:T(8,128)(2,1)S(1)}, bf16[384,128]{1,0:T(8,128)(2,1)S(1)}, u32[]{:S(2)}, u32[]{:S(2)}) collective-permute-start(bf16[384,128]{1,0:T(8,128)(2,1)S(1)} %shard_map.69.after_ref.refs_1_.refs_0_), channel_id=1, source_target_pairs={{0,4},{2,6},{4,0},{6,2},{1,5},{3,7},{5,1},{7,3},{8,12},{10,14},{12... | collective-permute-start | bytes 294920 | tf_op jit(solution)/shard_map/ppermute | solution.py:348
  25.2 1.7 %shard_map.70 = (f32[128,1536]{1,0:T(8,128)S(1)}, bf16[128,1536]{1,0:T(8,128)(2,1)S(1)}, bf16[128,1536]{1,0:T(8,128)(2,1)S(1)}) custom-call(s32[1,4]{1,0:T(1,128)S(1)} %copy-done.2, s32[1,4]{1,0:T(1,128)S(1)} %copy-done.3, bf16[128,3072]{1,0:T(8,128)(2,1)S(1)} %copy-done, bf16[128,3072]{1,0:T(8,128)(2,1)S(1)} %get-tuple-element.22.key_ref, ...), custom_call_target="tpu_custom_call" | custom-call | flops 100663296 | bytes 2752512 | tf_op jit(solution)/shard_map/pallas_call | solution.py:247
  26.9 4.3 %collective-permute-start.12 = (bf16[768,128]{1,0:T(8,128)(2,1)S(1)}, bf16[768,128]{1,0:T(8,128)(2,1)S(1)}, u32[]{:S(2)}, u32[]{:S(2)}) collective-permute-start(bf16[768,128]{1,0:T(8,128)(2,1)S(1)} %shard_map.71), channel_id=1, source_target_pairs={{0,24},{8,8},{16,16},{24,0},{1,25},{9,9},{17,17},{25,1},{2,26},{10... | collective-permute-start | bytes 589832 | tf_op jit(solution)/shard_map/ppermute | solution.py:353
  31.3 1.9 %collective-permute-start.10 = (bf16[768,128]{1,0:T(8,128)(2,1)S(1)}, bf16[768,128]{1,0:T(8,128)(2,1)S(1)}, u32[]{:S(2)}, u32[]{:S(2)}) collective-permute-start(bf16[768,128]{1,0:T(8,128)(2,1)S(1)} %shard_map.71), channel_id=1, source_target_pairs={{0,16},{8,8},{16,0},{24,24},{1,17},{9,9},{17,1},{25,25},{2,18},{10... | collective-permute-start | bytes 589832 | tf_op jit(solution)/shard_map/ppermute | solution.py:353
  33.2 2.4 %collective-permute-start.5 = (bf16[384,128]{1,0:T(8,128)(2,1)S(1)}, bf16[384,128]{1,0:T(8,128)(2,1)S(1)}, u32[]{:S(2)}, u32[]{:S(2)}) collective-permute-start(bf16[384,128]{1,0:T(8,128)(2,1)S(1)} %shard_map.69.after_ref.refs_1_.refs_0_), channel_id=1, source_target_pairs={{0,6},{2,4},{4,2},{6,0},{1,7},{3,5},{5,3},{7,1},{8,14},{10,12},{12... | collective-permute-start | bytes 294920 | tf_op jit(solution)/shard_map/ppermute | solution.py:348
  35.6 1.9 %collective-permute-start.13 = (bf16[384,128]{1,0:T(8,128)(2,1)S(1)}, bf16[384,128]{1,0:T(8,128)(2,1)S(1)}, u32[]{:S(2)}, u32[]{:S(2)}) collective-permute-start(bf16[384,128]{1,0:T(8,128)(2,1)S(1)} %collective-permute-done.9.refs_2_), channel_id=1, source_target_pairs={{0,24},{8,8},{16,16},{24,0},{1,25},{9,9},{17,17},{25,1},{2,26},{10... | collective-permute-start | bytes 294920 | tf_op jit(solution)/shard_map/ppermute | solution.py:353
  37.5 2.7 %collective-permute-start.11 = (bf16[384,128]{1,0:T(8,128)(2,1)S(1)}, bf16[384,128]{1,0:T(8,128)(2,1)S(1)}, u32[]{:S(2)}, u32[]{:S(2)}) collective-permute-start(bf16[384,128]{1,0:T(8,128)(2,1)S(1)} %collective-permute-done.9.refs_2_), channel_id=1, source_target_pairs={{0,16},{8,8},{16,0},{24,24},{1,17},{9,9},{17,1},{25,25},{2,18},{10... | collective-permute-start | bytes 294920 | tf_op jit(solution)/shard_map/ppermute | solution.py:353
  40.2 2.8 %collective-permute-done.13.refs_7_ = bf16[384,128]{1,0:T(8,128)(2,1)S(1)} collective-permute-done((bf16[384,128]{1,0:T(8,128)(2,1)S(1)}, bf16[384,128]{1,0:T(8,128)(2,1)S(1)}, u32[]{:S(2)}, u32[]{:S(2)}) %collective-permute-start.13) | collective-permute-done | bytes 98336 | tf_op jit(solution)/shard_map/ppermute | solution.py:353
  43.0 1.1 %collective-permute-done.11.refs_5_ = bf16[384,128]{1,0:T(8,128)(2,1)S(1)} collective-permute-done((bf16[384,128]{1,0:T(8,128)(2,1)S(1)}, bf16[384,128]{1,0:T(8,128)(2,1)S(1)}, u32[]{:S(2)}, u32[]{:S(2)}) %collective-permute-start.11) | collective-permute-done | bytes 98336 | tf_op jit(solution)/shard_map/ppermute | solution.py:353
  44.1 0.1 shard_map.72.state_ref
  44.2 1.9 %collective-permute-start.7 = (bf16[384,128]{1,0:T(8,128)(2,1)S(1)}, bf16[384,128]{1,0:T(8,128)(2,1)S(1)}, u32[]{:S(2)}, u32[]{:S(2)}) collective-permute-start(bf16[384,128]{1,0:T(8,128)(2,1)S(1)} %collective-permute-done.5.refs_3_), channel_id=1, source_target_pairs={{0,24},{8,8},{16,16},{24,0},{1,25},{9,9},{17,17},{25,1},{2,26},{10... | collective-permute-start | bytes 294920 | tf_op jit(solution)/shard_map/ppermute | solution.py:353
  46.2 1.9 %collective-permute-start.6 = (bf16[384,128]{1,0:T(8,128)(2,1)S(1)}, bf16[384,128]{1,0:T(8,128)(2,1)S(1)}, u32[]{:S(2)}, u32[]{:S(2)}) collective-permute-start(bf16[384,128]{1,0:T(8,128)(2,1)S(1)} %collective-permute-done.5.refs_3_), channel_id=1, source_target_pairs={{0,16},{8,8},{16,0},{24,24},{1,17},{9,9},{17,1},{25,25},{2,18},{10... | collective-permute-start | bytes 294920 | tf_op jit(solution)/shard_map/ppermute | solution.py:353
  48.1 0.4 shard_map.73.base_ref
  48.5 0.4 shard_map.74.base_ref
  48.8 3.5 %collective-permute-done.7.refs_1_ = bf16[384,128]{1,0:T(8,128)(2,1)S(1)} collective-permute-done((bf16[384,128]{1,0:T(8,128)(2,1)S(1)}, bf16[384,128]{1,0:T(8,128)(2,1)S(1)}, u32[]{:S(2)}, u32[]{:S(2)}) %collective-permute-start.7) | collective-permute-done | bytes 98336 | tf_op jit(solution)/shard_map/ppermute | solution.py:353
  52.3 2.0 %collective-permute-done.6.refs_0_ = bf16[384,128]{1,0:T(8,128)(2,1)S(1)} collective-permute-done((bf16[384,128]{1,0:T(8,128)(2,1)S(1)}, bf16[384,128]{1,0:T(8,128)(2,1)S(1)}, u32[]{:S(2)}, u32[]{:S(2)}) %collective-permute-start.6) | collective-permute-done | bytes 98336 | tf_op jit(solution)/shard_map/ppermute | solution.py:353
  54.4 0.1 collective-permute-start.15
  54.5 0.2 shard_map.76.done_ref
  54.7 1.0 %collective-permute-done.15.refs_0_ = bf16[384,128]{1,0:T(8,128)(2,1)S(1)} collective-permute-done((bf16[384,128]{1,0:T(8,128)(2,1)S(1)}, bf16[384,128]{1,0:T(8,128)(2,1)S(1)}, u32[]{:S(2)}, u32[]{:S(2)}) %collective-permute-start.15) | collective-permute-done | bytes 98336 | tf_op jit(solution)/shard_map/ppermute | solution.py:348
  55.7 1.0 %shard_map.77 = bf16[128,3072]{1,0:T(8,128)(2,1)} custom-call(bf16[128,1536]{1,0:T(8,128)(2,1)S(1)} %shard_map.76.done_ref, f32[128,1536]{1,0:T(8,128)S(1)} %shard_map.74.base_ref, bf16[128,1536]{1,0:T(8,128)(2,1)S(1)} %get-tuple-element.34.y_ref, bf16[384,128]{1,0:T(8,128)(2,1)S(1)} %collective-permute-done.15.refs_0_), custom_call_target="tpu_custom_call" | custom-call | flops 25165824 | bytes 1966080 | tf_op jit(solution)/shard_map/pallas_call | solution.py:334
  (22 shorter events, 0.4 us)
Async XLA Ops:
  1.7 1.8 %collective-permute-start = (bf16[1536,128]{1,0:T(8,128)(2,1)S(1)}, bf16[1536,128]{1,0:T(8,128)(2,1)S(1)}, u32[]{:S(2)}, u32[]{:S(2)}) collective-permute-start(bf16[1536,128]{1,0:T(8,128)(2,1)S(1)} %get-tuple-element.24), channel_id=1, source_target_pairs={{0,1},{1,0},{2,3},{3,2},{4,5},{5,4},{6,7},{7,6},{8,9},{9,8},{10,11... | collective-permute-start | bytes 1179656 | tf_op jit(solution)/shard_map/ppermute | solution.py:348
  2.7 6.6 %copy-start = (bf16[128,3072]{1,0:T(8,128)(2,1)S(1)}, bf16[128,3072]{1,0:T(8,128)(2,1)}, u32[]{:S(2)}) copy-start(bf16[128,3072]{1,0:T(8,128)(2,1)} %query_ref.3) | copy-start | bytes 2359300
  2.7 6.6 %copy-start.1 = (f32[3,24,128]{2,1,0:T(8,128)S(1)}, f32[3,24,128]{2,1,0:T(8,128)}, u32[]{:S(2)}) copy-start(f32[3,24,128]{2,1,0:T(8,128)} %weight_ref.3) | copy-start | bytes 110596
  3.6 8.7 %collective-permute-start.1 = (bf16[384,128]{1,0:T(8,128)(2,1)S(1)}, bf16[384,128]{1,0:T(8,128)(2,1)S(1)}, u32[]{:S(2)}, u32[]{:S(2)}) collective-permute-start(bf16[384,128]{1,0:T(8,128)(2,1)S(1)} %get-tuple-element.27), channel_id=1, source_target_pairs={{0,6},{2,4},{4,2},{6,0},{1,7},{3,5},{5,3},{7,1},{8,14},{10,12},{12... | collective-permute-start | bytes 294920 | tf_op jit(solution)/shard_map/ppermute | solution.py:348
  8.7 8.6 %collective-permute-start.2 = (bf16[384,128]{1,0:T(8,128)(2,1)S(1)}, bf16[384,128]{1,0:T(8,128)(2,1)S(1)}, u32[]{:S(2)}, u32[]{:S(2)}) collective-permute-start(bf16[384,128]{1,0:T(8,128)(2,1)S(1)} %get-tuple-element.28), channel_id=1, source_target_pairs={{0,4},{2,6},{4,0},{6,2},{1,5},{3,7},{5,1},{7,3},{8,12},{10,14},{12... | collective-permute-start | bytes 294920 | tf_op jit(solution)/shard_map/ppermute | solution.py:348
  8.7 0.7 %copy-start.2 = (s32[1,4]{1,0:T(1,128)S(1)}, s32[1,4]{1,0:T(1,128)}, u32[]{:S(2)}) copy-start(s32[1,4]{1,0:T(1,128)} %length_ref.3) | copy-start | bytes 52
  8.7 0.7 %copy-start.3 = (s32[1,4]{1,0:T(1,128)S(1)}, s32[1,4]{1,0:T(1,128)}, u32[]{:S(2)}) copy-start(s32[1,4]{1,0:T(1,128)} %back_ref.3) | copy-start | bytes 52
  8.7 8.6 %collective-permute-start.3 = (bf16[384,128]{1,0:T(8,128)(2,1)S(1)}, bf16[384,128]{1,0:T(8,128)(2,1)S(1)}, u32[]{:S(2)}, u32[]{:S(2)}) collective-permute-start(bf16[384,128]{1,0:T(8,128)(2,1)S(1)} %get-tuple-element.29), channel_id=1, source_target_pairs={{0,2},{2,0},{4,6},{6,4},{1,3},{3,1},{5,7},{7,5},{8,10},{10,8},{12,... | collective-permute-start | bytes 294920 | tf_op jit(solution)/shard_map/ppermute | solution.py:348
  17.3 4.7 %collective-permute-start.4 = (bf16[384,128]{1,0:T(8,128)(2,1)S(1)}, bf16[384,128]{1,0:T(8,128)(2,1)S(1)}, u32[]{:S(2)}, u32[]{:S(2)}) collective-permute-start(bf16[384,128]{1,0:T(8,128)(2,1)S(1)} %shard_map.68.own_ref), channel_id=1, source_target_pairs={{0,8},{8,0},{16,24},{24,16},{1,9},{9,1},{17,25},{25,17},{2,10},{10... | collective-permute-start | bytes 294920 | tf_op jit(solution)/shard_map/ppermute | solution.py:348
  22.1 4.8 %collective-permute-start.8 = (bf16[384,128]{1,0:T(8,128)(2,1)S(1)}, bf16[384,128]{1,0:T(8,128)(2,1)S(1)}, u32[]{:S(2)}, u32[]{:S(2)}) collective-permute-start(bf16[384,128]{1,0:T(8,128)(2,1)S(1)} %shard_map.69.after_ref.refs_1_.refs_0_), channel_id=1, source_target_pairs={{0,2},{2,0},{4,6},{6,4},{1,3},{3,1},{5,7},{7,5},{8,10},{10,8},{12,... | collective-permute-start | bytes 294920 | tf_op jit(solution)/shard_map/ppermute | solution.py:348
  22.7 12.9 %collective-permute-start.9 = (bf16[384,128]{1,0:T(8,128)(2,1)S(1)}, bf16[384,128]{1,0:T(8,128)(2,1)S(1)}, u32[]{:S(2)}, u32[]{:S(2)}) collective-permute-start(bf16[384,128]{1,0:T(8,128)(2,1)S(1)} %shard_map.69.after_ref.refs_1_.refs_0_), channel_id=1, source_target_pairs={{0,4},{2,6},{4,0},{6,2},{1,5},{3,7},{5,1},{7,3},{8,12},{10,14},{12... | collective-permute-start | bytes 294920 | tf_op jit(solution)/shard_map/ppermute | solution.py:348
  26.9 17.1 %collective-permute-start.12 = (bf16[768,128]{1,0:T(8,128)(2,1)S(1)}, bf16[768,128]{1,0:T(8,128)(2,1)S(1)}, u32[]{:S(2)}, u32[]{:S(2)}) collective-permute-start(bf16[768,128]{1,0:T(8,128)(2,1)S(1)} %shard_map.71), channel_id=1, source_target_pairs={{0,24},{8,8},{16,16},{24,0},{1,25},{9,9},{17,17},{25,1},{2,26},{10... | collective-permute-start | bytes 589832 | tf_op jit(solution)/shard_map/ppermute | solution.py:353
  31.3 12.8 %collective-permute-start.10 = (bf16[768,128]{1,0:T(8,128)(2,1)S(1)}, bf16[768,128]{1,0:T(8,128)(2,1)S(1)}, u32[]{:S(2)}, u32[]{:S(2)}) collective-permute-start(bf16[768,128]{1,0:T(8,128)(2,1)S(1)} %shard_map.71), channel_id=1, source_target_pairs={{0,16},{8,8},{16,0},{24,24},{1,17},{9,9},{17,1},{25,25},{2,18},{10... | collective-permute-start | bytes 589832 | tf_op jit(solution)/shard_map/ppermute | solution.py:353
  33.2 7.0 %collective-permute-start.5 = (bf16[384,128]{1,0:T(8,128)(2,1)S(1)}, bf16[384,128]{1,0:T(8,128)(2,1)S(1)}, u32[]{:S(2)}, u32[]{:S(2)}) collective-permute-start(bf16[384,128]{1,0:T(8,128)(2,1)S(1)} %shard_map.69.after_ref.refs_1_.refs_0_), channel_id=1, source_target_pairs={{0,6},{2,4},{4,2},{6,0},{1,7},{3,5},{5,3},{7,1},{8,14},{10,12},{12... | collective-permute-start | bytes 294920 | tf_op jit(solution)/shard_map/ppermute | solution.py:348
  35.6 7.4 %collective-permute-start.13 = (bf16[384,128]{1,0:T(8,128)(2,1)S(1)}, bf16[384,128]{1,0:T(8,128)(2,1)S(1)}, u32[]{:S(2)}, u32[]{:S(2)}) collective-permute-start(bf16[384,128]{1,0:T(8,128)(2,1)S(1)} %collective-permute-done.9.refs_2_), channel_id=1, source_target_pairs={{0,24},{8,8},{16,16},{24,0},{1,25},{9,9},{17,17},{25,1},{2,26},{10... | collective-permute-start | bytes 294920 | tf_op jit(solution)/shard_map/ppermute | solution.py:353
  37.5 6.5 %collective-permute-start.11 = (bf16[384,128]{1,0:T(8,128)(2,1)S(1)}, bf16[384,128]{1,0:T(8,128)(2,1)S(1)}, u32[]{:S(2)}, u32[]{:S(2)}) collective-permute-start(bf16[384,128]{1,0:T(8,128)(2,1)S(1)} %collective-permute-done.9.refs_2_), channel_id=1, source_target_pairs={{0,16},{8,8},{16,0},{24,24},{1,17},{9,9},{17,1},{25,25},{2,18},{10... | collective-permute-start | bytes 294920 | tf_op jit(solution)/shard_map/ppermute | solution.py:353
  44.2 4.3 %collective-permute-start.14 = (bf16[2688,128]{1,0:T(8,128)(2,1)S(1)}, bf16[2688,128]{1,0:T(8,128)(2,1)S(1)}, u32[]{:S(2)}, u32[]{:S(2)}) collective-permute-start(bf16[2688,128]{1,0:T(8,128)(2,1)S(1)} %shard_map.72.state_ref), channel_id=1, source_target_pairs={{0,1},{1,0},{2,3},{3,2},{4,5},{5,4},{6,7},{7,6},{8,9},{9,8},{10,11... | collective-permute-start | bytes 2064392 | tf_op jit(solution)/shard_map/ppermute | solution.py:348
  44.2 8.1 %collective-permute-start.7 = (bf16[384,128]{1,0:T(8,128)(2,1)S(1)}, bf16[384,128]{1,0:T(8,128)(2,1)S(1)}, u32[]{:S(2)}, u32[]{:S(2)}) collective-permute-start(bf16[384,128]{1,0:T(8,128)(2,1)S(1)} %collective-permute-done.5.refs_3_), channel_id=1, source_target_pairs={{0,24},{8,8},{16,16},{24,0},{1,25},{9,9},{17,17},{25,1},{2,26},{10... | collective-permute-start | bytes 294920 | tf_op jit(solution)/shard_map/ppermute | solution.py:353
  46.2 8.2 %collective-permute-start.6 = (bf16[384,128]{1,0:T(8,128)(2,1)S(1)}, bf16[384,128]{1,0:T(8,128)(2,1)S(1)}, u32[]{:S(2)}, u32[]{:S(2)}) collective-permute-start(bf16[384,128]{1,0:T(8,128)(2,1)S(1)} %collective-permute-done.5.refs_3_), channel_id=1, source_target_pairs={{0,16},{8,8},{16,0},{24,24},{1,17},{9,9},{17,1},{25,25},{2,18},{10... | collective-permute-start | bytes 294920 | tf_op jit(solution)/shard_map/ppermute | solution.py:353
  54.4 1.4 %collective-permute-start.15 = (bf16[384,128]{1,0:T(8,128)(2,1)S(1)}, bf16[384,128]{1,0:T(8,128)(2,1)S(1)}, u32[]{:S(2)}, u32[]{:S(2)}) collective-permute-start(bf16[384,128]{1,0:T(8,128)(2,1)S(1)} %shard_map.75.refs_0_), channel_id=1, source_target_pairs={{0,1},{1,0},{2,3},{3,2},{4,5},{5,4},{6,7},{7,6},{8,9},{9,8},{10,11... | collective-permute-start | bytes 294920 | tf_op jit(solution)/shard_map/ppermute | solution.py:348

commit v7 on v6

--- a/solution.py
+++ b/solution.py
@@ -139,49 +139,41 @@
     )(after, *in_vmem(own, *parts))
 
 
-def slot_kernel(own_ref, near_ref, out_ref):
+def slot_kernel(near_ref, across_ref, diagonal_ref, out_ref):
+    both = across_ref[...].astype(F32) + diagonal_ref[...].astype(F32)
     near = near_ref[...].astype(F32)
-    both = own_ref[...].astype(F32) + near
-    out_ref[...] = jnp.where(lax.axis_index("frame") == 0, both, near).astype(BF16)
-
-
-def choose_slot(own, near):
+    out_ref[...] = jnp.where(lax.axis_index("frame") == 2, both, near).astype(BF16)
+
+
+def choose_slot(near, across, diagonal):
     return pl.pallas_call(
         slot_kernel,
         out_shape=pltpu.VMEM(near.shape, BF16),
-        in_specs=[WHOLE] * 2,
+        in_specs=[WHOLE] * 3,
         out_specs=WHOLE,
         compiler_params=PARAMS,
         cost_estimate=SMALL,
-    )(*in_vmem(own, near))
-
-
-def pack_kernel(after, plain, pairs, *refs):
+    )(*in_vmem(near, across, diagonal))
+
+
+def pack_kernel(after, order, *refs):
     out_ref, refs = refs[-1], refs[after:-1]
-    row = 0
-    for ref in refs[:plain]:
-        out_ref[row : row + ref.shape[0], :] = ref[...]
-        row += ref.shape[0]
-    for n in range(pairs):
-        first, second = refs[plain + n], refs[plain + pairs + n]
-        chosen = jnp.where(
-            lax.axis_index("frame") == 2, first[...].astype(F32), second[...].astype(F32)
-        )
-        out_ref[row : row + first.shape[0], :] = chosen.astype(BF16)
-        row += first.shape[0]
-
-
-def pack(plain, pairs, after):
-    firsts, seconds = [p[0] for p in pairs], [p[1] for p in pairs]
-    rows = sum(array.shape[0] for array in plain + firsts)
-    return pl.pallas_call(
-        functools.partial(pack_kernel, len(after), len(plain), len(pairs)),
+    rows = refs[0].shape[0]
+    for place, ref in zip(order, refs):
+        out_ref[place * rows : (place + 1) * rows, :] = ref[...]
+
+
+def pack(pieces, order, after):
+    rows = sum(array.shape[0] for array in pieces)
+    pieces = [pieces[place] for place in order]
+    return pl.pallas_call(
+        functools.partial(pack_kernel, len(after), order),
         out_shape=pltpu.VMEM((rows, HEAD_DIM), BF16),
-        in_specs=[ANYWHERE] * len(after) + [WHOLE] * (len(plain) + 2 * len(pairs)),
+        in_specs=[ANYWHERE] * len(after) + [WHOLE] * len(pieces),
         out_specs=WHOLE,
         compiler_params=PARAMS,
         cost_estimate=SMALL,
-    )(*after, *in_vmem(*plain, *firsts, *seconds))
+    )(*after, *in_vmem(*pieces))
 
 
 def local_kernel(
@@ -348,11 +340,6 @@
     return lax.ppermute(array, axis, [(n, n ^ mask) for n in range(size)])
 
 
-def from_first(array, target, frames):
-    places = {0: target, target: 0}
-    return lax.ppermute(array, "frame", [(f, places.get(f, f)) for f in range(frames)])
-
-
 def body(sizes, queries, keys, values, level_weight, frame_len, window_back):
     frames, outer, chips = sizes
     low, high = (
@@ -360,11 +347,13 @@
     )
 
     def coefs(f):
-        return [[(0, jnp.where(f % 2 == 1, low, 0.0))], [(1, jnp.where(f >= 2, high, 0.0))]]
+        x_low = jnp.where(f % 2 == 1, low, 0.0)
+        x_high = jnp.where(f == 2, high, 0.0)
+        return [[(0, x_low), (1, x_high)], [(1, jnp.where(f == 3, high, 0.0))]]
 
     local = functools.partial(local_part, coefs, 2)
     rest = (frame_len, window_back, queries)
-    early = chips - 1 if chips > 1 else 1
+    early = max(chips - 1, 1)
 
     outgoing, keys, values = outgoing_state(keys, values)
     incoming = swap(outgoing, "core", 1, 2)
@@ -375,19 +364,21 @@
     state = sum_pieces(local_0, own, got, F32 if outer > 1 else BF16)
     if outer > 1:
         state = lax.psum(state, "outer").astype(BF16)
-    slot = choose_slot(state, swap(state, "frame", 1, frames))
+    slot = choose_slot(*(swap(state, "frame", mask, frames) for mask in (1, 2, 3)))
 
     x = [slot] + [swap(slot, "chip", d, chips) for d in range(1, chips)]
+    y = [swap(slot, "frame", 1, frames)]
     local_1, x_1, y_1 = local(1, *rest, keys, values, level_weight, slot)
-    fan = [pack(x[:2], [], [local_1])] + x[2:]
-    pairs = [(from_first(piece, 2, frames), from_first(piece, 3, frames)) for piece in fan]
-    late = pairs[1:][-1:]
-    own_states = pack(x, pairs[: len(pairs) - len(late)], [])
+    for piece in x[1:]:
+        piece, _ = lax.optimization_barrier((piece, local_1))
+        y.append(swap(piece, "frame", 1, frames))
+    late_own = y[1:][early - 1 :]
+    places = [0, *range(chips + early - 1, chips - 1, -1), *range(1, chips)]
+    own_states = pack(x + y[:early], places, [local_1])
     other_states = swap(own_states, "core", 1, 2)
     base_0 = read_middle(chips, early, local_0, x_0, y_0, own_states)
     base_1 = read_middle(chips, early, local_1, x_1, y_1, other_states)
-    late, base_0, base_1 = lax.optimization_barrier((late, base_0, base_1))
-    late_own = [pack([], late, [])] if late else []
+    late_own, base_0, base_1 = lax.optimization_barrier((late_own, base_0, base_1))
     late_other = [swap(piece, "core", 1, 2) for piece in late_own]
     done = read_late(chips, early, base_0, y_0, late_own)
     return read_last(chips, early, done, base_1, y_1, late_other)

time: 57 us -> 46.4 us (0.81)
  starting transfers between devices: 28.1 us -> 18.1 us
    ppermute x6 -> x0, starting transfers between devices: 14.7 us -> none  [from_first(): lax.ppermute(array, 'frame', [(f, places.get(f, f)) for f in range(frames)])]
    ppermute x6 -> x0, waiting for transfers between devices: 9.35 us -> none  [from_first(): lax.ppermute(array, 'frame', [(f, places.get(f, f)) for f in range(frames)])]
    ppermute x10 -> x16, waiting for transfers between devices: 11.1 us -> 20.2 us  [swap(): return lax.ppermute(array, axis, [(n, n ^ mask) for n in range(size)])]
    ppermute x10 -> x16, starting transfers between devices: 13.5 us -> 18.1 us  [swap(): return lax.ppermute(array, axis, [(n, n ^ mask) for n in range(size)])]
  transfers between devices with their start and end apart: 16 -> 16, of which waited for: 9 -> 13; matrix products, arithmetic and copies ran while one was open for 0% -> 0% of each run, Pallas kernels for 9% -> 11%
where the time goes in v7:
time: 46.4 us; the launch traced here: 46.2 us
  waiting for transfers between devices  20.2 us (44%)
  starting transfers between devices  18.1 us (39%)
  Pallas kernels  7.8 us (17%)
    ppermute x16, waiting for transfers between devices, swap(): return lax.ppermute(array, axis, [(n, n ^ mask) for n in range(size)])  20.2 us
    ppermute x16, starting transfers between devices, swap(): return lax.ppermute(array, axis, [(n, n ^ mask) for n in range(size)])  18.1 us
    pallas_call x2, Pallas kernels, local_part(): pl.pallas_call(functools.partial(local_kernel, coefs, turn), out_shape=[p...  3.44 us
    pallas_call x1, Pallas kernels, outgoing_state(): pl.pallas_call(first_kernel, out_shape=[pltpu.VMEM((half * dim, dim), BF1...  1.69 us
    pallas_call x1, Pallas kernels, read_last(): pl.pallas_call(functools.partial(last_kernel, chips, early), out_shape=ja...  1 us
  transfers between devices with their start and end apart: 16, of which 13 were waited for; matrix products, arithmetic and copies ran while one was open for 0% of the time, Pallas kernels for 11%

profile of v7, /device:TPU:0, one launch (start us, length us, event | category | flops | bytes accessed | tf_op | source)
XLA Modules:
  0.0 46.2 jit_solution(11221348311340039352)
XLA Ops:
  0.0 1.7 %shard_map.64 = (bf16[1536,128]{1,0:T(8,128)(2,1)S(1)}, bf16[128,3072]{1,0:T(8,128)(2,1)S(1)}, bf16[128,3072]{1,0:T(8,128)(2,1)S(1)}) custom-call(bf16[128,3072]{1,0:T(8,128)(2,1)} %key_ref.1, bf16[128,3072]{1,0:T(8,128)(2,1)} %value_ref.1), custom_call_target="tpu_custom_call" | custom-call | flops 50331648 | bytes 1572864 | tf_op jit(solution)/shard_map/pallas_call | solution.py:72
  1.7 0.5 %collective-permute-start = (bf16[1536,128]{1,0:T(8,128)(2,1)S(1)}, bf16[1536,128]{1,0:T(8,128)(2,1)S(1)}, u32[]{:S(2)}, u32[]{:S(2)}) collective-permute-start(bf16[1536,128]{1,0:T(8,128)(2,1)S(1)} %get-tuple-element.26), channel_id=1, source_target_pairs={{0,1},{1,0},{2,3},{3,2},{4,5},{5,4},{6,7},{7,6},{8,9},{9,8},{10,11... | collective-permute-start | bytes 1179656 | tf_op jit(solution)/shard_map/ppermute | solution.py:340
  2.2 0.5 %shard_map.65.mine_ref = f32[1536,128]{1,0:T(8,128)S(1)} custom-call(bf16[128,3072]{1,0:T(8,128)(2,1)S(1)} %get-tuple-element.24.key_ref, bf16[128,3072]{1,0:T(8,128)(2,1)S(1)} %get-tuple-element.25.value_ref), custom_call_target="tpu_custom_call" | custom-call | flops 50331648 | bytes 1572864 | tf_op jit(solution)/shard_map/pallas_call | solution.py:92
  2.7 0.8 %collective-permute-done.other_ref = bf16[1536,128]{1,0:T(8,128)(2,1)S(1)} collective-permute-done((bf16[1536,128]{1,0:T(8,128)(2,1)S(1)}, bf16[1536,128]{1,0:T(8,128)(2,1)S(1)}, u32[]{:S(2)}, u32[]{:S(2)}) %collective-permute-start) | collective-permute-done | bytes 393248 | tf_op jit(solution)/shard_map/ppermute | solution.py:340
  3.6 5.1 %collective-permute-start.1 = (bf16[384,128]{1,0:T(8,128)(2,1)S(1)}, bf16[384,128]{1,0:T(8,128)(2,1)S(1)}, u32[]{:S(2)}, u32[]{:S(2)}) collective-permute-start(bf16[384,128]{1,0:T(8,128)(2,1)S(1)} %get-tuple-element.29), channel_id=1, source_target_pairs={{0,6},{2,4},{4,2},{6,0},{1,7},{3,5},{5,3},{7,1},{8,14},{10,12},{12... | collective-permute-start | bytes 294920 | tf_op jit(solution)/shard_map/ppermute | solution.py:340
  8.7 0.6 %collective-permute-start.3 = (bf16[384,128]{1,0:T(8,128)(2,1)S(1)}, bf16[384,128]{1,0:T(8,128)(2,1)S(1)}, u32[]{:S(2)}, u32[]{:S(2)}) collective-permute-start(bf16[384,128]{1,0:T(8,128)(2,1)S(1)} %get-tuple-element.31), channel_id=1, source_target_pairs={{0,2},{2,0},{4,6},{6,4},{1,3},{3,1},{5,7},{7,5},{8,10},{10,8},{12,... | collective-permute-start | bytes 294920 | tf_op jit(solution)/shard_map/ppermute | solution.py:340
  9.4 1.7 %shard_map.67 = (f32[128,1536]{1,0:T(8,128)S(1)}, bf16[128,1536]{1,0:T(8,128)(2,1)S(1)}, bf16[128,1536]{1,0:T(8,128)(2,1)S(1)}) custom-call(s32[1,4]{1,0:T(1,128)S(1)} %copy-done.2, s32[1,4]{1,0:T(1,128)S(1)} %copy-done.3, bf16[128,3072]{1,0:T(8,128)(2,1)S(1)} %copy-done, bf16[128,3072]{1,0:T(8,128)(2,1)S(1)} %get-tuple-element.24.key_ref, ...), custom_call_target="tpu_custom_call" | custom-call | flops 100663296 | bytes 2752512 | tf_op jit(solution)/shard_map/pallas_call | solution.py:239
  11.1 1.3 %collective-permute-done.1.refs_0_ = bf16[384,128]{1,0:T(8,128)(2,1)S(1)} collective-permute-done((bf16[384,128]{1,0:T(8,128)(2,1)S(1)}, bf16[384,128]{1,0:T(8,128)(2,1)S(1)}, u32[]{:S(2)}, u32[]{:S(2)}) %collective-permute-start.1) | collective-permute-done | bytes 98336 | tf_op jit(solution)/shard_map/ppermute | solution.py:340
  12.4 4.9 %collective-permute-done.2.refs_1_ = bf16[384,128]{1,0:T(8,128)(2,1)S(1)} collective-permute-done((bf16[384,128]{1,0:T(8,128)(2,1)S(1)}, bf16[384,128]{1,0:T(8,128)(2,1)S(1)}, u32[]{:S(2)}, u32[]{:S(2)}) %collective-permute-start.2) | collective-permute-done | bytes 98336 | tf_op jit(solution)/shard_map/ppermute | solution.py:340
  17.3 2.5 %collective-permute-start.6 = (bf16[384,128]{1,0:T(8,128)(2,1)S(1)}, bf16[384,128]{1,0:T(8,128)(2,1)S(1)}, u32[]{:S(2)}, u32[]{:S(2)}) collective-permute-start(bf16[384,128]{1,0:T(8,128)(2,1)S(1)} %shard_map.68), channel_id=1, source_target_pairs={{0,24},{8,16},{16,8},{24,0},{1,25},{9,17},{17,9},{25,1},{2,26},{10... | collective-permute-start | bytes 294920 | tf_op jit(solution)/shard_map/ppermute | solution.py:340
  19.8 0.5 %collective-permute-start.5 = (bf16[384,128]{1,0:T(8,128)(2,1)S(1)}, bf16[384,128]{1,0:T(8,128)(2,1)S(1)}, u32[]{:S(2)}, u32[]{:S(2)}) collective-permute-start(bf16[384,128]{1,0:T(8,128)(2,1)S(1)} %shard_map.68), channel_id=1, source_target_pairs={{0,16},{8,24},{16,0},{24,8},{1,17},{9,25},{17,1},{25,9},{2,18},{10... | collective-permute-start | bytes 294920 | tf_op jit(solution)/shard_map/ppermute | solution.py:340
  20.3 0.5 %collective-permute-start.4 = (bf16[384,128]{1,0:T(8,128)(2,1)S(1)}, bf16[384,128]{1,0:T(8,128)(2,1)S(1)}, u32[]{:S(2)}, u32[]{:S(2)}) collective-permute-start(bf16[384,128]{1,0:T(8,128)(2,1)S(1)} %shard_map.68), channel_id=1, source_target_pairs={{0,8},{8,0},{16,24},{24,16},{1,9},{9,1},{17,25},{25,17},{2,10},{10... | collective-permute-start | bytes 294920 | tf_op jit(solution)/shard_map/ppermute | solution.py:340
  20.9 2.3 %collective-permute-done.6.diagonal_ref = bf16[384,128]{1,0:T(8,128)(2,1)S(1)} collective-permute-done((bf16[384,128]{1,0:T(8,128)(2,1)S(1)}, bf16[384,128]{1,0:T(8,128)(2,1)S(1)}, u32[]{:S(2)}, u32[]{:S(2)}) %collective-permute-start.6) | collective-permute-done | bytes 98336 | tf_op jit(solution)/shard_map/ppermute | solution.py:340
  23.2 1.4 %collective-permute-done.5.across_ref = bf16[384,128]{1,0:T(8,128)(2,1)S(1)} collective-permute-done((bf16[384,128]{1,0:T(8,128)(2,1)S(1)}, bf16[384,128]{1,0:T(8,128)(2,1)S(1)}, u32[]{:S(2)}, u32[]{:S(2)}) %collective-permute-start.5) | collective-permute-done | bytes 98336 | tf_op jit(solution)/shard_map/ppermute | solution.py:340
  24.6 0.3 collective-permute-done.4.near_ref
  25.0 0.6 %collective-permute-start.11 = (bf16[384,128]{1,0:T(8,128)(2,1)S(1)}, bf16[384,128]{1,0:T(8,128)(2,1)S(1)}, u32[]{:S(2)}, u32[]{:S(2)}) collective-permute-start(bf16[384,128]{1,0:T(8,128)(2,1)S(1)} %shard_map.69.after_ref.refs_1_), channel_id=1, source_target_pairs={{0,2},{2,0},{4,6},{6,4},{1,3},{3,1},{5,7},{7,5},{8,10},{10,8},{12,... | collective-permute-start | bytes 294920 | tf_op jit(solution)/shard_map/ppermute | solution.py:340
  25.6 2.5 %collective-permute-start.9 = (bf16[384,128]{1,0:T(8,128)(2,1)S(1)}, bf16[384,128]{1,0:T(8,128)(2,1)S(1)}, u32[]{:S(2)}, u32[]{:S(2)}) collective-permute-start(bf16[384,128]{1,0:T(8,128)(2,1)S(1)} %shard_map.69.after_ref.refs_1_), channel_id=1, source_target_pairs={{0,4},{2,6},{4,0},{6,2},{1,5},{3,7},{5,1},{7,3},{8,12},{10,14},{12... | collective-permute-start | bytes 294920 | tf_op jit(solution)/shard_map/ppermute | solution.py:340
  28.1 1.0 %collective-permute-start.13 = (bf16[384,128]{1,0:T(8,128)(2,1)S(1)}, bf16[384,128]{1,0:T(8,128)(2,1)S(1)}, u32[]{:S(2)}, u32[]{:S(2)}) collective-permute-start(bf16[384,128]{1,0:T(8,128)(2,1)S(1)} %shard_map.69.after_ref.refs_1_), channel_id=1, source_target_pairs={{0,8},{8,0},{16,24},{24,16},{1,9},{9,1},{17,25},{25,17},{2,10},{10... | collective-permute-start | bytes 294920 | tf_op jit(solution)/shard_map/ppermute | solution.py:340
  29.1 1.3 %collective-permute-start.7 = (bf16[384,128]{1,0:T(8,128)(2,1)S(1)}, bf16[384,128]{1,0:T(8,128)(2,1)S(1)}, u32[]{:S(2)}, u32[]{:S(2)}) collective-permute-start(bf16[384,128]{1,0:T(8,128)(2,1)S(1)} %shard_map.69.after_ref.refs_1_), channel_id=1, source_target_pairs={{0,6},{2,4},{4,2},{6,0},{1,7},{3,5},{5,3},{7,1},{8,14},{10,12},{12... | collective-permute-start | bytes 294920 | tf_op jit(solution)/shard_map/ppermute | solution.py:340
  30.5 1.7 %shard_map.70 = (f32[128,1536]{1,0:T(8,128)S(1)}, bf16[128,1536]{1,0:T(8,128)(2,1)S(1)}, bf16[128,1536]{1,0:T(8,128)(2,1)S(1)}) custom-call(s32[1,4]{1,0:T(1,128)S(1)} %copy-done.2, s32[1,4]{1,0:T(1,128)S(1)} %copy-done.3, bf16[128,3072]{1,0:T(8,128)(2,1)S(1)} %copy-done, bf16[128,3072]{1,0:T(8,128)(2,1)S(1)} %get-tuple-element.24.key_ref, ...), custom_call_target="tpu_custom_call" | custom-call | flops 100663296 | bytes 2752512 | tf_op jit(solution)/shard_map/pallas_call | solution.py:239
  32.2 1.1 %collective-permute-start.12 = (bf16[384,128]{1,0:T(8,128)(2,1)S(1)}, bf16[384,128]{1,0:T(8,128)(2,1)S(1)}, u32[]{:S(2)}, u32[]{:S(2)}) collective-permute-start(bf16[384,128]{1,0:T(8,128)(2,1)S(1)} %collective-permute-done.11.refs_5_), channel_id=1, source_target_pairs={{0,8},{8,0},{16,24},{24,16},{1,9},{9,1},{17,25},{25,17},{2,10},{10... | collective-permute-start | bytes 294920 | tf_op jit(solution)/shard_map/ppermute | solution.py:340
  33.3 0.7 %collective-permute-done.9.refs_6_ = bf16[384,128]{1,0:T(8,128)(2,1)S(1)} collective-permute-done((bf16[384,128]{1,0:T(8,128)(2,1)S(1)}, bf16[384,128]{1,0:T(8,128)(2,1)S(1)}, u32[]{:S(2)}, u32[]{:S(2)}) %collective-permute-start.9) | collective-permute-done | bytes 98336 | tf_op jit(solution)/shard_map/ppermute | solution.py:340
  33.9 0.8 %collective-permute-start.10 = (bf16[384,128]{1,0:T(8,128)(2,1)S(1)}, bf16[384,128]{1,0:T(8,128)(2,1)S(1)}, u32[]{:S(2)}, u32[]{:S(2)}) collective-permute-start(bf16[384,128]{1,0:T(8,128)(2,1)S(1)} %collective-permute-done.9.refs_6_), channel_id=1, source_target_pairs={{0,8},{8,0},{16,24},{24,16},{1,9},{9,1},{17,25},{25,17},{2,10},{10... | collective-permute-start | bytes 294920 | tf_op jit(solution)/shard_map/ppermute | solution.py:340
  34.8 0.9 %collective-permute-done.7.refs_7_ = bf16[384,128]{1,0:T(8,128)(2,1)S(1)} collective-permute-done((bf16[384,128]{1,0:T(8,128)(2,1)S(1)}, bf16[384,128]{1,0:T(8,128)(2,1)S(1)}, u32[]{:S(2)}, u32[]{:S(2)}) %collective-permute-start.7) | collective-permute-done | bytes 98336 | tf_op jit(solution)/shard_map/ppermute | solution.py:340
  35.7 1.2 %collective-permute-done.12.refs_3_ = bf16[384,128]{1,0:T(8,128)(2,1)S(1)} collective-permute-done((bf16[384,128]{1,0:T(8,128)(2,1)S(1)}, bf16[384,128]{1,0:T(8,128)(2,1)S(1)}, u32[]{:S(2)}, u32[]{:S(2)}) %collective-permute-start.12) | collective-permute-done | bytes 98336 | tf_op jit(solution)/shard_map/ppermute | solution.py:340
  36.9 1.7 %collective-permute-done.10.refs_2_ = bf16[384,128]{1,0:T(8,128)(2,1)S(1)} collective-permute-done((bf16[384,128]{1,0:T(8,128)(2,1)S(1)}, bf16[384,128]{1,0:T(8,128)(2,1)S(1)}, u32[]{:S(2)}, u32[]{:S(2)}) %collective-permute-start.10) | collective-permute-done | bytes 98336 | tf_op jit(solution)/shard_map/ppermute | solution.py:340
  38.7 0.9 %collective-permute-start.8 = (bf16[384,128]{1,0:T(8,128)(2,1)S(1)}, bf16[384,128]{1,0:T(8,128)(2,1)S(1)}, u32[]{:S(2)}, u32[]{:S(2)}) collective-permute-start(bf16[384,128]{1,0:T(8,128)(2,1)S(1)} %collective-permute-done.7.refs_7_), channel_id=1, source_target_pairs={{0,8},{8,0},{16,24},{24,16},{1,9},{9,1},{17,25},{25,17},{2,10},{10... | collective-permute-start | bytes 294920 | tf_op jit(solution)/shard_map/ppermute | solution.py:340
  39.9 0.9 %collective-permute-done.14.state_ref = bf16[2688,128]{1,0:T(8,128)(2,1)S(1)} collective-permute-done((bf16[2688,128]{1,0:T(8,128)(2,1)S(1)}, bf16[2688,128]{1,0:T(8,128)(2,1)S(1)}, u32[]{:S(2)}, u32[]{:S(2)}) %collective-permute-start.14) | collective-permute-done | bytes 688160 | tf_op jit(solution)/shard_map/ppermute | solution.py:340
  40.8 0.3 shard_map.73.base_ref
  41.2 2.7 %collective-permute-done.8.refs_0_ = bf16[384,128]{1,0:T(8,128)(2,1)S(1)} collective-permute-done((bf16[384,128]{1,0:T(8,128)(2,1)S(1)}, bf16[384,128]{1,0:T(8,128)(2,1)S(1)}, u32[]{:S(2)}, u32[]{:S(2)}) %collective-permute-start.8) | collective-permute-done | bytes 98336 | tf_op jit(solution)/shard_map/ppermute | solution.py:340
  44.2 1.1 %collective-permute-done.15.refs_0_ = bf16[384,128]{1,0:T(8,128)(2,1)S(1)} collective-permute-done((bf16[384,128]{1,0:T(8,128)(2,1)S(1)}, bf16[384,128]{1,0:T(8,128)(2,1)S(1)}, u32[]{:S(2)}, u32[]{:S(2)}) %collective-permute-start.15) | collective-permute-done | bytes 98336 | tf_op jit(solution)/shard_map/ppermute | solution.py:340
  45.2 1.0 %shard_map.75 = bf16[128,3072]{1,0:T(8,128)(2,1)} custom-call(bf16[128,1536]{1,0:T(8,128)(2,1)S(1)} %shard_map.74.done_ref, f32[128,1536]{1,0:T(8,128)S(1)} %shard_map.73.base_ref, bf16[128,1536]{1,0:T(8,128)(2,1)S(1)} %get-tuple-element.39.y_ref, bf16[384,128]{1,0:T(8,128)(2,1)S(1)} %collective-permute-done.15.refs_0_), custom_call_target="tpu_custom_call" | custom-call | flops 25165824 | bytes 1966080 | tf_op jit(solution)/shard_map/pallas_call | solution.py:326
  (20 shorter events, 0.9 us)
Async XLA Ops:
  1.7 1.8 %collective-permute-start = (bf16[1536,128]{1,0:T(8,128)(2,1)S(1)}, bf16[1536,128]{1,0:T(8,128)(2,1)S(1)}, u32[]{:S(2)}, u32[]{:S(2)}) collective-permute-start(bf16[1536,128]{1,0:T(8,128)(2,1)S(1)} %get-tuple-element.26), channel_id=1, source_target_pairs={{0,1},{1,0},{2,3},{3,2},{4,5},{5,4},{6,7},{7,6},{8,9},{9,8},{10,11... | collective-permute-start | bytes 1179656 | tf_op jit(solution)/shard_map/ppermute | solution.py:340
  2.7 6.6 %copy-start = (bf16[128,3072]{1,0:T(8,128)(2,1)S(1)}, bf16[128,3072]{1,0:T(8,128)(2,1)}, u32[]{:S(2)}) copy-start(bf16[128,3072]{1,0:T(8,128)(2,1)} %query_ref.3) | copy-start | bytes 2359300
  2.7 6.6 %copy-start.1 = (f32[3,24,128]{2,1,0:T(8,128)S(1)}, f32[3,24,128]{2,1,0:T(8,128)}, u32[]{:S(2)}) copy-start(f32[3,24,128]{2,1,0:T(8,128)} %weight_ref.3) | copy-start | bytes 110596
  3.6 8.7 %collective-permute-start.1 = (bf16[384,128]{1,0:T(8,128)(2,1)S(1)}, bf16[384,128]{1,0:T(8,128)(2,1)S(1)}, u32[]{:S(2)}, u32[]{:S(2)}) collective-permute-start(bf16[384,128]{1,0:T(8,128)(2,1)S(1)} %get-tuple-element.29), channel_id=1, source_target_pairs={{0,6},{2,4},{4,2},{6,0},{1,7},{3,5},{5,3},{7,1},{8,14},{10,12},{12... | collective-permute-start | bytes 294920 | tf_op jit(solution)/shard_map/ppermute | solution.py:340
  8.7 8.6 %collective-permute-start.2 = (bf16[384,128]{1,0:T(8,128)(2,1)S(1)}, bf16[384,128]{1,0:T(8,128)(2,1)S(1)}, u32[]{:S(2)}, u32[]{:S(2)}) collective-permute-start(bf16[384,128]{1,0:T(8,128)(2,1)S(1)} %get-tuple-element.30), channel_id=1, source_target_pairs={{0,4},{2,6},{4,0},{6,2},{1,5},{3,7},{5,1},{7,3},{8,12},{10,14},{12... | collective-permute-start | bytes 294920 | tf_op jit(solution)/shard_map/ppermute | solution.py:340
  8.7 0.7 %copy-start.2 = (s32[1,4]{1,0:T(1,128)S(1)}, s32[1,4]{1,0:T(1,128)}, u32[]{:S(2)}) copy-start(s32[1,4]{1,0:T(1,128)} %length_ref.3) | copy-start | bytes 52
  8.7 0.7 %copy-start.3 = (s32[1,4]{1,0:T(1,128)S(1)}, s32[1,4]{1,0:T(1,128)}, u32[]{:S(2)}) copy-start(s32[1,4]{1,0:T(1,128)} %back_ref.3) | copy-start | bytes 52
  8.7 8.6 %collective-permute-start.3 = (bf16[384,128]{1,0:T(8,128)(2,1)S(1)}, bf16[384,128]{1,0:T(8,128)(2,1)S(1)}, u32[]{:S(2)}, u32[]{:S(2)}) collective-permute-start(bf16[384,128]{1,0:T(8,128)(2,1)S(1)} %get-tuple-element.31), channel_id=1, source_target_pairs={{0,2},{2,0},{4,6},{6,4},{1,3},{3,1},{5,7},{7,5},{8,10},{10,8},{12,... | collective-permute-start | bytes 294920 | tf_op jit(solution)/shard_map/ppermute | solution.py:340
  17.3 5.9 %collective-permute-start.6 = (bf16[384,128]{1,0:T(8,128)(2,1)S(1)}, bf16[384,128]{1,0:T(8,128)(2,1)S(1)}, u32[]{:S(2)}, u32[]{:S(2)}) collective-permute-start(bf16[384,128]{1,0:T(8,128)(2,1)S(1)} %shard_map.68), channel_id=1, source_target_pairs={{0,24},{8,16},{16,8},{24,0},{1,25},{9,17},{17,9},{25,1},{2,26},{10... | collective-permute-start | bytes 294920 | tf_op jit(solution)/shard_map/ppermute | solution.py:340
  19.8 4.8 %collective-permute-start.5 = (bf16[384,128]{1,0:T(8,128)(2,1)S(1)}, bf16[384,128]{1,0:T(8,128)(2,1)S(1)}, u32[]{:S(2)}, u32[]{:S(2)}) collective-permute-start(bf16[384,128]{1,0:T(8,128)(2,1)S(1)} %shard_map.68), channel_id=1, source_target_pairs={{0,16},{8,24},{16,0},{24,8},{1,17},{9,25},{17,1},{25,9},{2,18},{10... | collective-permute-start | bytes 294920 | tf_op jit(solution)/shard_map/ppermute | solution.py:340
  20.3 4.6 %collective-permute-start.4 = (bf16[384,128]{1,0:T(8,128)(2,1)S(1)}, bf16[384,128]{1,0:T(8,128)(2,1)S(1)}, u32[]{:S(2)}, u32[]{:S(2)}) collective-permute-start(bf16[384,128]{1,0:T(8,128)(2,1)S(1)} %shard_map.68), channel_id=1, source_target_pairs={{0,8},{8,0},{16,24},{24,16},{1,9},{9,1},{17,25},{25,17},{2,10},{10... | collective-permute-start | bytes 294920 | tf_op jit(solution)/shard_map/ppermute | solution.py:340
  25.0 7.2 %collective-permute-start.11 = (bf16[384,128]{1,0:T(8,128)(2,1)S(1)}, bf16[384,128]{1,0:T(8,128)(2,1)S(1)}, u32[]{:S(2)}, u32[]{:S(2)}) collective-permute-start(bf16[384,128]{1,0:T(8,128)(2,1)S(1)} %shard_map.69.after_ref.refs_1_), channel_id=1, source_target_pairs={{0,2},{2,0},{4,6},{6,4},{1,3},{3,1},{5,7},{7,5},{8,10},{10,8},{12,... | collective-permute-start | bytes 294920 | tf_op jit(solution)/shard_map/ppermute | solution.py:340
  25.6 8.3 %collective-permute-start.9 = (bf16[384,128]{1,0:T(8,128)(2,1)S(1)}, bf16[384,128]{1,0:T(8,128)(2,1)S(1)}, u32[]{:S(2)}, u32[]{:S(2)}) collective-permute-start(bf16[384,128]{1,0:T(8,128)(2,1)S(1)} %shard_map.69.after_ref.refs_1_), channel_id=1, source_target_pairs={{0,4},{2,6},{4,0},{6,2},{1,5},{3,7},{5,1},{7,3},{8,12},{10,14},{12... | collective-permute-start | bytes 294920 | tf_op jit(solution)/shard_map/ppermute | solution.py:340
  28.1 6.7 %collective-permute-start.13 = (bf16[384,128]{1,0:T(8,128)(2,1)S(1)}, bf16[384,128]{1,0:T(8,128)(2,1)S(1)}, u32[]{:S(2)}, u32[]{:S(2)}) collective-permute-start(bf16[384,128]{1,0:T(8,128)(2,1)S(1)} %shard_map.69.after_ref.refs_1_), channel_id=1, source_target_pairs={{0,8},{8,0},{16,24},{24,16},{1,9},{9,1},{17,25},{25,17},{2,10},{10... | collective-permute-start | bytes 294920 | tf_op jit(solution)/shard_map/ppermute | solution.py:340
  29.1 6.5 %collective-permute-start.7 = (bf16[384,128]{1,0:T(8,128)(2,1)S(1)}, bf16[384,128]{1,0:T(8,128)(2,1)S(1)}, u32[]{:S(2)}, u32[]{:S(2)}) collective-permute-start(bf16[384,128]{1,0:T(8,128)(2,1)S(1)} %shard_map.69.after_ref.refs_1_), channel_id=1, source_target_pairs={{0,6},{2,4},{4,2},{6,0},{1,7},{3,5},{5,3},{7,1},{8,14},{10,12},{12... | collective-permute-start | bytes 294920 | tf_op jit(solution)/shard_map/ppermute | solution.py:340
  32.2 4.7 %collective-permute-start.12 = (bf16[384,128]{1,0:T(8,128)(2,1)S(1)}, bf16[384,128]{1,0:T(8,128)(2,1)S(1)}, u32[]{:S(2)}, u32[]{:S(2)}) collective-permute-start(bf16[384,128]{1,0:T(8,128)(2,1)S(1)} %collective-permute-done.11.refs_5_), channel_id=1, source_target_pairs={{0,8},{8,0},{16,24},{24,16},{1,9},{9,1},{17,25},{25,17},{2,10},{10... | collective-permute-start | bytes 294920 | tf_op jit(solution)/shard_map/ppermute | solution.py:340
  33.9 4.6 %collective-permute-start.10 = (bf16[384,128]{1,0:T(8,128)(2,1)S(1)}, bf16[384,128]{1,0:T(8,128)(2,1)S(1)}, u32[]{:S(2)}, u32[]{:S(2)}) collective-permute-start(bf16[384,128]{1,0:T(8,128)(2,1)S(1)} %collective-permute-done.9.refs_6_), channel_id=1, source_target_pairs={{0,8},{8,0},{16,24},{24,16},{1,9},{9,1},{17,25},{25,17},{2,10},{10... | collective-permute-start | bytes 294920 | tf_op jit(solution)/shard_map/ppermute | solution.py:340
  38.6 2.2 %collective-permute-start.14 = (bf16[2688,128]{1,0:T(8,128)(2,1)S(1)}, bf16[2688,128]{1,0:T(8,128)(2,1)S(1)}, u32[]{:S(2)}, u32[]{:S(2)}) collective-permute-start(bf16[2688,128]{1,0:T(8,128)(2,1)S(1)} %shard_map.71.state_ref), channel_id=1, source_target_pairs={{0,1},{1,0},{2,3},{3,2},{4,5},{5,4},{6,7},{7,6},{8,9},{9,8},{10,11... | collective-permute-start | bytes 2064392 | tf_op jit(solution)/shard_map/ppermute | solution.py:340
  38.7 5.2 %collective-permute-start.8 = (bf16[384,128]{1,0:T(8,128)(2,1)S(1)}, bf16[384,128]{1,0:T(8,128)(2,1)S(1)}, u32[]{:S(2)}, u32[]{:S(2)}) collective-permute-start(bf16[384,128]{1,0:T(8,128)(2,1)S(1)} %collective-permute-done.7.refs_7_), channel_id=1, source_target_pairs={{0,8},{8,0},{16,24},{24,16},{1,9},{9,1},{17,25},{25,17},{2,10},{10... | collective-permute-start | bytes 294920 | tf_op jit(solution)/shard_map/ppermute | solution.py:340
  43.9 1.3 %collective-permute-start.15 = (bf16[384,128]{1,0:T(8,128)(2,1)S(1)}, bf16[384,128]{1,0:T(8,128)(2,1)S(1)}, u32[]{:S(2)}, u32[]{:S(2)}) collective-permute-start(bf16[384,128]{1,0:T(8,128)(2,1)S(1)} %collective-permute-done.8.refs_0_), channel_id=1, source_target_pairs={{0,1},{1,0},{2,3},{3,2},{4,5},{5,4},{6,7},{7,6},{8,9},{9,8},{10,11... | collective-permute-start | bytes 294920 | tf_op jit(solution)/shard_map/ppermute | solution.py:340

commit v8 on v7

--- a/solution.py
+++ b/solution.py
@@ -19,6 +19,7 @@
 ANYWHERE = pl.BlockSpec(memory_space=pl.ANY)
 IN_HBM = pl.BlockSpec(memory_space=pltpu.HBM)
 SMALL = pl.CostEstimate(flops=1024, bytes_accessed=1024, transcendentals=0)
+LARGE = pl.CostEstimate(flops=2 * 10**10, bytes_accessed=1024, transcendentals=0)
 PARAMS = pltpu.CompilerParams(vmem_limit_bytes=VMEM_LIMIT)
 
 
@@ -282,16 +283,15 @@
         in_specs=[WHOLE] * 4,
         out_specs=WHOLE,
         compiler_params=PARAMS,
-        cost_estimate=pl.CostEstimate(
-            flops=2 * local.size * HEAD_DIM, bytes_accessed=8 * local.size, transcendentals=0
-        ),
+        cost_estimate=LARGE,
     )(*in_vmem(local, x, y, states))
 
 
 def late_half(chips, early, base_ref, y_ref, *refs):
     out_ref = refs[-1]
+    rows = base_ref.shape[1] // chips
     for d in range(chips):
-        states = [(y_ref, refs[0], 0)] if d >= early else []
+        states = [(y_ref, refs[0], (d - early) * rows)] if d >= early else []
         for at, result in read_heads(d, chips, base_ref, states):
             out_ref[:, at] = result.astype(BF16)
 
@@ -353,7 +353,7 @@
 
     local = functools.partial(local_part, coefs, 2)
     rest = (frame_len, window_back, queries)
-    early = max(chips - 1, 1)
+    early = 1
 
     outgoing, keys, values = outgoing_state(keys, values)
     incoming = swap(outgoing, "core", 1, 2)
@@ -372,13 +372,13 @@
     for piece in x[1:]:
         piece, _ = lax.optimization_barrier((piece, local_1))
         y.append(swap(piece, "frame", 1, frames))
-    late_own = y[1:][early - 1 :]
-    places = [0, *range(chips + early - 1, chips - 1, -1), *range(1, chips)]
+    places = [0, *reversed(range(1, chips + early))]
     own_states = pack(x + y[:early], places, [local_1])
     other_states = swap(own_states, "core", 1, 2)
     base_0 = read_middle(chips, early, local_0, x_0, y_0, own_states)
     base_1 = read_middle(chips, early, local_1, x_1, y_1, other_states)
-    late_own, base_0, base_1 = lax.optimization_barrier((late_own, base_0, base_1))
+    late = y[early:]
+    late_own = [pack(late, list(range(len(late))), [])] if late else []
     late_other = [swap(piece, "core", 1, 2) for piece in late_own]
     done = read_late(chips, early, base_0, y_0, late_own)
     return read_last(chips, early, done, base_1, y_1, late_other)

time: 46.4 us -> 43.5 us (0.938)
  waiting for transfers between devices: 20.2 us -> 17 us
    ppermute x16, waiting for transfers between devices: 20.2 us -> 17 us  [swap(): return lax.ppermute(array, axis, [(n, n ^ mask) for n in range(size)])]
  transfers between devices with their start and end apart: 16 -> 16, of which waited for: 13 -> 11; matrix products, arithmetic and copies ran while one was open for 0% -> 0% of each run, Pallas kernels for 11% -> 11%
where the time goes in v8:
time: 43.5 us; the launch traced here: 43.4 us
  starting transfers between devices  18.5 us (43%)
  waiting for transfers between devices  17 us (39%)
  Pallas kernels  7.76 us (18%)
    ppermute x16, starting transfers between devices, swap(): return lax.ppermute(array, axis, [(n, n ^ mask) for n in range(size)])  18.5 us
    ppermute x16, waiting for transfers between devices, swap(): return lax.ppermute(array, axis, [(n, n ^ mask) for n in range(size)])  17 us
    pallas_call x2, Pallas kernels, local_part(): pl.pallas_call(functools.partial(local_kernel, coefs, turn), out_shape=[p...  3.44 us
    pallas_call x1, Pallas kernels, outgoing_state(): pl.pallas_call(first_kernel, out_shape=[pltpu.VMEM((half * dim, dim), BF1...  1.69 us
    pallas_call x1, Pallas kernels, read_last(): pl.pallas_call(functools.partial(last_kernel, chips, early), out_shape=ja...  1.02 us
  transfers between devices with their start and end apart: 16, of which 11 were waited for; matrix products, arithmetic and copies ran while one was open for 0% of the time, Pallas kernels for 11%

profile of v8, /device:TPU:0, one launch (start us, length us, event | category | flops | bytes accessed | tf_op | source)
XLA Modules:
  0.0 43.4 jit_solution(6908505169348019220)
XLA Ops:
  0.0 1.7 %shard_map.64 = (bf16[1536,128]{1,0:T(8,128)(2,1)S(1)}, bf16[128,3072]{1,0:T(8,128)(2,1)S(1)}, bf16[128,3072]{1,0:T(8,128)(2,1)S(1)}) custom-call(bf16[128,3072]{1,0:T(8,128)(2,1)} %key_ref.1, bf16[128,3072]{1,0:T(8,128)(2,1)} %value_ref.1), custom_call_target="tpu_custom_call" | custom-call | flops 50331648 | bytes 1572864 | tf_op jit(solution)/shard_map/pallas_call | solution.py:73
  1.7 0.5 %collective-permute-start = (bf16[1536,128]{1,0:T(8,128)(2,1)S(1)}, bf16[1536,128]{1,0:T(8,128)(2,1)S(1)}, u32[]{:S(2)}, u32[]{:S(2)}) collective-permute-start(bf16[1536,128]{1,0:T(8,128)(2,1)S(1)} %get-tuple-element.23), channel_id=1, source_target_pairs={{0,1},{1,0},{2,3},{3,2},{4,5},{5,4},{6,7},{7,6},{8,9},{9,8},{10,11... | collective-permute-start | bytes 1179656 | tf_op jit(solution)/shard_map/ppermute | solution.py:340
  2.2 0.5 %shard_map.65.mine_ref = f32[1536,128]{1,0:T(8,128)S(1)} custom-call(bf16[128,3072]{1,0:T(8,128)(2,1)S(1)} %get-tuple-element.21.key_ref, bf16[128,3072]{1,0:T(8,128)(2,1)S(1)} %get-tuple-element.22.value_ref), custom_call_target="tpu_custom_call" | custom-call | flops 50331648 | bytes 1572864 | tf_op jit(solution)/shard_map/pallas_call | solution.py:93
  2.7 0.8 %collective-permute-done.other_ref = bf16[1536,128]{1,0:T(8,128)(2,1)S(1)} collective-permute-done((bf16[1536,128]{1,0:T(8,128)(2,1)S(1)}, bf16[1536,128]{1,0:T(8,128)(2,1)S(1)}, u32[]{:S(2)}, u32[]{:S(2)}) %collective-permute-start) | collective-permute-done | bytes 393248 | tf_op jit(solution)/shard_map/ppermute | solution.py:340
  3.6 5.1 %collective-permute-start.1 = (bf16[384,128]{1,0:T(8,128)(2,1)S(1)}, bf16[384,128]{1,0:T(8,128)(2,1)S(1)}, u32[]{:S(2)}, u32[]{:S(2)}) collective-permute-start(bf16[384,128]{1,0:T(8,128)(2,1)S(1)} %get-tuple-element.28), channel_id=1, source_target_pairs={{0,6},{2,4},{4,2},{6,0},{1,7},{3,5},{5,3},{7,1},{8,14},{10,12},{12... | collective-permute-start | bytes 294920 | tf_op jit(solution)/shard_map/ppermute | solution.py:340
  8.7 0.6 %collective-permute-start.3 = (bf16[384,128]{1,0:T(8,128)(2,1)S(1)}, bf16[384,128]{1,0:T(8,128)(2,1)S(1)}, u32[]{:S(2)}, u32[]{:S(2)}) collective-permute-start(bf16[384,128]{1,0:T(8,128)(2,1)S(1)} %get-tuple-element.30), channel_id=1, source_target_pairs={{0,2},{2,0},{4,6},{6,4},{1,3},{3,1},{5,7},{7,5},{8,10},{10,8},{12,... | collective-permute-start | bytes 294920 | tf_op jit(solution)/shard_map/ppermute | solution.py:340
  9.4 1.7 %shard_map.67 = (f32[128,1536]{1,0:T(8,128)S(1)}, bf16[128,1536]{1,0:T(8,128)(2,1)S(1)}, bf16[128,1536]{1,0:T(8,128)(2,1)S(1)}) custom-call(s32[1,4]{1,0:T(1,128)S(1)} %copy-done.2, s32[1,4]{1,0:T(1,128)S(1)} %copy-done.3, bf16[128,3072]{1,0:T(8,128)(2,1)S(1)} %copy-done, bf16[128,3072]{1,0:T(8,128)(2,1)S(1)} %get-tuple-element.21.key_ref, ...), custom_call_target="tpu_custom_call" | custom-call | flops 100663296 | bytes 2752512 | tf_op jit(solution)/shard_map/pallas_call | solution.py:240
  11.1 1.3 %collective-permute-done.1.refs_0_ = bf16[384,128]{1,0:T(8,128)(2,1)S(1)} collective-permute-done((bf16[384,128]{1,0:T(8,128)(2,1)S(1)}, bf16[384,128]{1,0:T(8,128)(2,1)S(1)}, u32[]{:S(2)}, u32[]{:S(2)}) %collective-permute-start.1) | collective-permute-done | bytes 98336 | tf_op jit(solution)/shard_map/ppermute | solution.py:340
  12.4 4.9 %collective-permute-done.2.refs_1_ = bf16[384,128]{1,0:T(8,128)(2,1)S(1)} collective-permute-done((bf16[384,128]{1,0:T(8,128)(2,1)S(1)}, bf16[384,128]{1,0:T(8,128)(2,1)S(1)}, u32[]{:S(2)}, u32[]{:S(2)}) %collective-permute-start.2) | collective-permute-done | bytes 98336 | tf_op jit(solution)/shard_map/ppermute | solution.py:340
  17.3 2.5 %collective-permute-start.6 = (bf16[384,128]{1,0:T(8,128)(2,1)S(1)}, bf16[384,128]{1,0:T(8,128)(2,1)S(1)}, u32[]{:S(2)}, u32[]{:S(2)}) collective-permute-start(bf16[384,128]{1,0:T(8,128)(2,1)S(1)} %shard_map.68), channel_id=1, source_target_pairs={{0,24},{8,16},{16,8},{24,0},{1,25},{9,17},{17,9},{25,1},{2,26},{10... | collective-permute-start | bytes 294920 | tf_op jit(solution)/shard_map/ppermute | solution.py:340
  19.8 0.5 %collective-permute-start.5 = (bf16[384,128]{1,0:T(8,128)(2,1)S(1)}, bf16[384,128]{1,0:T(8,128)(2,1)S(1)}, u32[]{:S(2)}, u32[]{:S(2)}) collective-permute-start(bf16[384,128]{1,0:T(8,128)(2,1)S(1)} %shard_map.68), channel_id=1, source_target_pairs={{0,16},{8,24},{16,0},{24,8},{1,17},{9,25},{17,1},{25,9},{2,18},{10... | collective-permute-start | bytes 294920 | tf_op jit(solution)/shard_map/ppermute | solution.py:340
  20.3 0.5 %collective-permute-start.4 = (bf16[384,128]{1,0:T(8,128)(2,1)S(1)}, bf16[384,128]{1,0:T(8,128)(2,1)S(1)}, u32[]{:S(2)}, u32[]{:S(2)}) collective-permute-start(bf16[384,128]{1,0:T(8,128)(2,1)S(1)} %shard_map.68), channel_id=1, source_target_pairs={{0,8},{8,0},{16,24},{24,16},{1,9},{9,1},{17,25},{25,17},{2,10},{10... | collective-permute-start | bytes 294920 | tf_op jit(solution)/shard_map/ppermute | solution.py:340
  20.9 2.3 %collective-permute-done.6.diagonal_ref = bf16[384,128]{1,0:T(8,128)(2,1)S(1)} collective-permute-done((bf16[384,128]{1,0:T(8,128)(2,1)S(1)}, bf16[384,128]{1,0:T(8,128)(2,1)S(1)}, u32[]{:S(2)}, u32[]{:S(2)}) %collective-permute-start.6) | collective-permute-done | bytes 98336 | tf_op jit(solution)/shard_map/ppermute | solution.py:340
  23.2 1.4 %collective-permute-done.5.across_ref = bf16[384,128]{1,0:T(8,128)(2,1)S(1)} collective-permute-done((bf16[384,128]{1,0:T(8,128)(2,1)S(1)}, bf16[384,128]{1,0:T(8,128)(2,1)S(1)}, u32[]{:S(2)}, u32[]{:S(2)}) %collective-permute-start.5) | collective-permute-done | bytes 98336 | tf_op jit(solution)/shard_map/ppermute | solution.py:340
  24.6 0.3 collective-permute-done.4.near_ref
  25.0 0.6 %collective-permute-start.10 = (bf16[384,128]{1,0:T(8,128)(2,1)S(1)}, bf16[384,128]{1,0:T(8,128)(2,1)S(1)}, u32[]{:S(2)}, u32[]{:S(2)}) collective-permute-start(bf16[384,128]{1,0:T(8,128)(2,1)S(1)} %shard_map.69.after_ref.refs_1_), channel_id=1, source_target_pairs={{0,2},{2,0},{4,6},{6,4},{1,3},{3,1},{5,7},{7,5},{8,10},{10,8},{12,... | collective-permute-start | bytes 294920 | tf_op jit(solution)/shard_map/ppermute | solution.py:340
  25.6 2.5 %collective-permute-start.9 = (bf16[384,128]{1,0:T(8,128)(2,1)S(1)}, bf16[384,128]{1,0:T(8,128)(2,1)S(1)}, u32[]{:S(2)}, u32[]{:S(2)}) collective-permute-start(bf16[384,128]{1,0:T(8,128)(2,1)S(1)} %shard_map.69.after_ref.refs_1_), channel_id=1, source_target_pairs={{0,4},{2,6},{4,0},{6,2},{1,5},{3,7},{5,1},{7,3},{8,12},{10,14},{12... | collective-permute-start | bytes 294920 | tf_op jit(solution)/shard_map/ppermute | solution.py:340
  28.1 1.3 %collective-permute-start.8 = (bf16[384,128]{1,0:T(8,128)(2,1)S(1)}, bf16[384,128]{1,0:T(8,128)(2,1)S(1)}, u32[]{:S(2)}, u32[]{:S(2)}) collective-permute-start(bf16[384,128]{1,0:T(8,128)(2,1)S(1)} %shard_map.69.after_ref.refs_1_), channel_id=1, source_target_pairs={{0,6},{2,4},{4,2},{6,0},{1,7},{3,5},{5,3},{7,1},{8,14},{10,12},{12... | collective-permute-start | bytes 294920 | tf_op jit(solution)/shard_map/ppermute | solution.py:340
  29.5 1.0 %collective-permute-start.7 = (bf16[384,128]{1,0:T(8,128)(2,1)S(1)}, bf16[384,128]{1,0:T(8,128)(2,1)S(1)}, u32[]{:S(2)}, u32[]{:S(2)}) collective-permute-start(bf16[384,128]{1,0:T(8,128)(2,1)S(1)} %shard_map.69.after_ref.refs_1_), channel_id=1, source_target_pairs={{0,8},{8,0},{16,24},{24,16},{1,9},{9,1},{17,25},{25,17},{2,10},{10... | collective-permute-start | bytes 294920 | tf_op jit(solution)/shard_map/ppermute | solution.py:340
  30.5 1.7 %shard_map.70 = (f32[128,1536]{1,0:T(8,128)S(1)}, bf16[128,1536]{1,0:T(8,128)(2,1)S(1)}, bf16[128,1536]{1,0:T(8,128)(2,1)S(1)}) custom-call(s32[1,4]{1,0:T(1,128)S(1)} %copy-done.2, s32[1,4]{1,0:T(1,128)S(1)} %copy-done.3, bf16[128,3072]{1,0:T(8,128)(2,1)S(1)} %copy-done, bf16[128,3072]{1,0:T(8,128)(2,1)S(1)} %get-tuple-element.21.key_ref, ...), custom_call_target="tpu_custom_call" | custom-call | flops 100663296 | bytes 2752512 | tf_op jit(solution)/shard_map/pallas_call | solution.py:240
  32.2 1.1 %collective-permute-start.11 = (bf16[384,128]{1,0:T(8,128)(2,1)S(1)}, bf16[384,128]{1,0:T(8,128)(2,1)S(1)}, u32[]{:S(2)}, u32[]{:S(2)}) collective-permute-start(bf16[384,128]{1,0:T(8,128)(2,1)S(1)} %collective-permute-done.10.refs_5_), channel_id=1, source_target_pairs={{0,8},{8,0},{16,24},{24,16},{1,9},{9,1},{17,25},{25,17},{2,10},{10... | collective-permute-start | bytes 294920 | tf_op jit(solution)/shard_map/ppermute | solution.py:340
  33.3 1.7 %collective-permute-done.9.refs_4_ = bf16[384,128]{1,0:T(8,128)(2,1)S(1)} collective-permute-done((bf16[384,128]{1,0:T(8,128)(2,1)S(1)}, bf16[384,128]{1,0:T(8,128)(2,1)S(1)}, u32[]{:S(2)}, u32[]{:S(2)}) %collective-permute-start.9) | collective-permute-done | bytes 98336 | tf_op jit(solution)/shard_map/ppermute | solution.py:340
  35.0 0.7 %collective-permute-start.12 = (bf16[384,128]{1,0:T(8,128)(2,1)S(1)}, bf16[384,128]{1,0:T(8,128)(2,1)S(1)}, u32[]{:S(2)}, u32[]{:S(2)}) collective-permute-start(bf16[384,128]{1,0:T(8,128)(2,1)S(1)} %collective-permute-done.9.refs_4_), channel_id=1, source_target_pairs={{0,8},{8,0},{16,24},{24,16},{1,9},{9,1},{17,25},{25,17},{2,10},{10... | collective-permute-start | bytes 294920 | tf_op jit(solution)/shard_map/ppermute | solution.py:340
  35.7 1.3 %collective-permute-start.13 = (bf16[384,128]{1,0:T(8,128)(2,1)S(1)}, bf16[384,128]{1,0:T(8,128)(2,1)S(1)}, u32[]{:S(2)}, u32[]{:S(2)}) collective-permute-start(bf16[384,128]{1,0:T(8,128)(2,1)S(1)} %collective-permute-done.8.refs_3_), channel_id=1, source_target_pairs={{0,8},{8,0},{16,24},{24,16},{1,9},{9,1},{17,25},{25,17},{2,10},{10... | collective-permute-start | bytes 294920 | tf_op jit(solution)/shard_map/ppermute | solution.py:340
  37.2 0.3 shard_map.72.base_ref
  37.5 0.1 collective-permute-done.11.refs_0_
  37.5 2.1 %collective-permute-done.12.refs_1_ = bf16[384,128]{1,0:T(8,128)(2,1)S(1)} collective-permute-done((bf16[384,128]{1,0:T(8,128)(2,1)S(1)}, bf16[384,128]{1,0:T(8,128)(2,1)S(1)}, u32[]{:S(2)}, u32[]{:S(2)}) %collective-permute-start.12) | collective-permute-done | bytes 98336 | tf_op jit(solution)/shard_map/ppermute | solution.py:340
  39.6 1.1 %collective-permute-done.13.refs_2_ = bf16[384,128]{1,0:T(8,128)(2,1)S(1)} collective-permute-done((bf16[384,128]{1,0:T(8,128)(2,1)S(1)}, bf16[384,128]{1,0:T(8,128)(2,1)S(1)}, u32[]{:S(2)}, u32[]{:S(2)}) %collective-permute-start.13) | collective-permute-done | bytes 98336 | tf_op jit(solution)/shard_map/ppermute | solution.py:340
  40.8 0.3 shard_map.74.done_ref
  41.1 0.3 shard_map.75.base_ref
  41.4 1.0 %collective-permute-done.15.refs_0_ = bf16[1152,128]{1,0:T(8,128)(2,1)S(1)} collective-permute-done((bf16[1152,128]{1,0:T(8,128)(2,1)S(1)}, bf16[1152,128]{1,0:T(8,128)(2,1)S(1)}, u32[]{:S(2)}, u32[]{:S(2)}) %collective-permute-start.15) | collective-permute-done | bytes 294944 | tf_op jit(solution)/shard_map/ppermute | solution.py:340
  42.3 1.0 %shard_map.76 = bf16[128,3072]{1,0:T(8,128)(2,1)} custom-call(bf16[128,1536]{1,0:T(8,128)(2,1)S(1)} %shard_map.74.done_ref, f32[128,1536]{1,0:T(8,128)S(1)} %shard_map.75.base_ref, bf16[128,1536]{1,0:T(8,128)(2,1)S(1)} %get-tuple-element.36.y_ref, bf16[1152,128]{1,0:T(8,128)(2,1)S(1)} %collective-permute-done.15.refs_0_), custom_call_target="tpu_custom_call" | custom-call | flops 25165824 | bytes 1966080 | tf_op jit(solution)/shard_map/pallas_call | solution.py:326
  (21 shorter events, 0.4 us)
Async XLA Ops:
  1.7 1.8 %collective-permute-start = (bf16[1536,128]{1,0:T(8,128)(2,1)S(1)}, bf16[1536,128]{1,0:T(8,128)(2,1)S(1)}, u32[]{:S(2)}, u32[]{:S(2)}) collective-permute-start(bf16[1536,128]{1,0:T(8,128)(2,1)S(1)} %get-tuple-element.23), channel_id=1, source_target_pairs={{0,1},{1,0},{2,3},{3,2},{4,5},{5,4},{6,7},{7,6},{8,9},{9,8},{10,11... | collective-permute-start | bytes 1179656 | tf_op jit(solution)/shard_map/ppermute | solution.py:340
  2.7 6.6 %copy-start = (bf16[128,3072]{1,0:T(8,128)(2,1)S(1)}, bf16[128,3072]{1,0:T(8,128)(2,1)}, u32[]{:S(2)}) copy-start(bf16[128,3072]{1,0:T(8,128)(2,1)} %query_ref.3) | copy-start | bytes 2359300
  2.7 6.6 %copy-start.1 = (f32[3,24,128]{2,1,0:T(8,128)S(1)}, f32[3,24,128]{2,1,0:T(8,128)}, u32[]{:S(2)}) copy-start(f32[3,24,128]{2,1,0:T(8,128)} %weight_ref.3) | copy-start | bytes 110596
  3.6 8.7 %collective-permute-start.1 = (bf16[384,128]{1,0:T(8,128)(2,1)S(1)}, bf16[384,128]{1,0:T(8,128)(2,1)S(1)}, u32[]{:S(2)}, u32[]{:S(2)}) collective-permute-start(bf16[384,128]{1,0:T(8,128)(2,1)S(1)} %get-tuple-element.28), channel_id=1, source_target_pairs={{0,6},{2,4},{4,2},{6,0},{1,7},{3,5},{5,3},{7,1},{8,14},{10,12},{12... | collective-permute-start | bytes 294920 | tf_op jit(solution)/shard_map/ppermute | solution.py:340
  8.7 8.6 %collective-permute-start.2 = (bf16[384,128]{1,0:T(8,128)(2,1)S(1)}, bf16[384,128]{1,0:T(8,128)(2,1)S(1)}, u32[]{:S(2)}, u32[]{:S(2)}) collective-permute-start(bf16[384,128]{1,0:T(8,128)(2,1)S(1)} %get-tuple-element.29), channel_id=1, source_target_pairs={{0,4},{2,6},{4,0},{6,2},{1,5},{3,7},{5,1},{7,3},{8,12},{10,14},{12... | collective-permute-start | bytes 294920 | tf_op jit(solution)/shard_map/ppermute | solution.py:340
  8.7 0.7 %copy-start.2 = (s32[1,4]{1,0:T(1,128)S(1)}, s32[1,4]{1,0:T(1,128)}, u32[]{:S(2)}) copy-start(s32[1,4]{1,0:T(1,128)} %length_ref.3) | copy-start | bytes 52
  8.7 0.7 %copy-start.3 = (s32[1,4]{1,0:T(1,128)S(1)}, s32[1,4]{1,0:T(1,128)}, u32[]{:S(2)}) copy-start(s32[1,4]{1,0:T(1,128)} %back_ref.3) | copy-start | bytes 52
  8.7 8.6 %collective-permute-start.3 = (bf16[384,128]{1,0:T(8,128)(2,1)S(1)}, bf16[384,128]{1,0:T(8,128)(2,1)S(1)}, u32[]{:S(2)}, u32[]{:S(2)}) collective-permute-start(bf16[384,128]{1,0:T(8,128)(2,1)S(1)} %get-tuple-element.30), channel_id=1, source_target_pairs={{0,2},{2,0},{4,6},{6,4},{1,3},{3,1},{5,7},{7,5},{8,10},{10,8},{12,... | collective-permute-start | bytes 294920 | tf_op jit(solution)/shard_map/ppermute | solution.py:340
  17.3 5.9 %collective-permute-start.6 = (bf16[384,128]{1,0:T(8,128)(2,1)S(1)}, bf16[384,128]{1,0:T(8,128)(2,1)S(1)}, u32[]{:S(2)}, u32[]{:S(2)}) collective-permute-start(bf16[384,128]{1,0:T(8,128)(2,1)S(1)} %shard_map.68), channel_id=1, source_target_pairs={{0,24},{8,16},{16,8},{24,0},{1,25},{9,17},{17,9},{25,1},{2,26},{10... | collective-permute-start | bytes 294920 | tf_op jit(solution)/shard_map/ppermute | solution.py:340
  19.8 4.8 %collective-permute-start.5 = (bf16[384,128]{1,0:T(8,128)(2,1)S(1)}, bf16[384,128]{1,0:T(8,128)(2,1)S(1)}, u32[]{:S(2)}, u32[]{:S(2)}) collective-permute-start(bf16[384,128]{1,0:T(8,128)(2,1)S(1)} %shard_map.68), channel_id=1, source_target_pairs={{0,16},{8,24},{16,0},{24,8},{1,17},{9,25},{17,1},{25,9},{2,18},{10... | collective-permute-start | bytes 294920 | tf_op jit(solution)/shard_map/ppermute | solution.py:340
  20.3 4.6 %collective-permute-start.4 = (bf16[384,128]{1,0:T(8,128)(2,1)S(1)}, bf16[384,128]{1,0:T(8,128)(2,1)S(1)}, u32[]{:S(2)}, u32[]{:S(2)}) collective-permute-start(bf16[384,128]{1,0:T(8,128)(2,1)S(1)} %shard_map.68), channel_id=1, source_target_pairs={{0,8},{8,0},{16,24},{24,16},{1,9},{9,1},{17,25},{25,17},{2,10},{10... | collective-permute-start | bytes 294920 | tf_op jit(solution)/shard_map/ppermute | solution.py:340
  25.0 7.2 %collective-permute-start.10 = (bf16[384,128]{1,0:T(8,128)(2,1)S(1)}, bf16[384,128]{1,0:T(8,128)(2,1)S(1)}, u32[]{:S(2)}, u32[]{:S(2)}) collective-permute-start(bf16[384,128]{1,0:T(8,128)(2,1)S(1)} %shard_map.69.after_ref.refs_1_), channel_id=1, source_target_pairs={{0,2},{2,0},{4,6},{6,4},{1,3},{3,1},{5,7},{7,5},{8,10},{10,8},{12,... | collective-permute-start | bytes 294920 | tf_op jit(solution)/shard_map/ppermute | solution.py:340
  25.6 9.4 %collective-permute-start.9 = (bf16[384,128]{1,0:T(8,128)(2,1)S(1)}, bf16[384,128]{1,0:T(8,128)(2,1)S(1)}, u32[]{:S(2)}, u32[]{:S(2)}) collective-permute-start(bf16[384,128]{1,0:T(8,128)(2,1)S(1)} %shard_map.69.after_ref.refs_1_), channel_id=1, source_target_pairs={{0,4},{2,6},{4,0},{6,2},{1,5},{3,7},{5,1},{7,3},{8,12},{10,14},{12... | collective-permute-start | bytes 294920 | tf_op jit(solution)/shard_map/ppermute | solution.py:340
  28.1 7.6 %collective-permute-start.8 = (bf16[384,128]{1,0:T(8,128)(2,1)S(1)}, bf16[384,128]{1,0:T(8,128)(2,1)S(1)}, u32[]{:S(2)}, u32[]{:S(2)}) collective-permute-start(bf16[384,128]{1,0:T(8,128)(2,1)S(1)} %shard_map.69.after_ref.refs_1_), channel_id=1, source_target_pairs={{0,6},{2,4},{4,2},{6,0},{1,7},{3,5},{5,3},{7,1},{8,14},{10,12},{12... | collective-permute-start | bytes 294920 | tf_op jit(solution)/shard_map/ppermute | solution.py:340
  29.5 7.6 %collective-permute-start.7 = (bf16[384,128]{1,0:T(8,128)(2,1)S(1)}, bf16[384,128]{1,0:T(8,128)(2,1)S(1)}, u32[]{:S(2)}, u32[]{:S(2)}) collective-permute-start(bf16[384,128]{1,0:T(8,128)(2,1)S(1)} %shard_map.69.after_ref.refs_1_), channel_id=1, source_target_pairs={{0,8},{8,0},{16,24},{24,16},{1,9},{9,1},{17,25},{25,17},{2,10},{10... | collective-permute-start | bytes 294920 | tf_op jit(solution)/shard_map/ppermute | solution.py:340
  32.2 5.3 %collective-permute-start.11 = (bf16[384,128]{1,0:T(8,128)(2,1)S(1)}, bf16[384,128]{1,0:T(8,128)(2,1)S(1)}, u32[]{:S(2)}, u32[]{:S(2)}) collective-permute-start(bf16[384,128]{1,0:T(8,128)(2,1)S(1)} %collective-permute-done.10.refs_5_), channel_id=1, source_target_pairs={{0,8},{8,0},{16,24},{24,16},{1,9},{9,1},{17,25},{25,17},{2,10},{10... | collective-permute-start | bytes 294920 | tf_op jit(solution)/shard_map/ppermute | solution.py:340
  35.0 4.6 %collective-permute-start.12 = (bf16[384,128]{1,0:T(8,128)(2,1)S(1)}, bf16[384,128]{1,0:T(8,128)(2,1)S(1)}, u32[]{:S(2)}, u32[]{:S(2)}) collective-permute-start(bf16[384,128]{1,0:T(8,128)(2,1)S(1)} %collective-permute-done.9.refs_4_), channel_id=1, source_target_pairs={{0,8},{8,0},{16,24},{24,16},{1,9},{9,1},{17,25},{25,17},{2,10},{10... | collective-permute-start | bytes 294920 | tf_op jit(solution)/shard_map/ppermute | solution.py:340
  35.7 4.9 %collective-permute-start.13 = (bf16[384,128]{1,0:T(8,128)(2,1)S(1)}, bf16[384,128]{1,0:T(8,128)(2,1)S(1)}, u32[]{:S(2)}, u32[]{:S(2)}) collective-permute-start(bf16[384,128]{1,0:T(8,128)(2,1)S(1)} %collective-permute-done.8.refs_3_), channel_id=1, source_target_pairs={{0,8},{8,0},{16,24},{24,16},{1,9},{9,1},{17,25},{25,17},{2,10},{10... | collective-permute-start | bytes 294920 | tf_op jit(solution)/shard_map/ppermute | solution.py:340
  37.1 4.0 %collective-permute-start.14 = (bf16[1920,128]{1,0:T(8,128)(2,1)S(1)}, bf16[1920,128]{1,0:T(8,128)(2,1)S(1)}, u32[]{:S(2)}, u32[]{:S(2)}) collective-permute-start(bf16[1920,128]{1,0:T(8,128)(2,1)S(1)} %shard_map.71.state_ref), channel_id=1, source_target_pairs={{0,1},{1,0},{2,3},{3,2},{4,5},{5,4},{6,7},{7,6},{8,9},{9,8},{10,11... | collective-permute-start | bytes 1474568 | tf_op jit(solution)/shard_map/ppermute | solution.py:340
  40.7 1.6 %collective-permute-start.15 = (bf16[1152,128]{1,0:T(8,128)(2,1)S(1)}, bf16[1152,128]{1,0:T(8,128)(2,1)S(1)}, u32[]{:S(2)}, u32[]{:S(2)}) collective-permute-start(bf16[1152,128]{1,0:T(8,128)(2,1)S(1)} %shard_map.73.refs_0_), channel_id=1, source_target_pairs={{0,1},{1,0},{2,3},{3,2},{4,5},{5,4},{6,7},{7,6},{8,9},{9,8},{10,11... | collective-permute-start | bytes 884744 | tf_op jit(solution)/shard_map/ppermute | solution.py:340

commit v9 on v8

--- a/solution.py
+++ b/solution.py
@@ -40,8 +40,9 @@
     return [pltpu.with_memory_space_constraint(array, pltpu.VMEM) for array in arrays]
 
 
-def states_of(first, keys, values, out_ref):
+def states_of(first, keys, values, out_ref, ready=lambda h: None):
     for h in range(out_ref.shape[0] // HEAD_DIM):
+        ready(h)
         at = columns(first + h)
         key_rows = keys[:, at].astype(F32)
         normal = (key_rows * inverse_rms(key_rows)).astype(BF16)
@@ -51,31 +52,41 @@
         out_ref[h * HEAD_DIM : (h + 1) * HEAD_DIM, :] = state.astype(out_ref.dtype)
 
 
-def first_kernel(key_ref, value_ref, out_ref, keys, values, sems):
+def first_kernel(parts, key_ref, value_ref, out_ref, keys, values, sems):
     mine, other = core_heads()
+    half = HEADS // 2
+    starts = [(other + h, half // parts) for h in range(0, half, half // parts)] + [(mine, half)]
     copies = []
-    for n, first in enumerate((other, mine)):
-        at = columns(first, HEADS // 2)
-        for s, (ref, held) in enumerate(((key_ref, keys), (value_ref, values))):
-            copies.append(pltpu.make_async_copy(ref.at[:, at], held.at[:, at], sems.at[n, s]))
-            copies[-1].start()
-    copies[0].wait()
-    copies[1].wait()
-    states_of(other, keys, values, out_ref)
-    copies[2].wait()
-    copies[3].wait()
+    for n, (first, heads) in enumerate(starts):
+        at = columns(first, heads)
+        pair = [
+            pltpu.make_async_copy(ref.at[:, at], held.at[:, at], sems.at[n, s])
+            for s, (ref, held) in enumerate(((key_ref, keys), (value_ref, values)))
+        ]
+        for copy in pair:
+            copy.start()
+        copies.append(pair)
+
+    def ready(h):
+        if h % (half // parts) == 0:
+            for copy in copies[h // (half // parts)]:
+                copy.wait()
+
+    states_of(other, keys, values, out_ref, ready)
+    for copy in copies[-1]:
+        copy.wait()
 
 
 def outgoing_state(keys, values):
     dim, half = HEAD_DIM, HEADS // 2
-    rows = keys.shape[0]
+    rows, parts = keys.shape[0], math.gcd(half, 3)
     keys, values = (pltpu.with_memory_space_constraint(x, pltpu.HBM) for x in (keys, values))
     return pl.pallas_call(
-        first_kernel,
+        functools.partial(first_kernel, parts),
         out_shape=[pltpu.VMEM((half * dim, dim), BF16)] + [pltpu.VMEM(keys.shape, BF16)] * 2,
         in_specs=[IN_HBM, IN_HBM],
         out_specs=[WHOLE] * 3,
-        scratch_shapes=[pltpu.SemaphoreType.DMA((2, 2))],
+        scratch_shapes=[pltpu.SemaphoreType.DMA((parts + 1, 2))],
         compiler_params=PARAMS,
         cost_estimate=pl.CostEstimate(
             flops=2 * half * rows * dim * dim, bytes_accessed=8 * half * rows * dim, transcendentals=0
@@ -140,21 +151,21 @@
     )(after, *in_vmem(own, *parts))
 
 
-def slot_kernel(near_ref, across_ref, diagonal_ref, out_ref):
+def slot_kernel(after_ref, near_ref, across_ref, diagonal_ref, out_ref):
     both = across_ref[...].astype(F32) + diagonal_ref[...].astype(F32)
     near = near_ref[...].astype(F32)
     out_ref[...] = jnp.where(lax.axis_index("frame") == 2, both, near).astype(BF16)
 
 
-def choose_slot(near, across, diagonal):
+def choose_slot(after, near, across, diagonal):
     return pl.pallas_call(
         slot_kernel,
         out_shape=pltpu.VMEM(near.shape, BF16),
-        in_specs=[WHOLE] * 3,
+        in_specs=[ANYWHERE] + [WHOLE] * 3,
         out_specs=WHOLE,
         compiler_params=PARAMS,
         cost_estimate=SMALL,
-    )(*in_vmem(near, across, diagonal))
+    )(after, *in_vmem(near, across, diagonal))
 
 
 def pack_kernel(after, order, *refs):
@@ -283,57 +294,49 @@
         in_specs=[WHOLE] * 4,
         out_specs=WHOLE,
         compiler_params=PARAMS,
-        cost_estimate=LARGE,
+        cost_estimate=SMALL,
     )(*in_vmem(local, x, y, states))
 
 
-def late_half(chips, early, base_ref, y_ref, *refs):
-    out_ref = refs[-1]
+def late_kernel(turn, chips, early, base_ref, y_ref, *refs):
+    *state_refs, out_ref, held, sems = refs
     rows = base_ref.shape[1] // chips
+    half = core_heads()[turn]
+    copies = []
     for d in range(chips):
-        states = [(y_ref, refs[0], (d - early) * rows)] if d >= early else []
+        states = [(y_ref, state_refs[0], (d - early) * rows)] if d >= early else []
         for at, result in read_heads(d, chips, base_ref, states):
-            out_ref[:, at] = result.astype(BF16)
-
-
-def read_late(chips, early, base, y, states):
-    return pl.pallas_call(
-        functools.partial(late_half, chips, early),
-        out_shape=pltpu.VMEM(base.shape, BF16),
-        in_specs=[WHOLE] * (2 + len(states)),
-        out_specs=WHOLE,
-        compiler_params=PARAMS,
-        cost_estimate=pl.CostEstimate(
-            flops=base.size * HEAD_DIM, bytes_accessed=6 * base.size, transcendentals=0
-        ),
-    )(*in_vmem(base, y, *states))
-
-
-def last_kernel(chips, early, done_ref, base_ref, y_ref, *refs):
-    *state_refs, out_ref, held, sems = refs
-    mine, other = core_heads()
-    first = pltpu.make_async_copy(done_ref, out_ref.at[:, columns(mine, HEADS // 2)], sems.at[0])
-    first.start()
-    late_half(chips, early, base_ref, y_ref, *state_refs, held)
-    second = pltpu.make_async_copy(held, out_ref.at[:, columns(other, HEADS // 2)], sems.at[1])
-    second.start()
-    first.wait()
-    second.wait()
-
-
-def read_last(chips, early, done, base, y, states):
+            held[:, at] = result.astype(BF16)
+        count = HEADS // 2 // chips
+        first = (lax.axis_index("chip") ^ d) * count
+        copies.append(
+            pltpu.make_async_copy(
+                held.at[:, columns(first, count)], out_ref.at[:, columns(half + first, count)], sems.at[d]
+            )
+        )
+        copies[-1].start()
+    for copy in copies:
+        copy.wait()
+
+
+def aliased_kernel(turn, chips, early, out_before_ref, *refs):
+    late_kernel(turn, chips, early, *refs)
+
+
+def write_late(turn, chips, early, base, y, states, out=None):
     tokens, width = base.shape
-    return pl.pallas_call(
-        functools.partial(last_kernel, chips, early),
+    before = [] if out is None else [out]
+    kernel = late_kernel if out is None else aliased_kernel
+    return pl.pallas_call(
+        functools.partial(kernel, turn, chips, early),
         out_shape=jax.ShapeDtypeStruct((tokens, 2 * width), BF16),
-        in_specs=[WHOLE] * (3 + len(states)),
+        in_specs=[ANYWHERE] * len(before) + [WHOLE] * (2 + len(states)),
         out_specs=ANYWHERE,
-        scratch_shapes=[pltpu.VMEM((tokens, width), BF16), pltpu.SemaphoreType.DMA((2,))],
-        compiler_params=PARAMS,
-        cost_estimate=pl.CostEstimate(
-            flops=base.size * HEAD_DIM, bytes_accessed=10 * base.size, transcendentals=0
-        ),
-    )(*in_vmem(done, base, y, *states))
+        input_output_aliases={0: 0} if before else {},
+        scratch_shapes=[pltpu.VMEM((tokens, width), BF16), pltpu.SemaphoreType.DMA((chips,))],
+        compiler_params=PARAMS,
+        cost_estimate=SMALL if before else LARGE,
+    )(*before, *in_vmem(base, y, *states))
 
 
 def swap(array, axis, mask, size):
@@ -364,14 +367,12 @@
     state = sum_pieces(local_0, own, got, F32 if outer > 1 else BF16)
     if outer > 1:
         state = lax.psum(state, "outer").astype(BF16)
-    slot = choose_slot(*(swap(state, "frame", mask, frames) for mask in (1, 2, 3)))
+    local_1, x_1, y_1 = local(1, *rest, keys, values, level_weight, state)
+    slot = choose_slot(local_1, *(swap(state, "frame", mask, frames) for mask in (1, 2, 3)))
 
     x = [slot] + [swap(slot, "chip", d, chips) for d in range(1, chips)]
     y = [swap(slot, "frame", 1, frames)]
-    local_1, x_1, y_1 = local(1, *rest, keys, values, level_weight, slot)
-    for piece in x[1:]:
-        piece, _ = lax.optimization_barrier((piece, local_1))
-        y.append(swap(piece, "frame", 1, frames))
+    y += [swap(piece, "frame", 1, frames) for piece in x[1:]]
     places = [0, *reversed(range(1, chips + early))]
     own_states = pack(x + y[:early], places, [local_1])
     other_states = swap(own_states, "core", 1, 2)
@@ -380,8 +381,8 @@
     late = y[early:]
     late_own = [pack(late, list(range(len(late))), [])] if late else []
     late_other = [swap(piece, "core", 1, 2) for piece in late_own]
-    done = read_late(chips, early, base_0, y_0, late_own)
-    return read_last(chips, early, done, base_1, y_1, late_other)
+    out = write_late(0, chips, early, base_0, y_0, late_own)
+    return write_late(1, chips, early, base_1, y_1, late_other, out)
 
 
 def solution(mesh):

time: 43.5 us -> 43.8 us (level)
  Pallas kernels: 7.76 us -> 8.71 us
  waiting for transfers between devices: 17 us -> 16.4 us
    pallas_call x3, Pallas kernels: 2.97 us -> 3.92 us  [the longest x1 2.02 us: outgoing_state(): pl.pallas_call(functools.partial(first_kernel, parts), out_shape=[pltpu.V...]
    ppermute x16, waiting for transfers between devices: 17 us -> 16.4 us  [swap(): return lax.ppermute(array, axis, [(n, n ^ mask) for n in range(size)])]
  transfers between devices with their start and end apart: 16 -> 16, of which waited for: 11 -> 10; matrix products, arithmetic and copies ran while one was open for 0% -> 0% of each run, Pallas kernels for 11% -> 13%
where the time goes in v9:
time: 43.8 us; the launch traced here: 43.6 us
  starting transfers between devices  18.4 us (42%)
  waiting for transfers between devices  16.4 us (37%)
  Pallas kernels  8.71 us (20%)
    ppermute x16, starting transfers between devices, swap(): return lax.ppermute(array, axis, [(n, n ^ mask) for n in range(size)])  18.4 us
    ppermute x16, waiting for transfers between devices, swap(): return lax.ppermute(array, axis, [(n, n ^ mask) for n in range(size)])  16.4 us
    pallas_call x2, Pallas kernels, local_part(): pl.pallas_call(functools.partial(local_kernel, coefs, turn), out_shape=[p...  3.44 us
    pallas_call x1, Pallas kernels, outgoing_state(): pl.pallas_call(functools.partial(first_kernel, parts), out_shape=[pltpu.V...  2.02 us
    pallas_call x2, Pallas kernels, write_late(): pl.pallas_call(functools.partial(kernel, turn, chips, early), out_shape=j...  1.9 us
  transfers between devices with their start and end apart: 16, of which 10 were waited for; matrix products, arithmetic and copies ran while one was open for 0% of the time, Pallas kernels for 13%

profile of v9, /device:TPU:0, one launch (start us, length us, event | category | flops | bytes accessed | tf_op | source)
XLA Modules:
  0.0 43.6 jit_solution(7322149270453878599)
XLA Ops:
  0.0 2.0 %shard_map.64 = (bf16[1536,128]{1,0:T(8,128)(2,1)S(1)}, bf16[128,3072]{1,0:T(8,128)(2,1)S(1)}, bf16[128,3072]{1,0:T(8,128)(2,1)S(1)}) custom-call(bf16[128,3072]{1,0:T(8,128)(2,1)} %key_ref.1, bf16[128,3072]{1,0:T(8,128)(2,1)} %value_ref.1), custom_call_target="tpu_custom_call" | custom-call | flops 50331648 | bytes 1572864 | tf_op jit(solution)/shard_map/pallas_call | solution.py:84
  2.0 0.5 %collective-permute-start = (bf16[1536,128]{1,0:T(8,128)(2,1)S(1)}, bf16[1536,128]{1,0:T(8,128)(2,1)S(1)}, u32[]{:S(2)}, u32[]{:S(2)}) collective-permute-start(bf16[1536,128]{1,0:T(8,128)(2,1)S(1)} %get-tuple-element.20), channel_id=1, source_target_pairs={{0,1},{1,0},{2,3},{3,2},{4,5},{5,4},{6,7},{7,6},{8,9},{9,8},{10,11... | collective-permute-start | bytes 1179656 | tf_op jit(solution)/shard_map/ppermute | solution.py:343
  2.5 0.5 %shard_map.65.mine_ref = f32[1536,128]{1,0:T(8,128)S(1)} custom-call(bf16[128,3072]{1,0:T(8,128)(2,1)S(1)} %get-tuple-element.18.key_ref, bf16[128,3072]{1,0:T(8,128)(2,1)S(1)} %get-tuple-element.19.value_ref), custom_call_target="tpu_custom_call" | custom-call | flops 50331648 | bytes 1572864 | tf_op jit(solution)/shard_map/pallas_call | solution.py:104
  3.1 0.8 %collective-permute-done.other_ref = bf16[1536,128]{1,0:T(8,128)(2,1)S(1)} collective-permute-done((bf16[1536,128]{1,0:T(8,128)(2,1)S(1)}, bf16[1536,128]{1,0:T(8,128)(2,1)S(1)}, u32[]{:S(2)}, u32[]{:S(2)}) %collective-permute-start) | collective-permute-done | bytes 393248 | tf_op jit(solution)/shard_map/ppermute | solution.py:343
  3.9 0.1 shard_map.66
  4.0 5.0 %collective-permute-start.1 = (bf16[384,128]{1,0:T(8,128)(2,1)S(1)}, bf16[384,128]{1,0:T(8,128)(2,1)S(1)}, u32[]{:S(2)}, u32[]{:S(2)}) collective-permute-start(bf16[384,128]{1,0:T(8,128)(2,1)S(1)} %get-tuple-element.25), channel_id=1, source_target_pairs={{0,6},{2,4},{4,2},{6,0},{1,7},{3,5},{5,3},{7,1},{8,14},{10,12},{12... | collective-permute-start | bytes 294920 | tf_op jit(solution)/shard_map/ppermute | solution.py:343
  9.0 0.6 %collective-permute-start.3 = (bf16[384,128]{1,0:T(8,128)(2,1)S(1)}, bf16[384,128]{1,0:T(8,128)(2,1)S(1)}, u32[]{:S(2)}, u32[]{:S(2)}) collective-permute-start(bf16[384,128]{1,0:T(8,128)(2,1)S(1)} %get-tuple-element.27), channel_id=1, source_target_pairs={{0,2},{2,0},{4,6},{6,4},{1,3},{3,1},{5,7},{7,5},{8,10},{10,8},{12,... | collective-permute-start | bytes 294920 | tf_op jit(solution)/shard_map/ppermute | solution.py:343
  9.7 1.7 %shard_map.67 = (f32[128,1536]{1,0:T(8,128)S(1)}, bf16[128,1536]{1,0:T(8,128)(2,1)S(1)}, bf16[128,1536]{1,0:T(8,128)(2,1)S(1)}) custom-call(s32[1,4]{1,0:T(1,128)S(1)} %copy-done.2, s32[1,4]{1,0:T(1,128)S(1)} %copy-done.3, bf16[128,3072]{1,0:T(8,128)(2,1)S(1)} %copy-done, bf16[128,3072]{1,0:T(8,128)(2,1)S(1)} %get-tuple-element.18.key_ref, ...), custom_call_target="tpu_custom_call" | custom-call | flops 100663296 | bytes 2752512 | tf_op jit(solution)/shard_map/pallas_call | solution.py:251
  11.4 1.3 %collective-permute-done.1.refs_0_ = bf16[384,128]{1,0:T(8,128)(2,1)S(1)} collective-permute-done((bf16[384,128]{1,0:T(8,128)(2,1)S(1)}, bf16[384,128]{1,0:T(8,128)(2,1)S(1)}, u32[]{:S(2)}, u32[]{:S(2)}) %collective-permute-start.1) | collective-permute-done | bytes 98336 | tf_op jit(solution)/shard_map/ppermute | solution.py:343
  12.7 4.9 %collective-permute-done.2.refs_1_ = bf16[384,128]{1,0:T(8,128)(2,1)S(1)} collective-permute-done((bf16[384,128]{1,0:T(8,128)(2,1)S(1)}, bf16[384,128]{1,0:T(8,128)(2,1)S(1)}, u32[]{:S(2)}, u32[]{:S(2)}) %collective-permute-start.2) | collective-permute-done | bytes 98336 | tf_op jit(solution)/shard_map/ppermute | solution.py:343
  17.7 2.5 %collective-permute-start.6 = (bf16[384,128]{1,0:T(8,128)(2,1)S(1)}, bf16[384,128]{1,0:T(8,128)(2,1)S(1)}, u32[]{:S(2)}, u32[]{:S(2)}) collective-permute-start(bf16[384,128]{1,0:T(8,128)(2,1)S(1)} %shard_map.68.after_ref), channel_id=1, source_target_pairs={{0,24},{8,16},{16,8},{24,0},{1,25},{9,17},{17,9},{25,1},{2,26},{10... | collective-permute-start | bytes 294920 | tf_op jit(solution)/shard_map/ppermute | solution.py:343
  20.2 0.5 %collective-permute-start.5 = (bf16[384,128]{1,0:T(8,128)(2,1)S(1)}, bf16[384,128]{1,0:T(8,128)(2,1)S(1)}, u32[]{:S(2)}, u32[]{:S(2)}) collective-permute-start(bf16[384,128]{1,0:T(8,128)(2,1)S(1)} %shard_map.68.after_ref), channel_id=1, source_target_pairs={{0,16},{8,24},{16,0},{24,8},{1,17},{9,25},{17,1},{25,9},{2,18},{10... | collective-permute-start | bytes 294920 | tf_op jit(solution)/shard_map/ppermute | solution.py:343
  20.7 0.5 %collective-permute-start.4 = (bf16[384,128]{1,0:T(8,128)(2,1)S(1)}, bf16[384,128]{1,0:T(8,128)(2,1)S(1)}, u32[]{:S(2)}, u32[]{:S(2)}) collective-permute-start(bf16[384,128]{1,0:T(8,128)(2,1)S(1)} %shard_map.68.after_ref), channel_id=1, source_target_pairs={{0,8},{8,0},{16,24},{24,16},{1,9},{9,1},{17,25},{25,17},{2,10},{10... | collective-permute-start | bytes 294920 | tf_op jit(solution)/shard_map/ppermute | solution.py:343
  21.2 1.7 %shard_map.69 = (f32[128,1536]{1,0:T(8,128)S(1)}, bf16[128,1536]{1,0:T(8,128)(2,1)S(1)}, bf16[128,1536]{1,0:T(8,128)(2,1)S(1)}) custom-call(s32[1,4]{1,0:T(1,128)S(1)} %copy-done.2, s32[1,4]{1,0:T(1,128)S(1)} %copy-done.3, bf16[128,3072]{1,0:T(8,128)(2,1)S(1)} %copy-done, bf16[128,3072]{1,0:T(8,128)(2,1)S(1)} %get-tuple-element.18.key_ref, ...), custom_call_target="tpu_custom_call" | custom-call | flops 100663296 | bytes 2752512 | tf_op jit(solution)/shard_map/pallas_call | solution.py:251
  22.9 0.6 %collective-permute-done.6.diagonal_ref = bf16[384,128]{1,0:T(8,128)(2,1)S(1)} collective-permute-done((bf16[384,128]{1,0:T(8,128)(2,1)S(1)}, bf16[384,128]{1,0:T(8,128)(2,1)S(1)}, u32[]{:S(2)}, u32[]{:S(2)}) %collective-permute-start.6) | collective-permute-done | bytes 98336 | tf_op jit(solution)/shard_map/ppermute | solution.py:343
  23.5 1.4 %collective-permute-done.5.across_ref = bf16[384,128]{1,0:T(8,128)(2,1)S(1)} collective-permute-done((bf16[384,128]{1,0:T(8,128)(2,1)S(1)}, bf16[384,128]{1,0:T(8,128)(2,1)S(1)}, u32[]{:S(2)}, u32[]{:S(2)}) %collective-permute-start.5) | collective-permute-done | bytes 98336 | tf_op jit(solution)/shard_map/ppermute | solution.py:343
  25.0 0.3 collective-permute-done.4.near_ref
  25.3 0.6 %collective-permute-start.10 = (bf16[384,128]{1,0:T(8,128)(2,1)S(1)}, bf16[384,128]{1,0:T(8,128)(2,1)S(1)}, u32[]{:S(2)}, u32[]{:S(2)}) collective-permute-start(bf16[384,128]{1,0:T(8,128)(2,1)S(1)} %shard_map.70.refs_1_), channel_id=1, source_target_pairs={{0,2},{2,0},{4,6},{6,4},{1,3},{3,1},{5,7},{7,5},{8,10},{10,8},{12,... | collective-permute-start | bytes 294920 | tf_op jit(solution)/shard_map/ppermute | solution.py:343
  25.9 2.5 %collective-permute-start.9 = (bf16[384,128]{1,0:T(8,128)(2,1)S(1)}, bf16[384,128]{1,0:T(8,128)(2,1)S(1)}, u32[]{:S(2)}, u32[]{:S(2)}) collective-permute-start(bf16[384,128]{1,0:T(8,128)(2,1)S(1)} %shard_map.70.refs_1_), channel_id=1, source_target_pairs={{0,4},{2,6},{4,0},{6,2},{1,5},{3,7},{5,1},{7,3},{8,12},{10,14},{12... | collective-permute-start | bytes 294920 | tf_op jit(solution)/shard_map/ppermute | solution.py:343
  28.4 1.3 %collective-permute-start.8 = (bf16[384,128]{1,0:T(8,128)(2,1)S(1)}, bf16[384,128]{1,0:T(8,128)(2,1)S(1)}, u32[]{:S(2)}, u32[]{:S(2)}) collective-permute-start(bf16[384,128]{1,0:T(8,128)(2,1)S(1)} %shard_map.70.refs_1_), channel_id=1, source_target_pairs={{0,6},{2,4},{4,2},{6,0},{1,7},{3,5},{5,3},{7,1},{8,14},{10,12},{12... | collective-permute-start | bytes 294920 | tf_op jit(solution)/shard_map/ppermute | solution.py:343
  29.8 1.0 %collective-permute-start.7 = (bf16[384,128]{1,0:T(8,128)(2,1)S(1)}, bf16[384,128]{1,0:T(8,128)(2,1)S(1)}, u32[]{:S(2)}, u32[]{:S(2)}) collective-permute-start(bf16[384,128]{1,0:T(8,128)(2,1)S(1)} %shard_map.70.refs_1_), channel_id=1, source_target_pairs={{0,8},{8,0},{16,24},{24,16},{1,9},{9,1},{17,25},{25,17},{2,10},{10... | collective-permute-start | bytes 294920 | tf_op jit(solution)/shard_map/ppermute | solution.py:343
  30.8 1.0 %collective-permute-start.11 = (bf16[384,128]{1,0:T(8,128)(2,1)S(1)}, bf16[384,128]{1,0:T(8,128)(2,1)S(1)}, u32[]{:S(2)}, u32[]{:S(2)}) collective-permute-start(bf16[384,128]{1,0:T(8,128)(2,1)S(1)} %collective-permute-done.10.refs_5_), channel_id=1, source_target_pairs={{0,8},{8,0},{16,24},{24,16},{1,9},{9,1},{17,25},{25,17},{2,10},{10... | collective-permute-start | bytes 294920 | tf_op jit(solution)/shard_map/ppermute | solution.py:343
  31.8 3.5 %collective-permute-done.9.refs_4_ = bf16[384,128]{1,0:T(8,128)(2,1)S(1)} collective-permute-done((bf16[384,128]{1,0:T(8,128)(2,1)S(1)}, bf16[384,128]{1,0:T(8,128)(2,1)S(1)}, u32[]{:S(2)}, u32[]{:S(2)}) %collective-permute-start.9) | collective-permute-done | bytes 98336 | tf_op jit(solution)/shard_map/ppermute | solution.py:343
  35.3 0.7 %collective-permute-start.12 = (bf16[384,128]{1,0:T(8,128)(2,1)S(1)}, bf16[384,128]{1,0:T(8,128)(2,1)S(1)}, u32[]{:S(2)}, u32[]{:S(2)}) collective-permute-start(bf16[384,128]{1,0:T(8,128)(2,1)S(1)} %collective-permute-done.9.refs_4_), channel_id=1, source_target_pairs={{0,8},{8,0},{16,24},{24,16},{1,9},{9,1},{17,25},{25,17},{2,10},{10... | collective-permute-start | bytes 294920 | tf_op jit(solution)/shard_map/ppermute | solution.py:343
  36.1 1.3 %collective-permute-start.13 = (bf16[384,128]{1,0:T(8,128)(2,1)S(1)}, bf16[384,128]{1,0:T(8,128)(2,1)S(1)}, u32[]{:S(2)}, u32[]{:S(2)}) collective-permute-start(bf16[384,128]{1,0:T(8,128)(2,1)S(1)} %collective-permute-done.8.refs_3_), channel_id=1, source_target_pairs={{0,8},{8,0},{16,24},{24,16},{1,9},{9,1},{17,25},{25,17},{2,10},{10... | collective-permute-start | bytes 294920 | tf_op jit(solution)/shard_map/ppermute | solution.py:343
  37.5 0.3 shard_map.72.base_ref
  37.8 2.2 %collective-permute-done.12.refs_1_ = bf16[384,128]{1,0:T(8,128)(2,1)S(1)} collective-permute-done((bf16[384,128]{1,0:T(8,128)(2,1)S(1)}, bf16[384,128]{1,0:T(8,128)(2,1)S(1)}, u32[]{:S(2)}, u32[]{:S(2)}) %collective-permute-start.12) | collective-permute-done | bytes 98336 | tf_op jit(solution)/shard_map/ppermute | solution.py:343
  40.0 1.1 %collective-permute-done.13.refs_2_ = bf16[384,128]{1,0:T(8,128)(2,1)S(1)} collective-permute-done((bf16[384,128]{1,0:T(8,128)(2,1)S(1)}, bf16[384,128]{1,0:T(8,128)(2,1)S(1)}, u32[]{:S(2)}, u32[]{:S(2)}) %collective-permute-start.13) | collective-permute-done | bytes 98336 | tf_op jit(solution)/shard_map/ppermute | solution.py:343
  41.1 1.0 %shard_map.74.out_before_ref = bf16[128,3072]{1,0:T(8,128)(2,1)} custom-call(f32[128,1536]{1,0:T(8,128)S(1)} %shard_map.72.base_ref, bf16[128,1536]{1,0:T(8,128)(2,1)S(1)} %get-tuple-element.24.y_ref, bf16[1152,128]{1,0:T(8,128)(2,1)S(1)} %shard_map.73.refs_0_), custom_call_target="tpu_custom_call" | custom-call | flops 20000000000 | bytes 1024 | tf_op jit(solution)/shard_map/pallas_call | solution.py:330
  42.1 0.3 shard_map.75.refs_0_
  42.4 0.3 collective-permute-done.15.refs_2_
  42.7 0.9 %shard_map.76 = bf16[128,3072]{1,0:T(8,128)(2,1)} custom-call(bf16[128,3072]{1,0:T(8,128)(2,1)} %shard_map.74.out_before_ref, f32[128,1536]{1,0:T(8,128)S(1)} %shard_map.75.refs_0_, bf16[128,1536]{1,0:T(8,128)(2,1)S(1)} %get-tuple-element.30.y_ref.refs_1_, bf16[1152,128]{1,0:T(8,128)(2,1)S(1)} %collective-permute-done.15.refs_2_), custom_call_target="tpu_custom_call", output_to_operand_aliasing={{}: (0, {})} | custom-call | flops 1024 | bytes 1024 | tf_op jit(solution)/shard_map/pallas_call | solution.py:330
  (21 shorter events, 0.3 us)
Async XLA Ops:
  2.0 1.9 %collective-permute-start = (bf16[1536,128]{1,0:T(8,128)(2,1)S(1)}, bf16[1536,128]{1,0:T(8,128)(2,1)S(1)}, u32[]{:S(2)}, u32[]{:S(2)}) collective-permute-start(bf16[1536,128]{1,0:T(8,128)(2,1)S(1)} %get-tuple-element.20), channel_id=1, source_target_pairs={{0,1},{1,0},{2,3},{3,2},{4,5},{5,4},{6,7},{7,6},{8,9},{9,8},{10,11... | collective-permute-start | bytes 1179656 | tf_op jit(solution)/shard_map/ppermute | solution.py:343
  3.1 6.6 %copy-start = (bf16[128,3072]{1,0:T(8,128)(2,1)S(1)}, bf16[128,3072]{1,0:T(8,128)(2,1)}, u32[]{:S(2)}) copy-start(bf16[128,3072]{1,0:T(8,128)(2,1)} %query_ref.3) | copy-start | bytes 2359300
  3.1 6.6 %copy-start.1 = (f32[3,24,128]{2,1,0:T(8,128)S(1)}, f32[3,24,128]{2,1,0:T(8,128)}, u32[]{:S(2)}) copy-start(f32[3,24,128]{2,1,0:T(8,128)} %weight_ref.3) | copy-start | bytes 110596
  4.0 8.7 %collective-permute-start.1 = (bf16[384,128]{1,0:T(8,128)(2,1)S(1)}, bf16[384,128]{1,0:T(8,128)(2,1)S(1)}, u32[]{:S(2)}, u32[]{:S(2)}) collective-permute-start(bf16[384,128]{1,0:T(8,128)(2,1)S(1)} %get-tuple-element.25), channel_id=1, source_target_pairs={{0,6},{2,4},{4,2},{6,0},{1,7},{3,5},{5,3},{7,1},{8,14},{10,12},{12... | collective-permute-start | bytes 294920 | tf_op jit(solution)/shard_map/ppermute | solution.py:343
  9.0 8.6 %collective-permute-start.2 = (bf16[384,128]{1,0:T(8,128)(2,1)S(1)}, bf16[384,128]{1,0:T(8,128)(2,1)S(1)}, u32[]{:S(2)}, u32[]{:S(2)}) collective-permute-start(bf16[384,128]{1,0:T(8,128)(2,1)S(1)} %get-tuple-element.26), channel_id=1, source_target_pairs={{0,4},{2,6},{4,0},{6,2},{1,5},{3,7},{5,1},{7,3},{8,12},{10,14},{12... | collective-permute-start | bytes 294920 | tf_op jit(solution)/shard_map/ppermute | solution.py:343
  9.0 0.7 %copy-start.2 = (s32[1,4]{1,0:T(1,128)S(1)}, s32[1,4]{1,0:T(1,128)}, u32[]{:S(2)}) copy-start(s32[1,4]{1,0:T(1,128)} %length_ref.3) | copy-start | bytes 52
  9.0 0.7 %copy-start.3 = (s32[1,4]{1,0:T(1,128)S(1)}, s32[1,4]{1,0:T(1,128)}, u32[]{:S(2)}) copy-start(s32[1,4]{1,0:T(1,128)} %back_ref.3) | copy-start | bytes 52
  9.0 8.6 %collective-permute-start.3 = (bf16[384,128]{1,0:T(8,128)(2,1)S(1)}, bf16[384,128]{1,0:T(8,128)(2,1)S(1)}, u32[]{:S(2)}, u32[]{:S(2)}) collective-permute-start(bf16[384,128]{1,0:T(8,128)(2,1)S(1)} %get-tuple-element.27), channel_id=1, source_target_pairs={{0,2},{2,0},{4,6},{6,4},{1,3},{3,1},{5,7},{7,5},{8,10},{10,8},{12,... | collective-permute-start | bytes 294920 | tf_op jit(solution)/shard_map/ppermute | solution.py:343
  17.7 5.9 %collective-permute-start.6 = (bf16[384,128]{1,0:T(8,128)(2,1)S(1)}, bf16[384,128]{1,0:T(8,128)(2,1)S(1)}, u32[]{:S(2)}, u32[]{:S(2)}) collective-permute-start(bf16[384,128]{1,0:T(8,128)(2,1)S(1)} %shard_map.68.after_ref), channel_id=1, source_target_pairs={{0,24},{8,16},{16,8},{24,0},{1,25},{9,17},{17,9},{25,1},{2,26},{10... | collective-permute-start | bytes 294920 | tf_op jit(solution)/shard_map/ppermute | solution.py:343
  20.2 4.8 %collective-permute-start.5 = (bf16[384,128]{1,0:T(8,128)(2,1)S(1)}, bf16[384,128]{1,0:T(8,128)(2,1)S(1)}, u32[]{:S(2)}, u32[]{:S(2)}) collective-permute-start(bf16[384,128]{1,0:T(8,128)(2,1)S(1)} %shard_map.68.after_ref), channel_id=1, source_target_pairs={{0,16},{8,24},{16,0},{24,8},{1,17},{9,25},{17,1},{25,9},{2,18},{10... | collective-permute-start | bytes 294920 | tf_op jit(solution)/shard_map/ppermute | solution.py:343
  20.7 4.6 %collective-permute-start.4 = (bf16[384,128]{1,0:T(8,128)(2,1)S(1)}, bf16[384,128]{1,0:T(8,128)(2,1)S(1)}, u32[]{:S(2)}, u32[]{:S(2)}) collective-permute-start(bf16[384,128]{1,0:T(8,128)(2,1)S(1)} %shard_map.68.after_ref), channel_id=1, source_target_pairs={{0,8},{8,0},{16,24},{24,16},{1,9},{9,1},{17,25},{25,17},{2,10},{10... | collective-permute-start | bytes 294920 | tf_op jit(solution)/shard_map/ppermute | solution.py:343
  25.3 5.5 %collective-permute-start.10 = (bf16[384,128]{1,0:T(8,128)(2,1)S(1)}, bf16[384,128]{1,0:T(8,128)(2,1)S(1)}, u32[]{:S(2)}, u32[]{:S(2)}) collective-permute-start(bf16[384,128]{1,0:T(8,128)(2,1)S(1)} %shard_map.70.refs_1_), channel_id=1, source_target_pairs={{0,2},{2,0},{4,6},{6,4},{1,3},{3,1},{5,7},{7,5},{8,10},{10,8},{12,... | collective-permute-start | bytes 294920 | tf_op jit(solution)/shard_map/ppermute | solution.py:343
  25.9 9.4 %collective-permute-start.9 = (bf16[384,128]{1,0:T(8,128)(2,1)S(1)}, bf16[384,128]{1,0:T(8,128)(2,1)S(1)}, u32[]{:S(2)}, u32[]{:S(2)}) collective-permute-start(bf16[384,128]{1,0:T(8,128)(2,1)S(1)} %shard_map.70.refs_1_), channel_id=1, source_target_pairs={{0,4},{2,6},{4,0},{6,2},{1,5},{3,7},{5,1},{7,3},{8,12},{10,14},{12... | collective-permute-start | bytes 294920 | tf_op jit(solution)/shard_map/ppermute | solution.py:343
  28.4 7.6 %collective-permute-start.8 = (bf16[384,128]{1,0:T(8,128)(2,1)S(1)}, bf16[384,128]{1,0:T(8,128)(2,1)S(1)}, u32[]{:S(2)}, u32[]{:S(2)}) collective-permute-start(bf16[384,128]{1,0:T(8,128)(2,1)S(1)} %shard_map.70.refs_1_), channel_id=1, source_target_pairs={{0,6},{2,4},{4,2},{6,0},{1,7},{3,5},{5,3},{7,1},{8,14},{10,12},{12... | collective-permute-start | bytes 294920 | tf_op jit(solution)/shard_map/ppermute | solution.py:343
  29.8 7.6 %collective-permute-start.7 = (bf16[384,128]{1,0:T(8,128)(2,1)S(1)}, bf16[384,128]{1,0:T(8,128)(2,1)S(1)}, u32[]{:S(2)}, u32[]{:S(2)}) collective-permute-start(bf16[384,128]{1,0:T(8,128)(2,1)S(1)} %shard_map.70.refs_1_), channel_id=1, source_target_pairs={{0,8},{8,0},{16,24},{24,16},{1,9},{9,1},{17,25},{25,17},{2,10},{10... | collective-permute-start | bytes 294920 | tf_op jit(solution)/shard_map/ppermute | solution.py:343
  30.8 7.0 %collective-permute-start.11 = (bf16[384,128]{1,0:T(8,128)(2,1)S(1)}, bf16[384,128]{1,0:T(8,128)(2,1)S(1)}, u32[]{:S(2)}, u32[]{:S(2)}) collective-permute-start(bf16[384,128]{1,0:T(8,128)(2,1)S(1)} %collective-permute-done.10.refs_5_), channel_id=1, source_target_pairs={{0,8},{8,0},{16,24},{24,16},{1,9},{9,1},{17,25},{25,17},{2,10},{10... | collective-permute-start | bytes 294920 | tf_op jit(solution)/shard_map/ppermute | solution.py:343
  35.3 4.6 %collective-permute-start.12 = (bf16[384,128]{1,0:T(8,128)(2,1)S(1)}, bf16[384,128]{1,0:T(8,128)(2,1)S(1)}, u32[]{:S(2)}, u32[]{:S(2)}) collective-permute-start(bf16[384,128]{1,0:T(8,128)(2,1)S(1)} %collective-permute-done.9.refs_4_), channel_id=1, source_target_pairs={{0,8},{8,0},{16,24},{24,16},{1,9},{9,1},{17,25},{25,17},{2,10},{10... | collective-permute-start | bytes 294920 | tf_op jit(solution)/shard_map/ppermute | solution.py:343
  36.1 4.9 %collective-permute-start.13 = (bf16[384,128]{1,0:T(8,128)(2,1)S(1)}, bf16[384,128]{1,0:T(8,128)(2,1)S(1)}, u32[]{:S(2)}, u32[]{:S(2)}) collective-permute-start(bf16[384,128]{1,0:T(8,128)(2,1)S(1)} %collective-permute-done.8.refs_3_), channel_id=1, source_target_pairs={{0,8},{8,0},{16,24},{24,16},{1,9},{9,1},{17,25},{25,17},{2,10},{10... | collective-permute-start | bytes 294920 | tf_op jit(solution)/shard_map/ppermute | solution.py:343
  37.4 4.7 %collective-permute-start.14 = (bf16[1920,128]{1,0:T(8,128)(2,1)S(1)}, bf16[1920,128]{1,0:T(8,128)(2,1)S(1)}, u32[]{:S(2)}, u32[]{:S(2)}) collective-permute-start(bf16[1920,128]{1,0:T(8,128)(2,1)S(1)} %shard_map.71.state_ref), channel_id=1, source_target_pairs={{0,1},{1,0},{2,3},{3,2},{4,5},{5,4},{6,7},{7,6},{8,9},{9,8},{10,11... | collective-permute-start | bytes 1474568 | tf_op jit(solution)/shard_map/ppermute | solution.py:343
  41.0 1.6 %collective-permute-start.15 = (bf16[1152,128]{1,0:T(8,128)(2,1)S(1)}, bf16[1152,128]{1,0:T(8,128)(2,1)S(1)}, u32[]{:S(2)}, u32[]{:S(2)}) collective-permute-start(bf16[1152,128]{1,0:T(8,128)(2,1)S(1)} %shard_map.73.refs_0_), channel_id=1, source_target_pairs={{0,1},{1,0},{2,3},{3,2},{4,5},{5,4},{6,7},{7,6},{8,9},{9,8},{10,11... | collective-permute-start | bytes 884744 | tf_op jit(solution)/shard_map/ppermute | solution.py:343

commit v10 on v9

--- a/solution.py
+++ b/solution.py
@@ -79,7 +79,7 @@
 
 def outgoing_state(keys, values):
     dim, half = HEAD_DIM, HEADS // 2
-    rows, parts = keys.shape[0], math.gcd(half, 3)
+    rows, parts = keys.shape[0], 1
     keys, values = (pltpu.with_memory_space_constraint(x, pltpu.HBM) for x in (keys, values))
     return pl.pallas_call(
         functools.partial(first_kernel, parts),
@@ -151,21 +151,21 @@
     )(after, *in_vmem(own, *parts))
 
 
-def slot_kernel(after_ref, near_ref, across_ref, diagonal_ref, out_ref):
-    both = across_ref[...].astype(F32) + diagonal_ref[...].astype(F32)
-    near = near_ref[...].astype(F32)
-    out_ref[...] = jnp.where(lax.axis_index("frame") == 2, both, near).astype(BF16)
-
-
-def choose_slot(after, near, across, diagonal):
+def slot_kernel(after_ref, before_ref, first_ref, out_ref):
+    before = before_ref[...].astype(F32)
+    both = first_ref[...].astype(F32) + before
+    out_ref[...] = jnp.where(lax.axis_index("frame") == 2, both, before).astype(BF16)
+
+
+def choose_slot(after, before, first):
     return pl.pallas_call(
         slot_kernel,
-        out_shape=pltpu.VMEM(near.shape, BF16),
-        in_specs=[ANYWHERE] + [WHOLE] * 3,
+        out_shape=pltpu.VMEM(before.shape, BF16),
+        in_specs=[ANYWHERE] + [WHOLE] * 2,
         out_specs=WHOLE,
         compiler_params=PARAMS,
         cost_estimate=SMALL,
-    )(after, *in_vmem(near, across, diagonal))
+    )(after, *in_vmem(before, first))
 
 
 def pack_kernel(after, order, *refs):
@@ -368,12 +368,13 @@
     if outer > 1:
         state = lax.psum(state, "outer").astype(BF16)
     local_1, x_1, y_1 = local(1, *rest, keys, values, level_weight, state)
-    slot = choose_slot(local_1, *(swap(state, "frame", mask, frames) for mask in (1, 2, 3)))
+    shifted = lax.ppermute(state, "frame", [(f, (f + 1) % frames) for f in range(frames)])
+    slot = choose_slot(local_1, shifted, swap(state, "frame", 2, frames))
 
     x = [slot] + [swap(slot, "chip", d, chips) for d in range(1, chips)]
     y = [swap(slot, "frame", 1, frames)]
     y += [swap(piece, "frame", 1, frames) for piece in x[1:]]
-    places = [0, *reversed(range(1, chips + early))]
+    places = [0, *range(chips + early - 1, 2, -1), *range(1, min(3, chips + early))]
     own_states = pack(x + y[:early], places, [local_1])
     other_states = swap(own_states, "core", 1, 2)
     base_0 = read_middle(chips, early, local_0, x_0, y_0, own_states)

time: 43.8 us -> 41.8 us (0.954)
  starting transfers between devices: 18.4 us -> 17.3 us
  waiting for transfers between devices: 16.4 us -> 15.9 us
    ppermute x16 -> x14, starting transfers between devices: 18.4 us -> 15.8 us  [swap(): return lax.ppermute(array, axis, [(n, n ^ mask) for n in range(size)])]
    ppermute x16 -> x14, waiting for transfers between devices: 16.4 us -> 14.5 us  [swap(): return lax.ppermute(array, axis, [(n, n ^ mask) for n in range(size)])]
    ppermute x0 -> x1, starting transfers between devices: none -> 1.49 us  [body(): lax.ppermute(state, 'frame', [(f, (f + 1) % frames) for f in range(frames)])]
    ppermute x0 -> x1, waiting for transfers between devices: none -> 1.36 us  [body(): lax.ppermute(state, 'frame', [(f, (f + 1) % frames) for f in range(frames)])]
  transfers between devices with their start and end apart: 16 -> 15, of which waited for: 10 -> 10; matrix products, arithmetic and copies ran while one was open for 0% -> 0% of each run, Pallas kernels for 13% -> 13%
where the time goes in v10:
time: 41.8 us; the launch traced here: 41.6 us
  starting transfers between devices  17.3 us (41%)
  waiting for transfers between devices  15.9 us (38%)
  Pallas kernels  8.37 us (20%)
    ppermute x14, starting transfers between devices, swap(): return lax.ppermute(array, axis, [(n, n ^ mask) for n in range(size)])  15.8 us
    ppermute x14, waiting for transfers between devices, swap(): return lax.ppermute(array, axis, [(n, n ^ mask) for n in range(size)])  14.5 us
    pallas_call x2, Pallas kernels, local_part(): pl.pallas_call(functools.partial(local_kernel, coefs, turn), out_shape=[p...  3.44 us
    pallas_call x2, Pallas kernels, write_late(): pl.pallas_call(functools.partial(kernel, turn, chips, early), out_shape=j...  1.89 us
    pallas_call x1, Pallas kernels, outgoing_state(): pl.pallas_call(functools.partial(first_kernel, parts), out_shape=[pltpu.V...  1.69 us
    ppermute x1, starting transfers between devices, body(): lax.ppermute(state, 'frame', [(f, (f + 1) % frames) for f in range(frames)])  1.49 us
    ppermute x1, waiting for transfers between devices, body(): lax.ppermute(state, 'frame', [(f, (f + 1) % frames) for f in range(frames)])  1.36 us
  transfers between devices with their start and end apart: 15, of which 10 were waited for; matrix products, arithmetic and copies ran while one was open for 0% of the time, Pallas kernels for 13%

profile of v10, /device:TPU:0, one launch (start us, length us, event | category | flops | bytes accessed | tf_op | source)
XLA Modules:
  0.0 41.6 jit_solution(16572404216455027655)
XLA Ops:
  0.0 1.7 %shard_map.64 = (bf16[1536,128]{1,0:T(8,128)(2,1)S(1)}, bf16[128,3072]{1,0:T(8,128)(2,1)S(1)}, bf16[128,3072]{1,0:T(8,128)(2,1)S(1)}) custom-call(bf16[128,3072]{1,0:T(8,128)(2,1)} %key_ref.1, bf16[128,3072]{1,0:T(8,128)(2,1)} %value_ref.1), custom_call_target="tpu_custom_call" | custom-call | flops 50331648 | bytes 1572864 | tf_op jit(solution)/shard_map/pallas_call | solution.py:84
  1.7 0.5 %collective-permute-start = (bf16[1536,128]{1,0:T(8,128)(2,1)S(1)}, bf16[1536,128]{1,0:T(8,128)(2,1)S(1)}, u32[]{:S(2)}, u32[]{:S(2)}) collective-permute-start(bf16[1536,128]{1,0:T(8,128)(2,1)S(1)} %get-tuple-element.20), channel_id=1, source_target_pairs={{0,1},{1,0},{2,3},{3,2},{4,5},{5,4},{6,7},{7,6},{8,9},{9,8},{10,11... | collective-permute-start | bytes 1179656 | tf_op jit(solution)/shard_map/ppermute | solution.py:343
  2.2 0.5 %shard_map.65.mine_ref = f32[1536,128]{1,0:T(8,128)S(1)} custom-call(bf16[128,3072]{1,0:T(8,128)(2,1)S(1)} %get-tuple-element.18.key_ref, bf16[128,3072]{1,0:T(8,128)(2,1)S(1)} %get-tuple-element.19.value_ref), custom_call_target="tpu_custom_call" | custom-call | flops 50331648 | bytes 1572864 | tf_op jit(solution)/shard_map/pallas_call | solution.py:104
  2.7 0.8 %collective-permute-done.other_ref = bf16[1536,128]{1,0:T(8,128)(2,1)S(1)} collective-permute-done((bf16[1536,128]{1,0:T(8,128)(2,1)S(1)}, bf16[1536,128]{1,0:T(8,128)(2,1)S(1)}, u32[]{:S(2)}, u32[]{:S(2)}) %collective-permute-start) | collective-permute-done | bytes 393248 | tf_op jit(solution)/shard_map/ppermute | solution.py:343
  3.5 0.1 shard_map.66
  3.6 5.1 %collective-permute-start.1 = (bf16[384,128]{1,0:T(8,128)(2,1)S(1)}, bf16[384,128]{1,0:T(8,128)(2,1)S(1)}, u32[]{:S(2)}, u32[]{:S(2)}) collective-permute-start(bf16[384,128]{1,0:T(8,128)(2,1)S(1)} %get-tuple-element.25), channel_id=1, source_target_pairs={{0,6},{2,4},{4,2},{6,0},{1,7},{3,5},{5,3},{7,1},{8,14},{10,12},{12... | collective-permute-start | bytes 294920 | tf_op jit(solution)/shard_map/ppermute | solution.py:343
  8.7 0.6 %collective-permute-start.3 = (bf16[384,128]{1,0:T(8,128)(2,1)S(1)}, bf16[384,128]{1,0:T(8,128)(2,1)S(1)}, u32[]{:S(2)}, u32[]{:S(2)}) collective-permute-start(bf16[384,128]{1,0:T(8,128)(2,1)S(1)} %get-tuple-element.27), channel_id=1, source_target_pairs={{0,2},{2,0},{4,6},{6,4},{1,3},{3,1},{5,7},{7,5},{8,10},{10,8},{12,... | collective-permute-start | bytes 294920 | tf_op jit(solution)/shard_map/ppermute | solution.py:343
  9.4 1.7 %shard_map.67 = (f32[128,1536]{1,0:T(8,128)S(1)}, bf16[128,1536]{1,0:T(8,128)(2,1)S(1)}, bf16[128,1536]{1,0:T(8,128)(2,1)S(1)}) custom-call(s32[1,4]{1,0:T(1,128)S(1)} %copy-done.2, s32[1,4]{1,0:T(1,128)S(1)} %copy-done.3, bf16[128,3072]{1,0:T(8,128)(2,1)S(1)} %copy-done, bf16[128,3072]{1,0:T(8,128)(2,1)S(1)} %get-tuple-element.18.key_ref, ...), custom_call_target="tpu_custom_call" | custom-call | flops 100663296 | bytes 2752512 | tf_op jit(solution)/shard_map/pallas_call | solution.py:251
  11.1 1.3 %collective-permute-done.1.refs_0_ = bf16[384,128]{1,0:T(8,128)(2,1)S(1)} collective-permute-done((bf16[384,128]{1,0:T(8,128)(2,1)S(1)}, bf16[384,128]{1,0:T(8,128)(2,1)S(1)}, u32[]{:S(2)}, u32[]{:S(2)}) %collective-permute-start.1) | collective-permute-done | bytes 98336 | tf_op jit(solution)/shard_map/ppermute | solution.py:343
  12.4 4.9 %collective-permute-done.2.refs_1_ = bf16[384,128]{1,0:T(8,128)(2,1)S(1)} collective-permute-done((bf16[384,128]{1,0:T(8,128)(2,1)S(1)}, bf16[384,128]{1,0:T(8,128)(2,1)S(1)}, u32[]{:S(2)}, u32[]{:S(2)}) %collective-permute-start.2) | collective-permute-done | bytes 98336 | tf_op jit(solution)/shard_map/ppermute | solution.py:343
  17.3 1.6 %collective-permute-start.5 = (bf16[384,128]{1,0:T(8,128)(2,1)S(1)}, bf16[384,128]{1,0:T(8,128)(2,1)S(1)}, u32[]{:S(2)}, u32[]{:S(2)}) collective-permute-start(bf16[384,128]{1,0:T(8,128)(2,1)S(1)} %shard_map.68.after_ref), channel_id=1, source_target_pairs={{0,16},{8,24},{16,0},{24,8},{1,17},{9,25},{17,1},{25,9},{2,18},{10... | collective-permute-start | bytes 294920 | tf_op jit(solution)/shard_map/ppermute | solution.py:343
  18.9 1.5 %collective-permute-start.4 = (bf16[384,128]{1,0:T(8,128)(2,1)S(1)}, bf16[384,128]{1,0:T(8,128)(2,1)S(1)}, u32[]{:S(2)}, u32[]{:S(2)}) collective-permute-start(bf16[384,128]{1,0:T(8,128)(2,1)S(1)} %shard_map.68.after_ref), channel_id=1, source_target_pairs={{0,8},{8,16},{16,24},{24,0},{1,9},{9,17},{17,25},{25,1},{2,10},{10... | collective-permute-start | bytes 294920 | tf_op jit(solution)/shard_map/ppermute | solution.py:371
  20.4 1.7 %shard_map.69 = (f32[128,1536]{1,0:T(8,128)S(1)}, bf16[128,1536]{1,0:T(8,128)(2,1)S(1)}, bf16[128,1536]{1,0:T(8,128)(2,1)S(1)}) custom-call(s32[1,4]{1,0:T(1,128)S(1)} %copy-done.2, s32[1,4]{1,0:T(1,128)S(1)} %copy-done.3, bf16[128,3072]{1,0:T(8,128)(2,1)S(1)} %copy-done, bf16[128,3072]{1,0:T(8,128)(2,1)S(1)} %get-tuple-element.18.key_ref, ...), custom_call_target="tpu_custom_call" | custom-call | flops 100663296 | bytes 2752512 | tf_op jit(solution)/shard_map/pallas_call | solution.py:251
  22.1 0.9 %collective-permute-done.5.first_ref = bf16[384,128]{1,0:T(8,128)(2,1)S(1)} collective-permute-done((bf16[384,128]{1,0:T(8,128)(2,1)S(1)}, bf16[384,128]{1,0:T(8,128)(2,1)S(1)}, u32[]{:S(2)}, u32[]{:S(2)}) %collective-permute-start.5) | collective-permute-done | bytes 98336 | tf_op jit(solution)/shard_map/ppermute | solution.py:343
  23.1 1.4 %collective-permute-done.4.before_ref = bf16[384,128]{1,0:T(8,128)(2,1)S(1)} collective-permute-done((bf16[384,128]{1,0:T(8,128)(2,1)S(1)}, bf16[384,128]{1,0:T(8,128)(2,1)S(1)}, u32[]{:S(2)}, u32[]{:S(2)}) %collective-permute-start.4) | collective-permute-done | bytes 98336 | tf_op jit(solution)/shard_map/ppermute | solution.py:371
  24.5 0.3 collective-permute-start.9
  24.8 2.8 %collective-permute-start.8 = (bf16[384,128]{1,0:T(8,128)(2,1)S(1)}, bf16[384,128]{1,0:T(8,128)(2,1)S(1)}, u32[]{:S(2)}, u32[]{:S(2)}) collective-permute-start(bf16[384,128]{1,0:T(8,128)(2,1)S(1)} %shard_map.70.refs_1_), channel_id=1, source_target_pairs={{0,2},{2,0},{4,6},{6,4},{1,3},{3,1},{5,7},{7,5},{8,10},{10,8},{12,... | collective-permute-start | bytes 294920 | tf_op jit(solution)/shard_map/ppermute | solution.py:343
  27.6 1.3 %collective-permute-start.7 = (bf16[384,128]{1,0:T(8,128)(2,1)S(1)}, bf16[384,128]{1,0:T(8,128)(2,1)S(1)}, u32[]{:S(2)}, u32[]{:S(2)}) collective-permute-start(bf16[384,128]{1,0:T(8,128)(2,1)S(1)} %shard_map.70.refs_1_), channel_id=1, source_target_pairs={{0,6},{2,4},{4,2},{6,0},{1,7},{3,5},{5,3},{7,1},{8,14},{10,12},{12... | collective-permute-start | bytes 294920 | tf_op jit(solution)/shard_map/ppermute | solution.py:343
  28.9 0.6 %collective-permute-start.6 = (bf16[384,128]{1,0:T(8,128)(2,1)S(1)}, bf16[384,128]{1,0:T(8,128)(2,1)S(1)}, u32[]{:S(2)}, u32[]{:S(2)}) collective-permute-start(bf16[384,128]{1,0:T(8,128)(2,1)S(1)} %shard_map.70.refs_1_), channel_id=1, source_target_pairs={{0,8},{8,0},{16,24},{24,16},{1,9},{9,1},{17,25},{25,17},{2,10},{10... | collective-permute-start | bytes 294920 | tf_op jit(solution)/shard_map/ppermute | solution.py:343
  29.5 2.8 %collective-permute-done.9.refs_5_ = bf16[384,128]{1,0:T(8,128)(2,1)S(1)} collective-permute-done((bf16[384,128]{1,0:T(8,128)(2,1)S(1)}, bf16[384,128]{1,0:T(8,128)(2,1)S(1)}, u32[]{:S(2)}, u32[]{:S(2)}) %collective-permute-start.9) | collective-permute-done | bytes 98336 | tf_op jit(solution)/shard_map/ppermute | solution.py:343
  32.3 0.8 %collective-permute-start.11 = (bf16[384,128]{1,0:T(8,128)(2,1)S(1)}, bf16[384,128]{1,0:T(8,128)(2,1)S(1)}, u32[]{:S(2)}, u32[]{:S(2)}) collective-permute-start(bf16[384,128]{1,0:T(8,128)(2,1)S(1)} %collective-permute-done.9.refs_5_), channel_id=1, source_target_pairs={{0,8},{8,0},{16,24},{24,16},{1,9},{9,1},{17,25},{25,17},{2,10},{10... | collective-permute-start | bytes 294920 | tf_op jit(solution)/shard_map/ppermute | solution.py:343
  33.1 1.3 %collective-permute-start.10 = (bf16[384,128]{1,0:T(8,128)(2,1)S(1)}, bf16[384,128]{1,0:T(8,128)(2,1)S(1)}, u32[]{:S(2)}, u32[]{:S(2)}) collective-permute-start(bf16[384,128]{1,0:T(8,128)(2,1)S(1)} %collective-permute-done.8.refs_4_), channel_id=1, source_target_pairs={{0,8},{8,0},{16,24},{24,16},{1,9},{9,1},{17,25},{25,17},{2,10},{10... | collective-permute-start | bytes 294920 | tf_op jit(solution)/shard_map/ppermute | solution.py:343
  34.3 0.8 %collective-permute-start.12 = (bf16[384,128]{1,0:T(8,128)(2,1)S(1)}, bf16[384,128]{1,0:T(8,128)(2,1)S(1)}, u32[]{:S(2)}, u32[]{:S(2)}) collective-permute-start(bf16[384,128]{1,0:T(8,128)(2,1)S(1)} %collective-permute-done.7.refs_3_), channel_id=1, source_target_pairs={{0,8},{8,0},{16,24},{24,16},{1,9},{9,1},{17,25},{25,17},{2,10},{10... | collective-permute-start | bytes 294920 | tf_op jit(solution)/shard_map/ppermute | solution.py:343
  35.1 0.1 collective-permute-start.13
  35.2 0.3 shard_map.72.base_ref
  35.5 1.4 %collective-permute-done.11.refs_1_ = bf16[384,128]{1,0:T(8,128)(2,1)S(1)} collective-permute-done((bf16[384,128]{1,0:T(8,128)(2,1)S(1)}, bf16[384,128]{1,0:T(8,128)(2,1)S(1)}, u32[]{:S(2)}, u32[]{:S(2)}) %collective-permute-start.11) | collective-permute-done | bytes 98336 | tf_op jit(solution)/shard_map/ppermute | solution.py:343
  36.9 1.1 %collective-permute-done.10.refs_0_ = bf16[384,128]{1,0:T(8,128)(2,1)S(1)} collective-permute-done((bf16[384,128]{1,0:T(8,128)(2,1)S(1)}, bf16[384,128]{1,0:T(8,128)(2,1)S(1)}, u32[]{:S(2)}, u32[]{:S(2)}) %collective-permute-start.10) | collective-permute-done | bytes 98336 | tf_op jit(solution)/shard_map/ppermute | solution.py:343
  38.0 1.1 %collective-permute-done.12.refs_2_ = bf16[384,128]{1,0:T(8,128)(2,1)S(1)} collective-permute-done((bf16[384,128]{1,0:T(8,128)(2,1)S(1)}, bf16[384,128]{1,0:T(8,128)(2,1)S(1)}, u32[]{:S(2)}, u32[]{:S(2)}) %collective-permute-start.12) | collective-permute-done | bytes 98336 | tf_op jit(solution)/shard_map/ppermute | solution.py:343
  39.1 0.9 %shard_map.74.out_before_ref = bf16[128,3072]{1,0:T(8,128)(2,1)} custom-call(f32[128,1536]{1,0:T(8,128)S(1)} %shard_map.72.base_ref, bf16[128,1536]{1,0:T(8,128)(2,1)S(1)} %get-tuple-element.24.y_ref, bf16[1152,128]{1,0:T(8,128)(2,1)S(1)} %shard_map.73.refs_0_), custom_call_target="tpu_custom_call" | custom-call | flops 20000000000 | bytes 1024 | tf_op jit(solution)/shard_map/pallas_call | solution.py:330
  40.1 0.3 shard_map.75.refs_0_
  40.4 0.3 collective-permute-done.14.refs_2_
  40.7 0.9 %shard_map.76 = bf16[128,3072]{1,0:T(8,128)(2,1)} custom-call(bf16[128,3072]{1,0:T(8,128)(2,1)} %shard_map.74.out_before_ref, f32[128,1536]{1,0:T(8,128)S(1)} %shard_map.75.refs_0_, bf16[128,1536]{1,0:T(8,128)(2,1)S(1)} %get-tuple-element.30.y_ref.refs_1_, bf16[1152,128]{1,0:T(8,128)(2,1)S(1)} %collective-permute-done.14.refs_2_), custom_call_target="tpu_custom_call", output_to_operand_aliasing={{}: (0, {})} | custom-call | flops 1024 | bytes 1024 | tf_op jit(solution)/shard_map/pallas_call | solution.py:330
  (19 shorter events, 0.3 us)
Async XLA Ops:
  1.7 1.8 %collective-permute-start = (bf16[1536,128]{1,0:T(8,128)(2,1)S(1)}, bf16[1536,128]{1,0:T(8,128)(2,1)S(1)}, u32[]{:S(2)}, u32[]{:S(2)}) collective-permute-start(bf16[1536,128]{1,0:T(8,128)(2,1)S(1)} %get-tuple-element.20), channel_id=1, source_target_pairs={{0,1},{1,0},{2,3},{3,2},{4,5},{5,4},{6,7},{7,6},{8,9},{9,8},{10,11... | collective-permute-start | bytes 1179656 | tf_op jit(solution)/shard_map/ppermute | solution.py:343
  2.7 6.6 %copy-start = (bf16[128,3072]{1,0:T(8,128)(2,1)S(1)}, bf16[128,3072]{1,0:T(8,128)(2,1)}, u32[]{:S(2)}) copy-start(bf16[128,3072]{1,0:T(8,128)(2,1)} %query_ref.3) | copy-start | bytes 2359300
  2.7 6.6 %copy-start.1 = (f32[3,24,128]{2,1,0:T(8,128)S(1)}, f32[3,24,128]{2,1,0:T(8,128)}, u32[]{:S(2)}) copy-start(f32[3,24,128]{2,1,0:T(8,128)} %weight_ref.3) | copy-start | bytes 110596
  3.6 8.7 %collective-permute-start.1 = (bf16[384,128]{1,0:T(8,128)(2,1)S(1)}, bf16[384,128]{1,0:T(8,128)(2,1)S(1)}, u32[]{:S(2)}, u32[]{:S(2)}) collective-permute-start(bf16[384,128]{1,0:T(8,128)(2,1)S(1)} %get-tuple-element.25), channel_id=1, source_target_pairs={{0,6},{2,4},{4,2},{6,0},{1,7},{3,5},{5,3},{7,1},{8,14},{10,12},{12... | collective-permute-start | bytes 294920 | tf_op jit(solution)/shard_map/ppermute | solution.py:343
  8.7 8.6 %collective-permute-start.2 = (bf16[384,128]{1,0:T(8,128)(2,1)S(1)}, bf16[384,128]{1,0:T(8,128)(2,1)S(1)}, u32[]{:S(2)}, u32[]{:S(2)}) collective-permute-start(bf16[384,128]{1,0:T(8,128)(2,1)S(1)} %get-tuple-element.26), channel_id=1, source_target_pairs={{0,4},{2,6},{4,0},{6,2},{1,5},{3,7},{5,1},{7,3},{8,12},{10,14},{12... | collective-permute-start | bytes 294920 | tf_op jit(solution)/shard_map/ppermute | solution.py:343
  8.7 0.7 %copy-start.2 = (s32[1,4]{1,0:T(1,128)S(1)}, s32[1,4]{1,0:T(1,128)}, u32[]{:S(2)}) copy-start(s32[1,4]{1,0:T(1,128)} %length_ref.3) | copy-start | bytes 52
  8.7 0.7 %copy-start.3 = (s32[1,4]{1,0:T(1,128)S(1)}, s32[1,4]{1,0:T(1,128)}, u32[]{:S(2)}) copy-start(s32[1,4]{1,0:T(1,128)} %back_ref.3) | copy-start | bytes 52
  8.7 8.6 %collective-permute-start.3 = (bf16[384,128]{1,0:T(8,128)(2,1)S(1)}, bf16[384,128]{1,0:T(8,128)(2,1)S(1)}, u32[]{:S(2)}, u32[]{:S(2)}) collective-permute-start(bf16[384,128]{1,0:T(8,128)(2,1)S(1)} %get-tuple-element.27), channel_id=1, source_target_pairs={{0,2},{2,0},{4,6},{6,4},{1,3},{3,1},{5,7},{7,5},{8,10},{10,8},{12,... | collective-permute-start | bytes 294920 | tf_op jit(solution)/shard_map/ppermute | solution.py:343
  17.3 5.7 %collective-permute-start.5 = (bf16[384,128]{1,0:T(8,128)(2,1)S(1)}, bf16[384,128]{1,0:T(8,128)(2,1)S(1)}, u32[]{:S(2)}, u32[]{:S(2)}) collective-permute-start(bf16[384,128]{1,0:T(8,128)(2,1)S(1)} %shard_map.68.after_ref), channel_id=1, source_target_pairs={{0,16},{8,24},{16,0},{24,8},{1,17},{9,25},{17,1},{25,9},{2,18},{10... | collective-permute-start | bytes 294920 | tf_op jit(solution)/shard_map/ppermute | solution.py:343
  18.9 5.5 %collective-permute-start.4 = (bf16[384,128]{1,0:T(8,128)(2,1)S(1)}, bf16[384,128]{1,0:T(8,128)(2,1)S(1)}, u32[]{:S(2)}, u32[]{:S(2)}) collective-permute-start(bf16[384,128]{1,0:T(8,128)(2,1)S(1)} %shard_map.68.after_ref), channel_id=1, source_target_pairs={{0,8},{8,16},{16,24},{24,0},{1,9},{9,17},{17,25},{25,1},{2,10},{10... | collective-permute-start | bytes 294920 | tf_op jit(solution)/shard_map/ppermute | solution.py:371
  24.5 7.8 %collective-permute-start.9 = (bf16[384,128]{1,0:T(8,128)(2,1)S(1)}, bf16[384,128]{1,0:T(8,128)(2,1)S(1)}, u32[]{:S(2)}, u32[]{:S(2)}) collective-permute-start(bf16[384,128]{1,0:T(8,128)(2,1)S(1)} %shard_map.70.refs_1_), channel_id=1, source_target_pairs={{0,4},{2,6},{4,0},{6,2},{1,5},{3,7},{5,1},{7,3},{8,12},{10,14},{12... | collective-permute-start | bytes 294920 | tf_op jit(solution)/shard_map/ppermute | solution.py:343
  24.8 8.3 %collective-permute-start.8 = (bf16[384,128]{1,0:T(8,128)(2,1)S(1)}, bf16[384,128]{1,0:T(8,128)(2,1)S(1)}, u32[]{:S(2)}, u32[]{:S(2)}) collective-permute-start(bf16[384,128]{1,0:T(8,128)(2,1)S(1)} %shard_map.70.refs_1_), channel_id=1, source_target_pairs={{0,2},{2,0},{4,6},{6,4},{1,3},{3,1},{5,7},{7,5},{8,10},{10,8},{12,... | collective-permute-start | bytes 294920 | tf_op jit(solution)/shard_map/ppermute | solution.py:343
  27.6 6.8 %collective-permute-start.7 = (bf16[384,128]{1,0:T(8,128)(2,1)S(1)}, bf16[384,128]{1,0:T(8,128)(2,1)S(1)}, u32[]{:S(2)}, u32[]{:S(2)}) collective-permute-start(bf16[384,128]{1,0:T(8,128)(2,1)S(1)} %shard_map.70.refs_1_), channel_id=1, source_target_pairs={{0,6},{2,4},{4,2},{6,0},{1,7},{3,5},{5,3},{7,1},{8,14},{10,12},{12... | collective-permute-start | bytes 294920 | tf_op jit(solution)/shard_map/ppermute | solution.py:343
  28.9 6.2 %collective-permute-start.6 = (bf16[384,128]{1,0:T(8,128)(2,1)S(1)}, bf16[384,128]{1,0:T(8,128)(2,1)S(1)}, u32[]{:S(2)}, u32[]{:S(2)}) collective-permute-start(bf16[384,128]{1,0:T(8,128)(2,1)S(1)} %shard_map.70.refs_1_), channel_id=1, source_target_pairs={{0,8},{8,0},{16,24},{24,16},{1,9},{9,1},{17,25},{25,17},{2,10},{10... | collective-permute-start | bytes 294920 | tf_op jit(solution)/shard_map/ppermute | solution.py:343
  32.3 4.6 %collective-permute-start.11 = (bf16[384,128]{1,0:T(8,128)(2,1)S(1)}, bf16[384,128]{1,0:T(8,128)(2,1)S(1)}, u32[]{:S(2)}, u32[]{:S(2)}) collective-permute-start(bf16[384,128]{1,0:T(8,128)(2,1)S(1)} %collective-permute-done.9.refs_5_), channel_id=1, source_target_pairs={{0,8},{8,0},{16,24},{24,16},{1,9},{9,1},{17,25},{25,17},{2,10},{10... | collective-permute-start | bytes 294920 | tf_op jit(solution)/shard_map/ppermute | solution.py:343
  33.1 4.9 %collective-permute-start.10 = (bf16[384,128]{1,0:T(8,128)(2,1)S(1)}, bf16[384,128]{1,0:T(8,128)(2,1)S(1)}, u32[]{:S(2)}, u32[]{:S(2)}) collective-permute-start(bf16[384,128]{1,0:T(8,128)(2,1)S(1)} %collective-permute-done.8.refs_4_), channel_id=1, source_target_pairs={{0,8},{8,0},{16,24},{24,16},{1,9},{9,1},{17,25},{25,17},{2,10},{10... | collective-permute-start | bytes 294920 | tf_op jit(solution)/shard_map/ppermute | solution.py:343
  34.3 4.7 %collective-permute-start.12 = (bf16[384,128]{1,0:T(8,128)(2,1)S(1)}, bf16[384,128]{1,0:T(8,128)(2,1)S(1)}, u32[]{:S(2)}, u32[]{:S(2)}) collective-permute-start(bf16[384,128]{1,0:T(8,128)(2,1)S(1)} %collective-permute-done.7.refs_3_), channel_id=1, source_target_pairs={{0,8},{8,0},{16,24},{24,16},{1,9},{9,1},{17,25},{25,17},{2,10},{10... | collective-permute-start | bytes 294920 | tf_op jit(solution)/shard_map/ppermute | solution.py:343
  35.1 4.9 %collective-permute-start.13 = (bf16[1920,128]{1,0:T(8,128)(2,1)S(1)}, bf16[1920,128]{1,0:T(8,128)(2,1)S(1)}, u32[]{:S(2)}, u32[]{:S(2)}) collective-permute-start(bf16[1920,128]{1,0:T(8,128)(2,1)S(1)} %shard_map.71.state_ref), channel_id=1, source_target_pairs={{0,1},{1,0},{2,3},{3,2},{4,5},{5,4},{6,7},{7,6},{8,9},{9,8},{10,11... | collective-permute-start | bytes 1474568 | tf_op jit(solution)/shard_map/ppermute | solution.py:343
  39.0 1.6 %collective-permute-start.14 = (bf16[1152,128]{1,0:T(8,128)(2,1)S(1)}, bf16[1152,128]{1,0:T(8,128)(2,1)S(1)}, u32[]{:S(2)}, u32[]{:S(2)}) collective-permute-start(bf16[1152,128]{1,0:T(8,128)(2,1)S(1)} %shard_map.73.refs_0_), channel_id=1, source_target_pairs={{0,1},{1,0},{2,3},{3,2},{4,5},{5,4},{6,7},{7,6},{8,9},{9,8},{10,11... | collective-permute-start | bytes 884744 | tf_op jit(solution)/shard_map/ppermute | solution.py:343

commit v11 on v10

--- a/solution.py
+++ b/solution.py
@@ -358,11 +358,13 @@
     rest = (frame_len, window_back, queries)
     early = 1
 
+    order = [*range(min(2, chips - 1), 0, -1), *range(3, chips)]
+
     outgoing, keys, values = outgoing_state(keys, values)
     incoming = swap(outgoing, "core", 1, 2)
     mine = own_state(keys, values)
     own, *sends = chip_pieces(mine, incoming, chips)
-    got = [swap(sends[d - 1], "chip", d, chips) for d in reversed(range(1, chips))]
+    got = [swap(sends[d - 1], "chip", d, chips) for d in order]
     local_0, x_0, y_0 = local(0, *rest, keys, values, level_weight, own)
     state = sum_pieces(local_0, own, got, F32 if outer > 1 else BF16)
     if outer > 1:
@@ -373,8 +375,12 @@
 
     x = [slot] + [swap(slot, "chip", d, chips) for d in range(1, chips)]
     y = [swap(slot, "frame", 1, frames)]
-    y += [swap(piece, "frame", 1, frames) for piece in x[1:]]
-    places = [0, *range(chips + early - 1, 2, -1), *range(1, min(3, chips + early))]
+    x_sent = list(x)
+    if chips > 2:
+        x_sent[2], _ = lax.optimization_barrier((x[2], x[1]))
+        x_sent[1], y[0] = lax.optimization_barrier((x[1], y[0]))
+    y += [swap(piece, "frame", 1, frames) for piece in x_sent[1:]]
+    places = [0, *range(3, chips), *range(1, min(3, chips)), *range(chips, chips + early)]
     own_states = pack(x + y[:early], places, [local_1])
     other_states = swap(own_states, "core", 1, 2)
     base_0 = read_middle(chips, early, local_0, x_0, y_0, own_states)

time: 41.8 us -> 42.4 us (1.014)
  local copies, waits for them, and re-layouts: 0.04 us -> 0.66 us
  waiting for transfers between devices: 15.9 us -> 15.3 us
  starting transfers between devices: 17.3 us -> 17.8 us
    unnamed x8, local copies, waits for them, and re-layouts: 0.04 us -> 0.66 us
    ppermute x14, waiting for transfers between devices: 14.5 us -> 13.9 us  [swap(): return lax.ppermute(array, axis, [(n, n ^ mask) for n in range(size)])]
    ppermute x14, starting transfers between devices: 15.8 us -> 16.3 us  [swap(): return lax.ppermute(array, axis, [(n, n ^ mask) for n in range(size)])]
  transfers between devices with their start and end apart: 15 -> 15, of which waited for: 10 -> 11; matrix products, arithmetic and copies ran while one was open for 0% -> 0% of each run, Pallas kernels for 13% -> 13%
where the time goes in v11:
time: 42.4 us; the launch traced here: 42.3 us
  starting transfers between devices  17.8 us (42%)
  waiting for transfers between devices  15.3 us (36%)
  Pallas kernels  8.38 us (20%)
  local copies, waits for them, and re-layouts  0.66 us (2%)
    ppermute x14, starting transfers between devices, swap(): return lax.ppermute(array, axis, [(n, n ^ mask) for n in range(size)])  16.3 us
    ppermute x14, waiting for transfers between devices, swap(): return lax.ppermute(array, axis, [(n, n ^ mask) for n in range(size)])  13.9 us
    pallas_call x2, Pallas kernels, local_part(): pl.pallas_call(functools.partial(local_kernel, coefs, turn), out_shape=[p...  3.44 us
    pallas_call x2, Pallas kernels, write_late(): pl.pallas_call(functools.partial(kernel, turn, chips, early), out_shape=j...  1.9 us
    pallas_call x1, Pallas kernels, outgoing_state(): pl.pallas_call(functools.partial(first_kernel, parts), out_shape=[pltpu.V...  1.69 us
    ppermute x1, starting transfers between devices, body(): lax.ppermute(state, 'frame', [(f, (f + 1) % frames) for f in range(frames)])  1.49 us
    ppermute x1, waiting for transfers between devices, body(): lax.ppermute(state, 'frame', [(f, (f + 1) % frames) for f in range(frames)])  1.36 us
  transfers between devices with their start and end apart: 15, of which 11 were waited for; matrix products, arithmetic and copies ran while one was open for 0% of the time, Pallas kernels for 13%

profile of v11, /device:TPU:0, one launch (start us, length us, event | category | flops | bytes accessed | tf_op | source)
XLA Modules:
  0.0 42.3 jit_solution(2291178244274004092)
XLA Ops:
  0.0 1.7 %shard_map.64 = (bf16[1536,128]{1,0:T(8,128)(2,1)S(1)}, bf16[128,3072]{1,0:T(8,128)(2,1)S(1)}, bf16[128,3072]{1,0:T(8,128)(2,1)S(1)}) custom-call(bf16[128,3072]{1,0:T(8,128)(2,1)} %key_ref.1, bf16[128,3072]{1,0:T(8,128)(2,1)} %value_ref.1), custom_call_target="tpu_custom_call" | custom-call | flops 50331648 | bytes 1572864 | tf_op jit(solution)/shard_map/pallas_call | solution.py:84
  1.7 0.5 %collective-permute-start = (bf16[1536,128]{1,0:T(8,128)(2,1)S(1)}, bf16[1536,128]{1,0:T(8,128)(2,1)S(1)}, u32[]{:S(2)}, u32[]{:S(2)}) collective-permute-start(bf16[1536,128]{1,0:T(8,128)(2,1)S(1)} %get-tuple-element.23), channel_id=1, source_target_pairs={{0,1},{1,0},{2,3},{3,2},{4,5},{5,4},{6,7},{7,6},{8,9},{9,8},{10,11... | collective-permute-start | bytes 1179656 | tf_op jit(solution)/shard_map/ppermute | solution.py:343
  2.2 0.5 %shard_map.65.mine_ref = f32[1536,128]{1,0:T(8,128)S(1)} custom-call(bf16[128,3072]{1,0:T(8,128)(2,1)S(1)} %get-tuple-element.21.key_ref, bf16[128,3072]{1,0:T(8,128)(2,1)S(1)} %get-tuple-element.22.value_ref), custom_call_target="tpu_custom_call" | custom-call | flops 50331648 | bytes 1572864 | tf_op jit(solution)/shard_map/pallas_call | solution.py:104
  2.7 0.8 %collective-permute-done.other_ref = bf16[1536,128]{1,0:T(8,128)(2,1)S(1)} collective-permute-done((bf16[1536,128]{1,0:T(8,128)(2,1)S(1)}, bf16[1536,128]{1,0:T(8,128)(2,1)S(1)}, u32[]{:S(2)}, u32[]{:S(2)}) %collective-permute-start) | collective-permute-done | bytes 393248 | tf_op jit(solution)/shard_map/ppermute | solution.py:343
  3.5 0.1 shard_map.66
  3.6 4.0 %collective-permute-start.1 = (bf16[384,128]{1,0:T(8,128)(2,1)S(1)}, bf16[384,128]{1,0:T(8,128)(2,1)S(1)}, u32[]{:S(2)}, u32[]{:S(2)}) collective-permute-start(bf16[384,128]{1,0:T(8,128)(2,1)S(1)} %get-tuple-element.28), channel_id=1, source_target_pairs={{0,4},{2,6},{4,0},{6,2},{1,5},{3,7},{5,1},{7,3},{8,12},{10,14},{12... | collective-permute-start | bytes 294920 | tf_op jit(solution)/shard_map/ppermute | solution.py:343
  7.7 1.6 %collective-permute-start.2 = (bf16[384,128]{1,0:T(8,128)(2,1)S(1)}, bf16[384,128]{1,0:T(8,128)(2,1)S(1)}, u32[]{:S(2)}, u32[]{:S(2)}) collective-permute-start(bf16[384,128]{1,0:T(8,128)(2,1)S(1)} %get-tuple-element.29), channel_id=1, source_target_pairs={{0,2},{2,0},{4,6},{6,4},{1,3},{3,1},{5,7},{7,5},{8,10},{10,8},{12,... | collective-permute-start | bytes 294920 | tf_op jit(solution)/shard_map/ppermute | solution.py:343
  9.3 0.6 %copy-done.2 = s32[1,4]{1,0:T(1,128)S(1)} copy-done((s32[1,4]{1,0:T(1,128)S(1)}, s32[1,4]{1,0:T(1,128)}, u32[]{:S(2)}) %copy-start.2) | copy-done | bytes 40
  9.9 1.7 %shard_map.67 = (f32[128,1536]{1,0:T(8,128)S(1)}, bf16[128,1536]{1,0:T(8,128)(2,1)S(1)}, bf16[128,1536]{1,0:T(8,128)(2,1)S(1)}) custom-call(s32[1,4]{1,0:T(1,128)S(1)} %copy-done.2, s32[1,4]{1,0:T(1,128)S(1)} %copy-done.3, bf16[128,3072]{1,0:T(8,128)(2,1)S(1)} %copy-done, bf16[128,3072]{1,0:T(8,128)(2,1)S(1)} %get-tuple-element.21.key_ref, ...), custom_call_target="tpu_custom_call" | custom-call | flops 100663296 | bytes 2752512 | tf_op jit(solution)/shard_map/pallas_call | solution.py:251
  11.7 1.8 %collective-permute-done.1.refs_0_ = bf16[384,128]{1,0:T(8,128)(2,1)S(1)} collective-permute-done((bf16[384,128]{1,0:T(8,128)(2,1)S(1)}, bf16[384,128]{1,0:T(8,128)(2,1)S(1)}, u32[]{:S(2)}, u32[]{:S(2)}) %collective-permute-start.1) | collective-permute-done | bytes 98336 | tf_op jit(solution)/shard_map/ppermute | solution.py:343
  13.4 2.8 %collective-permute-done.3.refs_2_ = bf16[384,128]{1,0:T(8,128)(2,1)S(1)} collective-permute-done((bf16[384,128]{1,0:T(8,128)(2,1)S(1)}, bf16[384,128]{1,0:T(8,128)(2,1)S(1)}, u32[]{:S(2)}, u32[]{:S(2)}) %collective-permute-start.3) | collective-permute-done | bytes 98336 | tf_op jit(solution)/shard_map/ppermute | solution.py:343
  16.3 1.6 %collective-permute-start.5 = (bf16[384,128]{1,0:T(8,128)(2,1)S(1)}, bf16[384,128]{1,0:T(8,128)(2,1)S(1)}, u32[]{:S(2)}, u32[]{:S(2)}) collective-permute-start(bf16[384,128]{1,0:T(8,128)(2,1)S(1)} %shard_map.68.after_ref), channel_id=1, source_target_pairs={{0,16},{8,24},{16,0},{24,8},{1,17},{9,25},{17,1},{25,9},{2,18},{10... | collective-permute-start | bytes 294920 | tf_op jit(solution)/shard_map/ppermute | solution.py:343
  17.9 1.5 %collective-permute-start.4 = (bf16[384,128]{1,0:T(8,128)(2,1)S(1)}, bf16[384,128]{1,0:T(8,128)(2,1)S(1)}, u32[]{:S(2)}, u32[]{:S(2)}) collective-permute-start(bf16[384,128]{1,0:T(8,128)(2,1)S(1)} %shard_map.68.after_ref), channel_id=1, source_target_pairs={{0,8},{8,16},{16,24},{24,0},{1,9},{9,17},{17,25},{25,1},{2,10},{10... | collective-permute-start | bytes 294920 | tf_op jit(solution)/shard_map/ppermute | solution.py:373
  19.3 1.7 %shard_map.69 = (f32[128,1536]{1,0:T(8,128)S(1)}, bf16[128,1536]{1,0:T(8,128)(2,1)S(1)}, bf16[128,1536]{1,0:T(8,128)(2,1)S(1)}) custom-call(s32[1,4]{1,0:T(1,128)S(1)} %copy-done.2, s32[1,4]{1,0:T(1,128)S(1)} %copy-done.3, bf16[128,3072]{1,0:T(8,128)(2,1)S(1)} %copy-done, bf16[128,3072]{1,0:T(8,128)(2,1)S(1)} %get-tuple-element.21.key_ref, ...), custom_call_target="tpu_custom_call" | custom-call | flops 100663296 | bytes 2752512 | tf_op jit(solution)/shard_map/pallas_call | solution.py:251
  21.1 0.9 %collective-permute-done.5.first_ref = bf16[384,128]{1,0:T(8,128)(2,1)S(1)} collective-permute-done((bf16[384,128]{1,0:T(8,128)(2,1)S(1)}, bf16[384,128]{1,0:T(8,128)(2,1)S(1)}, u32[]{:S(2)}, u32[]{:S(2)}) %collective-permute-start.5) | collective-permute-done | bytes 98336 | tf_op jit(solution)/shard_map/ppermute | solution.py:343
  22.0 1.4 %collective-permute-done.4.before_ref = bf16[384,128]{1,0:T(8,128)(2,1)S(1)} collective-permute-done((bf16[384,128]{1,0:T(8,128)(2,1)S(1)}, bf16[384,128]{1,0:T(8,128)(2,1)S(1)}, u32[]{:S(2)}, u32[]{:S(2)}) %collective-permute-start.4) | collective-permute-done | bytes 98336 | tf_op jit(solution)/shard_map/ppermute | solution.py:373
  23.4 3.6 %collective-permute-start.8 = (bf16[384,128]{1,0:T(8,128)(2,1)S(1)}, bf16[384,128]{1,0:T(8,128)(2,1)S(1)}, u32[]{:S(2)}, u32[]{:S(2)}) collective-permute-start(bf16[384,128]{1,0:T(8,128)(2,1)S(1)} %shard_map.70.refs_1_), channel_id=1, source_target_pairs={{0,4},{2,6},{4,0},{6,2},{1,5},{3,7},{5,1},{7,3},{8,12},{10,14},{12... | collective-permute-start | bytes 294920 | tf_op jit(solution)/shard_map/ppermute | solution.py:343
  27.0 0.6 %collective-permute-start.9 = (bf16[384,128]{1,0:T(8,128)(2,1)S(1)}, bf16[384,128]{1,0:T(8,128)(2,1)S(1)}, u32[]{:S(2)}, u32[]{:S(2)}) collective-permute-start(bf16[384,128]{1,0:T(8,128)(2,1)S(1)} %shard_map.70.refs_1_), channel_id=1, source_target_pairs={{0,8},{8,0},{16,24},{24,16},{1,9},{9,1},{17,25},{25,17},{2,10},{10... | collective-permute-start | bytes 294920 | tf_op jit(solution)/shard_map/ppermute | solution.py:343
  27.6 1.5 %collective-permute-start.6 = (bf16[384,128]{1,0:T(8,128)(2,1)S(1)}, bf16[384,128]{1,0:T(8,128)(2,1)S(1)}, u32[]{:S(2)}, u32[]{:S(2)}) collective-permute-start(bf16[384,128]{1,0:T(8,128)(2,1)S(1)} %shard_map.70.refs_1_), channel_id=1, source_target_pairs={{0,6},{2,4},{4,2},{6,0},{1,7},{3,5},{5,3},{7,1},{8,14},{10,12},{12... | collective-permute-start | bytes 294920 | tf_op jit(solution)/shard_map/ppermute | solution.py:343
  29.1 3.1 %collective-permute-done.8.refs_4_ = bf16[384,128]{1,0:T(8,128)(2,1)S(1)} collective-permute-done((bf16[384,128]{1,0:T(8,128)(2,1)S(1)}, bf16[384,128]{1,0:T(8,128)(2,1)S(1)}, u32[]{:S(2)}, u32[]{:S(2)}) %collective-permute-start.8) | collective-permute-done | bytes 98336 | tf_op jit(solution)/shard_map/ppermute | solution.py:343
  32.3 0.6 %collective-permute-done.7.refs_3_ = bf16[384,128]{1,0:T(8,128)(2,1)S(1)} collective-permute-done((bf16[384,128]{1,0:T(8,128)(2,1)S(1)}, bf16[384,128]{1,0:T(8,128)(2,1)S(1)}, u32[]{:S(2)}, u32[]{:S(2)}) %collective-permute-start.7) | collective-permute-done | bytes 98336 | tf_op jit(solution)/shard_map/ppermute | solution.py:343
  32.9 0.7 %collective-permute-start.10 = (bf16[384,128]{1,0:T(8,128)(2,1)S(1)}, bf16[384,128]{1,0:T(8,128)(2,1)S(1)}, u32[]{:S(2)}, u32[]{:S(2)}) collective-permute-start(bf16[384,128]{1,0:T(8,128)(2,1)S(1)} %collective-permute-done.7.refs_3_), channel_id=1, source_target_pairs={{0,8},{8,0},{16,24},{24,16},{1,9},{9,1},{17,25},{25,17},{2,10},{10... | collective-permute-start | bytes 294920 | tf_op jit(solution)/shard_map/ppermute | solution.py:343
  33.6 1.3 %collective-permute-start.11 = (bf16[384,128]{1,0:T(8,128)(2,1)S(1)}, bf16[384,128]{1,0:T(8,128)(2,1)S(1)}, u32[]{:S(2)}, u32[]{:S(2)}) collective-permute-start(bf16[384,128]{1,0:T(8,128)(2,1)S(1)} %collective-permute-done.8.refs_4_), channel_id=1, source_target_pairs={{0,8},{8,0},{16,24},{24,16},{1,9},{9,1},{17,25},{25,17},{2,10},{10... | collective-permute-start | bytes 294920 | tf_op jit(solution)/shard_map/ppermute | solution.py:343
  34.9 0.7 %collective-permute-start.12 = (bf16[384,128]{1,0:T(8,128)(2,1)S(1)}, bf16[384,128]{1,0:T(8,128)(2,1)S(1)}, u32[]{:S(2)}, u32[]{:S(2)}) collective-permute-start(bf16[384,128]{1,0:T(8,128)(2,1)S(1)} %collective-permute-done.6.refs_2_), channel_id=1, source_target_pairs={{0,8},{8,0},{16,24},{24,16},{1,9},{9,1},{17,25},{25,17},{2,10},{10... | collective-permute-start | bytes 294920 | tf_op jit(solution)/shard_map/ppermute | solution.py:343
  35.8 0.3 shard_map.72.base_ref
  36.1 1.5 %collective-permute-done.10.refs_0_ = bf16[384,128]{1,0:T(8,128)(2,1)S(1)} collective-permute-done((bf16[384,128]{1,0:T(8,128)(2,1)S(1)}, bf16[384,128]{1,0:T(8,128)(2,1)S(1)}, u32[]{:S(2)}, u32[]{:S(2)}) %collective-permute-start.10) | collective-permute-done | bytes 98336 | tf_op jit(solution)/shard_map/ppermute | solution.py:343
  37.5 1.1 %collective-permute-done.11.refs_1_ = bf16[384,128]{1,0:T(8,128)(2,1)S(1)} collective-permute-done((bf16[384,128]{1,0:T(8,128)(2,1)S(1)}, bf16[384,128]{1,0:T(8,128)(2,1)S(1)}, u32[]{:S(2)}, u32[]{:S(2)}) %collective-permute-start.11) | collective-permute-done | bytes 98336 | tf_op jit(solution)/shard_map/ppermute | solution.py:343
  38.6 1.1 %collective-permute-done.12.refs_2_ = bf16[384,128]{1,0:T(8,128)(2,1)S(1)} collective-permute-done((bf16[384,128]{1,0:T(8,128)(2,1)S(1)}, bf16[384,128]{1,0:T(8,128)(2,1)S(1)}, u32[]{:S(2)}, u32[]{:S(2)}) %collective-permute-start.12) | collective-permute-done | bytes 98336 | tf_op jit(solution)/shard_map/ppermute | solution.py:343
  39.7 0.9 %shard_map.74.out_before_ref = bf16[128,3072]{1,0:T(8,128)(2,1)} custom-call(f32[128,1536]{1,0:T(8,128)S(1)} %shard_map.72.base_ref, bf16[128,1536]{1,0:T(8,128)(2,1)S(1)} %get-tuple-element.27.y_ref, bf16[1152,128]{1,0:T(8,128)(2,1)S(1)} %shard_map.73.refs_0_), custom_call_target="tpu_custom_call" | custom-call | flops 20000000000 | bytes 1024 | tf_op jit(solution)/shard_map/pallas_call | solution.py:330
  40.7 0.3 shard_map.75.refs_0_
  41.0 0.3 collective-permute-done.14.refs_2_
  41.3 0.9 %shard_map.76 = bf16[128,3072]{1,0:T(8,128)(2,1)} custom-call(bf16[128,3072]{1,0:T(8,128)(2,1)} %shard_map.74.out_before_ref, f32[128,1536]{1,0:T(8,128)S(1)} %shard_map.75.refs_0_, bf16[128,1536]{1,0:T(8,128)(2,1)S(1)} %get-tuple-element.36.y_ref.refs_1_, bf16[1152,128]{1,0:T(8,128)(2,1)S(1)} %collective-permute-done.14.refs_2_), custom_call_target="tpu_custom_call", output_to_operand_aliasing={{}: (0, {})} | custom-call | flops 1024 | bytes 1024 | tf_op jit(solution)/shard_map/pallas_call | solution.py:330
  (19 shorter events, 0.3 us)
Async XLA Ops:
  1.7 1.8 %collective-permute-start = (bf16[1536,128]{1,0:T(8,128)(2,1)S(1)}, bf16[1536,128]{1,0:T(8,128)(2,1)S(1)}, u32[]{:S(2)}, u32[]{:S(2)}) collective-permute-start(bf16[1536,128]{1,0:T(8,128)(2,1)S(1)} %get-tuple-element.23), channel_id=1, source_target_pairs={{0,1},{1,0},{2,3},{3,2},{4,5},{5,4},{6,7},{7,6},{8,9},{9,8},{10,11... | collective-permute-start | bytes 1179656 | tf_op jit(solution)/shard_map/ppermute | solution.py:343
  2.7 6.6 %copy-start = (bf16[128,3072]{1,0:T(8,128)(2,1)S(1)}, bf16[128,3072]{1,0:T(8,128)(2,1)}, u32[]{:S(2)}) copy-start(bf16[128,3072]{1,0:T(8,128)(2,1)} %query_ref.3) | copy-start | bytes 2359300
  2.7 6.6 %copy-start.1 = (f32[3,24,128]{2,1,0:T(8,128)S(1)}, f32[3,24,128]{2,1,0:T(8,128)}, u32[]{:S(2)}) copy-start(f32[3,24,128]{2,1,0:T(8,128)} %weight_ref.3) | copy-start | bytes 110596
  3.6 9.8 %collective-permute-start.1 = (bf16[384,128]{1,0:T(8,128)(2,1)S(1)}, bf16[384,128]{1,0:T(8,128)(2,1)S(1)}, u32[]{:S(2)}, u32[]{:S(2)}) collective-permute-start(bf16[384,128]{1,0:T(8,128)(2,1)S(1)} %get-tuple-element.28), channel_id=1, source_target_pairs={{0,4},{2,6},{4,0},{6,2},{1,5},{3,7},{5,1},{7,3},{8,12},{10,14},{12... | collective-permute-start | bytes 294920 | tf_op jit(solution)/shard_map/ppermute | solution.py:343
  7.7 5.8 %collective-permute-start.2 = (bf16[384,128]{1,0:T(8,128)(2,1)S(1)}, bf16[384,128]{1,0:T(8,128)(2,1)S(1)}, u32[]{:S(2)}, u32[]{:S(2)}) collective-permute-start(bf16[384,128]{1,0:T(8,128)(2,1)S(1)} %get-tuple-element.29), channel_id=1, source_target_pairs={{0,2},{2,0},{4,6},{6,4},{1,3},{3,1},{5,7},{7,5},{8,10},{10,8},{12,... | collective-permute-start | bytes 294920 | tf_op jit(solution)/shard_map/ppermute | solution.py:343
  9.3 0.7 %copy-start.2 = (s32[1,4]{1,0:T(1,128)S(1)}, s32[1,4]{1,0:T(1,128)}, u32[]{:S(2)}) copy-start(s32[1,4]{1,0:T(1,128)} %length_ref.3) | copy-start | bytes 52
  9.3 0.7 %copy-start.3 = (s32[1,4]{1,0:T(1,128)S(1)}, s32[1,4]{1,0:T(1,128)}, u32[]{:S(2)}) copy-start(s32[1,4]{1,0:T(1,128)} %back_ref.3) | copy-start | bytes 52
  9.3 6.9 %collective-permute-start.3 = (bf16[384,128]{1,0:T(8,128)(2,1)S(1)}, bf16[384,128]{1,0:T(8,128)(2,1)S(1)}, u32[]{:S(2)}, u32[]{:S(2)}) collective-permute-start(bf16[384,128]{1,0:T(8,128)(2,1)S(1)} %get-tuple-element.30), channel_id=1, source_target_pairs={{0,6},{2,4},{4,2},{6,0},{1,7},{3,5},{5,3},{7,1},{8,14},{10,12},{12... | collective-permute-start | bytes 294920 | tf_op jit(solution)/shard_map/ppermute | solution.py:343
  16.3 5.7 %collective-permute-start.5 = (bf16[384,128]{1,0:T(8,128)(2,1)S(1)}, bf16[384,128]{1,0:T(8,128)(2,1)S(1)}, u32[]{:S(2)}, u32[]{:S(2)}) collective-permute-start(bf16[384,128]{1,0:T(8,128)(2,1)S(1)} %shard_map.68.after_ref), channel_id=1, source_target_pairs={{0,16},{8,24},{16,0},{24,8},{1,17},{9,25},{17,1},{25,9},{2,18},{10... | collective-permute-start | bytes 294920 | tf_op jit(solution)/shard_map/ppermute | solution.py:343
  17.9 5.5 %collective-permute-start.4 = (bf16[384,128]{1,0:T(8,128)(2,1)S(1)}, bf16[384,128]{1,0:T(8,128)(2,1)S(1)}, u32[]{:S(2)}, u32[]{:S(2)}) collective-permute-start(bf16[384,128]{1,0:T(8,128)(2,1)S(1)} %shard_map.68.after_ref), channel_id=1, source_target_pairs={{0,8},{8,16},{16,24},{24,0},{1,9},{9,17},{17,25},{25,1},{2,10},{10... | collective-permute-start | bytes 294920 | tf_op jit(solution)/shard_map/ppermute | solution.py:373
  23.4 8.9 %collective-permute-start.8 = (bf16[384,128]{1,0:T(8,128)(2,1)S(1)}, bf16[384,128]{1,0:T(8,128)(2,1)S(1)}, u32[]{:S(2)}, u32[]{:S(2)}) collective-permute-start(bf16[384,128]{1,0:T(8,128)(2,1)S(1)} %shard_map.70.refs_1_), channel_id=1, source_target_pairs={{0,4},{2,6},{4,0},{6,2},{1,5},{3,7},{5,1},{7,3},{8,12},{10,14},{12... | collective-permute-start | bytes 294920 | tf_op jit(solution)/shard_map/ppermute | solution.py:343
  27.0 5.9 %collective-permute-start.7 = (bf16[384,128]{1,0:T(8,128)(2,1)S(1)}, bf16[384,128]{1,0:T(8,128)(2,1)S(1)}, u32[]{:S(2)}, u32[]{:S(2)}) collective-permute-start(bf16[384,128]{1,0:T(8,128)(2,1)S(1)} %shard_map.70.refs_1_), channel_id=1, source_target_pairs={{0,2},{2,0},{4,6},{6,4},{1,3},{3,1},{5,7},{7,5},{8,10},{10,8},{12,... | collective-permute-start | bytes 294920 | tf_op jit(solution)/shard_map/ppermute | solution.py:343
  27.0 5.9 %collective-permute-start.9 = (bf16[384,128]{1,0:T(8,128)(2,1)S(1)}, bf16[384,128]{1,0:T(8,128)(2,1)S(1)}, u32[]{:S(2)}, u32[]{:S(2)}) collective-permute-start(bf16[384,128]{1,0:T(8,128)(2,1)S(1)} %shard_map.70.refs_1_), channel_id=1, source_target_pairs={{0,8},{8,0},{16,24},{24,16},{1,9},{9,1},{17,25},{25,17},{2,10},{10... | collective-permute-start | bytes 294920 | tf_op jit(solution)/shard_map/ppermute | solution.py:343
  27.6 7.3 %collective-permute-start.6 = (bf16[384,128]{1,0:T(8,128)(2,1)S(1)}, bf16[384,128]{1,0:T(8,128)(2,1)S(1)}, u32[]{:S(2)}, u32[]{:S(2)}) collective-permute-start(bf16[384,128]{1,0:T(8,128)(2,1)S(1)} %shard_map.70.refs_1_), channel_id=1, source_target_pairs={{0,6},{2,4},{4,2},{6,0},{1,7},{3,5},{5,3},{7,1},{8,14},{10,12},{12... | collective-permute-start | bytes 294920 | tf_op jit(solution)/shard_map/ppermute | solution.py:343
  32.9 4.6 %collective-permute-start.10 = (bf16[384,128]{1,0:T(8,128)(2,1)S(1)}, bf16[384,128]{1,0:T(8,128)(2,1)S(1)}, u32[]{:S(2)}, u32[]{:S(2)}) collective-permute-start(bf16[384,128]{1,0:T(8,128)(2,1)S(1)} %collective-permute-done.7.refs_3_), channel_id=1, source_target_pairs={{0,8},{8,0},{16,24},{24,16},{1,9},{9,1},{17,25},{25,17},{2,10},{10... | collective-permute-start | bytes 294920 | tf_op jit(solution)/shard_map/ppermute | solution.py:343
  33.6 5.0 %collective-permute-start.11 = (bf16[384,128]{1,0:T(8,128)(2,1)S(1)}, bf16[384,128]{1,0:T(8,128)(2,1)S(1)}, u32[]{:S(2)}, u32[]{:S(2)}) collective-permute-start(bf16[384,128]{1,0:T(8,128)(2,1)S(1)} %collective-permute-done.8.refs_4_), channel_id=1, source_target_pairs={{0,8},{8,0},{16,24},{24,16},{1,9},{9,1},{17,25},{25,17},{2,10},{10... | collective-permute-start | bytes 294920 | tf_op jit(solution)/shard_map/ppermute | solution.py:343
  34.9 4.7 %collective-permute-start.12 = (bf16[384,128]{1,0:T(8,128)(2,1)S(1)}, bf16[384,128]{1,0:T(8,128)(2,1)S(1)}, u32[]{:S(2)}, u32[]{:S(2)}) collective-permute-start(bf16[384,128]{1,0:T(8,128)(2,1)S(1)} %collective-permute-done.6.refs_2_), channel_id=1, source_target_pairs={{0,8},{8,0},{16,24},{24,16},{1,9},{9,1},{17,25},{25,17},{2,10},{10... | collective-permute-start | bytes 294920 | tf_op jit(solution)/shard_map/ppermute | solution.py:343
  35.7 5.0 %collective-permute-start.13 = (bf16[1920,128]{1,0:T(8,128)(2,1)S(1)}, bf16[1920,128]{1,0:T(8,128)(2,1)S(1)}, u32[]{:S(2)}, u32[]{:S(2)}) collective-permute-start(bf16[1920,128]{1,0:T(8,128)(2,1)S(1)} %shard_map.71.state_ref), channel_id=1, source_target_pairs={{0,1},{1,0},{2,3},{3,2},{4,5},{5,4},{6,7},{7,6},{8,9},{9,8},{10,11... | collective-permute-start | bytes 1474568 | tf_op jit(solution)/shard_map/ppermute | solution.py:343
  39.7 1.6 %collective-permute-start.14 = (bf16[1152,128]{1,0:T(8,128)(2,1)S(1)}, bf16[1152,128]{1,0:T(8,128)(2,1)S(1)}, u32[]{:S(2)}, u32[]{:S(2)}) collective-permute-start(bf16[1152,128]{1,0:T(8,128)(2,1)S(1)} %shard_map.73.refs_0_), channel_id=1, source_target_pairs={{0,1},{1,0},{2,3},{3,2},{4,5},{5,4},{6,7},{7,6},{8,9},{9,8},{10,11... | collective-permute-start | bytes 884744 | tf_op jit(solution)/shard_map/ppermute | solution.py:343

commit v12 on v10

--- a/solution.py
+++ b/solution.py
@@ -287,14 +287,14 @@
             out_ref[:, at] = result
 
 
-def read_middle(chips, early, local, x, y, states):
+def read_middle(cost, chips, early, local, x, y, states):
     return pl.pallas_call(
         functools.partial(middle_kernel, chips, early),
         out_shape=pltpu.VMEM(local.shape, F32),
         in_specs=[WHOLE] * 4,
         out_specs=WHOLE,
         compiler_params=PARAMS,
-        cost_estimate=SMALL,
+        cost_estimate=cost,
     )(*in_vmem(local, x, y, states))
 
 
@@ -304,7 +304,10 @@
     half = core_heads()[turn]
     copies = []
     for d in range(chips):
-        states = [(y_ref, state_refs[0], (d - early) * rows)] if d >= early else []
+        states = []
+        if d >= early:
+            ref = state_refs[0] if d < chips - 1 else state_refs[-1]
+            states.append((y_ref, ref, (d - early) * rows if d < chips - 1 else 0))
         for at, result in read_heads(d, chips, base_ref, states):
             held[:, at] = result.astype(BF16)
         count = HEADS // 2 // chips
@@ -358,11 +361,13 @@
     rest = (frame_len, window_back, queries)
     early = 1
 
+    order = [*range(min(2, chips - 1), 0, -1), *range(3, chips)]
+
     outgoing, keys, values = outgoing_state(keys, values)
     incoming = swap(outgoing, "core", 1, 2)
     mine = own_state(keys, values)
     own, *sends = chip_pieces(mine, incoming, chips)
-    got = [swap(sends[d - 1], "chip", d, chips) for d in reversed(range(1, chips))]
+    got = [swap(sends[d - 1], "chip", d, chips) for d in order]
     local_0, x_0, y_0 = local(0, *rest, keys, values, level_weight, own)
     state = sum_pieces(local_0, own, got, F32 if outer > 1 else BF16)
     if outer > 1:
@@ -377,11 +382,14 @@
     places = [0, *range(chips + early - 1, 2, -1), *range(1, min(3, chips + early))]
     own_states = pack(x + y[:early], places, [local_1])
     other_states = swap(own_states, "core", 1, 2)
-    base_0 = read_middle(chips, early, local_0, x_0, y_0, own_states)
-    base_1 = read_middle(chips, early, local_1, x_1, y_1, other_states)
-    late = y[early:]
-    late_own = [pack(late, list(range(len(late))), [])] if late else []
+    base_0 = read_middle(SMALL, chips, early, local_0, x_0, y_0, own_states)
+    base_1 = read_middle(LARGE, chips, early, local_1, x_1, y_1, other_states)
+    late_own = [pack(y[early:-1], list(range(chips - 1 - early)), [])] if chips - 1 > early else []
     late_other = [swap(piece, "core", 1, 2) for piece in late_own]
+    if chips > early:
+        last = y[-1]
+        late_own.append(last)
+        late_other.append(swap(last, "core", 1, 2))
     out = write_late(0, chips, early, base_0, y_0, late_own)
     return write_late(1, chips, early, base_1, y_1, late_other, out)
 

time: 41.8 us -> 42.3 us (1.012)
  waiting for transfers between devices: 15.9 us -> 14 us
  starting transfers between devices: 17.3 us -> 18.9 us
  local copies, waits for them, and re-layouts: 0.04 us -> 0.66 us
    ppermute x14 -> x15, waiting for transfers between devices: 14.5 us -> 12.6 us  [swap(): return lax.ppermute(array, axis, [(n, n ^ mask) for n in range(size)])]
    ppermute x14 -> x15, starting transfers between devices: 15.8 us -> 17.4 us  [swap(): return lax.ppermute(array, axis, [(n, n ^ mask) for n in range(size)])]
    unnamed x8, local copies, waits for them, and re-layouts: 0.04 us -> 0.66 us
  transfers between devices with their start and end apart: 15 -> 16, of which waited for: 10 -> 9; matrix products, arithmetic and copies ran while one was open for 0% -> 0% of each run, Pallas kernels for 13% -> 13%
where the time goes in v12:
time: 42.3 us; the launch traced here: 42.1 us
  starting transfers between devices  18.9 us (45%)
  waiting for transfers between devices  14 us (33%)
  Pallas kernels  8.36 us (20%)
  local copies, waits for them, and re-layouts  0.66 us (2%)
    ppermute x15, starting transfers between devices, swap(): return lax.ppermute(array, axis, [(n, n ^ mask) for n in range(size)])  17.4 us
    ppermute x15, waiting for transfers between devices, swap(): return lax.ppermute(array, axis, [(n, n ^ mask) for n in range(size)])  12.6 us
    pallas_call x2, Pallas kernels, local_part(): pl.pallas_call(functools.partial(local_kernel, coefs, turn), out_shape=[p...  3.43 us
    pallas_call x2, Pallas kernels, write_late(): pl.pallas_call(functools.partial(kernel, turn, chips, early), out_shape=j...  1.89 us
    pallas_call x1, Pallas kernels, outgoing_state(): pl.pallas_call(functools.partial(first_kernel, parts), out_shape=[pltpu.V...  1.69 us
    ppermute x1, starting transfers between devices, body(): lax.ppermute(state, 'frame', [(f, (f + 1) % frames) for f in range(frames)])  1.49 us
    ppermute x1, waiting for transfers between devices, body(): lax.ppermute(state, 'frame', [(f, (f + 1) % frames) for f in range(frames)])  1.36 us
  transfers between devices with their start and end apart: 16, of which 9 were waited for; matrix products, arithmetic and copies ran while one was open for 0% of the time, Pallas kernels for 13%

profile of v12, /device:TPU:0, one launch (start us, length us, event | category | flops | bytes accessed | tf_op | source)
XLA Modules:
  0.0 42.1 jit_solution(16044453231347814736)
XLA Ops:
  0.0 1.7 %shard_map.64 = (bf16[1536,128]{1,0:T(8,128)(2,1)S(1)}, bf16[128,3072]{1,0:T(8,128)(2,1)S(1)}, bf16[128,3072]{1,0:T(8,128)(2,1)S(1)}) custom-call(bf16[128,3072]{1,0:T(8,128)(2,1)} %key_ref.1, bf16[128,3072]{1,0:T(8,128)(2,1)} %value_ref.1), custom_call_target="tpu_custom_call" | custom-call | flops 50331648 | bytes 1572864 | tf_op jit(solution)/shard_map/pallas_call | solution.py:84
  1.7 0.5 %collective-permute-start = (bf16[1536,128]{1,0:T(8,128)(2,1)S(1)}, bf16[1536,128]{1,0:T(8,128)(2,1)S(1)}, u32[]{:S(2)}, u32[]{:S(2)}) collective-permute-start(bf16[1536,128]{1,0:T(8,128)(2,1)S(1)} %get-tuple-element.20), channel_id=1, source_target_pairs={{0,1},{1,0},{2,3},{3,2},{4,5},{5,4},{6,7},{7,6},{8,9},{9,8},{10,11... | collective-permute-start | bytes 1179656 | tf_op jit(solution)/shard_map/ppermute | solution.py:346
  2.2 0.5 %shard_map.65.mine_ref = f32[1536,128]{1,0:T(8,128)S(1)} custom-call(bf16[128,3072]{1,0:T(8,128)(2,1)S(1)} %get-tuple-element.18.key_ref, bf16[128,3072]{1,0:T(8,128)(2,1)S(1)} %get-tuple-element.19.value_ref), custom_call_target="tpu_custom_call" | custom-call | flops 50331648 | bytes 1572864 | tf_op jit(solution)/shard_map/pallas_call | solution.py:104
  2.7 0.8 %collective-permute-done.other_ref = bf16[1536,128]{1,0:T(8,128)(2,1)S(1)} collective-permute-done((bf16[1536,128]{1,0:T(8,128)(2,1)S(1)}, bf16[1536,128]{1,0:T(8,128)(2,1)S(1)}, u32[]{:S(2)}, u32[]{:S(2)}) %collective-permute-start) | collective-permute-done | bytes 393248 | tf_op jit(solution)/shard_map/ppermute | solution.py:346
  3.5 0.1 shard_map.66
  3.6 4.0 %collective-permute-start.1 = (bf16[384,128]{1,0:T(8,128)(2,1)S(1)}, bf16[384,128]{1,0:T(8,128)(2,1)S(1)}, u32[]{:S(2)}, u32[]{:S(2)}) collective-permute-start(bf16[384,128]{1,0:T(8,128)(2,1)S(1)} %get-tuple-element.25), channel_id=1, source_target_pairs={{0,4},{2,6},{4,0},{6,2},{1,5},{3,7},{5,1},{7,3},{8,12},{10,14},{12... | collective-permute-start | bytes 294920 | tf_op jit(solution)/shard_map/ppermute | solution.py:346
  7.7 1.6 %collective-permute-start.2 = (bf16[384,128]{1,0:T(8,128)(2,1)S(1)}, bf16[384,128]{1,0:T(8,128)(2,1)S(1)}, u32[]{:S(2)}, u32[]{:S(2)}) collective-permute-start(bf16[384,128]{1,0:T(8,128)(2,1)S(1)} %get-tuple-element.26), channel_id=1, source_target_pairs={{0,2},{2,0},{4,6},{6,4},{1,3},{3,1},{5,7},{7,5},{8,10},{10,8},{12,... | collective-permute-start | bytes 294920 | tf_op jit(solution)/shard_map/ppermute | solution.py:346
  9.3 0.6 %copy-done.2 = s32[1,4]{1,0:T(1,128)S(1)} copy-done((s32[1,4]{1,0:T(1,128)S(1)}, s32[1,4]{1,0:T(1,128)}, u32[]{:S(2)}) %copy-start.2) | copy-done | bytes 40
  9.9 1.7 %shard_map.67 = (f32[128,1536]{1,0:T(8,128)S(1)}, bf16[128,1536]{1,0:T(8,128)(2,1)S(1)}, bf16[128,1536]{1,0:T(8,128)(2,1)S(1)}) custom-call(s32[1,4]{1,0:T(1,128)S(1)} %copy-done.2, s32[1,4]{1,0:T(1,128)S(1)} %copy-done.3, bf16[128,3072]{1,0:T(8,128)(2,1)S(1)} %copy-done, bf16[128,3072]{1,0:T(8,128)(2,1)S(1)} %get-tuple-element.18.key_ref, ...), custom_call_target="tpu_custom_call" | custom-call | flops 100663296 | bytes 2752512 | tf_op jit(solution)/shard_map/pallas_call | solution.py:251
  11.7 1.8 %collective-permute-done.1.refs_0_ = bf16[384,128]{1,0:T(8,128)(2,1)S(1)} collective-permute-done((bf16[384,128]{1,0:T(8,128)(2,1)S(1)}, bf16[384,128]{1,0:T(8,128)(2,1)S(1)}, u32[]{:S(2)}, u32[]{:S(2)}) %collective-permute-start.1) | collective-permute-done | bytes 98336 | tf_op jit(solution)/shard_map/ppermute | solution.py:346
  13.4 2.8 %collective-permute-done.3.refs_2_ = bf16[384,128]{1,0:T(8,128)(2,1)S(1)} collective-permute-done((bf16[384,128]{1,0:T(8,128)(2,1)S(1)}, bf16[384,128]{1,0:T(8,128)(2,1)S(1)}, u32[]{:S(2)}, u32[]{:S(2)}) %collective-permute-start.3) | collective-permute-done | bytes 98336 | tf_op jit(solution)/shard_map/ppermute | solution.py:346
  16.3 1.6 %collective-permute-start.5 = (bf16[384,128]{1,0:T(8,128)(2,1)S(1)}, bf16[384,128]{1,0:T(8,128)(2,1)S(1)}, u32[]{:S(2)}, u32[]{:S(2)}) collective-permute-start(bf16[384,128]{1,0:T(8,128)(2,1)S(1)} %shard_map.68.after_ref), channel_id=1, source_target_pairs={{0,16},{8,24},{16,0},{24,8},{1,17},{9,25},{17,1},{25,9},{2,18},{10... | collective-permute-start | bytes 294920 | tf_op jit(solution)/shard_map/ppermute | solution.py:346
  17.9 1.5 %collective-permute-start.4 = (bf16[384,128]{1,0:T(8,128)(2,1)S(1)}, bf16[384,128]{1,0:T(8,128)(2,1)S(1)}, u32[]{:S(2)}, u32[]{:S(2)}) collective-permute-start(bf16[384,128]{1,0:T(8,128)(2,1)S(1)} %shard_map.68.after_ref), channel_id=1, source_target_pairs={{0,8},{8,16},{16,24},{24,0},{1,9},{9,17},{17,25},{25,1},{2,10},{10... | collective-permute-start | bytes 294920 | tf_op jit(solution)/shard_map/ppermute | solution.py:376
  19.3 1.7 %shard_map.69 = (f32[128,1536]{1,0:T(8,128)S(1)}, bf16[128,1536]{1,0:T(8,128)(2,1)S(1)}, bf16[128,1536]{1,0:T(8,128)(2,1)S(1)}) custom-call(s32[1,4]{1,0:T(1,128)S(1)} %copy-done.2, s32[1,4]{1,0:T(1,128)S(1)} %copy-done.3, bf16[128,3072]{1,0:T(8,128)(2,1)S(1)} %copy-done, bf16[128,3072]{1,0:T(8,128)(2,1)S(1)} %get-tuple-element.18.key_ref, ...), custom_call_target="tpu_custom_call" | custom-call | flops 100663296 | bytes 2752512 | tf_op jit(solution)/shard_map/pallas_call | solution.py:251
  21.1 0.9 %collective-permute-done.5.first_ref = bf16[384,128]{1,0:T(8,128)(2,1)S(1)} collective-permute-done((bf16[384,128]{1,0:T(8,128)(2,1)S(1)}, bf16[384,128]{1,0:T(8,128)(2,1)S(1)}, u32[]{:S(2)}, u32[]{:S(2)}) %collective-permute-start.5) | collective-permute-done | bytes 98336 | tf_op jit(solution)/shard_map/ppermute | solution.py:346
  22.0 1.4 %collective-permute-done.4.before_ref = bf16[384,128]{1,0:T(8,128)(2,1)S(1)} collective-permute-done((bf16[384,128]{1,0:T(8,128)(2,1)S(1)}, bf16[384,128]{1,0:T(8,128)(2,1)S(1)}, u32[]{:S(2)}, u32[]{:S(2)}) %collective-permute-start.4) | collective-permute-done | bytes 98336 | tf_op jit(solution)/shard_map/ppermute | solution.py:376
  23.4 3.6 %collective-permute-start.9 = (bf16[384,128]{1,0:T(8,128)(2,1)S(1)}, bf16[384,128]{1,0:T(8,128)(2,1)S(1)}, u32[]{:S(2)}, u32[]{:S(2)}) collective-permute-start(bf16[384,128]{1,0:T(8,128)(2,1)S(1)} %shard_map.70.refs_1_), channel_id=1, source_target_pairs={{0,4},{2,6},{4,0},{6,2},{1,5},{3,7},{5,1},{7,3},{8,12},{10,14},{12... | collective-permute-start | bytes 294920 | tf_op jit(solution)/shard_map/ppermute | solution.py:346
  27.0 1.5 %collective-permute-start.7 = (bf16[384,128]{1,0:T(8,128)(2,1)S(1)}, bf16[384,128]{1,0:T(8,128)(2,1)S(1)}, u32[]{:S(2)}, u32[]{:S(2)}) collective-permute-start(bf16[384,128]{1,0:T(8,128)(2,1)S(1)} %shard_map.70.refs_1_), channel_id=1, source_target_pairs={{0,6},{2,4},{4,2},{6,0},{1,7},{3,5},{5,3},{7,1},{8,14},{10,12},{12... | collective-permute-start | bytes 294920 | tf_op jit(solution)/shard_map/ppermute | solution.py:346
  28.6 0.6 %collective-permute-start.6 = (bf16[384,128]{1,0:T(8,128)(2,1)S(1)}, bf16[384,128]{1,0:T(8,128)(2,1)S(1)}, u32[]{:S(2)}, u32[]{:S(2)}) collective-permute-start(bf16[384,128]{1,0:T(8,128)(2,1)S(1)} %shard_map.70.refs_1_), channel_id=1, source_target_pairs={{0,8},{8,0},{16,24},{24,16},{1,9},{9,1},{17,25},{25,17},{2,10},{10... | collective-permute-start | bytes 294920 | tf_op jit(solution)/shard_map/ppermute | solution.py:346
  29.1 3.2 %collective-permute-done.9.refs_5_ = bf16[384,128]{1,0:T(8,128)(2,1)S(1)} collective-permute-done((bf16[384,128]{1,0:T(8,128)(2,1)S(1)}, bf16[384,128]{1,0:T(8,128)(2,1)S(1)}, u32[]{:S(2)}, u32[]{:S(2)}) %collective-permute-start.9) | collective-permute-done | bytes 98336 | tf_op jit(solution)/shard_map/ppermute | solution.py:346
  32.3 1.8 %collective-permute-start.11 = (bf16[384,128]{1,0:T(8,128)(2,1)S(1)}, bf16[384,128]{1,0:T(8,128)(2,1)S(1)}, u32[]{:S(2)}, u32[]{:S(2)}) collective-permute-start(bf16[384,128]{1,0:T(8,128)(2,1)S(1)} %collective-permute-done.9.refs_5_), channel_id=1, source_target_pairs={{0,8},{8,0},{16,24},{24,16},{1,9},{9,1},{17,25},{25,17},{2,10},{10... | collective-permute-start | bytes 294920 | tf_op jit(solution)/shard_map/ppermute | solution.py:346
  34.2 0.4 collective-permute-start.10
  34.6 1.6 %collective-permute-start.12 = (bf16[384,128]{1,0:T(8,128)(2,1)S(1)}, bf16[384,128]{1,0:T(8,128)(2,1)S(1)}, u32[]{:S(2)}, u32[]{:S(2)}) collective-permute-start(bf16[384,128]{1,0:T(8,128)(2,1)S(1)} %collective-permute-done.7.refs_3_), channel_id=1, source_target_pairs={{0,8},{8,0},{16,24},{24,16},{1,9},{9,1},{17,25},{25,17},{2,10},{10... | collective-permute-start | bytes 294920 | tf_op jit(solution)/shard_map/ppermute | solution.py:346
  36.3 0.1 collective-permute-start.13
  36.3 0.3 shard_map.72.base_ref
  36.6 0.3 collective-permute-done.11.refs_1_
  37.0 1.8 %collective-permute-done.10.refs_0_ = bf16[384,128]{1,0:T(8,128)(2,1)S(1)} collective-permute-done((bf16[384,128]{1,0:T(8,128)(2,1)S(1)}, bf16[384,128]{1,0:T(8,128)(2,1)S(1)}, u32[]{:S(2)}, u32[]{:S(2)}) %collective-permute-start.10) | collective-permute-done | bytes 98336 | tf_op jit(solution)/shard_map/ppermute | solution.py:346
  38.8 0.1 collective-permute-start.14
  38.9 1.0 %collective-permute-done.12.refs_1_ = bf16[384,128]{1,0:T(8,128)(2,1)S(1)} collective-permute-done((bf16[384,128]{1,0:T(8,128)(2,1)S(1)}, bf16[384,128]{1,0:T(8,128)(2,1)S(1)}, u32[]{:S(2)}, u32[]{:S(2)}) %collective-permute-start.12) | collective-permute-done | bytes 98336 | tf_op jit(solution)/shard_map/ppermute | solution.py:346
  39.9 1.0 %shard_map.74.out_before_ref = bf16[128,3072]{1,0:T(8,128)(2,1)} custom-call(f32[128,1536]{1,0:T(8,128)S(1)} %shard_map.72.base_ref, bf16[128,1536]{1,0:T(8,128)(2,1)S(1)} %get-tuple-element.24.y_ref, bf16[768,128]{1,0:T(8,128)(2,1)S(1)} %shard_map.73.refs_0_, bf16[384,128]{1,0:T(8,128)(2,1)S(1)} %collective-permute-done.12.refs_1_), custom_call_target="tpu_custom_call" | custom-call | flops 20000000000 | bytes 1024 | tf_op jit(solution)/shard_map/pallas_call | solution.py:333
  40.8 0.3 shard_map.75.refs_0_
  41.2 0.9 %shard_map.76 = bf16[128,3072]{1,0:T(8,128)(2,1)} custom-call(bf16[128,3072]{1,0:T(8,128)(2,1)} %shard_map.74.out_before_ref, f32[128,1536]{1,0:T(8,128)S(1)} %shard_map.75.refs_0_, bf16[128,1536]{1,0:T(8,128)(2,1)S(1)} %get-tuple-element.30.y_ref.refs_1_, bf16[768,128]{1,0:T(8,128)(2,1)S(1)} %collective-permute-done.14.refs_2_, ...), custom_call_target="tpu_custom_call", output_to_operand_aliasing={{}: (0, {})} | custom-call | flops 1024 | bytes 1024 | tf_op jit(solution)/shard_map/pallas_call | solution.py:333
  (21 shorter events, 0.2 us)
Async XLA Ops:
  1.7 1.8 %collective-permute-start = (bf16[1536,128]{1,0:T(8,128)(2,1)S(1)}, bf16[1536,128]{1,0:T(8,128)(2,1)S(1)}, u32[]{:S(2)}, u32[]{:S(2)}) collective-permute-start(bf16[1536,128]{1,0:T(8,128)(2,1)S(1)} %get-tuple-element.20), channel_id=1, source_target_pairs={{0,1},{1,0},{2,3},{3,2},{4,5},{5,4},{6,7},{7,6},{8,9},{9,8},{10,11... | collective-permute-start | bytes 1179656 | tf_op jit(solution)/shard_map/ppermute | solution.py:346
  2.7 6.6 %copy-start = (bf16[128,3072]{1,0:T(8,128)(2,1)S(1)}, bf16[128,3072]{1,0:T(8,128)(2,1)}, u32[]{:S(2)}) copy-start(bf16[128,3072]{1,0:T(8,128)(2,1)} %query_ref.3) | copy-start | bytes 2359300
  2.7 6.6 %copy-start.1 = (f32[3,24,128]{2,1,0:T(8,128)S(1)}, f32[3,24,128]{2,1,0:T(8,128)}, u32[]{:S(2)}) copy-start(f32[3,24,128]{2,1,0:T(8,128)} %weight_ref.3) | copy-start | bytes 110596
  3.6 9.8 %collective-permute-start.1 = (bf16[384,128]{1,0:T(8,128)(2,1)S(1)}, bf16[384,128]{1,0:T(8,128)(2,1)S(1)}, u32[]{:S(2)}, u32[]{:S(2)}) collective-permute-start(bf16[384,128]{1,0:T(8,128)(2,1)S(1)} %get-tuple-element.25), channel_id=1, source_target_pairs={{0,4},{2,6},{4,0},{6,2},{1,5},{3,7},{5,1},{7,3},{8,12},{10,14},{12... | collective-permute-start | bytes 294920 | tf_op jit(solution)/shard_map/ppermute | solution.py:346
  7.7 5.8 %collective-permute-start.2 = (bf16[384,128]{1,0:T(8,128)(2,1)S(1)}, bf16[384,128]{1,0:T(8,128)(2,1)S(1)}, u32[]{:S(2)}, u32[]{:S(2)}) collective-permute-start(bf16[384,128]{1,0:T(8,128)(2,1)S(1)} %get-tuple-element.26), channel_id=1, source_target_pairs={{0,2},{2,0},{4,6},{6,4},{1,3},{3,1},{5,7},{7,5},{8,10},{10,8},{12,... | collective-permute-start | bytes 294920 | tf_op jit(solution)/shard_map/ppermute | solution.py:346
  9.3 0.7 %copy-start.2 = (s32[1,4]{1,0:T(1,128)S(1)}, s32[1,4]{1,0:T(1,128)}, u32[]{:S(2)}) copy-start(s32[1,4]{1,0:T(1,128)} %length_ref.3) | copy-start | bytes 52
  9.3 0.7 %copy-start.3 = (s32[1,4]{1,0:T(1,128)S(1)}, s32[1,4]{1,0:T(1,128)}, u32[]{:S(2)}) copy-start(s32[1,4]{1,0:T(1,128)} %back_ref.3) | copy-start | bytes 52
  9.3 6.9 %collective-permute-start.3 = (bf16[384,128]{1,0:T(8,128)(2,1)S(1)}, bf16[384,128]{1,0:T(8,128)(2,1)S(1)}, u32[]{:S(2)}, u32[]{:S(2)}) collective-permute-start(bf16[384,128]{1,0:T(8,128)(2,1)S(1)} %get-tuple-element.27), channel_id=1, source_target_pairs={{0,6},{2,4},{4,2},{6,0},{1,7},{3,5},{5,3},{7,1},{8,14},{10,12},{12... | collective-permute-start | bytes 294920 | tf_op jit(solution)/shard_map/ppermute | solution.py:346
  16.3 5.7 %collective-permute-start.5 = (bf16[384,128]{1,0:T(8,128)(2,1)S(1)}, bf16[384,128]{1,0:T(8,128)(2,1)S(1)}, u32[]{:S(2)}, u32[]{:S(2)}) collective-permute-start(bf16[384,128]{1,0:T(8,128)(2,1)S(1)} %shard_map.68.after_ref), channel_id=1, source_target_pairs={{0,16},{8,24},{16,0},{24,8},{1,17},{9,25},{17,1},{25,9},{2,18},{10... | collective-permute-start | bytes 294920 | tf_op jit(solution)/shard_map/ppermute | solution.py:346
  17.9 5.5 %collective-permute-start.4 = (bf16[384,128]{1,0:T(8,128)(2,1)S(1)}, bf16[384,128]{1,0:T(8,128)(2,1)S(1)}, u32[]{:S(2)}, u32[]{:S(2)}) collective-permute-start(bf16[384,128]{1,0:T(8,128)(2,1)S(1)} %shard_map.68.after_ref), channel_id=1, source_target_pairs={{0,8},{8,16},{16,24},{24,0},{1,9},{9,17},{17,25},{25,1},{2,10},{10... | collective-permute-start | bytes 294920 | tf_op jit(solution)/shard_map/ppermute | solution.py:376
  23.4 8.9 %collective-permute-start.9 = (bf16[384,128]{1,0:T(8,128)(2,1)S(1)}, bf16[384,128]{1,0:T(8,128)(2,1)S(1)}, u32[]{:S(2)}, u32[]{:S(2)}) collective-permute-start(bf16[384,128]{1,0:T(8,128)(2,1)S(1)} %shard_map.70.refs_1_), channel_id=1, source_target_pairs={{0,4},{2,6},{4,0},{6,2},{1,5},{3,7},{5,1},{7,3},{8,12},{10,14},{12... | collective-permute-start | bytes 294920 | tf_op jit(solution)/shard_map/ppermute | solution.py:346
  27.0 7.2 %collective-permute-start.8 = (bf16[384,128]{1,0:T(8,128)(2,1)S(1)}, bf16[384,128]{1,0:T(8,128)(2,1)S(1)}, u32[]{:S(2)}, u32[]{:S(2)}) collective-permute-start(bf16[384,128]{1,0:T(8,128)(2,1)S(1)} %shard_map.70.refs_1_), channel_id=1, source_target_pairs={{0,2},{2,0},{4,6},{6,4},{1,3},{3,1},{5,7},{7,5},{8,10},{10,8},{12,... | collective-permute-start | bytes 294920 | tf_op jit(solution)/shard_map/ppermute | solution.py:346
  27.0 7.6 %collective-permute-start.7 = (bf16[384,128]{1,0:T(8,128)(2,1)S(1)}, bf16[384,128]{1,0:T(8,128)(2,1)S(1)}, u32[]{:S(2)}, u32[]{:S(2)}) collective-permute-start(bf16[384,128]{1,0:T(8,128)(2,1)S(1)} %shard_map.70.refs_1_), channel_id=1, source_target_pairs={{0,6},{2,4},{4,2},{6,0},{1,7},{3,5},{5,3},{7,1},{8,14},{10,12},{12... | collective-permute-start | bytes 294920 | tf_op jit(solution)/shard_map/ppermute | solution.py:346
  28.6 7.7 %collective-permute-start.6 = (bf16[384,128]{1,0:T(8,128)(2,1)S(1)}, bf16[384,128]{1,0:T(8,128)(2,1)S(1)}, u32[]{:S(2)}, u32[]{:S(2)}) collective-permute-start(bf16[384,128]{1,0:T(8,128)(2,1)S(1)} %shard_map.70.refs_1_), channel_id=1, source_target_pairs={{0,8},{8,0},{16,24},{24,16},{1,9},{9,1},{17,25},{25,17},{2,10},{10... | collective-permute-start | bytes 294920 | tf_op jit(solution)/shard_map/ppermute | solution.py:346
  32.3 4.6 %collective-permute-start.11 = (bf16[384,128]{1,0:T(8,128)(2,1)S(1)}, bf16[384,128]{1,0:T(8,128)(2,1)S(1)}, u32[]{:S(2)}, u32[]{:S(2)}) collective-permute-start(bf16[384,128]{1,0:T(8,128)(2,1)S(1)} %collective-permute-done.9.refs_5_), channel_id=1, source_target_pairs={{0,8},{8,0},{16,24},{24,16},{1,9},{9,1},{17,25},{25,17},{2,10},{10... | collective-permute-start | bytes 294920 | tf_op jit(solution)/shard_map/ppermute | solution.py:346
  34.2 4.6 %collective-permute-start.10 = (bf16[384,128]{1,0:T(8,128)(2,1)S(1)}, bf16[384,128]{1,0:T(8,128)(2,1)S(1)}, u32[]{:S(2)}, u32[]{:S(2)}) collective-permute-start(bf16[384,128]{1,0:T(8,128)(2,1)S(1)} %collective-permute-done.8.refs_4_), channel_id=1, source_target_pairs={{0,8},{8,0},{16,24},{24,16},{1,9},{9,1},{17,25},{25,17},{2,10},{10... | collective-permute-start | bytes 294920 | tf_op jit(solution)/shard_map/ppermute | solution.py:346
  34.6 5.2 %collective-permute-start.12 = (bf16[384,128]{1,0:T(8,128)(2,1)S(1)}, bf16[384,128]{1,0:T(8,128)(2,1)S(1)}, u32[]{:S(2)}, u32[]{:S(2)}) collective-permute-start(bf16[384,128]{1,0:T(8,128)(2,1)S(1)} %collective-permute-done.7.refs_3_), channel_id=1, source_target_pairs={{0,8},{8,0},{16,24},{24,16},{1,9},{9,1},{17,25},{25,17},{2,10},{10... | collective-permute-start | bytes 294920 | tf_op jit(solution)/shard_map/ppermute | solution.py:346
  36.3 4.6 %collective-permute-start.13 = (bf16[1920,128]{1,0:T(8,128)(2,1)S(1)}, bf16[1920,128]{1,0:T(8,128)(2,1)S(1)}, u32[]{:S(2)}, u32[]{:S(2)}) collective-permute-start(bf16[1920,128]{1,0:T(8,128)(2,1)S(1)} %shard_map.71.state_ref), channel_id=1, source_target_pairs={{0,1},{1,0},{2,3},{3,2},{4,5},{5,4},{6,7},{7,6},{8,9},{9,8},{10,11... | collective-permute-start | bytes 1474568 | tf_op jit(solution)/shard_map/ppermute | solution.py:346
  38.8 2.3 %collective-permute-start.14 = (bf16[768,128]{1,0:T(8,128)(2,1)S(1)}, bf16[768,128]{1,0:T(8,128)(2,1)S(1)}, u32[]{:S(2)}, u32[]{:S(2)}) collective-permute-start(bf16[768,128]{1,0:T(8,128)(2,1)S(1)} %shard_map.73.refs_0_), channel_id=1, source_target_pairs={{0,1},{1,0},{2,3},{3,2},{4,5},{5,4},{6,7},{7,6},{8,9},{9,8},{10,11... | collective-permute-start | bytes 589832 | tf_op jit(solution)/shard_map/ppermute | solution.py:346
  39.9 1.3 %collective-permute-start.15 = (bf16[384,128]{1,0:T(8,128)(2,1)S(1)}, bf16[384,128]{1,0:T(8,128)(2,1)S(1)}, u32[]{:S(2)}, u32[]{:S(2)}) collective-permute-start(bf16[384,128]{1,0:T(8,128)(2,1)S(1)} %collective-permute-done.12.refs_1_), channel_id=1, source_target_pairs={{0,1},{1,0},{2,3},{3,2},{4,5},{5,4},{6,7},{7,6},{8,9},{9,8},{10,11... | collective-permute-start | bytes 294920 | tf_op jit(solution)/shard_map/ppermute | solution.py:346

commit v13 on v10

--- a/solution.py
+++ b/solution.py
@@ -373,7 +373,10 @@
 
     x = [slot] + [swap(slot, "chip", d, chips) for d in range(1, chips)]
     y = [swap(slot, "frame", 1, frames)]
-    y += [swap(piece, "frame", 1, frames) for piece in x[1:]]
+    y += [swap(piece, "frame", 1, frames) for piece in x[1:3]]
+    for d in range(3, chips):
+        pairs = [(f * chips + c, (f ^ 1) * chips + (c ^ d)) for f in range(frames) for c in range(chips)]
+        y.append(lax.ppermute(slot, ("frame", "chip"), pairs))
     places = [0, *range(chips + early - 1, 2, -1), *range(1, min(3, chips + early))]
     own_states = pack(x + y[:early], places, [local_1])
     other_states = swap(own_states, "core", 1, 2)

time: 41.8 us -> 43.8 us (1.048)
  starting transfers between devices: 17.3 us -> 19.8 us
  waiting for transfers between devices: 15.9 us -> 15.3 us
    ppermute x0 -> x1, starting transfers between devices: none -> 3.35 us  [body(): y.append(lax.ppermute(slot, ('frame', 'chip'), pairs))]
    ppermute x14 -> x13, starting transfers between devices: 15.8 us -> 15 us  [swap(): return lax.ppermute(array, axis, [(n, n ^ mask) for n in range(size)])]
    ppermute x14 -> x13, waiting for transfers between devices: 14.5 us -> 13.9 us  [swap(): return lax.ppermute(array, axis, [(n, n ^ mask) for n in range(size)])]
  transfers between devices with their start and end apart: 15 -> 15, of which waited for: 10 -> 9; matrix products, arithmetic and copies ran while one was open for 0% -> 0% of each run, Pallas kernels for 13% -> 13%
where the time goes in v13:
time: 43.8 us; the launch traced here: 43.7 us
  starting transfers between devices  19.8 us (45%)
  waiting for transfers between devices  15.3 us (35%)
  Pallas kernels  8.38 us (19%)
    ppermute x13, starting transfers between devices, swap(): return lax.ppermute(array, axis, [(n, n ^ mask) for n in range(size)])  15 us
    ppermute x13, waiting for transfers between devices, swap(): return lax.ppermute(array, axis, [(n, n ^ mask) for n in range(size)])  13.9 us
    pallas_call x2, Pallas kernels, local_part(): pl.pallas_call(functools.partial(local_kernel, coefs, turn), out_shape=[p...  3.44 us
    ppermute x1, starting transfers between devices, body(): y.append(lax.ppermute(slot, ('frame', 'chip'), pairs))  3.35 us
    pallas_call x2, Pallas kernels, write_late(): pl.pallas_call(functools.partial(kernel, turn, chips, early), out_shape=j...  1.9 us
    pallas_call x1, Pallas kernels, outgoing_state(): pl.pallas_call(functools.partial(first_kernel, parts), out_shape=[pltpu.V...  1.69 us
    ppermute x1, starting transfers between devices, body(): lax.ppermute(state, 'frame', [(f, (f + 1) % frames) for f in range(frames)])  1.49 us
    ppermute x1, waiting for transfers between devices, body(): lax.ppermute(state, 'frame', [(f, (f + 1) % frames) for f in range(frames)])  1.36 us
  transfers between devices with their start and end apart: 15, of which 9 were waited for; matrix products, arithmetic and copies ran while one was open for 0% of the time, Pallas kernels for 13%

profile of v13, /device:TPU:0, one launch (start us, length us, event | category | flops | bytes accessed | tf_op | source)
XLA Modules:
  0.0 43.7 jit_solution(12976936983859934602)
XLA Ops:
  0.0 1.7 %shard_map.64 = (bf16[1536,128]{1,0:T(8,128)(2,1)S(1)}, bf16[128,3072]{1,0:T(8,128)(2,1)S(1)}, bf16[128,3072]{1,0:T(8,128)(2,1)S(1)}) custom-call(bf16[128,3072]{1,0:T(8,128)(2,1)} %key_ref.1, bf16[128,3072]{1,0:T(8,128)(2,1)} %value_ref.1), custom_call_target="tpu_custom_call" | custom-call | flops 50331648 | bytes 1572864 | tf_op jit(solution)/shard_map/pallas_call | solution.py:84
  1.7 0.5 %collective-permute-start = (bf16[1536,128]{1,0:T(8,128)(2,1)S(1)}, bf16[1536,128]{1,0:T(8,128)(2,1)S(1)}, u32[]{:S(2)}, u32[]{:S(2)}) collective-permute-start(bf16[1536,128]{1,0:T(8,128)(2,1)S(1)} %get-tuple-element.20), channel_id=1, source_target_pairs={{0,1},{1,0},{2,3},{3,2},{4,5},{5,4},{6,7},{7,6},{8,9},{9,8},{10,11... | collective-permute-start | bytes 1179656 | tf_op jit(solution)/shard_map/ppermute | solution.py:343
  2.2 0.5 %shard_map.65.mine_ref = f32[1536,128]{1,0:T(8,128)S(1)} custom-call(bf16[128,3072]{1,0:T(8,128)(2,1)S(1)} %get-tuple-element.18.key_ref, bf16[128,3072]{1,0:T(8,128)(2,1)S(1)} %get-tuple-element.19.value_ref), custom_call_target="tpu_custom_call" | custom-call | flops 50331648 | bytes 1572864 | tf_op jit(solution)/shard_map/pallas_call | solution.py:104
  2.7 0.8 %collective-permute-done.other_ref = bf16[1536,128]{1,0:T(8,128)(2,1)S(1)} collective-permute-done((bf16[1536,128]{1,0:T(8,128)(2,1)S(1)}, bf16[1536,128]{1,0:T(8,128)(2,1)S(1)}, u32[]{:S(2)}, u32[]{:S(2)}) %collective-permute-start) | collective-permute-done | bytes 393248 | tf_op jit(solution)/shard_map/ppermute | solution.py:343
  3.5 0.1 shard_map.66
  3.6 5.1 %collective-permute-start.1 = (bf16[384,128]{1,0:T(8,128)(2,1)S(1)}, bf16[384,128]{1,0:T(8,128)(2,1)S(1)}, u32[]{:S(2)}, u32[]{:S(2)}) collective-permute-start(bf16[384,128]{1,0:T(8,128)(2,1)S(1)} %get-tuple-element.25), channel_id=1, source_target_pairs={{0,6},{2,4},{4,2},{6,0},{1,7},{3,5},{5,3},{7,1},{8,14},{10,12},{12... | collective-permute-start | bytes 294920 | tf_op jit(solution)/shard_map/ppermute | solution.py:343
  8.7 0.6 %collective-permute-start.3 = (bf16[384,128]{1,0:T(8,128)(2,1)S(1)}, bf16[384,128]{1,0:T(8,128)(2,1)S(1)}, u32[]{:S(2)}, u32[]{:S(2)}) collective-permute-start(bf16[384,128]{1,0:T(8,128)(2,1)S(1)} %get-tuple-element.27), channel_id=1, source_target_pairs={{0,2},{2,0},{4,6},{6,4},{1,3},{3,1},{5,7},{7,5},{8,10},{10,8},{12,... | collective-permute-start | bytes 294920 | tf_op jit(solution)/shard_map/ppermute | solution.py:343
  9.4 1.7 %shard_map.67 = (f32[128,1536]{1,0:T(8,128)S(1)}, bf16[128,1536]{1,0:T(8,128)(2,1)S(1)}, bf16[128,1536]{1,0:T(8,128)(2,1)S(1)}) custom-call(s32[1,4]{1,0:T(1,128)S(1)} %copy-done.2, s32[1,4]{1,0:T(1,128)S(1)} %copy-done.3, bf16[128,3072]{1,0:T(8,128)(2,1)S(1)} %copy-done, bf16[128,3072]{1,0:T(8,128)(2,1)S(1)} %get-tuple-element.18.key_ref, ...), custom_call_target="tpu_custom_call" | custom-call | flops 100663296 | bytes 2752512 | tf_op jit(solution)/shard_map/pallas_call | solution.py:251
  11.1 1.3 %collective-permute-done.1.refs_0_ = bf16[384,128]{1,0:T(8,128)(2,1)S(1)} collective-permute-done((bf16[384,128]{1,0:T(8,128)(2,1)S(1)}, bf16[384,128]{1,0:T(8,128)(2,1)S(1)}, u32[]{:S(2)}, u32[]{:S(2)}) %collective-permute-start.1) | collective-permute-done | bytes 98336 | tf_op jit(solution)/shard_map/ppermute | solution.py:343
  12.4 4.9 %collective-permute-done.2.refs_1_ = bf16[384,128]{1,0:T(8,128)(2,1)S(1)} collective-permute-done((bf16[384,128]{1,0:T(8,128)(2,1)S(1)}, bf16[384,128]{1,0:T(8,128)(2,1)S(1)}, u32[]{:S(2)}, u32[]{:S(2)}) %collective-permute-start.2) | collective-permute-done | bytes 98336 | tf_op jit(solution)/shard_map/ppermute | solution.py:343
  17.3 1.6 %collective-permute-start.5 = (bf16[384,128]{1,0:T(8,128)(2,1)S(1)}, bf16[384,128]{1,0:T(8,128)(2,1)S(1)}, u32[]{:S(2)}, u32[]{:S(2)}) collective-permute-start(bf16[384,128]{1,0:T(8,128)(2,1)S(1)} %shard_map.68.after_ref), channel_id=1, source_target_pairs={{0,16},{8,24},{16,0},{24,8},{1,17},{9,25},{17,1},{25,9},{2,18},{10... | collective-permute-start | bytes 294920 | tf_op jit(solution)/shard_map/ppermute | solution.py:343
  18.9 1.5 %collective-permute-start.4 = (bf16[384,128]{1,0:T(8,128)(2,1)S(1)}, bf16[384,128]{1,0:T(8,128)(2,1)S(1)}, u32[]{:S(2)}, u32[]{:S(2)}) collective-permute-start(bf16[384,128]{1,0:T(8,128)(2,1)S(1)} %shard_map.68.after_ref), channel_id=1, source_target_pairs={{0,8},{8,16},{16,24},{24,0},{1,9},{9,17},{17,25},{25,1},{2,10},{10... | collective-permute-start | bytes 294920 | tf_op jit(solution)/shard_map/ppermute | solution.py:371
  20.4 1.7 %shard_map.69 = (f32[128,1536]{1,0:T(8,128)S(1)}, bf16[128,1536]{1,0:T(8,128)(2,1)S(1)}, bf16[128,1536]{1,0:T(8,128)(2,1)S(1)}) custom-call(s32[1,4]{1,0:T(1,128)S(1)} %copy-done.2, s32[1,4]{1,0:T(1,128)S(1)} %copy-done.3, bf16[128,3072]{1,0:T(8,128)(2,1)S(1)} %copy-done, bf16[128,3072]{1,0:T(8,128)(2,1)S(1)} %get-tuple-element.18.key_ref, ...), custom_call_target="tpu_custom_call" | custom-call | flops 100663296 | bytes 2752512 | tf_op jit(solution)/shard_map/pallas_call | solution.py:251
  22.1 0.9 %collective-permute-done.5.first_ref = bf16[384,128]{1,0:T(8,128)(2,1)S(1)} collective-permute-done((bf16[384,128]{1,0:T(8,128)(2,1)S(1)}, bf16[384,128]{1,0:T(8,128)(2,1)S(1)}, u32[]{:S(2)}, u32[]{:S(2)}) %collective-permute-start.5) | collective-permute-done | bytes 98336 | tf_op jit(solution)/shard_map/ppermute | solution.py:343
  23.1 1.4 %collective-permute-done.4.before_ref = bf16[384,128]{1,0:T(8,128)(2,1)S(1)} collective-permute-done((bf16[384,128]{1,0:T(8,128)(2,1)S(1)}, bf16[384,128]{1,0:T(8,128)(2,1)S(1)}, u32[]{:S(2)}, u32[]{:S(2)}) %collective-permute-start.4) | collective-permute-done | bytes 98336 | tf_op jit(solution)/shard_map/ppermute | solution.py:371
  24.5 0.3 collective-permute-start.9
  24.8 2.8 %collective-permute-start.8 = (bf16[384,128]{1,0:T(8,128)(2,1)S(1)}, bf16[384,128]{1,0:T(8,128)(2,1)S(1)}, u32[]{:S(2)}, u32[]{:S(2)}) collective-permute-start(bf16[384,128]{1,0:T(8,128)(2,1)S(1)} %shard_map.70.refs_1_), channel_id=1, source_target_pairs={{0,2},{2,0},{4,6},{6,4},{1,3},{3,1},{5,7},{7,5},{8,10},{10,8},{12,... | collective-permute-start | bytes 294920 | tf_op jit(solution)/shard_map/ppermute | solution.py:343
  27.6 1.3 %collective-permute-start.7 = (bf16[384,128]{1,0:T(8,128)(2,1)S(1)}, bf16[384,128]{1,0:T(8,128)(2,1)S(1)}, u32[]{:S(2)}, u32[]{:S(2)}) collective-permute-start(bf16[384,128]{1,0:T(8,128)(2,1)S(1)} %shard_map.70.refs_1_), channel_id=1, source_target_pairs={{0,6},{2,4},{4,2},{6,0},{1,7},{3,5},{5,3},{7,1},{8,14},{10,12},{12... | collective-permute-start | bytes 294920 | tf_op jit(solution)/shard_map/ppermute | solution.py:343
  28.9 0.6 %collective-permute-start.6 = (bf16[384,128]{1,0:T(8,128)(2,1)S(1)}, bf16[384,128]{1,0:T(8,128)(2,1)S(1)}, u32[]{:S(2)}, u32[]{:S(2)}) collective-permute-start(bf16[384,128]{1,0:T(8,128)(2,1)S(1)} %shard_map.70.refs_1_), channel_id=1, source_target_pairs={{0,8},{8,0},{16,24},{24,16},{1,9},{9,1},{17,25},{25,17},{2,10},{10... | collective-permute-start | bytes 294920 | tf_op jit(solution)/shard_map/ppermute | solution.py:343
  29.5 3.4 %collective-permute-start.12 = (bf16[384,128]{1,0:T(8,128)(2,1)S(1)}, bf16[384,128]{1,0:T(8,128)(2,1)S(1)}, u32[]{:S(2)}, u32[]{:S(2)}) collective-permute-start(bf16[384,128]{1,0:T(8,128)(2,1)S(1)} %shard_map.70.refs_1_), channel_id=1, source_target_pairs={{0,14},{2,12},{4,10},{6,8},{8,6},{10,4},{12,2},{14,0},{16,30},{18,... | collective-permute-start | bytes 294920 | tf_op jit(solution)/shard_map/ppermute | solution.py:379
  32.9 2.5 %collective-permute-done.9.refs_5_ = bf16[384,128]{1,0:T(8,128)(2,1)S(1)} collective-permute-done((bf16[384,128]{1,0:T(8,128)(2,1)S(1)}, bf16[384,128]{1,0:T(8,128)(2,1)S(1)}, u32[]{:S(2)}, u32[]{:S(2)}) %collective-permute-start.9) | collective-permute-done | bytes 98336 | tf_op jit(solution)/shard_map/ppermute | solution.py:343
  35.4 0.6 %collective-permute-start.11 = (bf16[384,128]{1,0:T(8,128)(2,1)S(1)}, bf16[384,128]{1,0:T(8,128)(2,1)S(1)}, u32[]{:S(2)}, u32[]{:S(2)}) collective-permute-start(bf16[384,128]{1,0:T(8,128)(2,1)S(1)} %collective-permute-done.9.refs_5_), channel_id=1, source_target_pairs={{0,8},{8,0},{16,24},{24,16},{1,9},{9,1},{17,25},{25,17},{2,10},{10... | collective-permute-start | bytes 294920 | tf_op jit(solution)/shard_map/ppermute | solution.py:343
  36.0 1.4 %collective-permute-start.10 = (bf16[384,128]{1,0:T(8,128)(2,1)S(1)}, bf16[384,128]{1,0:T(8,128)(2,1)S(1)}, u32[]{:S(2)}, u32[]{:S(2)}) collective-permute-start(bf16[384,128]{1,0:T(8,128)(2,1)S(1)} %collective-permute-done.8.refs_4_), channel_id=1, source_target_pairs={{0,8},{8,0},{16,24},{24,16},{1,9},{9,1},{17,25},{25,17},{2,10},{10... | collective-permute-start | bytes 294920 | tf_op jit(solution)/shard_map/ppermute | solution.py:343
  37.4 0.1 collective-permute-start.13
  37.5 0.3 shard_map.72.base_ref
  37.8 2.1 %collective-permute-done.11.refs_1_ = bf16[384,128]{1,0:T(8,128)(2,1)S(1)} collective-permute-done((bf16[384,128]{1,0:T(8,128)(2,1)S(1)}, bf16[384,128]{1,0:T(8,128)(2,1)S(1)}, u32[]{:S(2)}, u32[]{:S(2)}) %collective-permute-start.11) | collective-permute-done | bytes 98336 | tf_op jit(solution)/shard_map/ppermute | solution.py:343
  40.0 1.1 %collective-permute-done.10.refs_0_ = bf16[384,128]{1,0:T(8,128)(2,1)S(1)} collective-permute-done((bf16[384,128]{1,0:T(8,128)(2,1)S(1)}, bf16[384,128]{1,0:T(8,128)(2,1)S(1)}, u32[]{:S(2)}, u32[]{:S(2)}) %collective-permute-start.10) | collective-permute-done | bytes 98336 | tf_op jit(solution)/shard_map/ppermute | solution.py:343
  41.1 0.1 collective-permute-start.14
  41.1 1.0 %shard_map.74.out_before_ref = bf16[128,3072]{1,0:T(8,128)(2,1)} custom-call(f32[128,1536]{1,0:T(8,128)S(1)} %shard_map.72.base_ref, bf16[128,1536]{1,0:T(8,128)(2,1)S(1)} %get-tuple-element.24.y_ref, bf16[1152,128]{1,0:T(8,128)(2,1)S(1)} %shard_map.73.refs_0_), custom_call_target="tpu_custom_call" | custom-call | flops 20000000000 | bytes 1024 | tf_op jit(solution)/shard_map/pallas_call | solution.py:330
  42.1 0.3 shard_map.75.refs_0_
  42.4 0.3 collective-permute-done.14.refs_2_
  42.7 0.9 %shard_map.76 = bf16[128,3072]{1,0:T(8,128)(2,1)} custom-call(bf16[128,3072]{1,0:T(8,128)(2,1)} %shard_map.74.out_before_ref, f32[128,1536]{1,0:T(8,128)S(1)} %shard_map.75.refs_0_, bf16[128,1536]{1,0:T(8,128)(2,1)S(1)} %get-tuple-element.30.y_ref.refs_1_, bf16[1152,128]{1,0:T(8,128)(2,1)S(1)} %collective-permute-done.14.refs_2_), custom_call_target="tpu_custom_call", output_to_operand_aliasing={{}: (0, {})} | custom-call | flops 1024 | bytes 1024 | tf_op jit(solution)/shard_map/pallas_call | solution.py:330
  (19 shorter events, 0.2 us)
Async XLA Ops:
  1.7 1.8 %collective-permute-start = (bf16[1536,128]{1,0:T(8,128)(2,1)S(1)}, bf16[1536,128]{1,0:T(8,128)(2,1)S(1)}, u32[]{:S(2)}, u32[]{:S(2)}) collective-permute-start(bf16[1536,128]{1,0:T(8,128)(2,1)S(1)} %get-tuple-element.20), channel_id=1, source_target_pairs={{0,1},{1,0},{2,3},{3,2},{4,5},{5,4},{6,7},{7,6},{8,9},{9,8},{10,11... | collective-permute-start | bytes 1179656 | tf_op jit(solution)/shard_map/ppermute | solution.py:343
  2.7 6.6 %copy-start = (bf16[128,3072]{1,0:T(8,128)(2,1)S(1)}, bf16[128,3072]{1,0:T(8,128)(2,1)}, u32[]{:S(2)}) copy-start(bf16[128,3072]{1,0:T(8,128)(2,1)} %query_ref.3) | copy-start | bytes 2359300
  2.7 6.6 %copy-start.1 = (f32[3,24,128]{2,1,0:T(8,128)S(1)}, f32[3,24,128]{2,1,0:T(8,128)}, u32[]{:S(2)}) copy-start(f32[3,24,128]{2,1,0:T(8,128)} %weight_ref.3) | copy-start | bytes 110596
  3.6 8.7 %collective-permute-start.1 = (bf16[384,128]{1,0:T(8,128)(2,1)S(1)}, bf16[384,128]{1,0:T(8,128)(2,1)S(1)}, u32[]{:S(2)}, u32[]{:S(2)}) collective-permute-start(bf16[384,128]{1,0:T(8,128)(2,1)S(1)} %get-tuple-element.25), channel_id=1, source_target_pairs={{0,6},{2,4},{4,2},{6,0},{1,7},{3,5},{5,3},{7,1},{8,14},{10,12},{12... | collective-permute-start | bytes 294920 | tf_op jit(solution)/shard_map/ppermute | solution.py:343
  8.7 8.6 %collective-permute-start.2 = (bf16[384,128]{1,0:T(8,128)(2,1)S(1)}, bf16[384,128]{1,0:T(8,128)(2,1)S(1)}, u32[]{:S(2)}, u32[]{:S(2)}) collective-permute-start(bf16[384,128]{1,0:T(8,128)(2,1)S(1)} %get-tuple-element.26), channel_id=1, source_target_pairs={{0,4},{2,6},{4,0},{6,2},{1,5},{3,7},{5,1},{7,3},{8,12},{10,14},{12... | collective-permute-start | bytes 294920 | tf_op jit(solution)/shard_map/ppermute | solution.py:343
  8.7 0.7 %copy-start.2 = (s32[1,4]{1,0:T(1,128)S(1)}, s32[1,4]{1,0:T(1,128)}, u32[]{:S(2)}) copy-start(s32[1,4]{1,0:T(1,128)} %length_ref.3) | copy-start | bytes 52
  8.7 0.7 %copy-start.3 = (s32[1,4]{1,0:T(1,128)S(1)}, s32[1,4]{1,0:T(1,128)}, u32[]{:S(2)}) copy-start(s32[1,4]{1,0:T(1,128)} %back_ref.3) | copy-start | bytes 52
  8.7 8.6 %collective-permute-start.3 = (bf16[384,128]{1,0:T(8,128)(2,1)S(1)}, bf16[384,128]{1,0:T(8,128)(2,1)S(1)}, u32[]{:S(2)}, u32[]{:S(2)}) collective-permute-start(bf16[384,128]{1,0:T(8,128)(2,1)S(1)} %get-tuple-element.27), channel_id=1, source_target_pairs={{0,2},{2,0},{4,6},{6,4},{1,3},{3,1},{5,7},{7,5},{8,10},{10,8},{12,... | collective-permute-start | bytes 294920 | tf_op jit(solution)/shard_map/ppermute | solution.py:343
  17.3 5.7 %collective-permute-start.5 = (bf16[384,128]{1,0:T(8,128)(2,1)S(1)}, bf16[384,128]{1,0:T(8,128)(2,1)S(1)}, u32[]{:S(2)}, u32[]{:S(2)}) collective-permute-start(bf16[384,128]{1,0:T(8,128)(2,1)S(1)} %shard_map.68.after_ref), channel_id=1, source_target_pairs={{0,16},{8,24},{16,0},{24,8},{1,17},{9,25},{17,1},{25,9},{2,18},{10... | collective-permute-start | bytes 294920 | tf_op jit(solution)/shard_map/ppermute | solution.py:343
  18.9 5.5 %collective-permute-start.4 = (bf16[384,128]{1,0:T(8,128)(2,1)S(1)}, bf16[384,128]{1,0:T(8,128)(2,1)S(1)}, u32[]{:S(2)}, u32[]{:S(2)}) collective-permute-start(bf16[384,128]{1,0:T(8,128)(2,1)S(1)} %shard_map.68.after_ref), channel_id=1, source_target_pairs={{0,8},{8,16},{16,24},{24,0},{1,9},{9,17},{17,25},{25,1},{2,10},{10... | collective-permute-start | bytes 294920 | tf_op jit(solution)/shard_map/ppermute | solution.py:371
  24.5 10.9 %collective-permute-start.9 = (bf16[384,128]{1,0:T(8,128)(2,1)S(1)}, bf16[384,128]{1,0:T(8,128)(2,1)S(1)}, u32[]{:S(2)}, u32[]{:S(2)}) collective-permute-start(bf16[384,128]{1,0:T(8,128)(2,1)S(1)} %shard_map.70.refs_1_), channel_id=1, source_target_pairs={{0,4},{2,6},{4,0},{6,2},{1,5},{3,7},{5,1},{7,3},{8,12},{10,14},{12... | collective-permute-start | bytes 294920 | tf_op jit(solution)/shard_map/ppermute | solution.py:343
  24.8 11.1 %collective-permute-start.8 = (bf16[384,128]{1,0:T(8,128)(2,1)S(1)}, bf16[384,128]{1,0:T(8,128)(2,1)S(1)}, u32[]{:S(2)}, u32[]{:S(2)}) collective-permute-start(bf16[384,128]{1,0:T(8,128)(2,1)S(1)} %shard_map.70.refs_1_), channel_id=1, source_target_pairs={{0,2},{2,0},{4,6},{6,4},{1,3},{3,1},{5,7},{7,5},{8,10},{10,8},{12,... | collective-permute-start | bytes 294920 | tf_op jit(solution)/shard_map/ppermute | solution.py:343
  27.6 9.8 %collective-permute-start.7 = (bf16[384,128]{1,0:T(8,128)(2,1)S(1)}, bf16[384,128]{1,0:T(8,128)(2,1)S(1)}, u32[]{:S(2)}, u32[]{:S(2)}) collective-permute-start(bf16[384,128]{1,0:T(8,128)(2,1)S(1)} %shard_map.70.refs_1_), channel_id=1, source_target_pairs={{0,6},{2,4},{4,2},{6,0},{1,7},{3,5},{5,3},{7,1},{8,14},{10,12},{12... | collective-permute-start | bytes 294920 | tf_op jit(solution)/shard_map/ppermute | solution.py:343
  28.9 8.5 %collective-permute-start.6 = (bf16[384,128]{1,0:T(8,128)(2,1)S(1)}, bf16[384,128]{1,0:T(8,128)(2,1)S(1)}, u32[]{:S(2)}, u32[]{:S(2)}) collective-permute-start(bf16[384,128]{1,0:T(8,128)(2,1)S(1)} %shard_map.70.refs_1_), channel_id=1, source_target_pairs={{0,8},{8,0},{16,24},{24,16},{1,9},{9,1},{17,25},{25,17},{2,10},{10... | collective-permute-start | bytes 294920 | tf_op jit(solution)/shard_map/ppermute | solution.py:343
  29.5 8.3 %collective-permute-start.12 = (bf16[384,128]{1,0:T(8,128)(2,1)S(1)}, bf16[384,128]{1,0:T(8,128)(2,1)S(1)}, u32[]{:S(2)}, u32[]{:S(2)}) collective-permute-start(bf16[384,128]{1,0:T(8,128)(2,1)S(1)} %shard_map.70.refs_1_), channel_id=1, source_target_pairs={{0,14},{2,12},{4,10},{6,8},{8,6},{10,4},{12,2},{14,0},{16,30},{18,... | collective-permute-start | bytes 294920 | tf_op jit(solution)/shard_map/ppermute | solution.py:379
  35.4 4.6 %collective-permute-start.11 = (bf16[384,128]{1,0:T(8,128)(2,1)S(1)}, bf16[384,128]{1,0:T(8,128)(2,1)S(1)}, u32[]{:S(2)}, u32[]{:S(2)}) collective-permute-start(bf16[384,128]{1,0:T(8,128)(2,1)S(1)} %collective-permute-done.9.refs_5_), channel_id=1, source_target_pairs={{0,8},{8,0},{16,24},{24,16},{1,9},{9,1},{17,25},{25,17},{2,10},{10... | collective-permute-start | bytes 294920 | tf_op jit(solution)/shard_map/ppermute | solution.py:343
  36.0 5.1 %collective-permute-start.10 = (bf16[384,128]{1,0:T(8,128)(2,1)S(1)}, bf16[384,128]{1,0:T(8,128)(2,1)S(1)}, u32[]{:S(2)}, u32[]{:S(2)}) collective-permute-start(bf16[384,128]{1,0:T(8,128)(2,1)S(1)} %collective-permute-done.8.refs_4_), channel_id=1, source_target_pairs={{0,8},{8,0},{16,24},{24,16},{1,9},{9,1},{17,25},{25,17},{2,10},{10... | collective-permute-start | bytes 294920 | tf_op jit(solution)/shard_map/ppermute | solution.py:343
  37.4 4.7 %collective-permute-start.13 = (bf16[1920,128]{1,0:T(8,128)(2,1)S(1)}, bf16[1920,128]{1,0:T(8,128)(2,1)S(1)}, u32[]{:S(2)}, u32[]{:S(2)}) collective-permute-start(bf16[1920,128]{1,0:T(8,128)(2,1)S(1)} %shard_map.71.state_ref), channel_id=1, source_target_pairs={{0,1},{1,0},{2,3},{3,2},{4,5},{5,4},{6,7},{7,6},{8,9},{9,8},{10,11... | collective-permute-start | bytes 1474568 | tf_op jit(solution)/shard_map/ppermute | solution.py:343
  41.1 1.6 %collective-permute-start.14 = (bf16[1152,128]{1,0:T(8,128)(2,1)S(1)}, bf16[1152,128]{1,0:T(8,128)(2,1)S(1)}, u32[]{:S(2)}, u32[]{:S(2)}) collective-permute-start(bf16[1152,128]{1,0:T(8,128)(2,1)S(1)} %shard_map.73.refs_0_), channel_id=1, source_target_pairs={{0,1},{1,0},{2,3},{3,2},{4,5},{5,4},{6,7},{7,6},{8,9},{9,8},{10,11... | collective-permute-start | bytes 884744 | tf_op jit(solution)/shard_map/ppermute | solution.py:343

commit v14 on v10

--- a/solution.py
+++ b/solution.py
@@ -113,18 +113,19 @@
     )(*in_vmem(keys, values))
 
 
-def piece_kernel(mine_ref, other_ref, own_ref, *piece_refs):
+def piece_kernel(orders, mine_ref, other_ref, own_ref, *piece_refs):
     chip = lax.axis_index("chip")
     rows = own_ref.shape[0]
-    for d, ref in enumerate((own_ref,) + piece_refs):
-        at = pl.ds(pl.multiple_of((chip ^ d) * rows, rows), rows)
+    second = lax.axis_index("core") == 1
+    for (d, e), ref in zip(((0, 0), *orders), (own_ref,) + piece_refs):
+        at = pl.ds(pl.multiple_of((chip ^ jnp.where(second, e, d)) * rows, rows), rows)
         ref[...] = (mine_ref[at, :] + other_ref[at, :].astype(F32)).astype(ref.dtype)
 
 
-def chip_pieces(mine, other, chips):
+def chip_pieces(orders, mine, other, chips):
     shape = (mine.shape[0] // chips, HEAD_DIM)
     return pl.pallas_call(
-        piece_kernel,
+        functools.partial(piece_kernel, orders),
         out_shape=[pltpu.VMEM(shape, F32)] + [pltpu.VMEM(shape, BF16)] * (chips - 1),
         in_specs=[WHOLE, WHOLE],
         out_specs=[WHOLE] * chips,
@@ -151,21 +152,21 @@
     )(after, *in_vmem(own, *parts))
 
 
-def slot_kernel(after_ref, before_ref, first_ref, out_ref):
-    before = before_ref[...].astype(F32)
-    both = first_ref[...].astype(F32) + before
-    out_ref[...] = jnp.where(lax.axis_index("frame") == 2, both, before).astype(BF16)
-
-
-def choose_slot(after, before, first):
+def slot_kernel(after_ref, one_ref, two_ref, out_ref):
+    one, two = one_ref[...].astype(F32), two_ref[...].astype(F32)
+    before = jnp.where(lax.axis_index("core") == 0, one, two)
+    out_ref[...] = jnp.where(lax.axis_index("frame") == 2, one + two, before).astype(BF16)
+
+
+def choose_slot(after, one, two):
     return pl.pallas_call(
         slot_kernel,
-        out_shape=pltpu.VMEM(before.shape, BF16),
+        out_shape=pltpu.VMEM(one.shape, BF16),
         in_specs=[ANYWHERE] + [WHOLE] * 2,
         out_specs=WHOLE,
         compiler_params=PARAMS,
         cost_estimate=SMALL,
-    )(after, *in_vmem(before, first))
+    )(after, *in_vmem(one, two))
 
 
 def pack_kernel(after, order, *refs):
@@ -361,15 +362,31 @@
     outgoing, keys, values = outgoing_state(keys, values)
     incoming = swap(outgoing, "core", 1, 2)
     mine = own_state(keys, values)
-    own, *sends = chip_pieces(mine, incoming, chips)
-    got = [swap(sends[d - 1], "chip", d, chips) for d in reversed(range(1, chips))]
+    order = [*reversed(range(1, chips))]
+    orders = [*zip(order, order[-1:] + order[:-1])]
+    own, *sends = chip_pieces(orders, mine, incoming, chips)
+    got = [
+        lax.ppermute(
+            piece,
+            ("chip", "core"),
+            [(z * 2 + c, (z ^ pair[c]) * 2 + c) for z in range(chips) for c in range(2)],
+        )
+        for piece, pair in zip(sends, orders)
+    ]
     local_0, x_0, y_0 = local(0, *rest, keys, values, level_weight, own)
     state = sum_pieces(local_0, own, got, F32 if outer > 1 else BF16)
     if outer > 1:
         state = lax.psum(state, "outer").astype(BF16)
     local_1, x_1, y_1 = local(1, *rest, keys, values, level_weight, state)
-    shifted = lax.ppermute(state, "frame", [(f, (f + 1) % frames) for f in range(frames)])
-    slot = choose_slot(local_1, shifted, swap(state, "frame", 2, frames))
+    moved = [
+        lax.ppermute(
+            state,
+            ("frame", "core"),
+            [(f * 2 + c, ((f + 1) % frames if c == turn else f ^ 2) * 2 + c) for f in range(frames) for c in range(2)],
+        )
+        for turn in range(2)
+    ]
+    slot = choose_slot(local_1, *moved)
 
     x = [slot] + [swap(slot, "chip", d, chips) for d in range(1, chips)]
     y = [swap(slot, "frame", 1, frames)]

time: 41.8 us -> 45.5 us (1.089)
  waiting for transfers between devices: 15.9 us -> 20.9 us
  starting transfers between devices: 17.3 us -> 15.9 us
    ppermute x14 -> x10, starting transfers between devices: 15.8 us -> 7.12 us  [swap(): return lax.ppermute(array, axis, [(n, n ^ mask) for n in range(size)])]
    ppermute x1 -> x5, waiting for transfers between devices: 1.36 us -> 9.6 us  [the longest x3 6.71 us: body(): lax.ppermute(piece, ('chip', 'core'), [(z * 2 + c, (z ^ pair[c]) * 2 + c)...]
    ppermute x1 -> x5, starting transfers between devices: 1.49 us -> 8.76 us  [the longest x3 5.71 us: body(): lax.ppermute(piece, ('chip', 'core'), [(z * 2 + c, (z ^ pair[c]) * 2 + c)...]
    ppermute x14 -> x10, waiting for transfers between devices: 14.5 us -> 11.3 us  [swap(): return lax.ppermute(array, axis, [(n, n ^ mask) for n in range(size)])]
  transfers between devices with their start and end apart: 15 -> 15, of which waited for: 10 -> 10; matrix products, arithmetic and copies ran while one was open for 0% -> 0% of each run, Pallas kernels for 13% -> 12%
where the time goes in v14:
time: 45.5 us; the launch traced here: 45.3 us
  waiting for transfers between devices  20.9 us (46%)
  starting transfers between devices  15.9 us (35%)
  Pallas kernels  8.38 us (18%)
    ppermute x10, waiting for transfers between devices, swap(): return lax.ppermute(array, axis, [(n, n ^ mask) for n in range(size)])  11.3 us
    ppermute x10, starting transfers between devices, swap(): return lax.ppermute(array, axis, [(n, n ^ mask) for n in range(size)])  7.12 us
    ppermute x3, waiting for transfers between devices, body(): lax.ppermute(piece, ('chip', 'core'), [(z * 2 + c, (z ^ pair[c]) * 2 + c)...  6.71 us
    ppermute x3, starting transfers between devices, body(): lax.ppermute(piece, ('chip', 'core'), [(z * 2 + c, (z ^ pair[c]) * 2 + c)...  5.71 us
    pallas_call x2, Pallas kernels, local_part(): pl.pallas_call(functools.partial(local_kernel, coefs, turn), out_shape=[p...  3.44 us
    ppermute x2, starting transfers between devices, body(): lax.ppermute(state, ('frame', 'core'), [(f * 2 + c, ((f + 1) % frames if...  3.05 us
    ppermute x2, waiting for transfers between devices, body(): lax.ppermute(state, ('frame', 'core'), [(f * 2 + c, ((f + 1) % frames if...  2.9 us
    pallas_call x2, Pallas kernels, write_late(): pl.pallas_call(functools.partial(kernel, turn, chips, early), out_shape=j...  1.9 us
  transfers between devices with their start and end apart: 15, of which 10 were waited for; matrix products, arithmetic and copies ran while one was open for 0% of the time, Pallas kernels for 12%

profile of v14, /device:TPU:0, one launch (start us, length us, event | category | flops | bytes accessed | tf_op | source)
XLA Modules:
  0.0 45.3 jit_solution(12701077900937861979)
XLA Ops:
  0.0 1.7 %shard_map.64 = (bf16[1536,128]{1,0:T(8,128)(2,1)S(1)}, bf16[128,3072]{1,0:T(8,128)(2,1)S(1)}, bf16[128,3072]{1,0:T(8,128)(2,1)S(1)}) custom-call(bf16[128,3072]{1,0:T(8,128)(2,1)} %key_ref.1, bf16[128,3072]{1,0:T(8,128)(2,1)} %value_ref.1), custom_call_target="tpu_custom_call" | custom-call | flops 50331648 | bytes 1572864 | tf_op jit(solution)/shard_map/pallas_call | solution.py:84
  1.7 0.5 %collective-permute-start = (bf16[1536,128]{1,0:T(8,128)(2,1)S(1)}, bf16[1536,128]{1,0:T(8,128)(2,1)S(1)}, u32[]{:S(2)}, u32[]{:S(2)}) collective-permute-start(bf16[1536,128]{1,0:T(8,128)(2,1)S(1)} %get-tuple-element.20), channel_id=1, source_target_pairs={{0,1},{1,0},{2,3},{3,2},{4,5},{5,4},{6,7},{7,6},{8,9},{9,8},{10,11... | collective-permute-start | bytes 1179656 | tf_op jit(solution)/shard_map/ppermute | solution.py:344
  2.2 0.5 %shard_map.65.mine_ref = f32[1536,128]{1,0:T(8,128)S(1)} custom-call(bf16[128,3072]{1,0:T(8,128)(2,1)S(1)} %get-tuple-element.18.key_ref, bf16[128,3072]{1,0:T(8,128)(2,1)S(1)} %get-tuple-element.19.value_ref), custom_call_target="tpu_custom_call" | custom-call | flops 50331648 | bytes 1572864 | tf_op jit(solution)/shard_map/pallas_call | solution.py:104
  2.7 0.8 %collective-permute-done.other_ref = bf16[1536,128]{1,0:T(8,128)(2,1)S(1)} collective-permute-done((bf16[1536,128]{1,0:T(8,128)(2,1)S(1)}, bf16[1536,128]{1,0:T(8,128)(2,1)S(1)}, u32[]{:S(2)}, u32[]{:S(2)}) %collective-permute-start) | collective-permute-done | bytes 393248 | tf_op jit(solution)/shard_map/ppermute | solution.py:344
  3.5 0.1 shard_map.66
  3.6 5.1 %collective-permute-start.1 = (bf16[384,128]{1,0:T(8,128)(2,1)S(1)}, bf16[384,128]{1,0:T(8,128)(2,1)S(1)}, u32[]{:S(2)}, u32[]{:S(2)}) collective-permute-start(bf16[384,128]{1,0:T(8,128)(2,1)S(1)} %get-tuple-element.25), channel_id=1, source_target_pairs={{0,6},{1,3},{2,4},{3,1},{4,2},{5,7},{6,0},{7,5},{8,14},{9,11},{10,... | collective-permute-start | bytes 294920 | tf_op jit(solution)/shard_map/ppermute | solution.py:369
  8.7 0.6 %collective-permute-start.3 = (bf16[384,128]{1,0:T(8,128)(2,1)S(1)}, bf16[384,128]{1,0:T(8,128)(2,1)S(1)}, u32[]{:S(2)}, u32[]{:S(2)}) collective-permute-start(bf16[384,128]{1,0:T(8,128)(2,1)S(1)} %get-tuple-element.27), channel_id=1, source_target_pairs={{0,2},{1,5},{2,0},{3,7},{4,6},{5,1},{6,4},{7,3},{8,10},{9,13},{10,... | collective-permute-start | bytes 294920 | tf_op jit(solution)/shard_map/ppermute | solution.py:369
  9.4 1.7 %shard_map.67 = (f32[128,1536]{1,0:T(8,128)S(1)}, bf16[128,1536]{1,0:T(8,128)(2,1)S(1)}, bf16[128,1536]{1,0:T(8,128)(2,1)S(1)}) custom-call(s32[1,4]{1,0:T(1,128)S(1)} %copy-done.2, s32[1,4]{1,0:T(1,128)S(1)} %copy-done.3, bf16[128,3072]{1,0:T(8,128)(2,1)S(1)} %copy-done, bf16[128,3072]{1,0:T(8,128)(2,1)S(1)} %get-tuple-element.18.key_ref, ...), custom_call_target="tpu_custom_call" | custom-call | flops 100663296 | bytes 2752512 | tf_op jit(solution)/shard_map/pallas_call | solution.py:252
  11.1 1.2 %collective-permute-done.1.refs_0_ = bf16[384,128]{1,0:T(8,128)(2,1)S(1)} collective-permute-done((bf16[384,128]{1,0:T(8,128)(2,1)S(1)}, bf16[384,128]{1,0:T(8,128)(2,1)S(1)}, u32[]{:S(2)}, u32[]{:S(2)}) %collective-permute-start.1) | collective-permute-done | bytes 98336 | tf_op jit(solution)/shard_map/ppermute | solution.py:369
  12.3 5.5 %collective-permute-done.2.refs_1_ = bf16[384,128]{1,0:T(8,128)(2,1)S(1)} collective-permute-done((bf16[384,128]{1,0:T(8,128)(2,1)S(1)}, bf16[384,128]{1,0:T(8,128)(2,1)S(1)}, u32[]{:S(2)}, u32[]{:S(2)}) %collective-permute-start.2) | collective-permute-done | bytes 98336 | tf_op jit(solution)/shard_map/ppermute | solution.py:369
  17.8 0.1 shard_map.68.after_ref
  17.9 1.6 %collective-permute-start.5 = (bf16[384,128]{1,0:T(8,128)(2,1)S(1)}, bf16[384,128]{1,0:T(8,128)(2,1)S(1)}, u32[]{:S(2)}, u32[]{:S(2)}) collective-permute-start(bf16[384,128]{1,0:T(8,128)(2,1)S(1)} %shard_map.68.after_ref), channel_id=1, source_target_pairs={{0,16},{1,9},{8,24},{9,17},{16,0},{17,25},{24,8},{25,1},{2,18},{3,... | collective-permute-start | bytes 294920 | tf_op jit(solution)/shard_map/ppermute | solution.py:382
  19.4 1.5 %collective-permute-start.4 = (bf16[384,128]{1,0:T(8,128)(2,1)S(1)}, bf16[384,128]{1,0:T(8,128)(2,1)S(1)}, u32[]{:S(2)}, u32[]{:S(2)}) collective-permute-start(bf16[384,128]{1,0:T(8,128)(2,1)S(1)} %shard_map.68.after_ref), channel_id=1, source_target_pairs={{0,8},{1,17},{8,16},{9,25},{16,24},{17,1},{24,0},{25,9},{2,10},{3,... | collective-permute-start | bytes 294920 | tf_op jit(solution)/shard_map/ppermute | solution.py:382
  20.9 1.7 %shard_map.69 = (f32[128,1536]{1,0:T(8,128)S(1)}, bf16[128,1536]{1,0:T(8,128)(2,1)S(1)}, bf16[128,1536]{1,0:T(8,128)(2,1)S(1)}) custom-call(s32[1,4]{1,0:T(1,128)S(1)} %copy-done.2, s32[1,4]{1,0:T(1,128)S(1)} %copy-done.3, bf16[128,3072]{1,0:T(8,128)(2,1)S(1)} %copy-done, bf16[128,3072]{1,0:T(8,128)(2,1)S(1)} %get-tuple-element.18.key_ref, ...), custom_call_target="tpu_custom_call" | custom-call | flops 100663296 | bytes 2752512 | tf_op jit(solution)/shard_map/pallas_call | solution.py:252
  22.7 2.9 %collective-permute-done.5.two_ref = bf16[384,128]{1,0:T(8,128)(2,1)S(1)} collective-permute-done((bf16[384,128]{1,0:T(8,128)(2,1)S(1)}, bf16[384,128]{1,0:T(8,128)(2,1)S(1)}, u32[]{:S(2)}, u32[]{:S(2)}) %collective-permute-start.5) | collective-permute-done | bytes 98336 | tf_op jit(solution)/shard_map/ppermute | solution.py:382
  25.6 0.1 collective-permute-start.9
  25.7 2.8 %collective-permute-start.8 = (bf16[384,128]{1,0:T(8,128)(2,1)S(1)}, bf16[384,128]{1,0:T(8,128)(2,1)S(1)}, u32[]{:S(2)}, u32[]{:S(2)}) collective-permute-start(bf16[384,128]{1,0:T(8,128)(2,1)S(1)} %shard_map.70.refs_1_), channel_id=1, source_target_pairs={{0,2},{2,0},{4,6},{6,4},{1,3},{3,1},{5,7},{7,5},{8,10},{10,8},{12,... | collective-permute-start | bytes 294920 | tf_op jit(solution)/shard_map/ppermute | solution.py:344
  28.5 1.5 %collective-permute-start.7 = (bf16[384,128]{1,0:T(8,128)(2,1)S(1)}, bf16[384,128]{1,0:T(8,128)(2,1)S(1)}, u32[]{:S(2)}, u32[]{:S(2)}) collective-permute-start(bf16[384,128]{1,0:T(8,128)(2,1)S(1)} %shard_map.70.refs_1_), channel_id=1, source_target_pairs={{0,6},{2,4},{4,2},{6,0},{1,7},{3,5},{5,3},{7,1},{8,14},{10,12},{12... | collective-permute-start | bytes 294920 | tf_op jit(solution)/shard_map/ppermute | solution.py:344
  30.1 5.3 %collective-permute-done.9.refs_5_ = bf16[384,128]{1,0:T(8,128)(2,1)S(1)} collective-permute-done((bf16[384,128]{1,0:T(8,128)(2,1)S(1)}, bf16[384,128]{1,0:T(8,128)(2,1)S(1)}, u32[]{:S(2)}, u32[]{:S(2)}) %collective-permute-start.9) | collective-permute-done | bytes 98336 | tf_op jit(solution)/shard_map/ppermute | solution.py:344
  35.4 0.2 collective-permute-done.8.refs_4_
  35.5 1.9 %collective-permute-start.10 = (bf16[384,128]{1,0:T(8,128)(2,1)S(1)}, bf16[384,128]{1,0:T(8,128)(2,1)S(1)}, u32[]{:S(2)}, u32[]{:S(2)}) collective-permute-start(bf16[384,128]{1,0:T(8,128)(2,1)S(1)} %collective-permute-done.8.refs_4_), channel_id=1, source_target_pairs={{0,8},{8,0},{16,24},{24,16},{1,9},{9,1},{17,25},{25,17},{2,10},{10... | collective-permute-start | bytes 294920 | tf_op jit(solution)/shard_map/ppermute | solution.py:344
  37.4 0.2 collective-permute-start.12
  37.6 0.1 collective-permute-start.13
  37.7 0.3 shard_map.72.base_ref
  38.0 2.6 %collective-permute-done.11.refs_1_ = bf16[384,128]{1,0:T(8,128)(2,1)S(1)} collective-permute-done((bf16[384,128]{1,0:T(8,128)(2,1)S(1)}, bf16[384,128]{1,0:T(8,128)(2,1)S(1)}, u32[]{:S(2)}, u32[]{:S(2)}) %collective-permute-start.11) | collective-permute-done | bytes 98336 | tf_op jit(solution)/shard_map/ppermute | solution.py:344
  40.6 1.1 %collective-permute-done.10.refs_0_ = bf16[384,128]{1,0:T(8,128)(2,1)S(1)} collective-permute-done((bf16[384,128]{1,0:T(8,128)(2,1)S(1)}, bf16[384,128]{1,0:T(8,128)(2,1)S(1)}, u32[]{:S(2)}, u32[]{:S(2)}) %collective-permute-start.10) | collective-permute-done | bytes 98336 | tf_op jit(solution)/shard_map/ppermute | solution.py:344
  41.7 1.1 %collective-permute-done.12.refs_2_ = bf16[384,128]{1,0:T(8,128)(2,1)S(1)} collective-permute-done((bf16[384,128]{1,0:T(8,128)(2,1)S(1)}, bf16[384,128]{1,0:T(8,128)(2,1)S(1)}, u32[]{:S(2)}, u32[]{:S(2)}) %collective-permute-start.12) | collective-permute-done | bytes 98336 | tf_op jit(solution)/shard_map/ppermute | solution.py:344
  42.7 0.1 collective-permute-start.14
  42.8 0.9 %shard_map.74.out_before_ref = bf16[128,3072]{1,0:T(8,128)(2,1)} custom-call(f32[128,1536]{1,0:T(8,128)S(1)} %shard_map.72.base_ref, bf16[128,1536]{1,0:T(8,128)(2,1)S(1)} %get-tuple-element.24.y_ref, bf16[1152,128]{1,0:T(8,128)(2,1)S(1)} %shard_map.73.refs_0_), custom_call_target="tpu_custom_call" | custom-call | flops 20000000000 | bytes 1024 | tf_op jit(solution)/shard_map/pallas_call | solution.py:331
  43.8 0.3 shard_map.75.refs_0_
  44.1 0.3 collective-permute-done.14.refs_2_
  44.4 0.9 %shard_map.76 = bf16[128,3072]{1,0:T(8,128)(2,1)} custom-call(bf16[128,3072]{1,0:T(8,128)(2,1)} %shard_map.74.out_before_ref, f32[128,1536]{1,0:T(8,128)S(1)} %shard_map.75.refs_0_, bf16[128,1536]{1,0:T(8,128)(2,1)S(1)} %get-tuple-element.30.y_ref.refs_1_, bf16[1152,128]{1,0:T(8,128)(2,1)S(1)} %collective-permute-done.14.refs_2_), custom_call_target="tpu_custom_call", output_to_operand_aliasing={{}: (0, {})} | custom-call | flops 1024 | bytes 1024 | tf_op jit(solution)/shard_map/pallas_call | solution.py:331
  (19 shorter events, 0.2 us)
Async XLA Ops:
  1.7 1.8 %collective-permute-start = (bf16[1536,128]{1,0:T(8,128)(2,1)S(1)}, bf16[1536,128]{1,0:T(8,128)(2,1)S(1)}, u32[]{:S(2)}, u32[]{:S(2)}) collective-permute-start(bf16[1536,128]{1,0:T(8,128)(2,1)S(1)} %get-tuple-element.20), channel_id=1, source_target_pairs={{0,1},{1,0},{2,3},{3,2},{4,5},{5,4},{6,7},{7,6},{8,9},{9,8},{10,11... | collective-permute-start | bytes 1179656 | tf_op jit(solution)/shard_map/ppermute | solution.py:344
  2.7 6.6 %copy-start = (bf16[128,3072]{1,0:T(8,128)(2,1)S(1)}, bf16[128,3072]{1,0:T(8,128)(2,1)}, u32[]{:S(2)}) copy-start(bf16[128,3072]{1,0:T(8,128)(2,1)} %query_ref.3) | copy-start | bytes 2359300
  2.7 6.6 %copy-start.1 = (f32[3,24,128]{2,1,0:T(8,128)S(1)}, f32[3,24,128]{2,1,0:T(8,128)}, u32[]{:S(2)}) copy-start(f32[3,24,128]{2,1,0:T(8,128)} %weight_ref.3) | copy-start | bytes 110596
  3.6 8.7 %collective-permute-start.1 = (bf16[384,128]{1,0:T(8,128)(2,1)S(1)}, bf16[384,128]{1,0:T(8,128)(2,1)S(1)}, u32[]{:S(2)}, u32[]{:S(2)}) collective-permute-start(bf16[384,128]{1,0:T(8,128)(2,1)S(1)} %get-tuple-element.25), channel_id=1, source_target_pairs={{0,6},{1,3},{2,4},{3,1},{4,2},{5,7},{6,0},{7,5},{8,14},{9,11},{10,... | collective-permute-start | bytes 294920 | tf_op jit(solution)/shard_map/ppermute | solution.py:369
  8.7 9.1 %collective-permute-start.2 = (bf16[384,128]{1,0:T(8,128)(2,1)S(1)}, bf16[384,128]{1,0:T(8,128)(2,1)S(1)}, u32[]{:S(2)}, u32[]{:S(2)}) collective-permute-start(bf16[384,128]{1,0:T(8,128)(2,1)S(1)} %get-tuple-element.26), channel_id=1, source_target_pairs={{0,4},{1,7},{2,6},{3,5},{4,0},{5,3},{6,2},{7,1},{8,12},{9,15},{10,... | collective-permute-start | bytes 294920 | tf_op jit(solution)/shard_map/ppermute | solution.py:369
  8.7 0.7 %copy-start.2 = (s32[1,4]{1,0:T(1,128)S(1)}, s32[1,4]{1,0:T(1,128)}, u32[]{:S(2)}) copy-start(s32[1,4]{1,0:T(1,128)} %length_ref.3) | copy-start | bytes 52
  8.7 0.7 %copy-start.3 = (s32[1,4]{1,0:T(1,128)S(1)}, s32[1,4]{1,0:T(1,128)}, u32[]{:S(2)}) copy-start(s32[1,4]{1,0:T(1,128)} %back_ref.3) | copy-start | bytes 52
  8.7 9.1 %collective-permute-start.3 = (bf16[384,128]{1,0:T(8,128)(2,1)S(1)}, bf16[384,128]{1,0:T(8,128)(2,1)S(1)}, u32[]{:S(2)}, u32[]{:S(2)}) collective-permute-start(bf16[384,128]{1,0:T(8,128)(2,1)S(1)} %get-tuple-element.27), channel_id=1, source_target_pairs={{0,2},{1,5},{2,0},{3,7},{4,6},{5,1},{6,4},{7,3},{8,10},{9,13},{10,... | collective-permute-start | bytes 294920 | tf_op jit(solution)/shard_map/ppermute | solution.py:369
  17.9 7.7 %collective-permute-start.5 = (bf16[384,128]{1,0:T(8,128)(2,1)S(1)}, bf16[384,128]{1,0:T(8,128)(2,1)S(1)}, u32[]{:S(2)}, u32[]{:S(2)}) collective-permute-start(bf16[384,128]{1,0:T(8,128)(2,1)S(1)} %shard_map.68.after_ref), channel_id=1, source_target_pairs={{0,16},{1,9},{8,24},{9,17},{16,0},{17,25},{24,8},{25,1},{2,18},{3,... | collective-permute-start | bytes 294920 | tf_op jit(solution)/shard_map/ppermute | solution.py:382
  19.4 6.1 %collective-permute-start.4 = (bf16[384,128]{1,0:T(8,128)(2,1)S(1)}, bf16[384,128]{1,0:T(8,128)(2,1)S(1)}, u32[]{:S(2)}, u32[]{:S(2)}) collective-permute-start(bf16[384,128]{1,0:T(8,128)(2,1)S(1)} %shard_map.68.after_ref), channel_id=1, source_target_pairs={{0,8},{1,17},{8,16},{9,25},{16,24},{17,1},{24,0},{25,9},{2,10},{3,... | collective-permute-start | bytes 294920 | tf_op jit(solution)/shard_map/ppermute | solution.py:382
  25.6 9.8 %collective-permute-start.9 = (bf16[384,128]{1,0:T(8,128)(2,1)S(1)}, bf16[384,128]{1,0:T(8,128)(2,1)S(1)}, u32[]{:S(2)}, u32[]{:S(2)}) collective-permute-start(bf16[384,128]{1,0:T(8,128)(2,1)S(1)} %shard_map.70.refs_1_), channel_id=1, source_target_pairs={{0,4},{2,6},{4,0},{6,2},{1,5},{3,7},{5,1},{7,3},{8,12},{10,14},{12... | collective-permute-start | bytes 294920 | tf_op jit(solution)/shard_map/ppermute | solution.py:344
  25.7 9.8 %collective-permute-start.8 = (bf16[384,128]{1,0:T(8,128)(2,1)S(1)}, bf16[384,128]{1,0:T(8,128)(2,1)S(1)}, u32[]{:S(2)}, u32[]{:S(2)}) collective-permute-start(bf16[384,128]{1,0:T(8,128)(2,1)S(1)} %shard_map.70.refs_1_), channel_id=1, source_target_pairs={{0,2},{2,0},{4,6},{6,4},{1,3},{3,1},{5,7},{7,5},{8,10},{10,8},{12,... | collective-permute-start | bytes 294920 | tf_op jit(solution)/shard_map/ppermute | solution.py:344
  28.5 8.9 %collective-permute-start.7 = (bf16[384,128]{1,0:T(8,128)(2,1)S(1)}, bf16[384,128]{1,0:T(8,128)(2,1)S(1)}, u32[]{:S(2)}, u32[]{:S(2)}) collective-permute-start(bf16[384,128]{1,0:T(8,128)(2,1)S(1)} %shard_map.70.refs_1_), channel_id=1, source_target_pairs={{0,6},{2,4},{4,2},{6,0},{1,7},{3,5},{5,3},{7,1},{8,14},{10,12},{12... | collective-permute-start | bytes 294920 | tf_op jit(solution)/shard_map/ppermute | solution.py:344
  30.0 7.5 %collective-permute-start.6 = (bf16[384,128]{1,0:T(8,128)(2,1)S(1)}, bf16[384,128]{1,0:T(8,128)(2,1)S(1)}, u32[]{:S(2)}, u32[]{:S(2)}) collective-permute-start(bf16[384,128]{1,0:T(8,128)(2,1)S(1)} %shard_map.70.refs_1_), channel_id=1, source_target_pairs={{0,8},{8,0},{16,24},{24,16},{1,9},{9,1},{17,25},{25,17},{2,10},{10... | collective-permute-start | bytes 294920 | tf_op jit(solution)/shard_map/ppermute | solution.py:344
  35.4 5.2 %collective-permute-start.11 = (bf16[384,128]{1,0:T(8,128)(2,1)S(1)}, bf16[384,128]{1,0:T(8,128)(2,1)S(1)}, u32[]{:S(2)}, u32[]{:S(2)}) collective-permute-start(bf16[384,128]{1,0:T(8,128)(2,1)S(1)} %collective-permute-done.9.refs_5_), channel_id=1, source_target_pairs={{0,8},{8,0},{16,24},{24,16},{1,9},{9,1},{17,25},{25,17},{2,10},{10... | collective-permute-start | bytes 294920 | tf_op jit(solution)/shard_map/ppermute | solution.py:344
  35.5 6.1 %collective-permute-start.10 = (bf16[384,128]{1,0:T(8,128)(2,1)S(1)}, bf16[384,128]{1,0:T(8,128)(2,1)S(1)}, u32[]{:S(2)}, u32[]{:S(2)}) collective-permute-start(bf16[384,128]{1,0:T(8,128)(2,1)S(1)} %collective-permute-done.8.refs_4_), channel_id=1, source_target_pairs={{0,8},{8,0},{16,24},{24,16},{1,9},{9,1},{17,25},{25,17},{2,10},{10... | collective-permute-start | bytes 294920 | tf_op jit(solution)/shard_map/ppermute | solution.py:344
  37.4 5.3 %collective-permute-start.12 = (bf16[384,128]{1,0:T(8,128)(2,1)S(1)}, bf16[384,128]{1,0:T(8,128)(2,1)S(1)}, u32[]{:S(2)}, u32[]{:S(2)}) collective-permute-start(bf16[384,128]{1,0:T(8,128)(2,1)S(1)} %collective-permute-done.7.refs_3_), channel_id=1, source_target_pairs={{0,8},{8,0},{16,24},{24,16},{1,9},{9,1},{17,25},{25,17},{2,10},{10... | collective-permute-start | bytes 294920 | tf_op jit(solution)/shard_map/ppermute | solution.py:344
  37.6 6.2 %collective-permute-start.13 = (bf16[1920,128]{1,0:T(8,128)(2,1)S(1)}, bf16[1920,128]{1,0:T(8,128)(2,1)S(1)}, u32[]{:S(2)}, u32[]{:S(2)}) collective-permute-start(bf16[1920,128]{1,0:T(8,128)(2,1)S(1)} %shard_map.71.state_ref), channel_id=1, source_target_pairs={{0,1},{1,0},{2,3},{3,2},{4,5},{5,4},{6,7},{7,6},{8,9},{9,8},{10,11... | collective-permute-start | bytes 1474568 | tf_op jit(solution)/shard_map/ppermute | solution.py:344
  42.7 1.6 %collective-permute-start.14 = (bf16[1152,128]{1,0:T(8,128)(2,1)S(1)}, bf16[1152,128]{1,0:T(8,128)(2,1)S(1)}, u32[]{:S(2)}, u32[]{:S(2)}) collective-permute-start(bf16[1152,128]{1,0:T(8,128)(2,1)S(1)} %shard_map.73.refs_0_), channel_id=1, source_target_pairs={{0,1},{1,0},{2,3},{3,2},{4,5},{5,4},{6,7},{7,6},{8,9},{9,8},{10,11... | collective-permute-start | bytes 884744 | tf_op jit(solution)/shard_map/ppermute | solution.py:344

commit v15 on v10

--- a/solution.py
+++ b/solution.py
@@ -113,24 +113,25 @@
     )(*in_vmem(keys, values))
 
 
-def piece_kernel(mine_ref, other_ref, own_ref, *piece_refs):
+def piece_kernel(after, *refs):
+    mine_ref, other_ref, own_ref, *piece_refs = refs[after:]
     chip = lax.axis_index("chip")
     rows = own_ref.shape[0]
-    for d, ref in enumerate((own_ref,) + piece_refs):
+    for d, ref in enumerate([own_ref] + piece_refs):
         at = pl.ds(pl.multiple_of((chip ^ d) * rows, rows), rows)
         ref[...] = (mine_ref[at, :] + other_ref[at, :].astype(F32)).astype(ref.dtype)
 
 
-def chip_pieces(mine, other, chips):
+def chip_pieces(after, mine, other, chips):
     shape = (mine.shape[0] // chips, HEAD_DIM)
     return pl.pallas_call(
-        piece_kernel,
+        functools.partial(piece_kernel, len(after)),
         out_shape=[pltpu.VMEM(shape, F32)] + [pltpu.VMEM(shape, BF16)] * (chips - 1),
-        in_specs=[WHOLE, WHOLE],
+        in_specs=[ANYWHERE] * len(after) + [WHOLE, WHOLE],
         out_specs=[WHOLE] * chips,
         compiler_params=PARAMS,
         cost_estimate=SMALL,
-    )(*in_vmem(mine, other))
+    )(*after, *in_vmem(mine, other))
 
 
 def sum_kernel(after_ref, own_ref, *refs):
@@ -188,8 +189,24 @@
     )(*after, *in_vmem(*pieces))
 
 
-def local_kernel(
-    coefs, turn, length_ref, back_ref, query_ref, key_ref, value_ref, weight_ref, after_ref, local_ref, *read_refs
+def local_kernel(coefs, turn, core, *refs):
+    inputs, rest = refs[:6], refs[7:]
+    outputs = rest[-3:]
+
+    @pl.when(lax.axis_index("core") == core)
+    def _():
+        local_heads(coefs, turn, *inputs, *outputs)
+
+    if len(rest) > 3:
+
+        @pl.when(lax.axis_index("core") != core)
+        def _():
+            for ref, out_ref in zip(rest, outputs):
+                out_ref[...] = ref[...]
+
+
+def local_heads(
+    coefs, turn, length_ref, back_ref, query_ref, key_ref, value_ref, weight_ref, local_ref, *read_refs
 ):
     tokens = query_ref.shape[0]
     first = core_heads()[turn]
@@ -245,21 +262,23 @@
             read_ref[:, at] = (query * gains[:, which : which + 1]).astype(BF16)
 
 
-def local_part(coefs, slots, turn, frame_len, window_back, queries, keys, values, weights, after):
+def local_part(
+    coefs, frame_len, window_back, queries, keys, values, weights, turn, core, after, earlier=()
+):
     tokens, width = queries.shape
     width //= 2
     return pl.pallas_call(
-        functools.partial(local_kernel, coefs, turn),
-        out_shape=[pltpu.VMEM((tokens, width), F32)] + [pltpu.VMEM((tokens, width), BF16)] * slots,
-        in_specs=[SCALARS] * 2 + [WHOLE] * 4 + [ANYWHERE],
-        out_specs=[WHOLE] * (1 + slots),
+        functools.partial(local_kernel, coefs, turn, core),
+        out_shape=[pltpu.VMEM((tokens, width), F32)] + [pltpu.VMEM((tokens, width), BF16)] * 2,
+        in_specs=[SCALARS] * 2 + [WHOLE] * 4 + [ANYWHERE] + [WHOLE] * len(earlier),
+        out_specs=[WHOLE] * 3,
         compiler_params=PARAMS,
         cost_estimate=pl.CostEstimate(
             flops=4 * tokens * tokens * width,
             bytes_accessed=14 * tokens * width,
             transcendentals=tokens * width,
         ),
-    )(frame_len, window_back, queries, *in_vmem(keys, values), weights, after)
+    )(frame_len, window_back, queries, *in_vmem(keys, values), weights, after, *in_vmem(*earlier))
 
 
 def read_heads(d, chips, base_ref, states):
@@ -354,20 +373,22 @@
         x_high = jnp.where(f == 2, high, 0.0)
         return [[(0, x_low), (1, x_high)], [(1, jnp.where(f == 3, high, 0.0))]]
 
-    local = functools.partial(local_part, coefs, 2)
-    rest = (frame_len, window_back, queries)
     early = 1
 
     outgoing, keys, values = outgoing_state(keys, values)
     incoming = swap(outgoing, "core", 1, 2)
     mine = own_state(keys, values)
-    own, *sends = chip_pieces(mine, incoming, chips)
+    local = functools.partial(
+        local_part, coefs, frame_len, window_back, queries, keys, values, level_weight
+    )
+    first = [local(turn, 0, mine) for turn in range(2)]
+    own, *sends = chip_pieces([array for part in first for array in part[:1]], mine, incoming, chips)
     got = [swap(sends[d - 1], "chip", d, chips) for d in reversed(range(1, chips))]
-    local_0, x_0, y_0 = local(0, *rest, keys, values, level_weight, own)
+    local_0, x_0, y_0 = local(0, 1, own, first[0])
     state = sum_pieces(local_0, own, got, F32 if outer > 1 else BF16)
     if outer > 1:
         state = lax.psum(state, "outer").astype(BF16)
-    local_1, x_1, y_1 = local(1, *rest, keys, values, level_weight, state)
+    local_1, x_1, y_1 = local(1, 1, state, first[1])
     shifted = lax.ppermute(state, "frame", [(f, (f + 1) % frames) for f in range(frames)])
     slot = choose_slot(local_1, shifted, swap(state, "frame", 2, frames))
 

time: 41.8 us -> 42.3 us (1.012)
  Pallas kernels: 8.37 us -> 9.69 us
  waiting for transfers between devices: 15.9 us -> 15.1 us
  starting transfers between devices: 17.3 us -> 16.7 us
  local copies, waits for them, and re-layouts: 0.04 us -> 0.6 us
    pallas_call x3 -> x5, Pallas kernels: 3.53 us -> 4.85 us  [the longest x4 4.76 us: local_part(): pl.pallas_call(functools.partial(local_kernel, coefs, turn, core), out_sh...]
    ppermute x14, waiting for transfers between devices: 14.5 us -> 13.7 us  [swap(): return lax.ppermute(array, axis, [(n, n ^ mask) for n in range(size)])]
    unnamed x8, local copies, waits for them, and re-layouts: 0.04 us -> 0.6 us
    ppermute x14, starting transfers between devices: 15.8 us -> 15.2 us  [swap(): return lax.ppermute(array, axis, [(n, n ^ mask) for n in range(size)])]
  transfers between devices with their start and end apart: 15 -> 15, of which waited for: 10 -> 10; matrix products, arithmetic and copies ran while one was open for 0% -> 0% of each run, Pallas kernels for 13% -> 16%
where the time goes in v15:
time: 42.3 us; the launch traced here: 42.2 us
  starting transfers between devices  16.7 us (39%)
  waiting for transfers between devices  15.1 us (36%)
  Pallas kernels  9.69 us (23%)
  local copies, waits for them, and re-layouts  0.6 us (1%)
    ppermute x14, starting transfers between devices, swap(): return lax.ppermute(array, axis, [(n, n ^ mask) for n in range(size)])  15.2 us
    ppermute x14, waiting for transfers between devices, swap(): return lax.ppermute(array, axis, [(n, n ^ mask) for n in range(size)])  13.7 us
    pallas_call x4, Pallas kernels, local_part(): pl.pallas_call(functools.partial(local_kernel, coefs, turn, core), out_sh...  4.76 us
    pallas_call x2, Pallas kernels, write_late(): pl.pallas_call(functools.partial(kernel, turn, chips, early), out_shape=j...  1.88 us
    pallas_call x1, Pallas kernels, outgoing_state(): pl.pallas_call(functools.partial(first_kernel, parts), out_shape=[pltpu.V...  1.69 us
    ppermute x1, starting transfers between devices, body(): lax.ppermute(state, 'frame', [(f, (f + 1) % frames) for f in range(frames)])  1.48 us
    ppermute x1, waiting for transfers between devices, body(): lax.ppermute(state, 'frame', [(f, (f + 1) % frames) for f in range(frames)])  1.36 us
  transfers between devices with their start and end apart: 15, of which 10 were waited for; matrix products, arithmetic and copies ran while one was open for 0% of the time, Pallas kernels for 16%

profile of v15, /device:TPU:0, one launch (start us, length us, event | category | flops | bytes accessed | tf_op | source)
XLA Modules:
  0.0 42.2 jit_solution(2068537795622407656)
XLA Ops:
  0.0 1.7 %shard_map.64 = (bf16[1536,128]{1,0:T(8,128)(2,1)S(1)}, bf16[128,3072]{1,0:T(8,128)(2,1)S(1)}, bf16[128,3072]{1,0:T(8,128)(2,1)S(1)}) custom-call(bf16[128,3072]{1,0:T(8,128)(2,1)} %key_ref.1, bf16[128,3072]{1,0:T(8,128)(2,1)} %value_ref.1), custom_call_target="tpu_custom_call" | custom-call | flops 50331648 | bytes 1572864 | tf_op jit(solution)/shard_map/pallas_call | solution.py:84
  1.7 0.5 %collective-permute-start = (bf16[1536,128]{1,0:T(8,128)(2,1)S(1)}, bf16[1536,128]{1,0:T(8,128)(2,1)S(1)}, u32[]{:S(2)}, u32[]{:S(2)}) collective-permute-start(bf16[1536,128]{1,0:T(8,128)(2,1)S(1)} %get-tuple-element.28), channel_id=1, source_target_pairs={{0,1},{1,0},{2,3},{3,2},{4,5},{5,4},{6,7},{7,6},{8,9},{9,8},{10,11... | collective-permute-start | bytes 1179656 | tf_op jit(solution)/shard_map/ppermute | solution.py:362
  2.2 0.5 %shard_map.65.refs_6_.refs_2_ = f32[1536,128]{1,0:T(8,128)S(1)} custom-call(bf16[128,3072]{1,0:T(8,128)(2,1)S(1)} %get-tuple-element.24.key_ref.refs_3_, bf16[128,3072]{1,0:T(8,128)(2,1)S(1)} %get-tuple-element.25.value_ref.refs_4_), custom_call_target="tpu_custom_call" | custom-call | flops 50331648 | bytes 1572864 | tf_op jit(solution)/shard_map/pallas_call | solution.py:104
  2.7 0.6 %copy-done = bf16[128,3072]{1,0:T(8,128)(2,1)S(1)} copy-done((bf16[128,3072]{1,0:T(8,128)(2,1)S(1)}, bf16[128,3072]{1,0:T(8,128)(2,1)}, u32[]{:S(2)}) %copy-start) | copy-done | bytes 786456
  3.3 1.7 %shard_map.67 = (f32[128,1536]{1,0:T(8,128)S(1)}, bf16[128,1536]{1,0:T(8,128)(2,1)S(1)}, bf16[128,1536]{1,0:T(8,128)(2,1)S(1)}) custom-call(s32[1,4]{1,0:T(1,128)S(1)} %copy-done.2, s32[1,4]{1,0:T(1,128)S(1)} %copy-done.3, bf16[128,3072]{1,0:T(8,128)(2,1)S(1)} %copy-done, bf16[128,3072]{1,0:T(8,128)(2,1)S(1)} %get-tuple-element.24.key_ref.refs_3_, ...), custom_call_target="tpu_custom_call" | custom-call | flops 100663296 | bytes 2752512 | tf_op jit(solution)/shard_map/pallas_call | solution.py:270
  5.1 1.7 %shard_map.66 = (f32[128,1536]{1,0:T(8,128)S(1)}, bf16[128,1536]{1,0:T(8,128)(2,1)S(1)}, bf16[128,1536]{1,0:T(8,128)(2,1)S(1)}) custom-call(s32[1,4]{1,0:T(1,128)S(1)} %copy-done.2, s32[1,4]{1,0:T(1,128)S(1)} %copy-done.3, bf16[128,3072]{1,0:T(8,128)(2,1)S(1)} %copy-done, bf16[128,3072]{1,0:T(8,128)(2,1)S(1)} %get-tuple-element.24.key_ref.refs_3_, ...), custom_call_target="tpu_custom_call" | custom-call | flops 100663296 | bytes 2752512 | tf_op jit(solution)/shard_map/pallas_call | solution.py:270
  6.9 4.7 %collective-permute-start.1 = (bf16[384,128]{1,0:T(8,128)(2,1)S(1)}, bf16[384,128]{1,0:T(8,128)(2,1)S(1)}, u32[]{:S(2)}, u32[]{:S(2)}) collective-permute-start(bf16[384,128]{1,0:T(8,128)(2,1)S(1)} %get-tuple-element.35), channel_id=1, source_target_pairs={{0,6},{2,4},{4,2},{6,0},{1,7},{3,5},{5,3},{7,1},{8,14},{10,12},{12... | collective-permute-start | bytes 294920 | tf_op jit(solution)/shard_map/ppermute | solution.py:362
  11.6 0.6 %collective-permute-start.3 = (bf16[384,128]{1,0:T(8,128)(2,1)S(1)}, bf16[384,128]{1,0:T(8,128)(2,1)S(1)}, u32[]{:S(2)}, u32[]{:S(2)}) collective-permute-start(bf16[384,128]{1,0:T(8,128)(2,1)S(1)} %get-tuple-element.37), channel_id=1, source_target_pairs={{0,2},{2,0},{4,6},{6,4},{1,3},{3,1},{5,7},{7,5},{8,10},{10,8},{12,... | collective-permute-start | bytes 294920 | tf_op jit(solution)/shard_map/ppermute | solution.py:362
  12.3 0.7 %shard_map.69 = (f32[128,1536]{1,0:T(8,128)S(1)}, bf16[128,1536]{1,0:T(8,128)(2,1)S(1)}, bf16[128,1536]{1,0:T(8,128)(2,1)S(1)}) custom-call(s32[1,4]{1,0:T(1,128)S(1)} %copy-done.2, s32[1,4]{1,0:T(1,128)S(1)} %copy-done.3, bf16[128,3072]{1,0:T(8,128)(2,1)S(1)} %copy-done, bf16[128,3072]{1,0:T(8,128)(2,1)S(1)} %get-tuple-element.24.key_ref.refs_3_, ...), custom_call_target="tpu_custom_call" | custom-call | flops 100663296 | bytes 2752512 | tf_op jit(solution)/shard_map/pallas_call | solution.py:270
  12.9 1.3 %collective-permute-done.1.refs_0_ = bf16[384,128]{1,0:T(8,128)(2,1)S(1)} collective-permute-done((bf16[384,128]{1,0:T(8,128)(2,1)S(1)}, bf16[384,128]{1,0:T(8,128)(2,1)S(1)}, u32[]{:S(2)}, u32[]{:S(2)}) %collective-permute-start.1) | collective-permute-done | bytes 98336 | tf_op jit(solution)/shard_map/ppermute | solution.py:362
  14.3 4.0 %collective-permute-done.2.refs_1_ = bf16[384,128]{1,0:T(8,128)(2,1)S(1)} collective-permute-done((bf16[384,128]{1,0:T(8,128)(2,1)S(1)}, bf16[384,128]{1,0:T(8,128)(2,1)S(1)}, u32[]{:S(2)}, u32[]{:S(2)}) %collective-permute-start.2) | collective-permute-done | bytes 98336 | tf_op jit(solution)/shard_map/ppermute | solution.py:362
  18.4 1.6 %collective-permute-start.5 = (bf16[384,128]{1,0:T(8,128)(2,1)S(1)}, bf16[384,128]{1,0:T(8,128)(2,1)S(1)}, u32[]{:S(2)}, u32[]{:S(2)}) collective-permute-start(bf16[384,128]{1,0:T(8,128)(2,1)S(1)} %shard_map.70.refs_6_), channel_id=1, source_target_pairs={{0,16},{8,24},{16,0},{24,8},{1,17},{9,25},{17,1},{25,9},{2,18},{10... | collective-permute-start | bytes 294920 | tf_op jit(solution)/shard_map/ppermute | solution.py:362
  19.9 1.5 %collective-permute-start.4 = (bf16[384,128]{1,0:T(8,128)(2,1)S(1)}, bf16[384,128]{1,0:T(8,128)(2,1)S(1)}, u32[]{:S(2)}, u32[]{:S(2)}) collective-permute-start(bf16[384,128]{1,0:T(8,128)(2,1)S(1)} %shard_map.70.refs_6_), channel_id=1, source_target_pairs={{0,8},{8,16},{16,24},{24,0},{1,9},{9,17},{17,25},{25,1},{2,10},{10... | collective-permute-start | bytes 294920 | tf_op jit(solution)/shard_map/ppermute | solution.py:392
  21.4 0.7 %shard_map.71 = (f32[128,1536]{1,0:T(8,128)S(1)}, bf16[128,1536]{1,0:T(8,128)(2,1)S(1)}, bf16[128,1536]{1,0:T(8,128)(2,1)S(1)}) custom-call(s32[1,4]{1,0:T(1,128)S(1)} %copy-done.2, s32[1,4]{1,0:T(1,128)S(1)} %copy-done.3, bf16[128,3072]{1,0:T(8,128)(2,1)S(1)} %copy-done, bf16[128,3072]{1,0:T(8,128)(2,1)S(1)} %get-tuple-element.24.key_ref.refs_3_, ...), custom_call_target="tpu_custom_call" | custom-call | flops 100663296 | bytes 2752512 | tf_op jit(solution)/shard_map/pallas_call | solution.py:270
  22.1 2.0 %collective-permute-done.5.first_ref = bf16[384,128]{1,0:T(8,128)(2,1)S(1)} collective-permute-done((bf16[384,128]{1,0:T(8,128)(2,1)S(1)}, bf16[384,128]{1,0:T(8,128)(2,1)S(1)}, u32[]{:S(2)}, u32[]{:S(2)}) %collective-permute-start.5) | collective-permute-done | bytes 98336 | tf_op jit(solution)/shard_map/ppermute | solution.py:362
  24.1 1.4 %collective-permute-done.4.before_ref = bf16[384,128]{1,0:T(8,128)(2,1)S(1)} collective-permute-done((bf16[384,128]{1,0:T(8,128)(2,1)S(1)}, bf16[384,128]{1,0:T(8,128)(2,1)S(1)}, u32[]{:S(2)}, u32[]{:S(2)}) %collective-permute-start.4) | collective-permute-done | bytes 98336 | tf_op jit(solution)/shard_map/ppermute | solution.py:392
  25.5 0.9 %collective-permute-start.9 = (bf16[384,128]{1,0:T(8,128)(2,1)S(1)}, bf16[384,128]{1,0:T(8,128)(2,1)S(1)}, u32[]{:S(2)}, u32[]{:S(2)}) collective-permute-start(bf16[384,128]{1,0:T(8,128)(2,1)S(1)} %shard_map.72.refs_1_), channel_id=1, source_target_pairs={{0,4},{2,6},{4,0},{6,2},{1,5},{3,7},{5,1},{7,3},{8,12},{10,14},{12... | collective-permute-start | bytes 294920 | tf_op jit(solution)/shard_map/ppermute | solution.py:362
  26.4 2.1 %collective-permute-start.8 = (bf16[384,128]{1,0:T(8,128)(2,1)S(1)}, bf16[384,128]{1,0:T(8,128)(2,1)S(1)}, u32[]{:S(2)}, u32[]{:S(2)}) collective-permute-start(bf16[384,128]{1,0:T(8,128)(2,1)S(1)} %shard_map.72.refs_1_), channel_id=1, source_target_pairs={{0,2},{2,0},{4,6},{6,4},{1,3},{3,1},{5,7},{7,5},{8,10},{10,8},{12,... | collective-permute-start | bytes 294920 | tf_op jit(solution)/shard_map/ppermute | solution.py:362
  28.5 1.4 %collective-permute-start.7 = (bf16[384,128]{1,0:T(8,128)(2,1)S(1)}, bf16[384,128]{1,0:T(8,128)(2,1)S(1)}, u32[]{:S(2)}, u32[]{:S(2)}) collective-permute-start(bf16[384,128]{1,0:T(8,128)(2,1)S(1)} %shard_map.72.refs_1_), channel_id=1, source_target_pairs={{0,6},{2,4},{4,2},{6,0},{1,7},{3,5},{5,3},{7,1},{8,14},{10,12},{12... | collective-permute-start | bytes 294920 | tf_op jit(solution)/shard_map/ppermute | solution.py:362
  29.9 0.6 %collective-permute-start.6 = (bf16[384,128]{1,0:T(8,128)(2,1)S(1)}, bf16[384,128]{1,0:T(8,128)(2,1)S(1)}, u32[]{:S(2)}, u32[]{:S(2)}) collective-permute-start(bf16[384,128]{1,0:T(8,128)(2,1)S(1)} %shard_map.72.refs_1_), channel_id=1, source_target_pairs={{0,8},{8,0},{16,24},{24,16},{1,9},{9,1},{17,25},{25,17},{2,10},{10... | collective-permute-start | bytes 294920 | tf_op jit(solution)/shard_map/ppermute | solution.py:362
  30.5 1.7 %collective-permute-done.9.refs_5_ = bf16[384,128]{1,0:T(8,128)(2,1)S(1)} collective-permute-done((bf16[384,128]{1,0:T(8,128)(2,1)S(1)}, bf16[384,128]{1,0:T(8,128)(2,1)S(1)}, u32[]{:S(2)}, u32[]{:S(2)}) %collective-permute-start.9) | collective-permute-done | bytes 98336 | tf_op jit(solution)/shard_map/ppermute | solution.py:362
  32.3 0.8 %collective-permute-start.11 = (bf16[384,128]{1,0:T(8,128)(2,1)S(1)}, bf16[384,128]{1,0:T(8,128)(2,1)S(1)}, u32[]{:S(2)}, u32[]{:S(2)}) collective-permute-start(bf16[384,128]{1,0:T(8,128)(2,1)S(1)} %collective-permute-done.9.refs_5_), channel_id=1, source_target_pairs={{0,8},{8,0},{16,24},{24,16},{1,9},{9,1},{17,25},{25,17},{2,10},{10... | collective-permute-start | bytes 294920 | tf_op jit(solution)/shard_map/ppermute | solution.py:362
  33.0 1.3 %collective-permute-start.10 = (bf16[384,128]{1,0:T(8,128)(2,1)S(1)}, bf16[384,128]{1,0:T(8,128)(2,1)S(1)}, u32[]{:S(2)}, u32[]{:S(2)}) collective-permute-start(bf16[384,128]{1,0:T(8,128)(2,1)S(1)} %collective-permute-done.8.refs_4_), channel_id=1, source_target_pairs={{0,8},{8,0},{16,24},{24,16},{1,9},{9,1},{17,25},{25,17},{2,10},{10... | collective-permute-start | bytes 294920 | tf_op jit(solution)/shard_map/ppermute | solution.py:362
  34.3 0.7 %collective-permute-done.7.refs_3_ = bf16[384,128]{1,0:T(8,128)(2,1)S(1)} collective-permute-done((bf16[384,128]{1,0:T(8,128)(2,1)S(1)}, bf16[384,128]{1,0:T(8,128)(2,1)S(1)}, u32[]{:S(2)}, u32[]{:S(2)}) %collective-permute-start.7) | collective-permute-done | bytes 98336 | tf_op jit(solution)/shard_map/ppermute | solution.py:362
  35.0 0.6 %collective-permute-start.12 = (bf16[384,128]{1,0:T(8,128)(2,1)S(1)}, bf16[384,128]{1,0:T(8,128)(2,1)S(1)}, u32[]{:S(2)}, u32[]{:S(2)}) collective-permute-start(bf16[384,128]{1,0:T(8,128)(2,1)S(1)} %collective-permute-done.7.refs_3_), channel_id=1, source_target_pairs={{0,8},{8,0},{16,24},{24,16},{1,9},{9,1},{17,25},{25,17},{2,10},{10... | collective-permute-start | bytes 294920 | tf_op jit(solution)/shard_map/ppermute | solution.py:362
  35.7 0.3 shard_map.74.base_ref
  36.0 0.9 %collective-permute-done.11.refs_1_ = bf16[384,128]{1,0:T(8,128)(2,1)S(1)} collective-permute-done((bf16[384,128]{1,0:T(8,128)(2,1)S(1)}, bf16[384,128]{1,0:T(8,128)(2,1)S(1)}, u32[]{:S(2)}, u32[]{:S(2)}) %collective-permute-start.11) | collective-permute-done | bytes 98336 | tf_op jit(solution)/shard_map/ppermute | solution.py:362
  36.9 1.1 %collective-permute-done.10.refs_0_ = bf16[384,128]{1,0:T(8,128)(2,1)S(1)} collective-permute-done((bf16[384,128]{1,0:T(8,128)(2,1)S(1)}, bf16[384,128]{1,0:T(8,128)(2,1)S(1)}, u32[]{:S(2)}, u32[]{:S(2)}) %collective-permute-start.10) | collective-permute-done | bytes 98336 | tf_op jit(solution)/shard_map/ppermute | solution.py:362
  37.9 1.6 %collective-permute-done.12.refs_2_ = bf16[384,128]{1,0:T(8,128)(2,1)S(1)} collective-permute-done((bf16[384,128]{1,0:T(8,128)(2,1)S(1)}, bf16[384,128]{1,0:T(8,128)(2,1)S(1)}, u32[]{:S(2)}, u32[]{:S(2)}) %collective-permute-start.12) | collective-permute-done | bytes 98336 | tf_op jit(solution)/shard_map/ppermute | solution.py:362
  39.7 0.9 %shard_map.76.out_before_ref = bf16[128,3072]{1,0:T(8,128)(2,1)} custom-call(f32[128,1536]{1,0:T(8,128)S(1)} %shard_map.74.base_ref, bf16[128,1536]{1,0:T(8,128)(2,1)S(1)} %get-tuple-element.34.y_ref, bf16[1152,128]{1,0:T(8,128)(2,1)S(1)} %shard_map.75.refs_0_), custom_call_target="tpu_custom_call" | custom-call | flops 20000000000 | bytes 1024 | tf_op jit(solution)/shard_map/pallas_call | solution.py:349
  40.9 0.3 collective-permute-done.14.refs_2_
  41.3 0.9 %shard_map.78 = bf16[128,3072]{1,0:T(8,128)(2,1)} custom-call(bf16[128,3072]{1,0:T(8,128)(2,1)} %shard_map.76.out_before_ref, f32[128,1536]{1,0:T(8,128)S(1)} %shard_map.77.refs_0_, bf16[128,1536]{1,0:T(8,128)(2,1)S(1)} %get-tuple-element.42.y_ref.refs_1_, bf16[1152,128]{1,0:T(8,128)(2,1)S(1)} %collective-permute-done.14.refs_2_), custom_call_target="tpu_custom_call", output_to_operand_aliasing={{}: (0, {})} | custom-call | flops 1024 | bytes 1024 | tf_op jit(solution)/shard_map/pallas_call | solution.py:349
  (21 shorter events, 0.7 us)
Async XLA Ops:
  1.7 5.1 %collective-permute-start = (bf16[1536,128]{1,0:T(8,128)(2,1)S(1)}, bf16[1536,128]{1,0:T(8,128)(2,1)S(1)}, u32[]{:S(2)}, u32[]{:S(2)}) collective-permute-start(bf16[1536,128]{1,0:T(8,128)(2,1)S(1)} %get-tuple-element.28), channel_id=1, source_target_pairs={{0,1},{1,0},{2,3},{3,2},{4,5},{5,4},{6,7},{7,6},{8,9},{9,8},{10,11... | collective-permute-start | bytes 1179656 | tf_op jit(solution)/shard_map/ppermute | solution.py:362
  2.2 1.1 %copy-start = (bf16[128,3072]{1,0:T(8,128)(2,1)S(1)}, bf16[128,3072]{1,0:T(8,128)(2,1)}, u32[]{:S(2)}) copy-start(bf16[128,3072]{1,0:T(8,128)(2,1)} %refs_2_.7) | copy-start | bytes 2359300
  2.2 1.1 %copy-start.1 = (f32[3,24,128]{2,1,0:T(8,128)S(1)}, f32[3,24,128]{2,1,0:T(8,128)}, u32[]{:S(2)}) copy-start(f32[3,24,128]{2,1,0:T(8,128)} %refs_5_.7) | copy-start | bytes 110596
  2.2 1.1 %copy-start.2 = (s32[1,4]{1,0:T(1,128)S(1)}, s32[1,4]{1,0:T(1,128)}, u32[]{:S(2)}) copy-start(s32[1,4]{1,0:T(1,128)} %refs_0_.7) | copy-start | bytes 52
  2.2 1.1 %copy-start.3 = (s32[1,4]{1,0:T(1,128)S(1)}, s32[1,4]{1,0:T(1,128)}, u32[]{:S(2)}) copy-start(s32[1,4]{1,0:T(1,128)} %refs_1_.7) | copy-start | bytes 52
  6.9 7.4 %collective-permute-start.1 = (bf16[384,128]{1,0:T(8,128)(2,1)S(1)}, bf16[384,128]{1,0:T(8,128)(2,1)S(1)}, u32[]{:S(2)}, u32[]{:S(2)}) collective-permute-start(bf16[384,128]{1,0:T(8,128)(2,1)S(1)} %get-tuple-element.35), channel_id=1, source_target_pairs={{0,6},{2,4},{4,2},{6,0},{1,7},{3,5},{5,3},{7,1},{8,14},{10,12},{12... | collective-permute-start | bytes 294920 | tf_op jit(solution)/shard_map/ppermute | solution.py:362
  11.6 6.7 %collective-permute-start.2 = (bf16[384,128]{1,0:T(8,128)(2,1)S(1)}, bf16[384,128]{1,0:T(8,128)(2,1)S(1)}, u32[]{:S(2)}, u32[]{:S(2)}) collective-permute-start(bf16[384,128]{1,0:T(8,128)(2,1)S(1)} %get-tuple-element.36), channel_id=1, source_target_pairs={{0,4},{2,6},{4,0},{6,2},{1,5},{3,7},{5,1},{7,3},{8,12},{10,14},{12... | collective-permute-start | bytes 294920 | tf_op jit(solution)/shard_map/ppermute | solution.py:362
  11.6 6.7 %collective-permute-start.3 = (bf16[384,128]{1,0:T(8,128)(2,1)S(1)}, bf16[384,128]{1,0:T(8,128)(2,1)S(1)}, u32[]{:S(2)}, u32[]{:S(2)}) collective-permute-start(bf16[384,128]{1,0:T(8,128)(2,1)S(1)} %get-tuple-element.37), channel_id=1, source_target_pairs={{0,2},{2,0},{4,6},{6,4},{1,3},{3,1},{5,7},{7,5},{8,10},{10,8},{12,... | collective-permute-start | bytes 294920 | tf_op jit(solution)/shard_map/ppermute | solution.py:362
  18.4 5.7 %collective-permute-start.5 = (bf16[384,128]{1,0:T(8,128)(2,1)S(1)}, bf16[384,128]{1,0:T(8,128)(2,1)S(1)}, u32[]{:S(2)}, u32[]{:S(2)}) collective-permute-start(bf16[384,128]{1,0:T(8,128)(2,1)S(1)} %shard_map.70.refs_6_), channel_id=1, source_target_pairs={{0,16},{8,24},{16,0},{24,8},{1,17},{9,25},{17,1},{25,9},{2,18},{10... | collective-permute-start | bytes 294920 | tf_op jit(solution)/shard_map/ppermute | solution.py:362
  19.9 5.5 %collective-permute-start.4 = (bf16[384,128]{1,0:T(8,128)(2,1)S(1)}, bf16[384,128]{1,0:T(8,128)(2,1)S(1)}, u32[]{:S(2)}, u32[]{:S(2)}) collective-permute-start(bf16[384,128]{1,0:T(8,128)(2,1)S(1)} %shard_map.70.refs_6_), channel_id=1, source_target_pairs={{0,8},{8,16},{16,24},{24,0},{1,9},{9,17},{17,25},{25,1},{2,10},{10... | collective-permute-start | bytes 294920 | tf_op jit(solution)/shard_map/ppermute | solution.py:392
  25.5 6.8 %collective-permute-start.9 = (bf16[384,128]{1,0:T(8,128)(2,1)S(1)}, bf16[384,128]{1,0:T(8,128)(2,1)S(1)}, u32[]{:S(2)}, u32[]{:S(2)}) collective-permute-start(bf16[384,128]{1,0:T(8,128)(2,1)S(1)} %shard_map.72.refs_1_), channel_id=1, source_target_pairs={{0,4},{2,6},{4,0},{6,2},{1,5},{3,7},{5,1},{7,3},{8,12},{10,14},{12... | collective-permute-start | bytes 294920 | tf_op jit(solution)/shard_map/ppermute | solution.py:362
  26.4 6.6 %collective-permute-start.8 = (bf16[384,128]{1,0:T(8,128)(2,1)S(1)}, bf16[384,128]{1,0:T(8,128)(2,1)S(1)}, u32[]{:S(2)}, u32[]{:S(2)}) collective-permute-start(bf16[384,128]{1,0:T(8,128)(2,1)S(1)} %shard_map.72.refs_1_), channel_id=1, source_target_pairs={{0,2},{2,0},{4,6},{6,4},{1,3},{3,1},{5,7},{7,5},{8,10},{10,8},{12,... | collective-permute-start | bytes 294920 | tf_op jit(solution)/shard_map/ppermute | solution.py:362
  28.5 6.4 %collective-permute-start.7 = (bf16[384,128]{1,0:T(8,128)(2,1)S(1)}, bf16[384,128]{1,0:T(8,128)(2,1)S(1)}, u32[]{:S(2)}, u32[]{:S(2)}) collective-permute-start(bf16[384,128]{1,0:T(8,128)(2,1)S(1)} %shard_map.72.refs_1_), channel_id=1, source_target_pairs={{0,6},{2,4},{4,2},{6,0},{1,7},{3,5},{5,3},{7,1},{8,14},{10,12},{12... | collective-permute-start | bytes 294920 | tf_op jit(solution)/shard_map/ppermute | solution.py:362
  29.9 5.6 %collective-permute-start.6 = (bf16[384,128]{1,0:T(8,128)(2,1)S(1)}, bf16[384,128]{1,0:T(8,128)(2,1)S(1)}, u32[]{:S(2)}, u32[]{:S(2)}) collective-permute-start(bf16[384,128]{1,0:T(8,128)(2,1)S(1)} %shard_map.72.refs_1_), channel_id=1, source_target_pairs={{0,8},{8,0},{16,24},{24,16},{1,9},{9,1},{17,25},{25,17},{2,10},{10... | collective-permute-start | bytes 294920 | tf_op jit(solution)/shard_map/ppermute | solution.py:362
  32.3 4.6 %collective-permute-start.11 = (bf16[384,128]{1,0:T(8,128)(2,1)S(1)}, bf16[384,128]{1,0:T(8,128)(2,1)S(1)}, u32[]{:S(2)}, u32[]{:S(2)}) collective-permute-start(bf16[384,128]{1,0:T(8,128)(2,1)S(1)} %collective-permute-done.9.refs_5_), channel_id=1, source_target_pairs={{0,8},{8,0},{16,24},{24,16},{1,9},{9,1},{17,25},{25,17},{2,10},{10... | collective-permute-start | bytes 294920 | tf_op jit(solution)/shard_map/ppermute | solution.py:362
  33.0 4.9 %collective-permute-start.10 = (bf16[384,128]{1,0:T(8,128)(2,1)S(1)}, bf16[384,128]{1,0:T(8,128)(2,1)S(1)}, u32[]{:S(2)}, u32[]{:S(2)}) collective-permute-start(bf16[384,128]{1,0:T(8,128)(2,1)S(1)} %collective-permute-done.8.refs_4_), channel_id=1, source_target_pairs={{0,8},{8,0},{16,24},{24,16},{1,9},{9,1},{17,25},{25,17},{2,10},{10... | collective-permute-start | bytes 294920 | tf_op jit(solution)/shard_map/ppermute | solution.py:362
  35.0 4.6 %collective-permute-start.12 = (bf16[384,128]{1,0:T(8,128)(2,1)S(1)}, bf16[384,128]{1,0:T(8,128)(2,1)S(1)}, u32[]{:S(2)}, u32[]{:S(2)}) collective-permute-start(bf16[384,128]{1,0:T(8,128)(2,1)S(1)} %collective-permute-done.7.refs_3_), channel_id=1, source_target_pairs={{0,8},{8,0},{16,24},{24,16},{1,9},{9,1},{17,25},{25,17},{2,10},{10... | collective-permute-start | bytes 294920 | tf_op jit(solution)/shard_map/ppermute | solution.py:362
  35.6 5.0 %collective-permute-start.13 = (bf16[1920,128]{1,0:T(8,128)(2,1)S(1)}, bf16[1920,128]{1,0:T(8,128)(2,1)S(1)}, u32[]{:S(2)}, u32[]{:S(2)}) collective-permute-start(bf16[1920,128]{1,0:T(8,128)(2,1)S(1)} %shard_map.73.state_ref), channel_id=1, source_target_pairs={{0,1},{1,0},{2,3},{3,2},{4,5},{5,4},{6,7},{7,6},{8,9},{9,8},{10,11... | collective-permute-start | bytes 1474568 | tf_op jit(solution)/shard_map/ppermute | solution.py:362
  39.6 1.6 %collective-permute-start.14 = (bf16[1152,128]{1,0:T(8,128)(2,1)S(1)}, bf16[1152,128]{1,0:T(8,128)(2,1)S(1)}, u32[]{:S(2)}, u32[]{:S(2)}) collective-permute-start(bf16[1152,128]{1,0:T(8,128)(2,1)S(1)} %shard_map.75.refs_0_), channel_id=1, source_target_pairs={{0,1},{1,0},{2,3},{3,2},{4,5},{5,4},{6,7},{7,6},{8,9},{9,8},{10,11... | collective-permute-start | bytes 884744 | tf_op jit(solution)/shard_map/ppermute | solution.py:362

commit v16 on v12

--- a/solution.py
+++ b/solution.py
@@ -361,7 +361,7 @@
     rest = (frame_len, window_back, queries)
     early = 1
 
-    order = [*range(min(2, chips - 1), 0, -1), *range(3, chips)]
+    order = [*range(2, chips), *range(1, min(2, chips))]
 
     outgoing, keys, values = outgoing_state(keys, values)
     incoming = swap(outgoing, "core", 1, 2)

time: 42.3 us -> 41.9 us (level)
  starting transfers between devices: 18.9 us -> 17.7 us
  waiting for transfers between devices: 14 us -> 14.7 us
    ppermute x15, starting transfers between devices: 17.4 us -> 16.3 us  [swap(): return lax.ppermute(array, axis, [(n, n ^ mask) for n in range(size)])]
    ppermute x15, waiting for transfers between devices: 12.6 us -> 13.3 us  [swap(): return lax.ppermute(array, axis, [(n, n ^ mask) for n in range(size)])]
where the time goes in v16:
time: 41.9 us; the launch traced here: 41.4 us
  starting transfers between devices  17.7 us (42%)
  waiting for transfers between devices  14.7 us (35%)
  Pallas kernels  8.36 us (20%)
  local copies, waits for them, and re-layouts  0.44 us (1%)
    ppermute x15, starting transfers between devices, swap(): return lax.ppermute(array, axis, [(n, n ^ mask) for n in range(size)])  16.3 us
    ppermute x15, waiting for transfers between devices, swap(): return lax.ppermute(array, axis, [(n, n ^ mask) for n in range(size)])  13.3 us
    pallas_call x2, Pallas kernels, local_part(): pl.pallas_call(functools.partial(local_kernel, coefs, turn), out_shape=[p...  3.43 us
    pallas_call x2, Pallas kernels, write_late(): pl.pallas_call(functools.partial(kernel, turn, chips, early), out_shape=j...  1.89 us
    pallas_call x1, Pallas kernels, outgoing_state(): pl.pallas_call(functools.partial(first_kernel, parts), out_shape=[pltpu.V...  1.69 us
    ppermute x1, starting transfers between devices, body(): lax.ppermute(state, 'frame', [(f, (f + 1) % frames) for f in range(frames)])  1.49 us
    ppermute x1, waiting for transfers between devices, body(): lax.ppermute(state, 'frame', [(f, (f + 1) % frames) for f in range(frames)])  1.41 us
  transfers between devices with their start and end apart: 16, of which 9 were waited for; matrix products, arithmetic and copies ran while one was open for 0% of the time, Pallas kernels for 13%

profile of v16, /device:TPU:0, one launch (start us, length us, event | category | flops | bytes accessed | tf_op | source)
XLA Modules:
  0.0 41.4 jit_solution(13497378660206973123)
XLA Ops:
  0.0 1.7 %shard_map.64 = (bf16[1536,128]{1,0:T(8,128)(2,1)S(1)}, bf16[128,3072]{1,0:T(8,128)(2,1)S(1)}, bf16[128,3072]{1,0:T(8,128)(2,1)S(1)}) custom-call(bf16[128,3072]{1,0:T(8,128)(2,1)} %key_ref.1, bf16[128,3072]{1,0:T(8,128)(2,1)} %value_ref.1), custom_call_target="tpu_custom_call" | custom-call | flops 50331648 | bytes 1572864 | tf_op jit(solution)/shard_map/pallas_call | solution.py:84
  1.7 0.5 %collective-permute-start = (bf16[1536,128]{1,0:T(8,128)(2,1)S(1)}, bf16[1536,128]{1,0:T(8,128)(2,1)S(1)}, u32[]{:S(2)}, u32[]{:S(2)}) collective-permute-start(bf16[1536,128]{1,0:T(8,128)(2,1)S(1)} %get-tuple-element.20), channel_id=1, source_target_pairs={{0,1},{1,0},{2,3},{3,2},{4,5},{5,4},{6,7},{7,6},{8,9},{9,8},{10,11... | collective-permute-start | bytes 1179656 | tf_op jit(solution)/shard_map/ppermute | solution.py:346
  2.2 0.5 %shard_map.65.mine_ref = f32[1536,128]{1,0:T(8,128)S(1)} custom-call(bf16[128,3072]{1,0:T(8,128)(2,1)S(1)} %get-tuple-element.18.key_ref, bf16[128,3072]{1,0:T(8,128)(2,1)S(1)} %get-tuple-element.19.value_ref), custom_call_target="tpu_custom_call" | custom-call | flops 50331648 | bytes 1572864 | tf_op jit(solution)/shard_map/pallas_call | solution.py:104
  2.7 0.8 %collective-permute-done.other_ref = bf16[1536,128]{1,0:T(8,128)(2,1)S(1)} collective-permute-done((bf16[1536,128]{1,0:T(8,128)(2,1)S(1)}, bf16[1536,128]{1,0:T(8,128)(2,1)S(1)}, u32[]{:S(2)}, u32[]{:S(2)}) %collective-permute-start) | collective-permute-done | bytes 393248 | tf_op jit(solution)/shard_map/ppermute | solution.py:346
  3.5 0.1 shard_map.66
  3.6 4.0 %collective-permute-start.1 = (bf16[384,128]{1,0:T(8,128)(2,1)S(1)}, bf16[384,128]{1,0:T(8,128)(2,1)S(1)}, u32[]{:S(2)}, u32[]{:S(2)}) collective-permute-start(bf16[384,128]{1,0:T(8,128)(2,1)S(1)} %get-tuple-element.25), channel_id=1, source_target_pairs={{0,4},{2,6},{4,0},{6,2},{1,5},{3,7},{5,1},{7,3},{8,12},{10,14},{12... | collective-permute-start | bytes 294920 | tf_op jit(solution)/shard_map/ppermute | solution.py:346
  7.7 1.3 %collective-permute-start.2 = (bf16[384,128]{1,0:T(8,128)(2,1)S(1)}, bf16[384,128]{1,0:T(8,128)(2,1)S(1)}, u32[]{:S(2)}, u32[]{:S(2)}) collective-permute-start(bf16[384,128]{1,0:T(8,128)(2,1)S(1)} %get-tuple-element.26), channel_id=1, source_target_pairs={{0,6},{2,4},{4,2},{6,0},{1,7},{3,5},{5,3},{7,1},{8,14},{10,12},{12... | collective-permute-start | bytes 294920 | tf_op jit(solution)/shard_map/ppermute | solution.py:346
  9.0 0.2 collective-permute-start.3
  9.3 0.4 copy-done.2
  9.7 1.7 %shard_map.67 = (f32[128,1536]{1,0:T(8,128)S(1)}, bf16[128,1536]{1,0:T(8,128)(2,1)S(1)}, bf16[128,1536]{1,0:T(8,128)(2,1)S(1)}) custom-call(s32[1,4]{1,0:T(1,128)S(1)} %copy-done.2, s32[1,4]{1,0:T(1,128)S(1)} %copy-done.3, bf16[128,3072]{1,0:T(8,128)(2,1)S(1)} %copy-done, bf16[128,3072]{1,0:T(8,128)(2,1)S(1)} %get-tuple-element.18.key_ref, ...), custom_call_target="tpu_custom_call" | custom-call | flops 100663296 | bytes 2752512 | tf_op jit(solution)/shard_map/pallas_call | solution.py:251
  11.4 4.1 %collective-permute-done.1.refs_0_ = bf16[384,128]{1,0:T(8,128)(2,1)S(1)} collective-permute-done((bf16[384,128]{1,0:T(8,128)(2,1)S(1)}, bf16[384,128]{1,0:T(8,128)(2,1)S(1)}, u32[]{:S(2)}, u32[]{:S(2)}) %collective-permute-start.1) | collective-permute-done | bytes 98336 | tf_op jit(solution)/shard_map/ppermute | solution.py:346
  15.5 0.9 %collective-permute-done.3.refs_2_ = bf16[384,128]{1,0:T(8,128)(2,1)S(1)} collective-permute-done((bf16[384,128]{1,0:T(8,128)(2,1)S(1)}, bf16[384,128]{1,0:T(8,128)(2,1)S(1)}, u32[]{:S(2)}, u32[]{:S(2)}) %collective-permute-start.3) | collective-permute-done | bytes 98336 | tf_op jit(solution)/shard_map/ppermute | solution.py:346
  16.5 1.6 %collective-permute-start.5 = (bf16[384,128]{1,0:T(8,128)(2,1)S(1)}, bf16[384,128]{1,0:T(8,128)(2,1)S(1)}, u32[]{:S(2)}, u32[]{:S(2)}) collective-permute-start(bf16[384,128]{1,0:T(8,128)(2,1)S(1)} %shard_map.68.after_ref), channel_id=1, source_target_pairs={{0,16},{8,24},{16,0},{24,8},{1,17},{9,25},{17,1},{25,9},{2,18},{10... | collective-permute-start | bytes 294920 | tf_op jit(solution)/shard_map/ppermute | solution.py:346
  18.1 1.5 %collective-permute-start.4 = (bf16[384,128]{1,0:T(8,128)(2,1)S(1)}, bf16[384,128]{1,0:T(8,128)(2,1)S(1)}, u32[]{:S(2)}, u32[]{:S(2)}) collective-permute-start(bf16[384,128]{1,0:T(8,128)(2,1)S(1)} %shard_map.68.after_ref), channel_id=1, source_target_pairs={{0,8},{8,16},{16,24},{24,0},{1,9},{9,17},{17,25},{25,1},{2,10},{10... | collective-permute-start | bytes 294920 | tf_op jit(solution)/shard_map/ppermute | solution.py:376
  19.6 1.7 %shard_map.69 = (f32[128,1536]{1,0:T(8,128)S(1)}, bf16[128,1536]{1,0:T(8,128)(2,1)S(1)}, bf16[128,1536]{1,0:T(8,128)(2,1)S(1)}) custom-call(s32[1,4]{1,0:T(1,128)S(1)} %copy-done.2, s32[1,4]{1,0:T(1,128)S(1)} %copy-done.3, bf16[128,3072]{1,0:T(8,128)(2,1)S(1)} %copy-done, bf16[128,3072]{1,0:T(8,128)(2,1)S(1)} %get-tuple-element.18.key_ref, ...), custom_call_target="tpu_custom_call" | custom-call | flops 100663296 | bytes 2752512 | tf_op jit(solution)/shard_map/pallas_call | solution.py:251
  21.3 0.9 %collective-permute-done.5.first_ref = bf16[384,128]{1,0:T(8,128)(2,1)S(1)} collective-permute-done((bf16[384,128]{1,0:T(8,128)(2,1)S(1)}, bf16[384,128]{1,0:T(8,128)(2,1)S(1)}, u32[]{:S(2)}, u32[]{:S(2)}) %collective-permute-start.5) | collective-permute-done | bytes 98336 | tf_op jit(solution)/shard_map/ppermute | solution.py:346
  22.2 1.4 %collective-permute-done.4.before_ref = bf16[384,128]{1,0:T(8,128)(2,1)S(1)} collective-permute-done((bf16[384,128]{1,0:T(8,128)(2,1)S(1)}, bf16[384,128]{1,0:T(8,128)(2,1)S(1)}, u32[]{:S(2)}, u32[]{:S(2)}) %collective-permute-start.4) | collective-permute-done | bytes 98336 | tf_op jit(solution)/shard_map/ppermute | solution.py:376
  23.6 3.4 %collective-permute-start.9 = (bf16[384,128]{1,0:T(8,128)(2,1)S(1)}, bf16[384,128]{1,0:T(8,128)(2,1)S(1)}, u32[]{:S(2)}, u32[]{:S(2)}) collective-permute-start(bf16[384,128]{1,0:T(8,128)(2,1)S(1)} %shard_map.70.refs_1_), channel_id=1, source_target_pairs={{0,4},{2,6},{4,0},{6,2},{1,5},{3,7},{5,1},{7,3},{8,12},{10,14},{12... | collective-permute-start | bytes 294920 | tf_op jit(solution)/shard_map/ppermute | solution.py:346
  27.1 0.6 %collective-permute-start.8 = (bf16[384,128]{1,0:T(8,128)(2,1)S(1)}, bf16[384,128]{1,0:T(8,128)(2,1)S(1)}, u32[]{:S(2)}, u32[]{:S(2)}) collective-permute-start(bf16[384,128]{1,0:T(8,128)(2,1)S(1)} %shard_map.70.refs_1_), channel_id=1, source_target_pairs={{0,2},{2,0},{4,6},{6,4},{1,3},{3,1},{5,7},{7,5},{8,10},{10,8},{12,... | collective-permute-start | bytes 294920 | tf_op jit(solution)/shard_map/ppermute | solution.py:346
  27.7 0.9 %collective-permute-start.7 = (bf16[384,128]{1,0:T(8,128)(2,1)S(1)}, bf16[384,128]{1,0:T(8,128)(2,1)S(1)}, u32[]{:S(2)}, u32[]{:S(2)}) collective-permute-start(bf16[384,128]{1,0:T(8,128)(2,1)S(1)} %shard_map.70.refs_1_), channel_id=1, source_target_pairs={{0,6},{2,4},{4,2},{6,0},{1,7},{3,5},{5,3},{7,1},{8,14},{10,12},{12... | collective-permute-start | bytes 294920 | tf_op jit(solution)/shard_map/ppermute | solution.py:346
  28.6 0.6 %collective-permute-start.6 = (bf16[384,128]{1,0:T(8,128)(2,1)S(1)}, bf16[384,128]{1,0:T(8,128)(2,1)S(1)}, u32[]{:S(2)}, u32[]{:S(2)}) collective-permute-start(bf16[384,128]{1,0:T(8,128)(2,1)S(1)} %shard_map.70.refs_1_), channel_id=1, source_target_pairs={{0,8},{8,0},{16,24},{24,16},{1,9},{9,1},{17,25},{25,17},{2,10},{10... | collective-permute-start | bytes 294920 | tf_op jit(solution)/shard_map/ppermute | solution.py:346
  29.2 3.2 %collective-permute-done.9.refs_5_ = bf16[384,128]{1,0:T(8,128)(2,1)S(1)} collective-permute-done((bf16[384,128]{1,0:T(8,128)(2,1)S(1)}, bf16[384,128]{1,0:T(8,128)(2,1)S(1)}, u32[]{:S(2)}, u32[]{:S(2)}) %collective-permute-start.9) | collective-permute-done | bytes 98336 | tf_op jit(solution)/shard_map/ppermute | solution.py:346
  32.4 0.8 %collective-permute-start.11 = (bf16[384,128]{1,0:T(8,128)(2,1)S(1)}, bf16[384,128]{1,0:T(8,128)(2,1)S(1)}, u32[]{:S(2)}, u32[]{:S(2)}) collective-permute-start(bf16[384,128]{1,0:T(8,128)(2,1)S(1)} %collective-permute-done.9.refs_5_), channel_id=1, source_target_pairs={{0,8},{8,0},{16,24},{24,16},{1,9},{9,1},{17,25},{25,17},{2,10},{10... | collective-permute-start | bytes 294920 | tf_op jit(solution)/shard_map/ppermute | solution.py:346
  33.2 1.2 %collective-permute-start.10 = (bf16[384,128]{1,0:T(8,128)(2,1)S(1)}, bf16[384,128]{1,0:T(8,128)(2,1)S(1)}, u32[]{:S(2)}, u32[]{:S(2)}) collective-permute-start(bf16[384,128]{1,0:T(8,128)(2,1)S(1)} %collective-permute-done.8.refs_4_), channel_id=1, source_target_pairs={{0,8},{8,0},{16,24},{24,16},{1,9},{9,1},{17,25},{25,17},{2,10},{10... | collective-permute-start | bytes 294920 | tf_op jit(solution)/shard_map/ppermute | solution.py:346
  34.4 0.8 %collective-permute-start.12 = (bf16[384,128]{1,0:T(8,128)(2,1)S(1)}, bf16[384,128]{1,0:T(8,128)(2,1)S(1)}, u32[]{:S(2)}, u32[]{:S(2)}) collective-permute-start(bf16[384,128]{1,0:T(8,128)(2,1)S(1)} %collective-permute-done.7.refs_3_), channel_id=1, source_target_pairs={{0,8},{8,0},{16,24},{24,16},{1,9},{9,1},{17,25},{25,17},{2,10},{10... | collective-permute-start | bytes 294920 | tf_op jit(solution)/shard_map/ppermute | solution.py:346
  35.3 0.3 shard_map.72.base_ref
  35.6 1.4 %collective-permute-done.11.refs_1_ = bf16[384,128]{1,0:T(8,128)(2,1)S(1)} collective-permute-done((bf16[384,128]{1,0:T(8,128)(2,1)S(1)}, bf16[384,128]{1,0:T(8,128)(2,1)S(1)}, u32[]{:S(2)}, u32[]{:S(2)}) %collective-permute-start.11) | collective-permute-done | bytes 98336 | tf_op jit(solution)/shard_map/ppermute | solution.py:346
  37.0 1.1 %collective-permute-done.10.refs_0_ = bf16[384,128]{1,0:T(8,128)(2,1)S(1)} collective-permute-done((bf16[384,128]{1,0:T(8,128)(2,1)S(1)}, bf16[384,128]{1,0:T(8,128)(2,1)S(1)}, u32[]{:S(2)}, u32[]{:S(2)}) %collective-permute-start.10) | collective-permute-done | bytes 98336 | tf_op jit(solution)/shard_map/ppermute | solution.py:346
  38.2 1.0 %collective-permute-done.12.refs_1_ = bf16[384,128]{1,0:T(8,128)(2,1)S(1)} collective-permute-done((bf16[384,128]{1,0:T(8,128)(2,1)S(1)}, bf16[384,128]{1,0:T(8,128)(2,1)S(1)}, u32[]{:S(2)}, u32[]{:S(2)}) %collective-permute-start.12) | collective-permute-done | bytes 98336 | tf_op jit(solution)/shard_map/ppermute | solution.py:346
  39.1 1.0 %shard_map.74.out_before_ref = bf16[128,3072]{1,0:T(8,128)(2,1)} custom-call(f32[128,1536]{1,0:T(8,128)S(1)} %shard_map.72.base_ref, bf16[128,1536]{1,0:T(8,128)(2,1)S(1)} %get-tuple-element.24.y_ref, bf16[768,128]{1,0:T(8,128)(2,1)S(1)} %shard_map.73.refs_0_, bf16[384,128]{1,0:T(8,128)(2,1)S(1)} %collective-permute-done.12.refs_1_), custom_call_target="tpu_custom_call" | custom-call | flops 20000000000 | bytes 1024 | tf_op jit(solution)/shard_map/pallas_call | solution.py:333
  40.1 0.3 shard_map.75.refs_0_
  40.4 0.9 %shard_map.76 = bf16[128,3072]{1,0:T(8,128)(2,1)} custom-call(bf16[128,3072]{1,0:T(8,128)(2,1)} %shard_map.74.out_before_ref, f32[128,1536]{1,0:T(8,128)S(1)} %shard_map.75.refs_0_, bf16[128,1536]{1,0:T(8,128)(2,1)S(1)} %get-tuple-element.30.y_ref.refs_1_, bf16[768,128]{1,0:T(8,128)(2,1)S(1)} %collective-permute-done.14.refs_2_, ...), custom_call_target="tpu_custom_call", output_to_operand_aliasing={{}: (0, {})} | custom-call | flops 1024 | bytes 1024 | tf_op jit(solution)/shard_map/pallas_call | solution.py:333
  (21 shorter events, 0.4 us)
Async XLA Ops:
  1.7 1.8 %collective-permute-start = (bf16[1536,128]{1,0:T(8,128)(2,1)S(1)}, bf16[1536,128]{1,0:T(8,128)(2,1)S(1)}, u32[]{:S(2)}, u32[]{:S(2)}) collective-permute-start(bf16[1536,128]{1,0:T(8,128)(2,1)S(1)} %get-tuple-element.20), channel_id=1, source_target_pairs={{0,1},{1,0},{2,3},{3,2},{4,5},{5,4},{6,7},{7,6},{8,9},{9,8},{10,11... | collective-permute-start | bytes 1179656 | tf_op jit(solution)/shard_map/ppermute | solution.py:346
  2.7 6.6 %copy-start = (bf16[128,3072]{1,0:T(8,128)(2,1)S(1)}, bf16[128,3072]{1,0:T(8,128)(2,1)}, u32[]{:S(2)}) copy-start(bf16[128,3072]{1,0:T(8,128)(2,1)} %query_ref.3) | copy-start | bytes 2359300
  2.7 6.6 %copy-start.1 = (f32[3,24,128]{2,1,0:T(8,128)S(1)}, f32[3,24,128]{2,1,0:T(8,128)}, u32[]{:S(2)}) copy-start(f32[3,24,128]{2,1,0:T(8,128)} %weight_ref.3) | copy-start | bytes 110596
  3.6 11.9 %collective-permute-start.1 = (bf16[384,128]{1,0:T(8,128)(2,1)S(1)}, bf16[384,128]{1,0:T(8,128)(2,1)S(1)}, u32[]{:S(2)}, u32[]{:S(2)}) collective-permute-start(bf16[384,128]{1,0:T(8,128)(2,1)S(1)} %get-tuple-element.25), channel_id=1, source_target_pairs={{0,4},{2,6},{4,0},{6,2},{1,5},{3,7},{5,1},{7,3},{8,12},{10,14},{12... | collective-permute-start | bytes 294920 | tf_op jit(solution)/shard_map/ppermute | solution.py:346
  7.7 7.8 %collective-permute-start.2 = (bf16[384,128]{1,0:T(8,128)(2,1)S(1)}, bf16[384,128]{1,0:T(8,128)(2,1)S(1)}, u32[]{:S(2)}, u32[]{:S(2)}) collective-permute-start(bf16[384,128]{1,0:T(8,128)(2,1)S(1)} %get-tuple-element.26), channel_id=1, source_target_pairs={{0,6},{2,4},{4,2},{6,0},{1,7},{3,5},{5,3},{7,1},{8,14},{10,12},{12... | collective-permute-start | bytes 294920 | tf_op jit(solution)/shard_map/ppermute | solution.py:346
  9.0 0.7 %copy-start.2 = (s32[1,4]{1,0:T(1,128)S(1)}, s32[1,4]{1,0:T(1,128)}, u32[]{:S(2)}) copy-start(s32[1,4]{1,0:T(1,128)} %length_ref.3) | copy-start | bytes 52
  9.0 0.7 %copy-start.3 = (s32[1,4]{1,0:T(1,128)S(1)}, s32[1,4]{1,0:T(1,128)}, u32[]{:S(2)}) copy-start(s32[1,4]{1,0:T(1,128)} %back_ref.3) | copy-start | bytes 52
  9.0 7.4 %collective-permute-start.3 = (bf16[384,128]{1,0:T(8,128)(2,1)S(1)}, bf16[384,128]{1,0:T(8,128)(2,1)S(1)}, u32[]{:S(2)}, u32[]{:S(2)}) collective-permute-start(bf16[384,128]{1,0:T(8,128)(2,1)S(1)} %get-tuple-element.27), channel_id=1, source_target_pairs={{0,2},{2,0},{4,6},{6,4},{1,3},{3,1},{5,7},{7,5},{8,10},{10,8},{12,... | collective-permute-start | bytes 294920 | tf_op jit(solution)/shard_map/ppermute | solution.py:346
  16.5 5.7 %collective-permute-start.5 = (bf16[384,128]{1,0:T(8,128)(2,1)S(1)}, bf16[384,128]{1,0:T(8,128)(2,1)S(1)}, u32[]{:S(2)}, u32[]{:S(2)}) collective-permute-start(bf16[384,128]{1,0:T(8,128)(2,1)S(1)} %shard_map.68.after_ref), channel_id=1, source_target_pairs={{0,16},{8,24},{16,0},{24,8},{1,17},{9,25},{17,1},{25,9},{2,18},{10... | collective-permute-start | bytes 294920 | tf_op jit(solution)/shard_map/ppermute | solution.py:346
  18.1 5.5 %collective-permute-start.4 = (bf16[384,128]{1,0:T(8,128)(2,1)S(1)}, bf16[384,128]{1,0:T(8,128)(2,1)S(1)}, u32[]{:S(2)}, u32[]{:S(2)}) collective-permute-start(bf16[384,128]{1,0:T(8,128)(2,1)S(1)} %shard_map.68.after_ref), channel_id=1, source_target_pairs={{0,8},{8,16},{16,24},{24,0},{1,9},{9,17},{17,25},{25,1},{2,10},{10... | collective-permute-start | bytes 294920 | tf_op jit(solution)/shard_map/ppermute | solution.py:376
  23.6 8.7 %collective-permute-start.9 = (bf16[384,128]{1,0:T(8,128)(2,1)S(1)}, bf16[384,128]{1,0:T(8,128)(2,1)S(1)}, u32[]{:S(2)}, u32[]{:S(2)}) collective-permute-start(bf16[384,128]{1,0:T(8,128)(2,1)S(1)} %shard_map.70.refs_1_), channel_id=1, source_target_pairs={{0,4},{2,6},{4,0},{6,2},{1,5},{3,7},{5,1},{7,3},{8,12},{10,14},{12... | collective-permute-start | bytes 294920 | tf_op jit(solution)/shard_map/ppermute | solution.py:346
  27.1 6.1 %collective-permute-start.8 = (bf16[384,128]{1,0:T(8,128)(2,1)S(1)}, bf16[384,128]{1,0:T(8,128)(2,1)S(1)}, u32[]{:S(2)}, u32[]{:S(2)}) collective-permute-start(bf16[384,128]{1,0:T(8,128)(2,1)S(1)} %shard_map.70.refs_1_), channel_id=1, source_target_pairs={{0,2},{2,0},{4,6},{6,4},{1,3},{3,1},{5,7},{7,5},{8,10},{10,8},{12,... | collective-permute-start | bytes 294920 | tf_op jit(solution)/shard_map/ppermute | solution.py:346
  27.7 6.7 %collective-permute-start.7 = (bf16[384,128]{1,0:T(8,128)(2,1)S(1)}, bf16[384,128]{1,0:T(8,128)(2,1)S(1)}, u32[]{:S(2)}, u32[]{:S(2)}) collective-permute-start(bf16[384,128]{1,0:T(8,128)(2,1)S(1)} %shard_map.70.refs_1_), channel_id=1, source_target_pairs={{0,6},{2,4},{4,2},{6,0},{1,7},{3,5},{5,3},{7,1},{8,14},{10,12},{12... | collective-permute-start | bytes 294920 | tf_op jit(solution)/shard_map/ppermute | solution.py:346
  28.6 6.6 %collective-permute-start.6 = (bf16[384,128]{1,0:T(8,128)(2,1)S(1)}, bf16[384,128]{1,0:T(8,128)(2,1)S(1)}, u32[]{:S(2)}, u32[]{:S(2)}) collective-permute-start(bf16[384,128]{1,0:T(8,128)(2,1)S(1)} %shard_map.70.refs_1_), channel_id=1, source_target_pairs={{0,8},{8,0},{16,24},{24,16},{1,9},{9,1},{17,25},{25,17},{2,10},{10... | collective-permute-start | bytes 294920 | tf_op jit(solution)/shard_map/ppermute | solution.py:346
  32.4 4.6 %collective-permute-start.11 = (bf16[384,128]{1,0:T(8,128)(2,1)S(1)}, bf16[384,128]{1,0:T(8,128)(2,1)S(1)}, u32[]{:S(2)}, u32[]{:S(2)}) collective-permute-start(bf16[384,128]{1,0:T(8,128)(2,1)S(1)} %collective-permute-done.9.refs_5_), channel_id=1, source_target_pairs={{0,8},{8,0},{16,24},{24,16},{1,9},{9,1},{17,25},{25,17},{2,10},{10... | collective-permute-start | bytes 294920 | tf_op jit(solution)/shard_map/ppermute | solution.py:346
  33.2 4.9 %collective-permute-start.10 = (bf16[384,128]{1,0:T(8,128)(2,1)S(1)}, bf16[384,128]{1,0:T(8,128)(2,1)S(1)}, u32[]{:S(2)}, u32[]{:S(2)}) collective-permute-start(bf16[384,128]{1,0:T(8,128)(2,1)S(1)} %collective-permute-done.8.refs_4_), channel_id=1, source_target_pairs={{0,8},{8,0},{16,24},{24,16},{1,9},{9,1},{17,25},{25,17},{2,10},{10... | collective-permute-start | bytes 294920 | tf_op jit(solution)/shard_map/ppermute | solution.py:346
  34.4 4.7 %collective-permute-start.12 = (bf16[384,128]{1,0:T(8,128)(2,1)S(1)}, bf16[384,128]{1,0:T(8,128)(2,1)S(1)}, u32[]{:S(2)}, u32[]{:S(2)}) collective-permute-start(bf16[384,128]{1,0:T(8,128)(2,1)S(1)} %collective-permute-done.7.refs_3_), channel_id=1, source_target_pairs={{0,8},{8,0},{16,24},{24,16},{1,9},{9,1},{17,25},{25,17},{2,10},{10... | collective-permute-start | bytes 294920 | tf_op jit(solution)/shard_map/ppermute | solution.py:346
  35.2 4.8 %collective-permute-start.13 = (bf16[1920,128]{1,0:T(8,128)(2,1)S(1)}, bf16[1920,128]{1,0:T(8,128)(2,1)S(1)}, u32[]{:S(2)}, u32[]{:S(2)}) collective-permute-start(bf16[1920,128]{1,0:T(8,128)(2,1)S(1)} %shard_map.71.state_ref), channel_id=1, source_target_pairs={{0,1},{1,0},{2,3},{3,2},{4,5},{5,4},{6,7},{7,6},{8,9},{9,8},{10,11... | collective-permute-start | bytes 1474568 | tf_op jit(solution)/shard_map/ppermute | solution.py:346
  38.1 2.3 %collective-permute-start.14 = (bf16[768,128]{1,0:T(8,128)(2,1)S(1)}, bf16[768,128]{1,0:T(8,128)(2,1)S(1)}, u32[]{:S(2)}, u32[]{:S(2)}) collective-permute-start(bf16[768,128]{1,0:T(8,128)(2,1)S(1)} %shard_map.73.refs_0_), channel_id=1, source_target_pairs={{0,1},{1,0},{2,3},{3,2},{4,5},{5,4},{6,7},{7,6},{8,9},{9,8},{10,11... | collective-permute-start | bytes 589832 | tf_op jit(solution)/shard_map/ppermute | solution.py:346
  39.1 1.3 %collective-permute-start.15 = (bf16[384,128]{1,0:T(8,128)(2,1)S(1)}, bf16[384,128]{1,0:T(8,128)(2,1)S(1)}, u32[]{:S(2)}, u32[]{:S(2)}) collective-permute-start(bf16[384,128]{1,0:T(8,128)(2,1)S(1)} %collective-permute-done.12.refs_1_), channel_id=1, source_target_pairs={{0,1},{1,0},{2,3},{3,2},{4,5},{5,4},{6,7},{7,6},{8,9},{9,8},{10,11... | collective-permute-start | bytes 294920 | tf_op jit(solution)/shard_map/ppermute | solution.py:346

commit v17 on v16

--- a/solution.py
+++ b/solution.py
@@ -361,7 +361,7 @@
     rest = (frame_len, window_back, queries)
     early = 1
 
-    order = [*range(2, chips), *range(1, min(2, chips))]
+    order = [*reversed(range(1, chips))]
 
     outgoing, keys, values = outgoing_state(keys, values)
     incoming = swap(outgoing, "core", 1, 2)

time: 41.9 us -> 41.5 us (level)
  waiting for transfers between devices: 14.7 us -> 15.5 us
    ppermute x15, waiting for transfers between devices: 13.3 us -> 14.1 us  [swap(): return lax.ppermute(array, axis, [(n, n ^ mask) for n in range(size)])]
    ppermute x15, starting transfers between devices: 16.3 us -> 15.8 us  [swap(): return lax.ppermute(array, axis, [(n, n ^ mask) for n in range(size)])]
where the time goes in v17:
time: 41.5 us; the launch traced here: 41.3 us
  starting transfers between devices  17.3 us (42%)
  waiting for transfers between devices  15.5 us (37%)
  Pallas kernels  8.36 us (20%)
    ppermute x15, starting transfers between devices, swap(): return lax.ppermute(array, axis, [(n, n ^ mask) for n in range(size)])  15.8 us
    ppermute x15, waiting for transfers between devices, swap(): return lax.ppermute(array, axis, [(n, n ^ mask) for n in range(size)])  14.1 us
    pallas_call x2, Pallas kernels, local_part(): pl.pallas_call(functools.partial(local_kernel, coefs, turn), out_shape=[p...  3.43 us
    pallas_call x2, Pallas kernels, write_late(): pl.pallas_call(functools.partial(kernel, turn, chips, early), out_shape=j...  1.89 us
    pallas_call x1, Pallas kernels, outgoing_state(): pl.pallas_call(functools.partial(first_kernel, parts), out_shape=[pltpu.V...  1.69 us
    ppermute x1, starting transfers between devices, body(): lax.ppermute(state, 'frame', [(f, (f + 1) % frames) for f in range(frames)])  1.49 us
    ppermute x1, waiting for transfers between devices, body(): lax.ppermute(state, 'frame', [(f, (f + 1) % frames) for f in range(frames)])  1.36 us
  transfers between devices with their start and end apart: 16, of which 9 were waited for; matrix products, arithmetic and copies ran while one was open for 0% of the time, Pallas kernels for 13%

profile of v17, /device:TPU:0, one launch (start us, length us, event | category | flops | bytes accessed | tf_op | source)
XLA Modules:
  0.0 41.3 jit_solution(7853868615692197538)
XLA Ops:
  0.0 1.7 %shard_map.64 = (bf16[1536,128]{1,0:T(8,128)(2,1)S(1)}, bf16[128,3072]{1,0:T(8,128)(2,1)S(1)}, bf16[128,3072]{1,0:T(8,128)(2,1)S(1)}) custom-call(bf16[128,3072]{1,0:T(8,128)(2,1)} %key_ref.1, bf16[128,3072]{1,0:T(8,128)(2,1)} %value_ref.1), custom_call_target="tpu_custom_call" | custom-call | flops 50331648 | bytes 1572864 | tf_op jit(solution)/shard_map/pallas_call | solution.py:84
  1.7 0.5 %collective-permute-start = (bf16[1536,128]{1,0:T(8,128)(2,1)S(1)}, bf16[1536,128]{1,0:T(8,128)(2,1)S(1)}, u32[]{:S(2)}, u32[]{:S(2)}) collective-permute-start(bf16[1536,128]{1,0:T(8,128)(2,1)S(1)} %get-tuple-element.20), channel_id=1, source_target_pairs={{0,1},{1,0},{2,3},{3,2},{4,5},{5,4},{6,7},{7,6},{8,9},{9,8},{10,11... | collective-permute-start | bytes 1179656 | tf_op jit(solution)/shard_map/ppermute | solution.py:346
  2.2 0.5 %shard_map.65.mine_ref = f32[1536,128]{1,0:T(8,128)S(1)} custom-call(bf16[128,3072]{1,0:T(8,128)(2,1)S(1)} %get-tuple-element.18.key_ref, bf16[128,3072]{1,0:T(8,128)(2,1)S(1)} %get-tuple-element.19.value_ref), custom_call_target="tpu_custom_call" | custom-call | flops 50331648 | bytes 1572864 | tf_op jit(solution)/shard_map/pallas_call | solution.py:104
  2.7 0.8 %collective-permute-done.other_ref = bf16[1536,128]{1,0:T(8,128)(2,1)S(1)} collective-permute-done((bf16[1536,128]{1,0:T(8,128)(2,1)S(1)}, bf16[1536,128]{1,0:T(8,128)(2,1)S(1)}, u32[]{:S(2)}, u32[]{:S(2)}) %collective-permute-start) | collective-permute-done | bytes 393248 | tf_op jit(solution)/shard_map/ppermute | solution.py:346
  3.5 0.1 shard_map.66
  3.6 5.1 %collective-permute-start.1 = (bf16[384,128]{1,0:T(8,128)(2,1)S(1)}, bf16[384,128]{1,0:T(8,128)(2,1)S(1)}, u32[]{:S(2)}, u32[]{:S(2)}) collective-permute-start(bf16[384,128]{1,0:T(8,128)(2,1)S(1)} %get-tuple-element.25), channel_id=1, source_target_pairs={{0,6},{2,4},{4,2},{6,0},{1,7},{3,5},{5,3},{7,1},{8,14},{10,12},{12... | collective-permute-start | bytes 294920 | tf_op jit(solution)/shard_map/ppermute | solution.py:346
  8.7 0.6 %collective-permute-start.3 = (bf16[384,128]{1,0:T(8,128)(2,1)S(1)}, bf16[384,128]{1,0:T(8,128)(2,1)S(1)}, u32[]{:S(2)}, u32[]{:S(2)}) collective-permute-start(bf16[384,128]{1,0:T(8,128)(2,1)S(1)} %get-tuple-element.27), channel_id=1, source_target_pairs={{0,2},{2,0},{4,6},{6,4},{1,3},{3,1},{5,7},{7,5},{8,10},{10,8},{12,... | collective-permute-start | bytes 294920 | tf_op jit(solution)/shard_map/ppermute | solution.py:346
  9.4 1.7 %shard_map.67 = (f32[128,1536]{1,0:T(8,128)S(1)}, bf16[128,1536]{1,0:T(8,128)(2,1)S(1)}, bf16[128,1536]{1,0:T(8,128)(2,1)S(1)}) custom-call(s32[1,4]{1,0:T(1,128)S(1)} %copy-done.2, s32[1,4]{1,0:T(1,128)S(1)} %copy-done.3, bf16[128,3072]{1,0:T(8,128)(2,1)S(1)} %copy-done, bf16[128,3072]{1,0:T(8,128)(2,1)S(1)} %get-tuple-element.18.key_ref, ...), custom_call_target="tpu_custom_call" | custom-call | flops 100663296 | bytes 2752512 | tf_op jit(solution)/shard_map/pallas_call | solution.py:251
  11.1 1.3 %collective-permute-done.1.refs_0_ = bf16[384,128]{1,0:T(8,128)(2,1)S(1)} collective-permute-done((bf16[384,128]{1,0:T(8,128)(2,1)S(1)}, bf16[384,128]{1,0:T(8,128)(2,1)S(1)}, u32[]{:S(2)}, u32[]{:S(2)}) %collective-permute-start.1) | collective-permute-done | bytes 98336 | tf_op jit(solution)/shard_map/ppermute | solution.py:346
  12.4 4.9 %collective-permute-done.2.refs_1_ = bf16[384,128]{1,0:T(8,128)(2,1)S(1)} collective-permute-done((bf16[384,128]{1,0:T(8,128)(2,1)S(1)}, bf16[384,128]{1,0:T(8,128)(2,1)S(1)}, u32[]{:S(2)}, u32[]{:S(2)}) %collective-permute-start.2) | collective-permute-done | bytes 98336 | tf_op jit(solution)/shard_map/ppermute | solution.py:346
  17.3 1.6 %collective-permute-start.5 = (bf16[384,128]{1,0:T(8,128)(2,1)S(1)}, bf16[384,128]{1,0:T(8,128)(2,1)S(1)}, u32[]{:S(2)}, u32[]{:S(2)}) collective-permute-start(bf16[384,128]{1,0:T(8,128)(2,1)S(1)} %shard_map.68.after_ref), channel_id=1, source_target_pairs={{0,16},{8,24},{16,0},{24,8},{1,17},{9,25},{17,1},{25,9},{2,18},{10... | collective-permute-start | bytes 294920 | tf_op jit(solution)/shard_map/ppermute | solution.py:346
  18.9 1.5 %collective-permute-start.4 = (bf16[384,128]{1,0:T(8,128)(2,1)S(1)}, bf16[384,128]{1,0:T(8,128)(2,1)S(1)}, u32[]{:S(2)}, u32[]{:S(2)}) collective-permute-start(bf16[384,128]{1,0:T(8,128)(2,1)S(1)} %shard_map.68.after_ref), channel_id=1, source_target_pairs={{0,8},{8,16},{16,24},{24,0},{1,9},{9,17},{17,25},{25,1},{2,10},{10... | collective-permute-start | bytes 294920 | tf_op jit(solution)/shard_map/ppermute | solution.py:376
  20.4 1.7 %shard_map.69 = (f32[128,1536]{1,0:T(8,128)S(1)}, bf16[128,1536]{1,0:T(8,128)(2,1)S(1)}, bf16[128,1536]{1,0:T(8,128)(2,1)S(1)}) custom-call(s32[1,4]{1,0:T(1,128)S(1)} %copy-done.2, s32[1,4]{1,0:T(1,128)S(1)} %copy-done.3, bf16[128,3072]{1,0:T(8,128)(2,1)S(1)} %copy-done, bf16[128,3072]{1,0:T(8,128)(2,1)S(1)} %get-tuple-element.18.key_ref, ...), custom_call_target="tpu_custom_call" | custom-call | flops 100663296 | bytes 2752512 | tf_op jit(solution)/shard_map/pallas_call | solution.py:251
  22.1 0.9 %collective-permute-done.5.first_ref = bf16[384,128]{1,0:T(8,128)(2,1)S(1)} collective-permute-done((bf16[384,128]{1,0:T(8,128)(2,1)S(1)}, bf16[384,128]{1,0:T(8,128)(2,1)S(1)}, u32[]{:S(2)}, u32[]{:S(2)}) %collective-permute-start.5) | collective-permute-done | bytes 98336 | tf_op jit(solution)/shard_map/ppermute | solution.py:346
  23.1 1.4 %collective-permute-done.4.before_ref = bf16[384,128]{1,0:T(8,128)(2,1)S(1)} collective-permute-done((bf16[384,128]{1,0:T(8,128)(2,1)S(1)}, bf16[384,128]{1,0:T(8,128)(2,1)S(1)}, u32[]{:S(2)}, u32[]{:S(2)}) %collective-permute-start.4) | collective-permute-done | bytes 98336 | tf_op jit(solution)/shard_map/ppermute | solution.py:376
  24.5 0.3 collective-permute-start.9
  24.8 2.8 %collective-permute-start.8 = (bf16[384,128]{1,0:T(8,128)(2,1)S(1)}, bf16[384,128]{1,0:T(8,128)(2,1)S(1)}, u32[]{:S(2)}, u32[]{:S(2)}) collective-permute-start(bf16[384,128]{1,0:T(8,128)(2,1)S(1)} %shard_map.70.refs_1_), channel_id=1, source_target_pairs={{0,2},{2,0},{4,6},{6,4},{1,3},{3,1},{5,7},{7,5},{8,10},{10,8},{12,... | collective-permute-start | bytes 294920 | tf_op jit(solution)/shard_map/ppermute | solution.py:346
  27.6 1.3 %collective-permute-start.7 = (bf16[384,128]{1,0:T(8,128)(2,1)S(1)}, bf16[384,128]{1,0:T(8,128)(2,1)S(1)}, u32[]{:S(2)}, u32[]{:S(2)}) collective-permute-start(bf16[384,128]{1,0:T(8,128)(2,1)S(1)} %shard_map.70.refs_1_), channel_id=1, source_target_pairs={{0,6},{2,4},{4,2},{6,0},{1,7},{3,5},{5,3},{7,1},{8,14},{10,12},{12... | collective-permute-start | bytes 294920 | tf_op jit(solution)/shard_map/ppermute | solution.py:346
  28.9 0.6 %collective-permute-start.6 = (bf16[384,128]{1,0:T(8,128)(2,1)S(1)}, bf16[384,128]{1,0:T(8,128)(2,1)S(1)}, u32[]{:S(2)}, u32[]{:S(2)}) collective-permute-start(bf16[384,128]{1,0:T(8,128)(2,1)S(1)} %shard_map.70.refs_1_), channel_id=1, source_target_pairs={{0,8},{8,0},{16,24},{24,16},{1,9},{9,1},{17,25},{25,17},{2,10},{10... | collective-permute-start | bytes 294920 | tf_op jit(solution)/shard_map/ppermute | solution.py:346
  29.5 2.8 %collective-permute-done.9.refs_5_ = bf16[384,128]{1,0:T(8,128)(2,1)S(1)} collective-permute-done((bf16[384,128]{1,0:T(8,128)(2,1)S(1)}, bf16[384,128]{1,0:T(8,128)(2,1)S(1)}, u32[]{:S(2)}, u32[]{:S(2)}) %collective-permute-start.9) | collective-permute-done | bytes 98336 | tf_op jit(solution)/shard_map/ppermute | solution.py:346
  32.3 0.8 %collective-permute-start.11 = (bf16[384,128]{1,0:T(8,128)(2,1)S(1)}, bf16[384,128]{1,0:T(8,128)(2,1)S(1)}, u32[]{:S(2)}, u32[]{:S(2)}) collective-permute-start(bf16[384,128]{1,0:T(8,128)(2,1)S(1)} %collective-permute-done.9.refs_5_), channel_id=1, source_target_pairs={{0,8},{8,0},{16,24},{24,16},{1,9},{9,1},{17,25},{25,17},{2,10},{10... | collective-permute-start | bytes 294920 | tf_op jit(solution)/shard_map/ppermute | solution.py:346
  33.1 1.3 %collective-permute-start.10 = (bf16[384,128]{1,0:T(8,128)(2,1)S(1)}, bf16[384,128]{1,0:T(8,128)(2,1)S(1)}, u32[]{:S(2)}, u32[]{:S(2)}) collective-permute-start(bf16[384,128]{1,0:T(8,128)(2,1)S(1)} %collective-permute-done.8.refs_4_), channel_id=1, source_target_pairs={{0,8},{8,0},{16,24},{24,16},{1,9},{9,1},{17,25},{25,17},{2,10},{10... | collective-permute-start | bytes 294920 | tf_op jit(solution)/shard_map/ppermute | solution.py:346
  34.3 0.8 %collective-permute-start.12 = (bf16[384,128]{1,0:T(8,128)(2,1)S(1)}, bf16[384,128]{1,0:T(8,128)(2,1)S(1)}, u32[]{:S(2)}, u32[]{:S(2)}) collective-permute-start(bf16[384,128]{1,0:T(8,128)(2,1)S(1)} %collective-permute-done.7.refs_3_), channel_id=1, source_target_pairs={{0,8},{8,0},{16,24},{24,16},{1,9},{9,1},{17,25},{25,17},{2,10},{10... | collective-permute-start | bytes 294920 | tf_op jit(solution)/shard_map/ppermute | solution.py:346
  35.2 0.1 collective-permute-start.13
  35.2 0.3 shard_map.72.base_ref
  35.5 1.4 %collective-permute-done.11.refs_1_ = bf16[384,128]{1,0:T(8,128)(2,1)S(1)} collective-permute-done((bf16[384,128]{1,0:T(8,128)(2,1)S(1)}, bf16[384,128]{1,0:T(8,128)(2,1)S(1)}, u32[]{:S(2)}, u32[]{:S(2)}) %collective-permute-start.11) | collective-permute-done | bytes 98336 | tf_op jit(solution)/shard_map/ppermute | solution.py:346
  36.9 1.1 %collective-permute-done.10.refs_0_ = bf16[384,128]{1,0:T(8,128)(2,1)S(1)} collective-permute-done((bf16[384,128]{1,0:T(8,128)(2,1)S(1)}, bf16[384,128]{1,0:T(8,128)(2,1)S(1)}, u32[]{:S(2)}, u32[]{:S(2)}) %collective-permute-start.10) | collective-permute-done | bytes 98336 | tf_op jit(solution)/shard_map/ppermute | solution.py:346
  38.0 0.1 collective-permute-start.14
  38.1 1.0 %collective-permute-done.12.refs_1_ = bf16[384,128]{1,0:T(8,128)(2,1)S(1)} collective-permute-done((bf16[384,128]{1,0:T(8,128)(2,1)S(1)}, bf16[384,128]{1,0:T(8,128)(2,1)S(1)}, u32[]{:S(2)}, u32[]{:S(2)}) %collective-permute-start.12) | collective-permute-done | bytes 98336 | tf_op jit(solution)/shard_map/ppermute | solution.py:346
  39.0 1.0 %shard_map.74.out_before_ref = bf16[128,3072]{1,0:T(8,128)(2,1)} custom-call(f32[128,1536]{1,0:T(8,128)S(1)} %shard_map.72.base_ref, bf16[128,1536]{1,0:T(8,128)(2,1)S(1)} %get-tuple-element.24.y_ref, bf16[768,128]{1,0:T(8,128)(2,1)S(1)} %shard_map.73.refs_0_, bf16[384,128]{1,0:T(8,128)(2,1)S(1)} %collective-permute-done.12.refs_1_), custom_call_target="tpu_custom_call" | custom-call | flops 20000000000 | bytes 1024 | tf_op jit(solution)/shard_map/pallas_call | solution.py:333
  40.0 0.3 shard_map.75.refs_0_
  40.3 0.9 %shard_map.76 = bf16[128,3072]{1,0:T(8,128)(2,1)} custom-call(bf16[128,3072]{1,0:T(8,128)(2,1)} %shard_map.74.out_before_ref, f32[128,1536]{1,0:T(8,128)S(1)} %shard_map.75.refs_0_, bf16[128,1536]{1,0:T(8,128)(2,1)S(1)} %get-tuple-element.30.y_ref.refs_1_, bf16[768,128]{1,0:T(8,128)(2,1)S(1)} %collective-permute-done.14.refs_2_, ...), custom_call_target="tpu_custom_call", output_to_operand_aliasing={{}: (0, {})} | custom-call | flops 1024 | bytes 1024 | tf_op jit(solution)/shard_map/pallas_call | solution.py:333
  (21 shorter events, 0.2 us)
Async XLA Ops:
  1.7 1.8 %collective-permute-start = (bf16[1536,128]{1,0:T(8,128)(2,1)S(1)}, bf16[1536,128]{1,0:T(8,128)(2,1)S(1)}, u32[]{:S(2)}, u32[]{:S(2)}) collective-permute-start(bf16[1536,128]{1,0:T(8,128)(2,1)S(1)} %get-tuple-element.20), channel_id=1, source_target_pairs={{0,1},{1,0},{2,3},{3,2},{4,5},{5,4},{6,7},{7,6},{8,9},{9,8},{10,11... | collective-permute-start | bytes 1179656 | tf_op jit(solution)/shard_map/ppermute | solution.py:346
  2.7 6.6 %copy-start = (bf16[128,3072]{1,0:T(8,128)(2,1)S(1)}, bf16[128,3072]{1,0:T(8,128)(2,1)}, u32[]{:S(2)}) copy-start(bf16[128,3072]{1,0:T(8,128)(2,1)} %query_ref.3) | copy-start | bytes 2359300
  2.7 6.6 %copy-start.1 = (f32[3,24,128]{2,1,0:T(8,128)S(1)}, f32[3,24,128]{2,1,0:T(8,128)}, u32[]{:S(2)}) copy-start(f32[3,24,128]{2,1,0:T(8,128)} %weight_ref.3) | copy-start | bytes 110596
  3.6 8.7 %collective-permute-start.1 = (bf16[384,128]{1,0:T(8,128)(2,1)S(1)}, bf16[384,128]{1,0:T(8,128)(2,1)S(1)}, u32[]{:S(2)}, u32[]{:S(2)}) collective-permute-start(bf16[384,128]{1,0:T(8,128)(2,1)S(1)} %get-tuple-element.25), channel_id=1, source_target_pairs={{0,6},{2,4},{4,2},{6,0},{1,7},{3,5},{5,3},{7,1},{8,14},{10,12},{12... | collective-permute-start | bytes 294920 | tf_op jit(solution)/shard_map/ppermute | solution.py:346
  8.7 8.6 %collective-permute-start.2 = (bf16[384,128]{1,0:T(8,128)(2,1)S(1)}, bf16[384,128]{1,0:T(8,128)(2,1)S(1)}, u32[]{:S(2)}, u32[]{:S(2)}) collective-permute-start(bf16[384,128]{1,0:T(8,128)(2,1)S(1)} %get-tuple-element.26), channel_id=1, source_target_pairs={{0,4},{2,6},{4,0},{6,2},{1,5},{3,7},{5,1},{7,3},{8,12},{10,14},{12... | collective-permute-start | bytes 294920 | tf_op jit(solution)/shard_map/ppermute | solution.py:346
  8.7 0.7 %copy-start.2 = (s32[1,4]{1,0:T(1,128)S(1)}, s32[1,4]{1,0:T(1,128)}, u32[]{:S(2)}) copy-start(s32[1,4]{1,0:T(1,128)} %length_ref.3) | copy-start | bytes 52
  8.7 0.7 %copy-start.3 = (s32[1,4]{1,0:T(1,128)S(1)}, s32[1,4]{1,0:T(1,128)}, u32[]{:S(2)}) copy-start(s32[1,4]{1,0:T(1,128)} %back_ref.3) | copy-start | bytes 52
  8.7 8.6 %collective-permute-start.3 = (bf16[384,128]{1,0:T(8,128)(2,1)S(1)}, bf16[384,128]{1,0:T(8,128)(2,1)S(1)}, u32[]{:S(2)}, u32[]{:S(2)}) collective-permute-start(bf16[384,128]{1,0:T(8,128)(2,1)S(1)} %get-tuple-element.27), channel_id=1, source_target_pairs={{0,2},{2,0},{4,6},{6,4},{1,3},{3,1},{5,7},{7,5},{8,10},{10,8},{12,... | collective-permute-start | bytes 294920 | tf_op jit(solution)/shard_map/ppermute | solution.py:346
  17.3 5.7 %collective-permute-start.5 = (bf16[384,128]{1,0:T(8,128)(2,1)S(1)}, bf16[384,128]{1,0:T(8,128)(2,1)S(1)}, u32[]{:S(2)}, u32[]{:S(2)}) collective-permute-start(bf16[384,128]{1,0:T(8,128)(2,1)S(1)} %shard_map.68.after_ref), channel_id=1, source_target_pairs={{0,16},{8,24},{16,0},{24,8},{1,17},{9,25},{17,1},{25,9},{2,18},{10... | collective-permute-start | bytes 294920 | tf_op jit(solution)/shard_map/ppermute | solution.py:346
  18.9 5.5 %collective-permute-start.4 = (bf16[384,128]{1,0:T(8,128)(2,1)S(1)}, bf16[384,128]{1,0:T(8,128)(2,1)S(1)}, u32[]{:S(2)}, u32[]{:S(2)}) collective-permute-start(bf16[384,128]{1,0:T(8,128)(2,1)S(1)} %shard_map.68.after_ref), channel_id=1, source_target_pairs={{0,8},{8,16},{16,24},{24,0},{1,9},{9,17},{17,25},{25,1},{2,10},{10... | collective-permute-start | bytes 294920 | tf_op jit(solution)/shard_map/ppermute | solution.py:376
  24.5 7.8 %collective-permute-start.9 = (bf16[384,128]{1,0:T(8,128)(2,1)S(1)}, bf16[384,128]{1,0:T(8,128)(2,1)S(1)}, u32[]{:S(2)}, u32[]{:S(2)}) collective-permute-start(bf16[384,128]{1,0:T(8,128)(2,1)S(1)} %shard_map.70.refs_1_), channel_id=1, source_target_pairs={{0,4},{2,6},{4,0},{6,2},{1,5},{3,7},{5,1},{7,3},{8,12},{10,14},{12... | collective-permute-start | bytes 294920 | tf_op jit(solution)/shard_map/ppermute | solution.py:346
  24.8 8.3 %collective-permute-start.8 = (bf16[384,128]{1,0:T(8,128)(2,1)S(1)}, bf16[384,128]{1,0:T(8,128)(2,1)S(1)}, u32[]{:S(2)}, u32[]{:S(2)}) collective-permute-start(bf16[384,128]{1,0:T(8,128)(2,1)S(1)} %shard_map.70.refs_1_), channel_id=1, source_target_pairs={{0,2},{2,0},{4,6},{6,4},{1,3},{3,1},{5,7},{7,5},{8,10},{10,8},{12,... | collective-permute-start | bytes 294920 | tf_op jit(solution)/shard_map/ppermute | solution.py:346
  27.6 6.8 %collective-permute-start.7 = (bf16[384,128]{1,0:T(8,128)(2,1)S(1)}, bf16[384,128]{1,0:T(8,128)(2,1)S(1)}, u32[]{:S(2)}, u32[]{:S(2)}) collective-permute-start(bf16[384,128]{1,0:T(8,128)(2,1)S(1)} %shard_map.70.refs_1_), channel_id=1, source_target_pairs={{0,6},{2,4},{4,2},{6,0},{1,7},{3,5},{5,3},{7,1},{8,14},{10,12},{12... | collective-permute-start | bytes 294920 | tf_op jit(solution)/shard_map/ppermute | solution.py:346
  28.9 6.2 %collective-permute-start.6 = (bf16[384,128]{1,0:T(8,128)(2,1)S(1)}, bf16[384,128]{1,0:T(8,128)(2,1)S(1)}, u32[]{:S(2)}, u32[]{:S(2)}) collective-permute-start(bf16[384,128]{1,0:T(8,128)(2,1)S(1)} %shard_map.70.refs_1_), channel_id=1, source_target_pairs={{0,8},{8,0},{16,24},{24,16},{1,9},{9,1},{17,25},{25,17},{2,10},{10... | collective-permute-start | bytes 294920 | tf_op jit(solution)/shard_map/ppermute | solution.py:346
  32.3 4.6 %collective-permute-start.11 = (bf16[384,128]{1,0:T(8,128)(2,1)S(1)}, bf16[384,128]{1,0:T(8,128)(2,1)S(1)}, u32[]{:S(2)}, u32[]{:S(2)}) collective-permute-start(bf16[384,128]{1,0:T(8,128)(2,1)S(1)} %collective-permute-done.9.refs_5_), channel_id=1, source_target_pairs={{0,8},{8,0},{16,24},{24,16},{1,9},{9,1},{17,25},{25,17},{2,10},{10... | collective-permute-start | bytes 294920 | tf_op jit(solution)/shard_map/ppermute | solution.py:346
  33.1 4.9 %collective-permute-start.10 = (bf16[384,128]{1,0:T(8,128)(2,1)S(1)}, bf16[384,128]{1,0:T(8,128)(2,1)S(1)}, u32[]{:S(2)}, u32[]{:S(2)}) collective-permute-start(bf16[384,128]{1,0:T(8,128)(2,1)S(1)} %collective-permute-done.8.refs_4_), channel_id=1, source_target_pairs={{0,8},{8,0},{16,24},{24,16},{1,9},{9,1},{17,25},{25,17},{2,10},{10... | collective-permute-start | bytes 294920 | tf_op jit(solution)/shard_map/ppermute | solution.py:346
  34.3 4.7 %collective-permute-start.12 = (bf16[384,128]{1,0:T(8,128)(2,1)S(1)}, bf16[384,128]{1,0:T(8,128)(2,1)S(1)}, u32[]{:S(2)}, u32[]{:S(2)}) collective-permute-start(bf16[384,128]{1,0:T(8,128)(2,1)S(1)} %collective-permute-done.7.refs_3_), channel_id=1, source_target_pairs={{0,8},{8,0},{16,24},{24,16},{1,9},{9,1},{17,25},{25,17},{2,10},{10... | collective-permute-start | bytes 294920 | tf_op jit(solution)/shard_map/ppermute | solution.py:346
  35.2 4.8 %collective-permute-start.13 = (bf16[1920,128]{1,0:T(8,128)(2,1)S(1)}, bf16[1920,128]{1,0:T(8,128)(2,1)S(1)}, u32[]{:S(2)}, u32[]{:S(2)}) collective-permute-start(bf16[1920,128]{1,0:T(8,128)(2,1)S(1)} %shard_map.71.state_ref), channel_id=1, source_target_pairs={{0,1},{1,0},{2,3},{3,2},{4,5},{5,4},{6,7},{7,6},{8,9},{9,8},{10,11... | collective-permute-start | bytes 1474568 | tf_op jit(solution)/shard_map/ppermute | solution.py:346
  38.0 2.3 %collective-permute-start.14 = (bf16[768,128]{1,0:T(8,128)(2,1)S(1)}, bf16[768,128]{1,0:T(8,128)(2,1)S(1)}, u32[]{:S(2)}, u32[]{:S(2)}) collective-permute-start(bf16[768,128]{1,0:T(8,128)(2,1)S(1)} %shard_map.73.refs_0_), channel_id=1, source_target_pairs={{0,1},{1,0},{2,3},{3,2},{4,5},{5,4},{6,7},{7,6},{8,9},{9,8},{10,11... | collective-permute-start | bytes 589832 | tf_op jit(solution)/shard_map/ppermute | solution.py:346
  39.0 1.3 %collective-permute-start.15 = (bf16[384,128]{1,0:T(8,128)(2,1)S(1)}, bf16[384,128]{1,0:T(8,128)(2,1)S(1)}, u32[]{:S(2)}, u32[]{:S(2)}) collective-permute-start(bf16[384,128]{1,0:T(8,128)(2,1)S(1)} %collective-permute-done.12.refs_1_), channel_id=1, source_target_pairs={{0,1},{1,0},{2,3},{3,2},{4,5},{5,4},{6,7},{7,6},{8,9},{9,8},{10,11... | collective-permute-start | bytes 294920 | tf_op jit(solution)/shard_map/ppermute | solution.py:346
